TPU v7x, 256 devices: a whole 4x4x8 slice. The times are simulated.
256 devices in a mesh: seq: 32 (over z_lo, x, core), ch: 8 (over z_hi, y).
Axes of the slice: x: 4, y: 4, z: 8 (z_hi: 2, z_lo: 4; z = z_hi * 4 + z_lo), core: 2. Of those that a mesh axis runs over, the one named last changes fastest.
Arguments:
- queries: bfloat16 [16384, 4096], P('seq', 'ch'), may hold values from -6 to 6
- keys: bfloat16 [16384, 4096], P('seq', 'ch'), may hold values from -6 to 6
- values: bfloat16 [16384, 4096], P('seq', 'ch'), may hold values from -6 to 6
- filters: bfloat16 [16384, 4096], P('seq', 'ch'), may hold values from -2 to 2
- short_weights: float32 [3, 3, 4096], P(None, None, 'ch'), may hold values from -3 to 3
- skip_gain: float32 [4096], P('ch'), may hold values from -4 to 4
- stream: bfloat16 [16384, 4096], P('seq', 'ch'), may hold values from -25 to 25
- norm_gain: float32 [4096], P('ch'), may hold values from 0.25 to 1.75
Outputs:
- stream_out: bfloat16 [16384, 4096], P('seq', 'ch')
- normed: bfloat16 [16384, 4096], P('seq', 'ch')
All inputs are finite; a program needn't handle non-finite values.
Results may differ from a plain program's by a relative error of at most 0.014.
Values may be sent and summed in bfloat16 or wider, within the bound.
No kernel may reach another device: no remote copies, remote signals or barrier semaphores. Data moves between devices by JAX's collectives and lax.ppermute only.
A program may use at most 64 MiB of HBM per device.

v0:
```python
import math

import jax
import jax.numpy as jnp
from jax import lax
from jax.sharding import PartitionSpec as P

COLS = 128


def passed_along(block, axis, distance):
    devices = range(lax.axis_size(axis))
    route = [(i - distance, i) for i in devices if i - distance in devices]
    return lax.ppermute(block, axis, route)


def featurize(branch, previous, taps):
    extended = jnp.concatenate([previous, branch], 0).astype(jnp.float32)
    return taps[0] * extended[2:] + taps[1] * extended[1:-1] + taps[2] * extended[:-2]


def split_table(table):
    upper = table.astype(jnp.bfloat16)
    lower = (table - upper.astype(jnp.float32)).astype(jnp.bfloat16)
    return (upper, lower)


def split_product(pair, data):
    upper, lower = pair
    return jnp.dot(upper, data, preferred_element_type=jnp.float32) + jnp.dot(
        lower, data, preferred_element_type=jnp.float32
    )


def fine_dot(left, right):
    left_hi, left_lo = split_table(left)
    right_hi, right_lo = split_table(right)
    total = jnp.dot(left_hi, right_hi, preferred_element_type=jnp.float32)
    total = total + jnp.dot(left_lo, right_hi, preferred_element_type=jnp.float32)
    return total + jnp.dot(left_hi, right_lo, preferred_element_type=jnp.float32)


def spectral_tables(half_rows, cols):
    rows_all = 2 * half_rows
    total = rows_all * cols
    outer = jnp.arange(rows_all, dtype=jnp.int32)
    inner = jnp.arange(half_rows, dtype=jnp.int32)
    across = jnp.arange(cols, dtype=jnp.int32)
    first = (outer[:, None] * inner[None, :] % rows_all).astype(jnp.float32) * (
        2.0 * math.pi / rows_all
    )
    twist = (outer[:, None] * across[None, :] % total).astype(jnp.float32) * (2.0 * math.pi / total)
    second = (across[:, None] * across[None, :] % cols).astype(jnp.float32) * (2.0 * math.pi / cols)
    return (
        (jnp.cos(first), jnp.sin(first)),
        (jnp.cos(twist), jnp.sin(twist)),
        (jnp.cos(second), jnp.sin(second)),
    )


def to_blocks(series, half_rows, cols):
    width = series.shape[1]
    return (
        series.reshape(half_rows, cols, width).transpose(0, 2, 1).reshape(half_rows, width * cols)
    )


def forward(real_part, tables, width, cols):
    (first_cos, first_sin), (twist_cos, twist_sin), (second_cos, second_sin) = tables
    rows_all = first_cos.shape[0]
    cos_pair = split_table(first_cos)
    sin_pair = split_table(first_sin)
    section_re = split_product(cos_pair, real_part)
    section_im = -split_product(sin_pair, real_part)
    section_re = section_re.reshape(rows_all, width, cols)
    section_im = section_im.reshape(rows_all, width, cols)
    twist_c = twist_cos[:, None, :]
    twist_s = twist_sin[:, None, :]
    turned_re = section_re * twist_c + section_im * twist_s
    turned_im = section_im * twist_c - section_re * twist_s
    joined = jnp.concatenate([turned_re, turned_im], 2).reshape(rows_all * width, 2 * cols)
    table = jnp.concatenate(
        [
            jnp.concatenate([second_cos, -second_sin], 1),
            jnp.concatenate([second_sin, second_cos], 1),
        ],
        0,
    )
    result = fine_dot(joined, table).reshape(rows_all, width, 2 * cols)
    return (result[:, :, :cols], result[:, :, cols:])


def inverse(spec_re, spec_im, tables, width, cols):
    (first_cos, first_sin), (twist_cos, twist_sin), (second_cos, second_sin) = tables
    rows_all = first_cos.shape[0]
    half_rows = first_cos.shape[1]
    joined = jnp.concatenate([spec_re, spec_im], 2).reshape(rows_all * width, 2 * cols)
    table = jnp.concatenate(
        [
            jnp.concatenate([second_cos, second_sin], 1),
            jnp.concatenate([-second_sin, second_cos], 1),
        ],
        0,
    )
    result = fine_dot(joined, table).reshape(rows_all, width, 2 * cols)
    section_re = result[:, :, :cols]
    section_im = result[:, :, cols:]
    twist_c = twist_cos[:, None, :]
    twist_s = twist_sin[:, None, :]
    turned_re = (section_re * twist_c - section_im * twist_s).reshape(rows_all, width * cols)
    turned_im = (section_im * twist_c + section_re * twist_s).reshape(rows_all, width * cols)
    left = jnp.concatenate([first_cos.T, -first_sin.T], 1)
    right = jnp.concatenate([turned_re, turned_im], 0)
    signal = fine_dot(left, right) / (rows_all * cols)
    return (
        signal.reshape(half_rows, width, cols).transpose(0, 2, 1).reshape(half_rows * cols, width)
    )


def long_conv(product, filters):
    length, width = product.shape
    cols = COLS
    half_rows = length // cols
    tables = spectral_tables(half_rows, cols)
    signal_blocks = to_blocks(product, half_rows, cols)
    filter_blocks = to_blocks(filters, half_rows, cols)
    signal_re, signal_im = forward(signal_blocks, tables, width, cols)
    filter_re, filter_im = forward(filter_blocks, tables, width, cols)
    spec_re = signal_re * filter_re - signal_im * filter_im
    spec_im = signal_re * filter_im + signal_im * filter_re
    return inverse(spec_re, spec_im, tables, width, cols)


def shards(queries, keys, values, filters, short_weights, skip_gain, stream, norm_gain):
    tok_rows, width = queries.shape
    groups = lax.axis_size("seq")
    slab = width // groups
    start = lax.axis_index("seq") * slab
    skip_slab = lax.dynamic_slice_in_dim(skip_gain, start, slab, 0)
    edges = jnp.stack([queries[-2:], keys[-2:], values[-2:]], 0)
    previous = passed_along(edges, "seq", 1)
    qf = featurize(queries, previous[0], short_weights[0]).astype(jnp.bfloat16)
    key_f = featurize(keys, previous[1], short_weights[1])
    value_f = featurize(values, previous[2], short_weights[2])
    u_low = (key_f * value_f).astype(jnp.bfloat16)
    u_all, filter_all = (
        lax.all_to_all(u_low, "seq", split_axis=1, concat_axis=0, tiled=True),
        lax.all_to_all(filters, "seq", split_axis=1, concat_axis=0, tiled=True),
    )
    conv = long_conv(u_all, filter_all)
    y_low = (conv + skip_slab[None, :] * u_all.astype(jnp.float32)).astype(jnp.bfloat16)
    y_home = lax.all_to_all(y_low, "seq", split_axis=0, concat_axis=1, tiled=True)
    q_wide = lax.optimization_barrier(qf).astype(jnp.float32)
    gated = lax.optimization_barrier((q_wide * y_home.astype(jnp.float32)).astype(jnp.bfloat16))
    summed = stream.astype(jnp.float32) + gated.astype(jnp.float32)
    stream_out = summed.astype(jnp.bfloat16)
    squares = lax.psum(jnp.sum(summed * summed, axis=1), "ch")
    rms = jnp.sqrt(squares / (width * lax.axis_size("ch")) + 1e-05)
    normed = (summed / rms[:, None] * norm_gain[None, :]).astype(jnp.bfloat16)
    return (stream_out, normed)


def solution(mesh):
    in_specs = (
        P("seq", "ch"),
        P("seq", "ch"),
        P("seq", "ch"),
        P("seq", "ch"),
        P(None, None, "ch"),
        P("ch"),
        P("seq", "ch"),
        P("ch"),
    )
    out_specs = (P("seq", "ch"), P("seq", "ch"))
    return jax.shard_map(shards, mesh=mesh, in_specs=in_specs, out_specs=out_specs, check_vma=False)
```

profile of v0, /device:TPU:1, one launch (start us, length us, event | category | flops | bytes accessed | tf_op | source)
XLA Modules:
  0.0 134.9 jit_solution(2420930341898109173)
XLA Ops:
  0.7 0.8 slice_bitcast_fusion.5
  1.4 0.7 slice_bitcast_fusion.3
  2.4 4.5 %collective-permute-start = (bf16[3,2,512]{1,2,0:T(8,128)(2,1)S(1)}, bf16[3,2,512]{1,2,0:T(8,128)(2,1)S(1)}, u32[]{:S(2)}, u32[]{:S(2)}) collective-permute-start(bf16[3,2,512]{1,2,0:T(8,128)(2,1)S(1)} %copy.27), channel_id=1, source_target_pairs={{0,8},{8,16},{16,24},{24,32},{32,40},{40,48},{48,56},{56,64},{64,7... | collective-permute-start | bytes 18440 | tf_op jit(solution)/shard_map/ppermute | solution.py:14
  7.0 2.0 %copy.33 = bf16[512,512]{0,1:T(8,128)(2,1)} copy(bf16[512,512]{1,0:T(8,128)(2,1)} %param.11) | data formatting | bytes 1048576 | tf_op args[3]
  9.0 8.3 %all-to-all-start.1 = ((bf16[512,32,16]{0,2,1:T(8,128)(2,1)}), bf16[512,32,16]{0,2,1:T(8,128)(2,1)S(1)}, u32[]{:S(2)}, u32[]{:S(2)}) async-start(bf16[512,32,16]{0,2,1:T(8,128)(2,1)} %bitcast.22), calls=%async_computation.1 | async-start | bytes 1048576 | tf_op jit(solution)/shard_map/all_to_all | solution.py:148
  17.3 1.2 fusion.58
  18.6 1.2 sine_negate_fusion
  20.8 0.8 dynamic_slice.3
  21.6 0.7 slice_bitcast_fusion.1
  22.9 2.6 %fusion.13 = bf16[512,512]{0,1:T(8,128)(2,1)} fusion(f32[514,512]{0,1:T(8,128)S(1)} %maximum_convert_fusion.2, f32[514,512]{0,1:T(8,128)S(1)} %maximum_convert_fusion.1, f32[512]{0:T(512)S(1)} %bitcast.127, f32[512]{0:T(512)S(1)} %bitcast.128, f32[512]{0:T(512)S(1)} %bitcast.124, f32[512]{0:T(512)S(1)} %bitcast.125, f32[512]{0:T(512)S(1)} %bitcast.126, ...), kind=kLoop, calls=%fused_computation.49 | loop fusion | flops 3145728 | bytes 6828032 | tf_op jit(solution)/shard_map/convert_element_type | solution.py:145
  25.4 8.3 %all-to-all-done.1 = bf16[512,32,16]{0,2,1:T(8,128)(2,1)S(1)} async-done(((bf16[512,32,16]{0,2,1:T(8,128)(2,1)}), bf16[512,32,16]{0,2,1:T(8,128)(2,1)S(1)}, u32[]{:S(2)}, u32[]{:S(2)}) %all-to-all-start.1) | async-done | bytes 524320 | tf_op jit(solution)/shard_map/all_to_all | solution.py:148
  33.7 4.2 %all-to-all-start = ((bf16[512,32,16]{0,2,1:T(8,128)(2,1)}), bf16[512,32,16]{0,2,1:T(8,128)(2,1)S(1)}, u32[]{:S(2)}, u32[]{:S(2)}) async-start(bf16[512,32,16]{0,2,1:T(8,128)(2,1)} %bitcast.15), calls=%async_computation | async-start | bytes 1048576 | tf_op jit(solution)/shard_map/all_to_all | solution.py:147
  38.8 0.8 fusion.68
  39.7 0.8 convolution_add_fusion.7
  40.5 1.5 %reshape.155 = f32[4096,128]{1,0:T(8,128)} reshape(f32[256,2048]{1,0:T(8,128)S(1)} %convolution_add_fusion.7) | data formatting | bytes 4194304 | tf_op jit(solution)/shard_map/reshape | solution.py:75
  42.0 0.8 fusion.64
  42.9 0.8 fusion.3
  43.7 1.5 %reshape.156 = f32[4096,128]{1,0:T(8,128)} reshape(f32[256,2048]{1,0:T(8,128)S(1)} %fusion.3) | data formatting | bytes 4194304 | tf_op jit(solution)/shard_map/reshape | solution.py:76
  45.2 9.1 %all-to-all-done = bf16[512,32,16]{0,2,1:T(8,128)(2,1)S(1)} async-done(((bf16[512,32,16]{0,2,1:T(8,128)(2,1)}), bf16[512,32,16]{0,2,1:T(8,128)(2,1)S(1)}, u32[]{:S(2)}, u32[]{:S(2)}) %all-to-all-start) | async-done | bytes 524320 | tf_op jit(solution)/shard_map/all_to_all | solution.py:147
  55.2 0.8 fusion.66
  56.1 0.8 fusion.70
  56.9 2.2 %fusion.4 = f32[256,2048]{1,0:T(8,128)} fusion(f32[256,2048]{1,0:T(8,128)S(1)} %fusion.66, bf16[128,2048]{0,1:T(8,128)(2,1)S(1)} %bitcast.111), kind=kOutput, calls=%fused_computation.29 | convolution fusion | flops 135856128 | bytes 4718592 | tf_op jit(solution)/shard_map/dot_general | solution.py:30
  59.1 2.7 %reshape.151 = f32[4096,128]{1,0:T(8,128)} reshape(f32[256,2048]{1,0:T(8,128)} %fusion.4) | data formatting | bytes 4194304 | tf_op jit(solution)/shard_map/reshape | solution.py:76
  61.8 2.2 %convolution_add_fusion.9 = f32[256,2048]{1,0:T(8,128)} fusion(f32[256,2048]{1,0:T(8,128)S(1)} %fusion.70, bf16[128,2048]{0,1:T(8,128)(2,1)S(1)} %bitcast.112), kind=kOutput, calls=%fused_computation.30 | convolution fusion | flops 135331840 | bytes 4718592 | tf_op jit(solution)/shard_map/dot_general | solution.py:30
  64.1 2.9 %reshape.150 = f32[4096,128]{1,0:T(8,128)} reshape(f32[256,2048]{1,0:T(8,128)} %convolution_add_fusion.9) | data formatting | bytes 4194304 | tf_op jit(solution)/shard_map/reshape | solution.py:75
  67.0 3.7 %fusion.6 = (f32[4096,128]{1,0:T(8,128)S(1)}, f32[4096,128]{1,0:T(8,128)S(1)}, f32[4096,128]{1,0:T(8,128)S(1)}, f32[4096,128]{1,0:T(8,128)S(1)}) fusion(f32[4096,128]{1,0:T(8,128)} %reshape.150, f32[4096,128]{1,0:T(8,128)} %reshape.151, f32[256,128]{1,0:T(8,128)S(1)} %copy-done.2, f32[256,128]{1,0:T(8,128)S(1)} %copy-done.3, f32[4096,128]{1,0:T(8,128)S(1)} %copy-done, ...), kind=kLoop, calls=%fused_computation.34 | loop fusion | flops 6291456 | bytes 17039360 | tf_op jit(solution)/shard_map/add | solution.py:79
  70.7 0.7 fusion.25
  71.4 0.7 convolution_add_fusion.5
  72.1 0.8 convolution_add_fusion.4
  72.9 0.7 fusion.29
  73.6 0.7 convolution_add_fusion.3
  74.3 0.8 convolution_add_fusion.2
  75.1 0.5 multiply_subtract_fusion.1
  76.0 1.0 fusion
  77.0 0.7 fusion.128
  77.7 0.7 convolution_add_fusion.1
  78.5 0.7 convolution_add_fusion
  79.2 0.6 multiply_add_fusion
  79.7 0.9 bitcast_dynamic-update-slice_fusion.1
  80.6 0.9 bitcast_dynamic-update-slice_fusion
  82.4 0.5 fusion.10
  83.2 1.4 %fusion.21 = bf16[32,512,16]{1,2,0:T(8,128)(2,1)} fusion(f32[32,512,16]{1,0,2:T(8,128)S(1)} %reshape.163, f32[16]{0:T(128)S(1)} %dynamic_slice.3, bf16[512,32,16]{0,2,1:T(8,128)(2,1)S(1)} %all-to-all-done), kind=kLoop, calls=%fused_computation.67 | loop fusion | flops 1048576 | bytes 2097216 | tf_op jit(solution)/shard_map/convert_element_type | solution.py:151
  84.6 4.3 %all-to-all-start.2 = ((bf16[32,512,16]{1,2,0:T(8,128)(2,1)}), bf16[32,512,16]{1,2,0:T(8,128)(2,1)S(1)}, u32[]{:S(2)}, u32[]{:S(2)}) async-start(bf16[32,512,16]{1,2,0:T(8,128)(2,1)} %fusion.21), calls=%async_computation.2 | async-start | bytes 1048576 | tf_op jit(solution)/shard_map/all_to_all | solution.py:152
  89.7 0.9 fusion.18
  90.7 14.7 %all-to-all-done.2 = bf16[32,512,16]{1,2,0:T(8,128)(2,1)S(1)} async-done(((bf16[32,512,16]{1,2,0:T(8,128)(2,1)}), bf16[32,512,16]{1,2,0:T(8,128)(2,1)S(1)}, u32[]{:S(2)}, u32[]{:S(2)}) %all-to-all-start.2) | async-done | bytes 524320 | tf_op jit(solution)/shard_map/all_to_all | solution.py:152
  105.7 26.9 %psum.7 = f32[512]{0:T(512)S(1)} all-reduce(f32[512]{0:T(512)S(1)} %multiply_reduce_fusion), channel_id=1, replica_groups=mesh['seq'=32,'ch'=8] {'ch'}, use_global_device_ids=true, to_apply=%region_1.2 | all-reduce | flops 512 | bytes 4096 | tf_op jit(solution)/shard_map/psum | solution.py:157
  132.9 1.0 copy.38
  133.9 1.0 copy.39
  (50 shorter events, 6.5 us)
Async XLA Ops:
  0.6 19.7 %copy-start.4 = (bf16[512,512]{1,0:T(8,128)(2,1)S(1)}, bf16[512,512]{1,0:T(8,128)(2,1)}, u32[]{:S(2)}) copy-start(bf16[512,512]{1,0:T(8,128)(2,1)} %param.9) | copy-start | bytes 1572868
  0.6 19.1 %copy-start.9 = (f32[3,3,512]{2,1,0:T(4,128)S(1)}, f32[3,3,512]{2,1,0:T(4,128)}, u32[]{:S(2)}) copy-start(f32[3,3,512]{2,1,0:T(4,128)} %param.12) | copy-start | bytes 55300
  2.2 18.4 %copy-start.5 = (bf16[512,512]{1,0:T(8,128)(2,1)S(1)}, bf16[512,512]{1,0:T(8,128)(2,1)}, u32[]{:S(2)}) copy-start(bf16[512,512]{1,0:T(8,128)(2,1)} %param.10) | copy-start | bytes 1572868
  2.4 19.1 %collective-permute-start = (bf16[3,2,512]{1,2,0:T(8,128)(2,1)S(1)}, bf16[3,2,512]{1,2,0:T(8,128)(2,1)S(1)}, u32[]{:S(2)}, u32[]{:S(2)}) collective-permute-start(bf16[3,2,512]{1,2,0:T(8,128)(2,1)S(1)} %copy.27), channel_id=1, source_target_pairs={{0,8},{8,16},{16,24},{24,32},{32,40},{40,48},{48,56},{56,64},{64,7... | collective-permute-start | bytes 18440 | tf_op jit(solution)/shard_map/ppermute | solution.py:14
  9.0 24.7 %all-to-all-start.1 = ((bf16[512,32,16]{0,2,1:T(8,128)(2,1)}), bf16[512,32,16]{0,2,1:T(8,128)(2,1)S(1)}, u32[]{:S(2)}, u32[]{:S(2)}) async-start(bf16[512,32,16]{0,2,1:T(8,128)(2,1)} %bitcast.22), calls=%async_computation.1 | async-start | bytes 1048576 | tf_op jit(solution)/shard_map/all_to_all | solution.py:148
  33.7 20.6 %all-to-all-start = ((bf16[512,32,16]{0,2,1:T(8,128)(2,1)}), bf16[512,32,16]{0,2,1:T(8,128)(2,1)S(1)}, u32[]{:S(2)}, u32[]{:S(2)}) async-start(bf16[512,32,16]{0,2,1:T(8,128)(2,1)} %bitcast.15), calls=%async_computation | async-start | bytes 1048576 | tf_op jit(solution)/shard_map/all_to_all | solution.py:147
  64.0 2.9 %copy-start = (f32[4096,128]{1,0:T(8,128)S(1)}, f32[4096,128]{1,0:T(8,128)}, u32[]{:S(2)}) copy-start(f32[4096,128]{1,0:T(8,128)} %reshape.155) | copy-start | bytes 6291460
  64.0 2.9 %copy-start.2 = (f32[256,128]{1,0:T(8,128)S(1)}, f32[256,128]{1,0:T(8,128)}, u32[]{:S(2)}) copy-start(f32[256,128]{1,0:T(8,128)} %get-tuple-element.34) | copy-start | bytes 393220
  64.1 2.9 %copy-start.3 = (f32[256,128]{1,0:T(8,128)S(1)}, f32[256,128]{1,0:T(8,128)}, u32[]{:S(2)}) copy-start(f32[256,128]{1,0:T(8,128)} %get-tuple-element.35) | copy-start | bytes 393220
  80.6 0.9 copy-start.1
  83.2 5.8 %copy-start.6 = (bf16[512,512]{1,0:T(8,128)(2,1)S(1)}, bf16[512,512]{1,0:T(8,128)(2,1)}, u32[]{:S(2)}) copy-start(bf16[512,512]{1,0:T(8,128)(2,1)} %param.8) | copy-start | bytes 1572868
  83.2 6.0 %copy-start.7 = (bf16[512,512]{1,0:T(8,128)(2,1)S(1)}, bf16[512,512]{1,0:T(8,128)(2,1)}, u32[]{:S(2)}) copy-start(bf16[512,512]{1,0:T(8,128)(2,1)} %param.14) | copy-start | bytes 1572868
  84.6 4.8 %copy-start.8 = (bf16[2,512]{0,1:T(8,128)(2,1)S(1)}, bf16[2,512]{0,1:T(8,128)(2,1)}, u32[]{:S(2)}) copy-start(bf16[2,512]{0,1:T(8,128)(2,1)} %get-tuple-element.20) | copy-start | bytes 6148
  84.6 20.7 %all-to-all-start.2 = ((bf16[32,512,16]{1,2,0:T(8,128)(2,1)}), bf16[32,512,16]{1,2,0:T(8,128)(2,1)S(1)}, u32[]{:S(2)}, u32[]{:S(2)}) async-start(bf16[32,512,16]{1,2,0:T(8,128)(2,1)} %fusion.21), calls=%async_computation.2 | async-start | bytes 1048576 | tf_op jit(solution)/shard_map/all_to_all | solution.py:152
  90.7 42.0 %copy-start.10 = (f32[512]{0:T(512)S(1)}, f32[512]{0:T(512)}, u32[]{:S(2)}) copy-start(f32[512]{0:T(512)} %param.15) | copy-start | bytes 6148
where the time goes:
time: 137 us; the launch traced here: 135 us
  waiting for transfers between devices  32 us (23%)
  blocking collectives  26.9 us (20%)
  starting transfers between devices  21.3 us (16%)
  local copies, waits for them, and re-layouts  20.6 us (15%)
  matrix products  17.4 us (13%)
  other arithmetic  15.6 us (11%)
    psum x1, blocking collectives, shards(): squares = lax.psum(jnp.sum(summed * summed, axis=1), 'ch')  26.9 us
    all_to_all x1, waiting for transfers between devices, shards(): lax.all_to_all(y_low, 'seq', split_axis=0, concat_axis=1, tiled=True)  14.7 us
    all_to_all x1, waiting for transfers between devices, shards(): lax.all_to_all(u_low, 'seq', split_axis=1, concat_axis=0, tiled=True)  9.07 us
    all_to_all x1, starting transfers between devices, shards(): lax.all_to_all(filters, 'seq', split_axis=1, concat_axis=0, tiled=True)  8.33 us
    all_to_all x1, waiting for transfers between devices, shards(): lax.all_to_all(filters, 'seq', split_axis=1, concat_axis=0, tiled=True)  8.3 us
    dot_general x4, matrix products, split_product(): jnp.dot(lower, data, preferred_element_type=jnp.float32)  6.17 us
    unnamed x30, local copies, waits for them, and re-layouts  5.85 us
    ppermute x1, starting transfers between devices, passed_along(): return lax.ppermute(block, axis, route)  4.51 us
  transfers between devices with their start and end apart: 4, of which 3 were waited for; matrix products, arithmetic and copies ran while one was open for 14% of the time, Pallas kernels for 0%

commit v1 on v0

v1 whole, which is shorter than its diff:
```python
import jax
import jax.numpy as jnp
import numpy as np
from jax import lax
from jax.experimental import pallas as pl
from jax.experimental.pallas import tpu as pltpu
from jax.sharding import PartitionSpec as P

LANE = 128
EDGE = 16
GROUP = 4
VMEM_LIMIT = 48 * 1024 * 1024


def params():
    return pltpu.CompilerParams(vmem_limit_bytes=VMEM_LIMIT)


def tables():
    n = LANE * LANE
    a = np.arange(LANE, dtype=np.float64)
    first = -2.0 * np.pi * np.outer(a + 0.25, a) / LANE
    twist = -2.0 * np.pi * np.outer(a + 0.25, a) / n
    second = -2.0 * np.pi * np.outer(a, a) / LANE
    t1 = np.concatenate([np.cos(first), np.sin(first)], 0)
    cos2, sin2 = np.cos(second), np.sin(second)
    t2 = np.block([[cos2, sin2], [-sin2, cos2]])
    t2_inv = np.block([[cos2, -sin2], [sin2, cos2]])
    t1_inv = np.concatenate([np.cos(first).T, np.sin(first).T], 1) / n
    low = [jnp.asarray(t, jnp.bfloat16) for t in (t1, t2, t2_inv, t1_inv)]
    return (*low, jnp.asarray(np.cos(twist), jnp.float32), jnp.asarray(np.sin(twist), jnp.float32))


def edges_kernel(q_ref, k_ref, v_ref, out_ref):
    out_ref[0] = q_ref[...]
    out_ref[1] = k_ref[...]
    out_ref[2] = v_ref[...]


def last_rows(q, k, v):
    rows, width = q.shape
    spec = pl.BlockSpec((EDGE, width), lambda i: (rows // EDGE - 1, 0))
    return pl.pallas_call(
        edges_kernel,
        grid=(1,),
        in_specs=[spec] * 3,
        out_specs=pl.BlockSpec((3, EDGE, width), lambda i: (0, 0, 0)),
        out_shape=jax.ShapeDtypeStruct((3, EDGE, width), q.dtype),
        compiler_params=params(),
    )(q, k, v)


def put_turned(out_ref, j, block):
    depth = out_ref.shape[2]
    per = LANE // depth
    for g in range(block.shape[1] // LANE):
        turned = block[:, g * LANE : (g + 1) * LANE].T
        out_ref[g * per : (g + 1) * per, j] = turned.reshape(per, depth, LANE).astype(out_ref.dtype)


def turn_kernel(x_ref, out_ref):
    for j in range(out_ref.shape[1]):
        put_turned(out_ref, j, x_ref[j * LANE : (j + 1) * LANE, :].astype(jnp.float32))


def split_shape(x, groups):
    rows, width = x.shape
    return jax.ShapeDtypeStruct((groups, rows // LANE, width // groups, LANE), x.dtype)


def turn(x, groups):
    return pl.pallas_call(
        turn_kernel, out_shape=split_shape(x, groups), compiler_params=params()
    )(x)


def extend(ext_ref, x_ref, edge):
    rows = x_ref.shape[0]
    ext_ref[0:8, :] = edge[EDGE - 8 :, :].astype(jnp.float32)
    ext_ref[8 : 8 + rows, :] = x_ref[...].astype(jnp.float32)


def taps_of(ext_ref, taps, start, size):
    return (
        taps[0:1, :] * ext_ref[start + 8 : start + 8 + size, :]
        + taps[1:2, :] * ext_ref[start + 7 : start + 7 + size, :]
        + taps[2:3, :] * ext_ref[start + 6 : start + 6 + size, :]
    )


def product_kernel(k_ref, v_ref, edge_ref, taps_ref, out_ref, k_ext, v_ext):
    extend(k_ext, k_ref, edge_ref[1])
    extend(v_ext, v_ref, edge_ref[2])
    for j in range(out_ref.shape[1]):
        kf = taps_of(k_ext, taps_ref[1], j * LANE, LANE)
        vf = taps_of(v_ext, taps_ref[2], j * LANE, LANE)
        put_turned(out_ref, j, kf * vf)


def product(k, v, edge, taps, groups):
    rows, width = k.shape
    ext = pltpu.VMEM((rows + 8, width), jnp.float32)
    return pl.pallas_call(
        product_kernel,
        out_shape=split_shape(k, groups),
        scratch_shapes=[ext, ext],
        compiler_params=params(),
    )(k, v, edge, taps)


def gate_kernel(q_ref, edge_ref, taps_ref, out_ref, q_ext):
    extend(q_ext, q_ref, edge_ref[0])
    for j in range(out_ref.shape[0] // LANE):
        qf = taps_of(q_ext, taps_ref[0], j * LANE, LANE)
        out_ref[j * LANE : (j + 1) * LANE, :] = qf.astype(out_ref.dtype)


def gate(q, edge, taps):
    rows, width = q.shape
    return pl.pallas_call(
        gate_kernel,
        out_shape=jax.ShapeDtypeStruct(q.shape, q.dtype),
        scratch_shapes=[pltpu.VMEM((rows + 8, width), jnp.float32)],
        compiler_params=params(),
    )(q, edge, taps)


def mix(table, data):
    return jnp.dot(table, data, preferred_element_type=jnp.float32)


def conv_kernel(u_ref, f_ref, skip_ref, t1, t2, t2_inv, t1_inv, tw_c, tw_s, y_ref, u_wide, f_wide, y_wide):
    depth = skip_ref.shape[0]
    u_wide[...] = u_ref[...].astype(jnp.float32)
    f_wide[...] = f_ref[...].astype(jnp.float32)
    low = jnp.bfloat16

    def part(x, i):
        return x[:, i * LANE : (i + 1) * LANE]

    for start in range(0, depth, GROUP):
        chans = range(start, start + GROUP)
        rows = [pl.ds(c, LANE, stride=depth) for c in chans]
        data = [u_wide[r, :].astype(low) for r in rows] + [f_wide[r, :].astype(low) for r in rows]
        first = mix(t1[...], jnp.concatenate(data, 1))
        turned = []
        for i in range(2 * GROUP):
            re, im = part(first[:LANE], i), part(first[LANE:], i)
            c, s = tw_c[...], tw_s[...]
            turned.append(jnp.concatenate([re * c - im * s, re * s + im * c], 1).astype(low))
        spec = mix(jnp.concatenate(turned, 0), t2[...])
        prod = []
        for i in range(GROUP):
            a = spec[i * LANE : (i + 1) * LANE]
            b = spec[(GROUP + i) * LANE : (GROUP + i + 1) * LANE]
            ar, ai, br, bi = a[:, :LANE], a[:, LANE:], b[:, :LANE], b[:, LANE:]
            prod.append(jnp.concatenate([ar * br - ai * bi, ar * bi + ai * br], 1).astype(low))
        back = mix(jnp.concatenate(prod, 0), t2_inv[...])
        cols = []
        for i in range(GROUP):
            v = back[i * LANE : (i + 1) * LANE]
            re, im = v[:, :LANE], v[:, LANE:]
            c, s = tw_c[...], tw_s[...]
            cols.append(jnp.concatenate([re * c + im * s, im * c - re * s], 0).astype(low))
        conv = mix(t1_inv[...], jnp.concatenate(cols, 1))
        for i, r in enumerate(rows):
            y_wide[r, :] = part(conv, i)
    shape = (LANE, depth, LANE)
    y = y_wide[...].reshape(shape) + skip_ref[...][None] * u_wide[...].reshape(shape)
    y_ref[...] = y.reshape(y_ref.shape).astype(y_ref.dtype)


def long_conv(u, f, skip):
    wide = pltpu.VMEM(u.shape, jnp.float32)
    return pl.pallas_call(
        conv_kernel,
        out_shape=jax.ShapeDtypeStruct(u.shape, u.dtype),
        scratch_shapes=[wide] * 3,
        compiler_params=params(),
    )(u, f, skip, *tables())


def join_kernel(y_ref, qf_ref, stream_ref, out_ref, sum_ref, sq_ref):
    groups, slabs, depth, _ = y_ref.shape
    per = LANE // depth
    sq_ref[...] = jnp.zeros_like(sq_ref)
    for j in range(slabs):
        rows = slice(j * LANE, (j + 1) * LANE)
        squares = jnp.zeros((LANE, LANE), jnp.float32)
        for g in range(groups // per):
            cols = slice(g * LANE, (g + 1) * LANE)
            y = y_ref[g * per : (g + 1) * per, j].reshape(LANE, LANE).astype(jnp.float32).T
            gated = (qf_ref[rows, cols].astype(jnp.float32) * y).astype(jnp.bfloat16)
            summed = stream_ref[rows, cols].astype(jnp.float32) + gated.astype(jnp.float32)
            out_ref[rows, cols] = summed.astype(out_ref.dtype)
            sum_ref[rows, cols] = summed
            squares = squares + summed * summed
        total = jnp.sum(squares.T, axis=0, keepdims=True)
        for d in range(sq_ref.shape[0]):
            sq_ref[d, j : j + 1, :] = total


def join(y, qf, stream, fan):
    return pl.pallas_call(
        join_kernel,
        out_shape=(
            jax.ShapeDtypeStruct(stream.shape, stream.dtype),
            jax.ShapeDtypeStruct(stream.shape, jnp.float32),
            jax.ShapeDtypeStruct((fan, 8, LANE), jnp.float32),
        ),
        compiler_params=params(),
    )(y, qf, stream)


def norm_kernel(channels, sum_ref, sq_ref, gain_ref, out_ref):
    squares = jnp.sum(sq_ref[...], axis=0)
    scale = 1.0 / jnp.sqrt(squares / channels + 1e-05)
    for j in range(out_ref.shape[0] // LANE):
        rows = slice(j * LANE, (j + 1) * LANE)
        column = jnp.broadcast_to(scale[j : j + 1, :], (LANE, LANE)).T
        for g in range(out_ref.shape[1] // LANE):
            cols = slice(g * LANE, (g + 1) * LANE)
            out_ref[rows, cols] = (sum_ref[rows, cols] * column * gain_ref[:, cols]).astype(out_ref.dtype)


def norm(summed, squares, gain):
    channels = summed.shape[1] * squares.shape[0]

    def kernel(*refs):
        norm_kernel(channels, *refs)

    return pl.pallas_call(
        kernel,
        out_shape=jax.ShapeDtypeStruct(summed.shape, jnp.bfloat16),
        compiler_params=params(),
    )(summed, squares, gain[None, :])


def exchange(x, axis):
    return lax.all_to_all(x, axis, split_axis=0, concat_axis=0, tiled=True)


def shards(queries, keys, values, filters, short_weights, skip_gain, stream, norm_gain):
    groups = lax.axis_size("seq")
    fan = lax.axis_size("ch")
    rows, width = queries.shape
    slab = width // groups
    edge = last_rows(queries, keys, values)
    edge = lax.ppermute(edge, "seq", [(i, i + 1) for i in range(groups - 1)])
    f_all = exchange(turn(filters, groups), "seq")
    u_all = exchange(product(keys, values, edge, short_weights, groups), "seq")
    qf = gate(queries, edge, short_weights)
    skip = lax.dynamic_slice_in_dim(skip_gain, lax.axis_index("seq") * slab, slab, 0)
    skip = jnp.broadcast_to(skip[:, None], (slab, LANE))
    flat = (groups * rows // LANE * slab, LANE)
    y = long_conv(u_all.reshape(flat), f_all.reshape(flat), skip)
    y_home = exchange(y.reshape(u_all.shape), "seq")
    stream_out, summed, squares = join(y_home, qf, stream, fan)
    normed = norm(summed, exchange(squares, "ch"), norm_gain)
    return (stream_out, normed)


def solution(mesh):
    wide = P("seq", "ch")
    in_specs = (wide, wide, wide, wide, P(None, None, "ch"), P("ch"), wide, P("ch"))
    return jax.shard_map(shards, mesh=mesh, in_specs=in_specs, out_specs=(wide, wide), check_vma=False)
```

time: 137 us -> 96.5 us (0.70); the launches traced: 135 us -> 96 us
  local copies, waits for them, and re-layouts: 20.6 us -> 2.59 us
  matrix products: 17.4 us -> 0 us
  other arithmetic: 15.6 us -> 0 us
  waiting for transfers between devices: 32 us -> 42.5 us
  blocking collectives: 26.9 us -> 16.9 us
  Pallas kernels: 0 us -> 9.9 us
  starting transfers between devices: 21.3 us -> 23.3 us
    psum x1 -> x0, blocking collectives: 26.9 us -> none  [shards(): squares = lax.psum(jnp.sum(summed * summed, axis=1), 'ch')]
    dot_general x20 -> x0, matrix products: 17.4 us -> none  [the longest x4 6.17 us: split_product(): jnp.dot(lower, data, preferred_element_type=jnp.float32)]
    all_to_all x0 -> x1, blocking collectives: none -> 16.9 us  [exchange(): return lax.all_to_all(x, axis, split_axis=0, concat_axis=0, tiled=True)]
    pallas_call x0 -> x7, Pallas kernels: none -> 9.9 us  [the longest x1 4.25 us: long_conv(): pl.pallas_call(conv_kernel, out_shape=jax.ShapeDtypeStruct(u.shape, u.dty...]
    reshape x8 -> x0, local copies, waits for them, and re-layouts: 9.5 us -> none  [the longest x2 4.43 us: forward(): section_re = section_re.reshape(rows_all, width, cols)]
    all_to_all x3, waiting for transfers between devices: 32 us -> 41.1 us  [exchange(): return lax.all_to_all(x, axis, split_axis=0, concat_axis=0, tiled=True)]
    convert_element_type x9 -> x0, other arithmetic: 7.23 us -> none  [the longest x1 2.56 us: shards(): u_low = (key_f * value_f).astype(jnp.bfloat16)]
    add x2 -> x0, other arithmetic: 4.28 us -> none  [the longest x1 3.73 us: forward(): turned_re = section_re * twist_c + section_im * twist_s]
  transfers between devices with their start and end apart: 4 -> 4, of which waited for: 3 -> 4; matrix products, arithmetic and copies ran while one was open for 14% -> 1% of each run, Pallas kernels for 0% -> 2%
where the time goes in v1:
time: 96.5 us; the launch traced here: 96 us
  waiting for transfers between devices  42.5 us (44%)
  starting transfers between devices  23.3 us (24%)
  blocking collectives  16.9 us (18%)
  Pallas kernels  9.9 us (10%)
  local copies, waits for them, and re-layouts  2.59 us (3%)
    all_to_all x3, waiting for transfers between devices, exchange(): return lax.all_to_all(x, axis, split_axis=0, concat_axis=0, tiled=True)  41.1 us
    all_to_all x3, starting transfers between devices, exchange(): return lax.all_to_all(x, axis, split_axis=0, concat_axis=0, tiled=True)  19.7 us
    all_to_all x1, blocking collectives, exchange(): return lax.all_to_all(x, axis, split_axis=0, concat_axis=0, tiled=True)  16.9 us
    pallas_call x1, Pallas kernels, long_conv(): pl.pallas_call(conv_kernel, out_shape=jax.ShapeDtypeStruct(u.shape, u.dty...  4.25 us
    ppermute x1, starting transfers between devices, shards(): edge = lax.ppermute(edge, 'seq', [(i, i + 1) for i in range(groups - 1)])  3.54 us
  transfers between devices with their start and end apart: 4, of which 4 were waited for; matrix products, arithmetic and copies ran while one was open for 1% of the time, Pallas kernels for 2%

profile of v1, /device:TPU:1, one launch (start us, length us, event | category | flops | bytes accessed | tf_op | source)
XLA Modules:
  0.0 96.0 jit_solution(15965688772857880435)
XLA Ops:
  0.6 0.0 copy-start.4
  0.6 1.0 %copy-done.4 = bf16[512,512]{1,0:T(8,128)(2,1)S(1)} copy-done((bf16[512,512]{1,0:T(8,128)(2,1)S(1)}, bf16[512,512]{1,0:T(8,128)(2,1)}, u32[]{:S(2)}) %copy-start.4) | copy-done | bytes 524312
  1.7 0.0 copy-start.2
  1.7 1.0 %shard_map.151 = bf16[32,4,16,128]{3,2,1,0:T(8,128)(2,1)} custom-call(bf16[512,512]{1,0:T(8,128)(2,1)S(1)} %copy-done.4), custom_call_target="tpu_custom_call" | custom-call | tf_op jit(solution)/shard_map/pallas_call | solution.py:72
  2.7 0.0 copy-start
  2.7 0.0 copy-start.1
  2.7 10.1 %all-to-all-start.1 = ((bf16[32,4,16,128]{3,2,1,0:T(8,128)(2,1)}), bf16[32,4,16,128]{3,2,1,0:T(8,128)(2,1)S(1)}, u32[]{:S(2)}, u32[]{:S(2)}) async-start(bf16[32,4,16,128]{3,2,1,0:T(8,128)(2,1)} %shard_map.151), calls=%async_computation.1 | async-start | bytes 1048576 | tf_op jit(solution)/shard_map/all_to_all | solution.py:240
  12.8 0.0 copy-done.2
  12.8 0.0 copy-done
  12.9 0.0 copy-done.1
  12.9 0.0 copy-start.7
  12.9 3.5 %collective-permute-start = (bf16[3,16,512]{2,1,0:T(8,128)(2,1)S(1)}, bf16[3,16,512]{2,1,0:T(8,128)(2,1)S(1)}, u32[]{:S(2)}, u32[]{:S(2)}) collective-permute-start(bf16[3,16,512]{2,1,0:T(8,128)(2,1)S(1)} %shard_map.149), channel_id=1, source_target_pairs={{0,8},{8,16},{16,24},{24,32},{32,40},{40,48},{48,56},{56,64},{64,7... | collective-permute-start | bytes 147464 | tf_op jit(solution)/shard_map/ppermute | solution.py:249
  16.4 1.4 %collective-permute-done.edge_ref = bf16[3,16,512]{2,1,0:T(8,128)(2,1)S(1)} collective-permute-done((bf16[3,16,512]{2,1,0:T(8,128)(2,1)S(1)}, bf16[3,16,512]{2,1,0:T(8,128)(2,1)S(1)}, u32[]{:S(2)}, u32[]{:S(2)}) %collective-permute-start) | collective-permute-done | bytes 49184 | tf_op jit(solution)/shard_map/ppermute | solution.py:249
  17.9 0.0 copy-done.7
  17.9 1.8 %shard_map.150 = bf16[32,4,16,128]{3,2,1,0:T(8,128)(2,1)} custom-call(bf16[512,512]{1,0:T(8,128)(2,1)S(1)} %copy-done, bf16[512,512]{1,0:T(8,128)(2,1)S(1)} %copy-done.1, bf16[3,16,512]{2,1,0:T(8,128)(2,1)S(1)} %collective-permute-done.edge_ref, f32[3,3,512]{2,1,0:T(4,128)S(1)} %copy-done.7), custom_call_target="tpu_custom_call" | custom-call | tf_op jit(solution)/shard_map/pallas_call | solution.py:103
  19.6 0.0 copy-start.5
  19.6 0.0 copy-start.6
  19.6 9.6 %all-to-all-done.1 = bf16[32,4,16,128]{3,2,1,0:T(8,128)(2,1)S(1)} async-done(((bf16[32,4,16,128]{3,2,1,0:T(8,128)(2,1)}), bf16[32,4,16,128]{3,2,1,0:T(8,128)(2,1)S(1)}, u32[]{:S(2)}, u32[]{:S(2)}) %all-to-all-start.1) | async-done | bytes 524320 | tf_op jit(solution)/shard_map/all_to_all | solution.py:240
  29.2 0.0 copy-start.8
  29.2 0.0 copy-start.9
  29.2 0.0 copy-start.10
  29.2 0.0 copy-start.11
  29.2 5.4 %all-to-all-start = ((bf16[32,4,16,128]{3,2,1,0:T(8,128)(2,1)}), bf16[32,4,16,128]{3,2,1,0:T(8,128)(2,1)S(1)}, u32[]{:S(2)}, u32[]{:S(2)}) async-start(bf16[32,4,16,128]{3,2,1,0:T(8,128)(2,1)} %shard_map.150), calls=%async_computation | async-start | bytes 1048576 | tf_op jit(solution)/shard_map/all_to_all | solution.py:240
  34.7 0.8 dynamic_slice.3
  35.5 15.6 %all-to-all-done = bf16[32,4,16,128]{3,2,1,0:T(8,128)(2,1)S(1)} async-done(((bf16[32,4,16,128]{3,2,1,0:T(8,128)(2,1)}), bf16[32,4,16,128]{3,2,1,0:T(8,128)(2,1)S(1)}, u32[]{:S(2)}, u32[]{:S(2)}) %all-to-all-start) | async-done | bytes 524320 | tf_op jit(solution)/shard_map/all_to_all | solution.py:240
  51.1 0.1 broadcast_in_dim.4.skip_ref
  51.2 0.0 copy-done.5
  51.2 0.0 copy-done.6
  51.2 0.0 copy-done.8
  51.2 0.0 copy-done.9
  51.2 0.0 copy-done.10
  51.2 0.0 copy-done.11
  51.2 4.2 %shard_map.152 = bf16[2048,128]{1,0:T(8,128)(2,1)} custom-call(bf16[2048,128]{1,0:T(8,128)(2,1)S(1)} %bitcast.5, bf16[2048,128]{1,0:T(8,128)(2,1)S(1)} %bitcast.4, f32[16,128]{1,0:T(8,128)S(1)} %broadcast_in_dim.4.skip_ref, bf16[256,128]{1,0:T(8,128)(2,1)S(1)} %copy-done.11, bf16[256,256]{1,0:T(8,128)(2,1)S(1)} %copy-done.6, bf16[256,256]{1,0:T(8,128)(2,1)S(1)} %copy-done.5, ...), custom_call_target="tpu_custom_call" | custom-call | tf_op jit(solution)/shard_map/pallas_call | solution.py:175
  55.5 4.1 %all-to-all-start.2 = ((bf16[32,4,16,128]{3,2,1,0:T(8,128)(2,1)}), bf16[32,4,16,128]{3,2,1,0:T(8,128)(2,1)S(1)}, u32[]{:S(2)}, u32[]{:S(2)}) async-start(bf16[32,4,16,128]{3,2,1,0:T(8,128)(2,1)} %bitcast.2), calls=%async_computation.2 | async-start | bytes 1048576 | tf_op jit(solution)/shard_map/all_to_all | solution.py:240
  59.6 0.0 copy-start.3
  59.6 0.6 shard_map.153.qf_ref
  60.2 15.8 %all-to-all-done.2.y_ref = bf16[32,4,16,128]{3,2,1,0:T(8,128)(2,1)S(1)} async-done(((bf16[32,4,16,128]{3,2,1,0:T(8,128)(2,1)}), bf16[32,4,16,128]{3,2,1,0:T(8,128)(2,1)S(1)}, u32[]{:S(2)}, u32[]{:S(2)}) %all-to-all-start.2) | async-done | bytes 524320 | tf_op jit(solution)/shard_map/all_to_all | solution.py:240
  76.0 0.0 copy-done.3
  76.0 1.3 %shard_map.154 = (bf16[512,512]{1,0:T(8,128)(2,1)}, f32[512,512]{1,0:T(8,128)S(1)}, f32[8,8,128]{2,1,0:T(8,128)S(1)}) custom-call(bf16[32,4,16,128]{3,2,1,0:T(8,128)(2,1)S(1)} %all-to-all-done.2.y_ref, bf16[512,512]{1,0:T(8,128)(2,1)S(1)} %shard_map.153.qf_ref, bf16[512,512]{1,0:T(8,128)(2,1)S(1)} %copy-done.3), custom_call_target="tpu_custom_call" | custom-call | tf_op jit(solution)/shard_map/pallas_call | solution.py:204
  77.3 16.9 %all_to_all.20.refs_1_ = f32[8,8,128]{2,1,0:T(8,128)S(1)} all-to-all(f32[8,8,128]{2,1,0:T(8,128)S(1)} %get-tuple-element.7), channel_id=1, replica_groups=mesh['seq'=32,'ch'=8] {'ch'}, dimensions={0} | all-to-all | bytes 65536 | tf_op jit(solution)/shard_map/all_to_all | solution.py:240
  94.3 0.0 copy-start.12
  94.3 0.7 copy-done.12
  94.9 1.0 %shard_map.155 = bf16[512,512]{1,0:T(8,128)(2,1)} custom-call(f32[512,512]{1,0:T(8,128)S(1)} %get-tuple-element.6.refs_0_, f32[8,8,128]{2,1,0:T(8,128)S(1)} %all_to_all.20.refs_1_, f32[1,512]{1,0:T(1,128)S(1)} %bitcast.6), custom_call_target="tpu_custom_call" | custom-call | tf_op jit(solution)/shard_map/pallas_call | solution.py:232
  (1 shorter events, 0.0 us)
Async XLA Ops:
  0.6 1.0 %copy-start.4 = (bf16[512,512]{1,0:T(8,128)(2,1)S(1)}, bf16[512,512]{1,0:T(8,128)(2,1)}, u32[]{:S(2)}) copy-start(bf16[512,512]{1,0:T(8,128)(2,1)} %x_ref.1) | copy-start | bytes 1572868
  1.7 11.2 %copy-start.2 = (bf16[512,512]{1,0:T(8,128)(2,1)S(1)}, bf16[512,512]{1,0:T(8,128)(2,1)}, u32[]{:S(2)}) copy-start(bf16[512,512]{1,0:T(8,128)(2,1)} %q_ref.3) | copy-start | bytes 1572868
  2.7 10.2 %copy-start = (bf16[512,512]{1,0:T(8,128)(2,1)S(1)}, bf16[512,512]{1,0:T(8,128)(2,1)}, u32[]{:S(2)}) copy-start(bf16[512,512]{1,0:T(8,128)(2,1)} %k_ref.3) | copy-start | bytes 1572868
  2.7 10.2 %copy-start.1 = (bf16[512,512]{1,0:T(8,128)(2,1)S(1)}, bf16[512,512]{1,0:T(8,128)(2,1)}, u32[]{:S(2)}) copy-start(bf16[512,512]{1,0:T(8,128)(2,1)} %v_ref.3) | copy-start | bytes 1572868
  2.7 26.6 %all-to-all-start.1 = ((bf16[32,4,16,128]{3,2,1,0:T(8,128)(2,1)}), bf16[32,4,16,128]{3,2,1,0:T(8,128)(2,1)S(1)}, u32[]{:S(2)}, u32[]{:S(2)}) async-start(bf16[32,4,16,128]{3,2,1,0:T(8,128)(2,1)} %shard_map.151), calls=%async_computation.1 | async-start | bytes 1048576 | tf_op jit(solution)/shard_map/all_to_all | solution.py:240
  12.9 5.0 %copy-start.7 = (f32[3,3,512]{2,1,0:T(4,128)S(1)}, f32[3,3,512]{2,1,0:T(4,128)}, u32[]{:S(2)}) copy-start(f32[3,3,512]{2,1,0:T(4,128)} %taps_ref.3) | copy-start | bytes 55300
  12.9 5.0 %collective-permute-start = (bf16[3,16,512]{2,1,0:T(8,128)(2,1)S(1)}, bf16[3,16,512]{2,1,0:T(8,128)(2,1)S(1)}, u32[]{:S(2)}, u32[]{:S(2)}) collective-permute-start(bf16[3,16,512]{2,1,0:T(8,128)(2,1)S(1)} %shard_map.149), channel_id=1, source_target_pairs={{0,8},{8,16},{16,24},{24,32},{32,40},{40,48},{48,56},{56,64},{64,7... | collective-permute-start | bytes 147464 | tf_op jit(solution)/shard_map/ppermute | solution.py:249
  19.6 31.5 %copy-start.5 = (bf16[256,256]{1,0:T(8,128)(2,1)S(1)}, bf16[256,256]{1,0:T(8,128)(2,1)}, u32[]{:S(2)}) copy-start(bf16[256,256]{1,0:T(8,128)(2,1)} %constant.26.clone.t2_inv) | copy-start | bytes 393220
  19.6 31.5 %copy-start.6 = (bf16[256,256]{1,0:T(8,128)(2,1)S(1)}, bf16[256,256]{1,0:T(8,128)(2,1)}, u32[]{:S(2)}) copy-start(bf16[256,256]{1,0:T(8,128)(2,1)} %constant.25.clone.t2) | copy-start | bytes 393220
  29.2 21.9 %copy-start.8 = (f32[128,128]{1,0:T(8,128)S(1)}, f32[128,128]{1,0:T(8,128)}, u32[]{:S(2)}) copy-start(f32[128,128]{1,0:T(8,128)} %constant.29.clone.tw_s) | copy-start | bytes 196612
  29.2 21.9 %copy-start.9 = (f32[128,128]{1,0:T(8,128)S(1)}, f32[128,128]{1,0:T(8,128)}, u32[]{:S(2)}) copy-start(f32[128,128]{1,0:T(8,128)} %constant.28.clone.tw_c) | copy-start | bytes 196612
  29.2 22.0 %copy-start.10 = (bf16[128,256]{1,0:T(8,128)(2,1)S(1)}, bf16[128,256]{1,0:T(8,128)(2,1)}, u32[]{:S(2)}) copy-start(bf16[128,256]{1,0:T(8,128)(2,1)} %constant.27.clone.t1_inv) | copy-start | bytes 196612
  29.2 22.0 %copy-start.11 = (bf16[256,128]{1,0:T(8,128)(2,1)S(1)}, bf16[256,128]{1,0:T(8,128)(2,1)}, u32[]{:S(2)}) copy-start(bf16[256,128]{1,0:T(8,128)(2,1)} %constant.24.clone.t1) | copy-start | bytes 196612
  29.2 21.9 %all-to-all-start = ((bf16[32,4,16,128]{3,2,1,0:T(8,128)(2,1)}), bf16[32,4,16,128]{3,2,1,0:T(8,128)(2,1)S(1)}, u32[]{:S(2)}, u32[]{:S(2)}) async-start(bf16[32,4,16,128]{3,2,1,0:T(8,128)(2,1)} %shard_map.150), calls=%async_computation | async-start | bytes 1048576 | tf_op jit(solution)/shard_map/all_to_all | solution.py:240
  55.5 20.6 %all-to-all-start.2 = ((bf16[32,4,16,128]{3,2,1,0:T(8,128)(2,1)}), bf16[32,4,16,128]{3,2,1,0:T(8,128)(2,1)S(1)}, u32[]{:S(2)}, u32[]{:S(2)}) async-start(bf16[32,4,16,128]{3,2,1,0:T(8,128)(2,1)} %bitcast.2), calls=%async_computation.2 | async-start | bytes 1048576 | tf_op jit(solution)/shard_map/all_to_all | solution.py:240
  59.6 16.4 %copy-start.3 = (bf16[512,512]{1,0:T(8,128)(2,1)S(1)}, bf16[512,512]{1,0:T(8,128)(2,1)}, u32[]{:S(2)}) copy-start(bf16[512,512]{1,0:T(8,128)(2,1)} %stream_ref.1) | copy-start | bytes 1572868
  94.3 0.7 copy-start.12

commit v2 on v1

--- a/solution.py
+++ b/solution.py
@@ -9,11 +9,17 @@
 LANE = 128
 EDGE = 16
 GROUP = 4
+Z_SIZE = 4
+X_SIZE = 4
 VMEM_LIMIT = 48 * 1024 * 1024
 
 
-def params():
-    return pltpu.CompilerParams(vmem_limit_bytes=VMEM_LIMIT)
+def params(limit=VMEM_LIMIT):
+    return pltpu.CompilerParams(vmem_limit_bytes=limit)
+
+
+def cost(micros):
+    return pl.CostEstimate(flops=int(micros * 1e9), bytes_accessed=0, transcendentals=0)
 
 
 def tables():
@@ -31,22 +37,25 @@
     return (*low, jnp.asarray(np.cos(twist), jnp.float32), jnp.asarray(np.sin(twist), jnp.float32))
 
 
-def edges_kernel(q_ref, k_ref, v_ref, out_ref):
-    out_ref[0] = q_ref[...]
-    out_ref[1] = k_ref[...]
-    out_ref[2] = v_ref[...]
+def edges_kernel(q_ref, k_ref, v_ref, out_ref, sems):
+    rows = q_ref.shape[0]
+    copies = [
+        pltpu.make_async_copy(ref.at[pl.ds(rows - EDGE, EDGE), :], out_ref.at[i], sems.at[i])
+        for i, ref in enumerate((q_ref, k_ref, v_ref))
+    ]
+    for copy in copies:
+        copy.start()
+    for copy in copies:
+        copy.wait()
 
 
 def last_rows(q, k, v):
-    rows, width = q.shape
-    spec = pl.BlockSpec((EDGE, width), lambda i: (rows // EDGE - 1, 0))
     return pl.pallas_call(
         edges_kernel,
-        grid=(1,),
-        in_specs=[spec] * 3,
-        out_specs=pl.BlockSpec((3, EDGE, width), lambda i: (0, 0, 0)),
-        out_shape=jax.ShapeDtypeStruct((3, EDGE, width), q.dtype),
-        compiler_params=params(),
+        in_specs=[pl.BlockSpec(memory_space=pl.ANY)] * 3,
+        out_shape=jax.ShapeDtypeStruct((3, EDGE, q.shape[1]), q.dtype),
+        scratch_shapes=[pltpu.SemaphoreType.DMA((3,))],
+        compiler_params=params(60 * 1024 * 1024),
     )(q, k, v)
 
 
@@ -58,9 +67,22 @@
         out_ref[g * per : (g + 1) * per, j] = turned.reshape(per, depth, LANE).astype(out_ref.dtype)
 
 
-def turn_kernel(x_ref, out_ref):
-    for j in range(out_ref.shape[1]):
-        put_turned(out_ref, j, x_ref[j * LANE : (j + 1) * LANE, :].astype(jnp.float32))
+def place():
+    me = lax.axis_index("seq")
+    return me // (X_SIZE * 2), me // 2 % X_SIZE, me % 2
+
+
+def turn_kernel(x_ref, after_ref, *outs):
+    z, x, c = place()
+    depth = outs[0].shape[3]
+    for kz, out_ref in enumerate(outs):
+        g = (z + kz) % Z_SIZE
+        for j in range(out_ref.shape[2]):
+            block = x_ref[j * LANE : (j + 1) * LANE, pl.ds(pl.multiple_of(g * LANE, LANE), LANE)]
+            turned = block.astype(jnp.float32).T.astype(out_ref.dtype)
+            for d in range(X_SIZE * 2):
+                tile = turned[d * depth : (d + 1) * depth]
+                out_ref[(d // 2 - x + X_SIZE) % X_SIZE, (d % 2 - c + 2) % 2, j] = tile
 
 
 def split_shape(x, groups):
@@ -68,10 +90,47 @@
     return jax.ShapeDtypeStruct((groups, rows // LANE, width // groups, LANE), x.dtype)
 
 
-def turn(x, groups):
-    return pl.pallas_call(
-        turn_kernel, out_shape=split_shape(x, groups), compiler_params=params()
-    )(x)
+def turn(x, after, groups):
+    rows, width = x.shape
+    shape = jax.ShapeDtypeStruct((X_SIZE, 2, rows // LANE, width // groups, LANE), x.dtype)
+    return pl.pallas_call(
+        turn_kernel,
+        in_specs=[pl.BlockSpec(memory_space=pltpu.VMEM), pl.BlockSpec(memory_space=pl.ANY)],
+        out_shape=(shape,) * Z_SIZE,
+        cost_estimate=cost(10),
+        compiler_params=params(),
+    )(x, after)
+
+
+def pack_kernel(*refs):
+    ins, outs = refs[:Z_SIZE], refs[Z_SIZE:]
+    for d, out_ref in enumerate(outs):
+        for kz, in_ref in enumerate(ins):
+            out_ref[kz] = in_ref[d // 2, d % 2]
+
+
+def pack(parts):
+    shape = jax.ShapeDtypeStruct((Z_SIZE, *parts[0].shape[2:]), parts[0].dtype)
+    return pl.pallas_call(
+        pack_kernel, out_shape=(shape,) * (X_SIZE * 2), cost_estimate=cost(20), compiler_params=params()
+    )(*parts)
+
+
+def shift(block, dz, dx, dc):
+    route = []
+    for z in range(Z_SIZE):
+        for x in range(X_SIZE):
+            for c in range(2):
+                to = ((z + dz) % Z_SIZE * X_SIZE + (x + dx) % X_SIZE) * 2 + (c + dc) % 2
+                route.append(((z * X_SIZE + x) * 2 + c, to))
+    return lax.ppermute(block, "seq", route)
+
+
+def spread(x, after, groups):
+    parts = turn(x, after, groups)
+    parts = [parts[0]] + [shift(parts[k], k, 0, 0) for k in range(1, Z_SIZE)]
+    parts = pack(parts)
+    return [parts[0]] + [shift(parts[d], 0, d // 2, d % 2) for d in range(1, X_SIZE * 2)]
 
 
 def extend(ext_ref, x_ref, edge):
@@ -104,6 +163,7 @@
         product_kernel,
         out_shape=split_shape(k, groups),
         scratch_shapes=[ext, ext],
+        cost_estimate=cost(20),
         compiler_params=params(),
     )(k, v, edge, taps)
 
@@ -129,10 +189,17 @@
     return jnp.dot(table, data, preferred_element_type=jnp.float32)
 
 
-def conv_kernel(u_ref, f_ref, skip_ref, t1, t2, t2_inv, t1_inv, tw_c, tw_s, y_ref, u_wide, f_wide, y_wide):
+def conv_kernel(u_ref, skip_ref, t1, t2, t2_inv, t1_inv, tw_c, tw_s, *rest):
+    f_refs, (y_ref, u_wide, f_wide, y_wide) = rest[:-4], rest[-4:]
     depth = skip_ref.shape[0]
     u_wide[...] = u_ref[...].astype(jnp.float32)
-    f_wide[...] = f_ref[...].astype(jnp.float32)
+    z, x, c = place()
+    size = u_ref.shape[0] // (Z_SIZE * len(f_refs))
+    for d, f_ref in enumerate(f_refs):
+        for kz in range(Z_SIZE):
+            src = ((z - kz + Z_SIZE) % Z_SIZE * X_SIZE + (x - d // 2 + X_SIZE) % X_SIZE) * 2 + (c + d) % 2
+            row = pl.multiple_of(src * size, size)
+            f_wide[pl.ds(row, size), :] = f_ref[kz].reshape(size, LANE).astype(jnp.float32)
     low = jnp.bfloat16
 
     def part(x, i):
@@ -177,10 +244,10 @@
         out_shape=jax.ShapeDtypeStruct(u.shape, u.dtype),
         scratch_shapes=[wide] * 3,
         compiler_params=params(),
-    )(u, f, skip, *tables())
-
-
-def join_kernel(y_ref, qf_ref, stream_ref, out_ref, sum_ref, sq_ref):
+    )(u, skip, *tables(), *f)
+
+
+def join_kernel(y_ref, qf_ref, stream_ref, gain_ref, out_ref, sum_ref, sq_ref):
     groups, slabs, depth, _ = y_ref.shape
     per = LANE // depth
     sq_ref[...] = jnp.zeros_like(sq_ref)
@@ -193,14 +260,14 @@
             gated = (qf_ref[rows, cols].astype(jnp.float32) * y).astype(jnp.bfloat16)
             summed = stream_ref[rows, cols].astype(jnp.float32) + gated.astype(jnp.float32)
             out_ref[rows, cols] = summed.astype(out_ref.dtype)
-            sum_ref[rows, cols] = summed
+            sum_ref[rows, cols] = summed * gain_ref[:, cols]
             squares = squares + summed * summed
         total = jnp.sum(squares.T, axis=0, keepdims=True)
         for d in range(sq_ref.shape[0]):
             sq_ref[d, j : j + 1, :] = total
 
 
-def join(y, qf, stream, fan):
+def join(y, qf, stream, gain, fan):
     return pl.pallas_call(
         join_kernel,
         out_shape=(
@@ -209,10 +276,10 @@
             jax.ShapeDtypeStruct((fan, 8, LANE), jnp.float32),
         ),
         compiler_params=params(),
-    )(y, qf, stream)
-
-
-def norm_kernel(channels, sum_ref, sq_ref, gain_ref, out_ref):
+    )(y, qf, stream, gain[None, :])
+
+
+def norm_kernel(channels, sum_ref, sq_ref, out_ref):
     squares = jnp.sum(sq_ref[...], axis=0)
     scale = 1.0 / jnp.sqrt(squares / channels + 1e-05)
     for j in range(out_ref.shape[0] // LANE):
@@ -220,10 +287,10 @@
         column = jnp.broadcast_to(scale[j : j + 1, :], (LANE, LANE)).T
         for g in range(out_ref.shape[1] // LANE):
             cols = slice(g * LANE, (g + 1) * LANE)
-            out_ref[rows, cols] = (sum_ref[rows, cols] * column * gain_ref[:, cols]).astype(out_ref.dtype)
-
-
-def norm(summed, squares, gain):
+            out_ref[rows, cols] = (sum_ref[rows, cols] * column).astype(out_ref.dtype)
+
+
+def norm(summed, squares):
     channels = summed.shape[1] * squares.shape[0]
 
     def kernel(*refs):
@@ -233,7 +300,7 @@
         kernel,
         out_shape=jax.ShapeDtypeStruct(summed.shape, jnp.bfloat16),
         compiler_params=params(),
-    )(summed, squares, gain[None, :])
+    )(summed, squares)
 
 
 def exchange(x, axis):
@@ -245,18 +312,18 @@
     fan = lax.axis_size("ch")
     rows, width = queries.shape
     slab = width // groups
-    edge = last_rows(queries, keys, values)
-    edge = lax.ppermute(edge, "seq", [(i, i + 1) for i in range(groups - 1)])
-    f_all = exchange(turn(filters, groups), "seq")
+    own_edge = last_rows(queries, keys, values)
+    edge = lax.ppermute(own_edge, "seq", [(i, i + 1) for i in range(groups - 1)])
+    f_all = spread(filters, own_edge, groups)
     u_all = exchange(product(keys, values, edge, short_weights, groups), "seq")
     qf = gate(queries, edge, short_weights)
     skip = lax.dynamic_slice_in_dim(skip_gain, lax.axis_index("seq") * slab, slab, 0)
     skip = jnp.broadcast_to(skip[:, None], (slab, LANE))
     flat = (groups * rows // LANE * slab, LANE)
-    y = long_conv(u_all.reshape(flat), f_all.reshape(flat), skip)
+    y = long_conv(u_all.reshape(flat), f_all, skip)
     y_home = exchange(y.reshape(u_all.shape), "seq")
-    stream_out, summed, squares = join(y_home, qf, stream, fan)
-    normed = norm(summed, exchange(squares, "ch"), norm_gain)
+    stream_out, summed, squares = join(y_home, qf, stream, norm_gain, fan)
+    normed = norm(summed, exchange(squares, "ch"))
     return (stream_out, normed)
 
 

time: 96.5 us -> 84.9 us (0.88)
  waiting for transfers between devices: 42.5 us -> 22.6 us
  starting transfers between devices: 23.3 us -> 32.2 us
    all_to_all x3 -> x2, waiting for transfers between devices: 41.1 us -> 16.9 us  [exchange(): return lax.all_to_all(x, axis, split_axis=0, concat_axis=0, tiled=True)]
    ppermute x1 -> x11, starting transfers between devices: 3.54 us -> 18.9 us  [the longest x10 14.3 us: shift(): return lax.ppermute(block, 'seq', route)]
    all_to_all x3 -> x2, starting transfers between devices: 19.7 us -> 13.3 us  [exchange(): return lax.all_to_all(x, axis, split_axis=0, concat_axis=0, tiled=True)]
    ppermute x1 -> x11, waiting for transfers between devices: 1.43 us -> 5.73 us  [the longest x10 5.73 us: shift(): return lax.ppermute(block, 'seq', route)]
  transfers between devices with their start and end apart: 4 -> 13, of which waited for: 4 -> 6; matrix products, arithmetic and copies ran while one was open for 1% -> 1% of each run, Pallas kernels for 2% -> 3%
where the time goes in v2:
time: 84.9 us; the launch traced here: 84.4 us
  starting transfers between devices  32.2 us (38%)
  waiting for transfers between devices  22.6 us (27%)
  blocking collectives  16.3 us (19%)
  Pallas kernels  10.7 us (13%)
  local copies, waits for them, and re-layouts  1.69 us (2%)
    all_to_all x2, waiting for transfers between devices, exchange(): return lax.all_to_all(x, axis, split_axis=0, concat_axis=0, tiled=True)  16.9 us
    all_to_all x1, blocking collectives, exchange(): return lax.all_to_all(x, axis, split_axis=0, concat_axis=0, tiled=True)  16.3 us
    ppermute x10, starting transfers between devices, shift(): return lax.ppermute(block, 'seq', route)  14.3 us
    all_to_all x2, starting transfers between devices, exchange(): return lax.all_to_all(x, axis, split_axis=0, concat_axis=0, tiled=True)  13.3 us
    ppermute x10, waiting for transfers between devices, shift(): return lax.ppermute(block, 'seq', route)  5.73 us
    ppermute x1, starting transfers between devices, shards(): lax.ppermute(own_edge, 'seq', [(i, i + 1) for i in range(groups - 1)])  4.64 us
    pallas_call x1, Pallas kernels, long_conv(): pl.pallas_call(conv_kernel, out_shape=jax.ShapeDtypeStruct(u.shape, u.dty...  4.32 us
    pallas_call x1, Pallas kernels, product(): pl.pallas_call(product_kernel, out_shape=split_shape(k, groups), scratch_...  1.77 us
  transfers between devices with their start and end apart: 13, of which 6 were waited for; matrix products, arithmetic and copies ran while one was open for 1% of the time, Pallas kernels for 3%

profile of v2, /device:TPU:1, one launch (start us, length us, event | category | flops | bytes accessed | tf_op | source)
XLA Modules:
  0.0 84.4 jit_solution(9811123246565255546)
XLA Ops:
  0.6 0.0 copy-start.13
  0.6 1.5 %shard_map.149.after_ref = bf16[3,16,512]{2,1,0:T(8,128)(2,1)} custom-call(bf16[512,512]{1,0:T(8,128)(2,1)} %q_ref.3, bf16[512,512]{1,0:T(8,128)(2,1)} %k_ref.3, bf16[512,512]{1,0:T(8,128)(2,1)} %v_ref.3), custom_call_target="tpu_custom_call" | custom-call | tf_op jit(solution)/shard_map/pallas_call | solution.py:53
  2.1 0.0 copy-start.1
  2.1 0.0 copy-start.2
  2.1 4.6 %collective-permute-start = (bf16[3,16,512]{2,1,0:T(8,128)(2,1)}, bf16[3,16,512]{2,1,0:T(8,128)(2,1)S(1)}, u32[]{:S(2)}, u32[]{:S(2)}) collective-permute-start(bf16[3,16,512]{2,1,0:T(8,128)(2,1)} %shard_map.149.after_ref), channel_id=1, source_target_pairs={{0,8},{8,16},{16,24},{24,32},{32,40},{40,48},{48,56},{56,64},{64,7... | collective-permute-start | bytes 147464 | tf_op jit(solution)/shard_map/ppermute | solution.py:316
  6.8 0.0 copy-start.10
  6.8 0.8 copy-done.10
  7.6 0.2 shard_map.151
  7.8 1.7 %collective-permute-start.1 = (bf16[4,2,4,16,128]{4,3,2,1,0:T(8,128)(2,1)S(1)}, bf16[4,2,4,16,128]{4,3,2,1,0:T(8,128)(2,1)S(1)}, u32[]{:S(2)}, u32[]{:S(2)}) collective-permute-start(bf16[4,2,4,16,128]{4,3,2,1,0:T(8,128)(2,1)S(1)} %get-tuple-element.18), channel_id=1, source_target_pairs={{0,64},{8,72},{16,80},{24,88},{32,96},{40,104},{48,112},{56,120},{... | collective-permute-start | bytes 393224 | tf_op jit(solution)/shard_map/ppermute | solution.py:126
  9.5 3.0 %collective-permute-start.2 = (bf16[4,2,4,16,128]{4,3,2,1,0:T(8,128)(2,1)S(1)}, bf16[4,2,4,16,128]{4,3,2,1,0:T(8,128)(2,1)S(1)}, u32[]{:S(2)}, u32[]{:S(2)}) collective-permute-start(bf16[4,2,4,16,128]{4,3,2,1,0:T(8,128)(2,1)S(1)} %get-tuple-element.19), channel_id=1, source_target_pairs={{0,128},{8,136},{16,144},{24,152},{32,160},{40,168},{48,176},{56,1... | collective-permute-start | bytes 393224 | tf_op jit(solution)/shard_map/ppermute | solution.py:126
  12.5 0.7 collective-permute-start.3
  13.2 0.0 collective-permute-done.edge_ref
  13.3 1.8 %shard_map.150 = bf16[32,4,16,128]{3,2,1,0:T(8,128)(2,1)} custom-call(bf16[512,512]{1,0:T(8,128)(2,1)S(1)} %copy-done.1, bf16[512,512]{1,0:T(8,128)(2,1)S(1)} %copy-done.2, bf16[3,16,512]{2,1,0:T(8,128)(2,1)S(1)} %collective-permute-done.edge_ref, f32[3,3,512]{2,1,0:T(4,128)S(1)} %copy-done.11), custom_call_target="tpu_custom_call" | custom-call | flops 20000000000 | tf_op jit(solution)/shard_map/pallas_call | solution.py:162
  15.0 4.7 %all-to-all-start = ((bf16[32,4,16,128]{3,2,1,0:T(8,128)(2,1)}), bf16[32,4,16,128]{3,2,1,0:T(8,128)(2,1)S(1)}, u32[]{:S(2)}, u32[]{:S(2)}) async-start(bf16[32,4,16,128]{3,2,1,0:T(8,128)(2,1)} %shard_map.150), calls=%async_computation | async-start | bytes 1048576 | tf_op jit(solution)/shard_map/all_to_all | solution.py:307
  19.8 0.0 collective-permute-done.1.refs_1_
  19.8 1.5 %collective-permute-done.2.refs_2_ = bf16[4,2,4,16,128]{4,3,2,1,0:T(8,128)(2,1)S(1)} collective-permute-done((bf16[4,2,4,16,128]{4,3,2,1,0:T(8,128)(2,1)S(1)}, bf16[4,2,4,16,128]{4,3,2,1,0:T(8,128)(2,1)S(1)}, u32[]{:S(2)}, u32[]{:S(2)}) %collective-permute-start.2) | collective-permute-done | bytes 131104 | tf_op jit(solution)/shard_map/ppermute | solution.py:126
  21.2 0.0 collective-permute-done.3.refs_3_
  21.3 0.0 copy-start.7
  21.3 0.0 copy-start.8
  21.3 0.0 copy-start.9
  21.3 0.5 collective-permute-start.4
  21.8 1.2 %collective-permute-start.5 = (bf16[4,4,16,128]{3,2,1,0:T(8,128)(2,1)S(1)}, bf16[4,4,16,128]{3,2,1,0:T(8,128)(2,1)S(1)}, u32[]{:S(2)}, u32[]{:S(2)}) collective-permute-start(bf16[4,4,16,128]{3,2,1,0:T(8,128)(2,1)S(1)} %get-tuple-element.23), channel_id=1, source_target_pairs={{0,16},{8,24},{16,32},{24,40},{32,48},{40,56},{48,0},{56,8},{64,80... | collective-permute-start | bytes 196616 | tf_op jit(solution)/shard_map/ppermute | solution.py:126
  23.0 1.2 %collective-permute-start.6 = (bf16[4,4,16,128]{3,2,1,0:T(8,128)(2,1)S(1)}, bf16[4,4,16,128]{3,2,1,0:T(8,128)(2,1)S(1)}, u32[]{:S(2)}, u32[]{:S(2)}) collective-permute-start(bf16[4,4,16,128]{3,2,1,0:T(8,128)(2,1)S(1)} %get-tuple-element.24), channel_id=1, source_target_pairs={{0,24},{8,16},{16,40},{24,32},{32,56},{40,48},{48,8},{56,0},{64,88... | collective-permute-start | bytes 196616 | tf_op jit(solution)/shard_map/ppermute | solution.py:126
  24.3 1.8 %collective-permute-start.7 = (bf16[4,4,16,128]{3,2,1,0:T(8,128)(2,1)S(1)}, bf16[4,4,16,128]{3,2,1,0:T(8,128)(2,1)S(1)}, u32[]{:S(2)}, u32[]{:S(2)}) collective-permute-start(bf16[4,4,16,128]{3,2,1,0:T(8,128)(2,1)S(1)} %get-tuple-element.25), channel_id=1, source_target_pairs={{0,32},{8,40},{16,48},{24,56},{32,0},{40,8},{48,16},{56,24},{64,96... | collective-permute-start | bytes 196616 | tf_op jit(solution)/shard_map/ppermute | solution.py:126
  26.0 1.5 %collective-permute-start.8 = (bf16[4,4,16,128]{3,2,1,0:T(8,128)(2,1)S(1)}, bf16[4,4,16,128]{3,2,1,0:T(8,128)(2,1)S(1)}, u32[]{:S(2)}, u32[]{:S(2)}) collective-permute-start(bf16[4,4,16,128]{3,2,1,0:T(8,128)(2,1)S(1)} %get-tuple-element.26), channel_id=1, source_target_pairs={{0,40},{8,32},{16,56},{24,48},{32,8},{40,0},{48,24},{56,16},{64,10... | collective-permute-start | bytes 196616 | tf_op jit(solution)/shard_map/ppermute | solution.py:126
  27.6 0.0 collective-permute-done.4.rest_1_
  27.6 1.7 %collective-permute-start.9 = (bf16[4,4,16,128]{3,2,1,0:T(8,128)(2,1)S(1)}, bf16[4,4,16,128]{3,2,1,0:T(8,128)(2,1)S(1)}, u32[]{:S(2)}, u32[]{:S(2)}) collective-permute-start(bf16[4,4,16,128]{3,2,1,0:T(8,128)(2,1)S(1)} %get-tuple-element.27), channel_id=1, source_target_pairs={{0,48},{8,56},{16,0},{24,8},{32,16},{40,24},{48,32},{56,40},{64,11... | collective-permute-start | bytes 196616 | tf_op jit(solution)/shard_map/ppermute | solution.py:126
  29.2 0.0 collective-permute-done.5.rest_2_
  29.2 1.0 %collective-permute-start.10 = (bf16[4,4,16,128]{3,2,1,0:T(8,128)(2,1)S(1)}, bf16[4,4,16,128]{3,2,1,0:T(8,128)(2,1)S(1)}, u32[]{:S(2)}, u32[]{:S(2)}) collective-permute-start(bf16[4,4,16,128]{3,2,1,0:T(8,128)(2,1)S(1)} %get-tuple-element.28), channel_id=1, source_target_pairs={{0,56},{8,48},{16,8},{24,0},{32,24},{40,16},{48,40},{56,32},{64,12... | collective-permute-start | bytes 196616 | tf_op jit(solution)/shard_map/ppermute | solution.py:126
  30.2 0.8 dynamic_slice.3
  31.0 0.0 collective-permute-done.6.rest_3_
  31.0 1.8 %collective-permute-done.7.rest_4_ = bf16[4,4,16,128]{3,2,1,0:T(8,128)(2,1)S(1)} collective-permute-done((bf16[4,4,16,128]{3,2,1,0:T(8,128)(2,1)S(1)}, bf16[4,4,16,128]{3,2,1,0:T(8,128)(2,1)S(1)}, u32[]{:S(2)}, u32[]{:S(2)}) %collective-permute-start.7) | collective-permute-done | bytes 65568 | tf_op jit(solution)/shard_map/ppermute | solution.py:126
  32.8 2.1 %collective-permute-done.8.rest_5_ = bf16[4,4,16,128]{3,2,1,0:T(8,128)(2,1)S(1)} collective-permute-done((bf16[4,4,16,128]{3,2,1,0:T(8,128)(2,1)S(1)}, bf16[4,4,16,128]{3,2,1,0:T(8,128)(2,1)S(1)}, u32[]{:S(2)}, u32[]{:S(2)}) %collective-permute-start.8) | collective-permute-done | bytes 65568 | tf_op jit(solution)/shard_map/ppermute | solution.py:126
  34.9 0.0 collective-permute-done.9.rest_6_
  34.9 0.4 collective-permute-done.10.rest_7_
  35.2 1.1 %all-to-all-done = bf16[32,4,16,128]{3,2,1,0:T(8,128)(2,1)S(1)} async-done(((bf16[32,4,16,128]{3,2,1,0:T(8,128)(2,1)}), bf16[32,4,16,128]{3,2,1,0:T(8,128)(2,1)S(1)}, u32[]{:S(2)}, u32[]{:S(2)}) %all-to-all-start) | async-done | bytes 524320 | tf_op jit(solution)/shard_map/all_to_all | solution.py:307
  36.3 0.1 broadcast_in_dim.4.skip_ref
  36.4 0.0 copy-done.5
  36.4 4.3 %shard_map.153 = bf16[2048,128]{1,0:T(8,128)(2,1)} custom-call(bf16[2048,128]{1,0:T(8,128)(2,1)S(1)} %bitcast.3, f32[16,128]{1,0:T(8,128)S(1)} %broadcast_in_dim.4.skip_ref, bf16[256,128]{1,0:T(8,128)(2,1)S(1)} %copy-done.9, bf16[256,256]{1,0:T(8,128)(2,1)S(1)} %copy-done.5, bf16[256,256]{1,0:T(8,128)(2,1)S(1)} %copy-done.4, bf16[128,256]{1,0:T(8,128)(2,1)S(1)} %copy-done.8, ...), custom_call_target="tpu_custom_call" | custom-call | tf_op jit(solution)/shard_map/pallas_call | solution.py:242
  40.8 8.6 %all-to-all-start.1 = ((bf16[32,4,16,128]{3,2,1,0:T(8,128)(2,1)}), bf16[32,4,16,128]{3,2,1,0:T(8,128)(2,1)S(1)}, u32[]{:S(2)}, u32[]{:S(2)}) async-start(bf16[32,4,16,128]{3,2,1,0:T(8,128)(2,1)} %bitcast.1), calls=%async_computation.1 | async-start | bytes 1048576 | tf_op jit(solution)/shard_map/all_to_all | solution.py:307
  49.3 0.0 copy-start.3
  49.4 0.0 copy-start.12
  49.4 0.6 shard_map.154.qf_ref
  49.9 15.8 %all-to-all-done.1.y_ref = bf16[32,4,16,128]{3,2,1,0:T(8,128)(2,1)S(1)} async-done(((bf16[32,4,16,128]{3,2,1,0:T(8,128)(2,1)}), bf16[32,4,16,128]{3,2,1,0:T(8,128)(2,1)S(1)}, u32[]{:S(2)}, u32[]{:S(2)}) %all-to-all-start.1) | async-done | bytes 524320 | tf_op jit(solution)/shard_map/all_to_all | solution.py:307
  65.7 0.0 copy-done.12
  65.7 1.4 %shard_map.155 = (bf16[512,512]{1,0:T(8,128)(2,1)}, f32[512,512]{1,0:T(8,128)S(1)}, f32[8,8,128]{2,1,0:T(8,128)S(1)}) custom-call(bf16[32,4,16,128]{3,2,1,0:T(8,128)(2,1)S(1)} %all-to-all-done.1.y_ref, bf16[512,512]{1,0:T(8,128)(2,1)S(1)} %shard_map.154.qf_ref, bf16[512,512]{1,0:T(8,128)(2,1)S(1)} %copy-done.3, f32[1,512]{1,0:T(1,128)S(1)} %bitcast.4), custom_call_target="tpu_custom_call" | custom-call | tf_op jit(solution)/shard_map/pallas_call | solution.py:271
  67.1 16.3 %all_to_all.15.refs_1_ = f32[8,8,128]{2,1,0:T(8,128)S(1)} all-to-all(f32[8,8,128]{2,1,0:T(8,128)S(1)} %get-tuple-element.31), channel_id=1, replica_groups=mesh['seq'=32,'ch'=8] {'ch'}, dimensions={0} | all-to-all | bytes 65536 | tf_op jit(solution)/shard_map/all_to_all | solution.py:307
  83.4 1.0 %shard_map.156 = bf16[512,512]{1,0:T(8,128)(2,1)} custom-call(f32[512,512]{1,0:T(8,128)S(1)} %get-tuple-element.30.refs_0_, f32[8,8,128]{2,1,0:T(8,128)S(1)} %all_to_all.15.refs_1_), custom_call_target="tpu_custom_call" | custom-call | tf_op jit(solution)/shard_map/pallas_call | solution.py:299
  (17 shorter events, 0.1 us)
Async XLA Ops:
  0.6 6.1 %copy-start.13 = (bf16[512,512]{1,0:T(8,128)(2,1)S(1)}, bf16[512,512]{1,0:T(8,128)(2,1)}, u32[]{:S(2)}) copy-start(bf16[512,512]{1,0:T(8,128)(2,1)} %x_ref.1) | copy-start | bytes 1572868
  2.1 11.1 %copy-start.1 = (bf16[512,512]{1,0:T(8,128)(2,1)S(1)}, bf16[512,512]{1,0:T(8,128)(2,1)}, u32[]{:S(2)}) copy-start(bf16[512,512]{1,0:T(8,128)(2,1)} %k_ref.3) | copy-start | bytes 1572868
  2.1 11.1 %copy-start.2 = (bf16[512,512]{1,0:T(8,128)(2,1)S(1)}, bf16[512,512]{1,0:T(8,128)(2,1)}, u32[]{:S(2)}) copy-start(bf16[512,512]{1,0:T(8,128)(2,1)} %v_ref.3) | copy-start | bytes 1572868
  2.1 11.1 %collective-permute-start = (bf16[3,16,512]{2,1,0:T(8,128)(2,1)}, bf16[3,16,512]{2,1,0:T(8,128)(2,1)S(1)}, u32[]{:S(2)}, u32[]{:S(2)}) collective-permute-start(bf16[3,16,512]{2,1,0:T(8,128)(2,1)} %shard_map.149.after_ref), channel_id=1, source_target_pairs={{0,8},{8,16},{16,24},{24,32},{32,40},{40,48},{48,56},{56,64},{64,7... | collective-permute-start | bytes 147464 | tf_op jit(solution)/shard_map/ppermute | solution.py:316
  6.8 0.8 copy-start.10
  7.6 5.7 %copy-start.11 = (f32[3,3,512]{2,1,0:T(4,128)S(1)}, f32[3,3,512]{2,1,0:T(4,128)}, u32[]{:S(2)}) copy-start(f32[3,3,512]{2,1,0:T(4,128)} %taps_ref.3) | copy-start | bytes 55300
  7.8 12.0 %collective-permute-start.1 = (bf16[4,2,4,16,128]{4,3,2,1,0:T(8,128)(2,1)S(1)}, bf16[4,2,4,16,128]{4,3,2,1,0:T(8,128)(2,1)S(1)}, u32[]{:S(2)}, u32[]{:S(2)}) collective-permute-start(bf16[4,2,4,16,128]{4,3,2,1,0:T(8,128)(2,1)S(1)} %get-tuple-element.18), channel_id=1, source_target_pairs={{0,64},{8,72},{16,80},{24,88},{32,96},{40,104},{48,112},{56,120},{... | collective-permute-start | bytes 393224 | tf_op jit(solution)/shard_map/ppermute | solution.py:126
  9.5 11.7 %collective-permute-start.2 = (bf16[4,2,4,16,128]{4,3,2,1,0:T(8,128)(2,1)S(1)}, bf16[4,2,4,16,128]{4,3,2,1,0:T(8,128)(2,1)S(1)}, u32[]{:S(2)}, u32[]{:S(2)}) collective-permute-start(bf16[4,2,4,16,128]{4,3,2,1,0:T(8,128)(2,1)S(1)} %get-tuple-element.19), channel_id=1, source_target_pairs={{0,128},{8,136},{16,144},{24,152},{32,160},{40,168},{48,176},{56,1... | collective-permute-start | bytes 393224 | tf_op jit(solution)/shard_map/ppermute | solution.py:126
  12.5 8.7 %collective-permute-start.3 = (bf16[4,2,4,16,128]{4,3,2,1,0:T(8,128)(2,1)S(1)}, bf16[4,2,4,16,128]{4,3,2,1,0:T(8,128)(2,1)S(1)}, u32[]{:S(2)}, u32[]{:S(2)}) collective-permute-start(bf16[4,2,4,16,128]{4,3,2,1,0:T(8,128)(2,1)S(1)} %get-tuple-element.20), channel_id=1, source_target_pairs={{0,192},{8,200},{16,208},{24,216},{32,224},{40,232},{48,240},{56,2... | collective-permute-start | bytes 393224 | tf_op jit(solution)/shard_map/ppermute | solution.py:126
  15.0 21.3 %all-to-all-start = ((bf16[32,4,16,128]{3,2,1,0:T(8,128)(2,1)}), bf16[32,4,16,128]{3,2,1,0:T(8,128)(2,1)S(1)}, u32[]{:S(2)}, u32[]{:S(2)}) async-start(bf16[32,4,16,128]{3,2,1,0:T(8,128)(2,1)} %shard_map.150), calls=%async_computation | async-start | bytes 1048576 | tf_op jit(solution)/shard_map/all_to_all | solution.py:307
  21.2 15.1 %copy-start.4 = (bf16[256,256]{1,0:T(8,128)(2,1)S(1)}, bf16[256,256]{1,0:T(8,128)(2,1)}, u32[]{:S(2)}) copy-start(bf16[256,256]{1,0:T(8,128)(2,1)} %constant.26.clone.t2_inv) | copy-start | bytes 393220
  21.3 15.1 %copy-start.5 = (bf16[256,256]{1,0:T(8,128)(2,1)S(1)}, bf16[256,256]{1,0:T(8,128)(2,1)}, u32[]{:S(2)}) copy-start(bf16[256,256]{1,0:T(8,128)(2,1)} %constant.25.clone.t2) | copy-start | bytes 393220
  21.3 15.1 %copy-start.6 = (f32[128,128]{1,0:T(8,128)S(1)}, f32[128,128]{1,0:T(8,128)}, u32[]{:S(2)}) copy-start(f32[128,128]{1,0:T(8,128)} %constant.29.clone.tw_s) | copy-start | bytes 196612
  21.3 15.1 %copy-start.7 = (f32[128,128]{1,0:T(8,128)S(1)}, f32[128,128]{1,0:T(8,128)}, u32[]{:S(2)}) copy-start(f32[128,128]{1,0:T(8,128)} %constant.28.clone.tw_c) | copy-start | bytes 196612
  21.3 15.1 %copy-start.8 = (bf16[128,256]{1,0:T(8,128)(2,1)S(1)}, bf16[128,256]{1,0:T(8,128)(2,1)}, u32[]{:S(2)}) copy-start(bf16[128,256]{1,0:T(8,128)(2,1)} %constant.27.clone.t1_inv) | copy-start | bytes 196612
  21.3 15.1 %copy-start.9 = (bf16[256,128]{1,0:T(8,128)(2,1)S(1)}, bf16[256,128]{1,0:T(8,128)(2,1)}, u32[]{:S(2)}) copy-start(bf16[256,128]{1,0:T(8,128)(2,1)} %constant.24.clone.t1) | copy-start | bytes 196612
  21.3 6.2 %collective-permute-start.4 = (bf16[4,4,16,128]{3,2,1,0:T(8,128)(2,1)S(1)}, bf16[4,4,16,128]{3,2,1,0:T(8,128)(2,1)S(1)}, u32[]{:S(2)}, u32[]{:S(2)}) collective-permute-start(bf16[4,4,16,128]{3,2,1,0:T(8,128)(2,1)S(1)} %get-tuple-element.22), channel_id=1, source_target_pairs={{0,8},{8,0},{16,24},{24,16},{32,40},{40,32},{48,56},{56,48},{64,72... | collective-permute-start | bytes 196616 | tf_op jit(solution)/shard_map/ppermute | solution.py:126
  21.8 7.4 %collective-permute-start.5 = (bf16[4,4,16,128]{3,2,1,0:T(8,128)(2,1)S(1)}, bf16[4,4,16,128]{3,2,1,0:T(8,128)(2,1)S(1)}, u32[]{:S(2)}, u32[]{:S(2)}) collective-permute-start(bf16[4,4,16,128]{3,2,1,0:T(8,128)(2,1)S(1)} %get-tuple-element.23), channel_id=1, source_target_pairs={{0,16},{8,24},{16,32},{24,40},{32,48},{40,56},{48,0},{56,8},{64,80... | collective-permute-start | bytes 196616 | tf_op jit(solution)/shard_map/ppermute | solution.py:126
  23.0 7.9 %collective-permute-start.6 = (bf16[4,4,16,128]{3,2,1,0:T(8,128)(2,1)S(1)}, bf16[4,4,16,128]{3,2,1,0:T(8,128)(2,1)S(1)}, u32[]{:S(2)}, u32[]{:S(2)}) collective-permute-start(bf16[4,4,16,128]{3,2,1,0:T(8,128)(2,1)S(1)} %get-tuple-element.24), channel_id=1, source_target_pairs={{0,24},{8,16},{16,40},{24,32},{32,56},{40,48},{48,8},{56,0},{64,88... | collective-permute-start | bytes 196616 | tf_op jit(solution)/shard_map/ppermute | solution.py:126
  24.3 8.5 %collective-permute-start.7 = (bf16[4,4,16,128]{3,2,1,0:T(8,128)(2,1)S(1)}, bf16[4,4,16,128]{3,2,1,0:T(8,128)(2,1)S(1)}, u32[]{:S(2)}, u32[]{:S(2)}) collective-permute-start(bf16[4,4,16,128]{3,2,1,0:T(8,128)(2,1)S(1)} %get-tuple-element.25), channel_id=1, source_target_pairs={{0,32},{8,40},{16,48},{24,56},{32,0},{40,8},{48,16},{56,24},{64,96... | collective-permute-start | bytes 196616 | tf_op jit(solution)/shard_map/ppermute | solution.py:126
  26.0 8.8 %collective-permute-start.8 = (bf16[4,4,16,128]{3,2,1,0:T(8,128)(2,1)S(1)}, bf16[4,4,16,128]{3,2,1,0:T(8,128)(2,1)S(1)}, u32[]{:S(2)}, u32[]{:S(2)}) collective-permute-start(bf16[4,4,16,128]{3,2,1,0:T(8,128)(2,1)S(1)} %get-tuple-element.26), channel_id=1, source_target_pairs={{0,40},{8,32},{16,56},{24,48},{32,8},{40,0},{48,24},{56,16},{64,10... | collective-permute-start | bytes 196616 | tf_op jit(solution)/shard_map/ppermute | solution.py:126
  27.6 7.3 %collective-permute-start.9 = (bf16[4,4,16,128]{3,2,1,0:T(8,128)(2,1)S(1)}, bf16[4,4,16,128]{3,2,1,0:T(8,128)(2,1)S(1)}, u32[]{:S(2)}, u32[]{:S(2)}) collective-permute-start(bf16[4,4,16,128]{3,2,1,0:T(8,128)(2,1)S(1)} %get-tuple-element.27), channel_id=1, source_target_pairs={{0,48},{8,56},{16,0},{24,8},{32,16},{40,24},{48,32},{56,40},{64,11... | collective-permute-start | bytes 196616 | tf_op jit(solution)/shard_map/ppermute | solution.py:126
  29.2 6.0 %collective-permute-start.10 = (bf16[4,4,16,128]{3,2,1,0:T(8,128)(2,1)S(1)}, bf16[4,4,16,128]{3,2,1,0:T(8,128)(2,1)S(1)}, u32[]{:S(2)}, u32[]{:S(2)}) collective-permute-start(bf16[4,4,16,128]{3,2,1,0:T(8,128)(2,1)S(1)} %get-tuple-element.28), channel_id=1, source_target_pairs={{0,56},{8,48},{16,8},{24,0},{32,24},{40,16},{48,40},{56,32},{64,12... | collective-permute-start | bytes 196616 | tf_op jit(solution)/shard_map/ppermute | solution.py:126
  40.7 8.6 %copy-start = (bf16[512,512]{1,0:T(8,128)(2,1)S(1)}, bf16[512,512]{1,0:T(8,128)(2,1)}, u32[]{:S(2)}) copy-start(bf16[512,512]{1,0:T(8,128)(2,1)} %q_ref.3) | copy-start | bytes 1572868
  40.8 25.0 %all-to-all-start.1 = ((bf16[32,4,16,128]{3,2,1,0:T(8,128)(2,1)}), bf16[32,4,16,128]{3,2,1,0:T(8,128)(2,1)S(1)}, u32[]{:S(2)}, u32[]{:S(2)}) async-start(bf16[32,4,16,128]{3,2,1,0:T(8,128)(2,1)} %bitcast.1), calls=%async_computation.1 | async-start | bytes 1048576 | tf_op jit(solution)/shard_map/all_to_all | solution.py:307
  49.3 16.4 %copy-start.3 = (bf16[512,512]{1,0:T(8,128)(2,1)S(1)}, bf16[512,512]{1,0:T(8,128)(2,1)}, u32[]{:S(2)}) copy-start(bf16[512,512]{1,0:T(8,128)(2,1)} %stream_ref.1) | copy-start | bytes 1572868
  49.4 16.4 %copy-start.12 = (f32[512]{0:T(512)S(1)}, f32[512]{0:T(512)}, u32[]{:S(2)}) copy-start(f32[512]{0:T(512)} %param.21) | copy-start | bytes 6148

commit v3 on v2

v3 whole, which is shorter than its diff:
```python
import jax
import jax.numpy as jnp
import numpy as np
from jax import lax
from jax.experimental import pallas as pl
from jax.experimental.pallas import tpu as pltpu
from jax.sharding import PartitionSpec as P

LANE = 128
EDGE = 16
GROUP = 8
Z_SIZE = 4
X_SIZE = 4
AHEAD = 3
MIB = 1024 * 1024


def params(mebibytes):
    return pltpu.CompilerParams(vmem_limit_bytes=mebibytes * MIB)


def cost(micros):
    return pl.CostEstimate(flops=int(micros * 1e9), bytes_accessed=0, transcendentals=0)


def tables():
    n = LANE * LANE
    a = np.arange(LANE, dtype=np.float64)
    first = -2.0 * np.pi * np.outer(a + 0.25, a) / LANE
    twist = -2.0 * np.pi * np.outer(a + 0.25, a) / n
    second = -2.0 * np.pi * np.outer(a, a) / LANE
    t1 = np.concatenate([np.cos(first), np.sin(first)], 0)
    cos2, sin2 = np.cos(second), np.sin(second)
    t2 = np.block([[cos2, sin2], [-sin2, cos2]])
    t2_inv = np.block([[cos2, -sin2], [sin2, cos2]])
    t1_inv = np.concatenate([np.cos(first).T, np.sin(first).T], 1) / n
    low = [jnp.asarray(t, jnp.bfloat16) for t in (t1, t2, t2_inv, t1_inv)]
    return (*low, jnp.asarray(np.cos(twist), jnp.float32), jnp.asarray(np.sin(twist), jnp.float32))


def place():
    me = lax.axis_index("seq")
    return me // (X_SIZE * 2), me // 2 % X_SIZE, me % 2


HBM = pl.BlockSpec(memory_space=pl.ANY)
VMEM = pl.BlockSpec(memory_space=pltpu.VMEM)


def send(source, target, sem):
    copy = pltpu.make_async_copy(source, target, sem)
    copy.start()
    return copy


def wait_all(copies):
    for copy in copies:
        copy.wait()


def edge_rows(first, last):
    zero = jnp.zeros_like(first[:1])
    own = [first[0:1], first[1:2], zero, first[0:1]]
    passed = [last[EDGE - 1 :], zero, last[EDGE - 2 : EDGE - 1], last[EDGE - 1 :]]
    return own, passed


def lead_kernel(k_ref, v_ref, f_ref, *rest):
    outs, (f_buf, e_buf, out_buf, f_sem, e_sem, out_sem) = rest[:Z_SIZE], rest[Z_SIZE:]
    rows = f_ref.shape[0]
    slabs = outs[0].shape[2] - 1
    head, tail = pl.ds(0, EDGE), pl.ds(rows - EDGE, EDGE)
    pieces = [pl.ds(j * LANE, LANE) for j in range(slabs)]
    f_copies = [send(f_ref.at[p, :], f_buf.at[p, :], f_sem.at[j]) for j, p in enumerate(pieces)]
    sources = [k_ref.at[head, :], k_ref.at[tail, :], v_ref.at[head, :], v_ref.at[tail, :]]
    e_copies = [send(x, e_buf.at[i], e_sem.at[i]) for i, x in enumerate(sources)]
    z, x, c = place()
    depth = outs[0].shape[3]
    out_copies = []

    def put(j, block_of):
        for kz in range(Z_SIZE):
            g = (z + kz) % Z_SIZE
            block = block_of(pl.ds(pl.multiple_of(g * LANE, LANE), LANE))
            turned = block.T.astype(out_buf.dtype)
            for d in range(X_SIZE * 2):
                tile = turned[d * depth : (d + 1) * depth]
                out_buf[kz, (d // 2 - x + X_SIZE) % X_SIZE, (d % 2 - c + 2) % 2, j] = tile
        for kz, out_ref in enumerate(outs):
            out_copies.append(send(out_buf.at[kz, :, :, j], out_ref.at[:, :, j], out_sem.at[kz, j]))

    for j, p in enumerate(pieces):
        f_copies[j].wait()
        put(j, lambda cols, p=p: f_buf[p, cols].astype(jnp.float32))
    wait_all(e_copies)

    def edge_block(cols):
        k0, k1, v0, v1 = [e_buf[i, :, cols].astype(jnp.float32) for i in range(len(sources))]
        own_k, next_k = edge_rows(k0, k1)
        own_v, next_v = edge_rows(v0, v1)
        listed = own_k + own_v + next_k + next_v
        return jnp.concatenate(listed + [jnp.zeros((LANE - len(listed), LANE), jnp.float32)], 0)

    put(slabs, edge_block)
    wait_all(out_copies)


def lead(k, v, f, groups):
    rows, width = f.shape
    slabs = AHEAD
    shape = jax.ShapeDtypeStruct((X_SIZE, 2, slabs + 1, width // groups, LANE), f.dtype)
    return pl.pallas_call(
        lead_kernel,
        in_specs=[HBM] * 3,
        out_specs=(HBM,) * Z_SIZE,
        out_shape=(shape,) * Z_SIZE,
        scratch_shapes=[
            pltpu.VMEM((slabs * LANE, width), f.dtype),
            pltpu.VMEM((4, EDGE, width), f.dtype),
            pltpu.VMEM((Z_SIZE, *shape.shape), f.dtype),
            pltpu.SemaphoreType.DMA((slabs,)),
            pltpu.SemaphoreType.DMA((4,)),
            pltpu.SemaphoreType.DMA((Z_SIZE, slabs + 1)),
        ],
        cost_estimate=cost(10),
        compiler_params=params(60),
    )(k, v, f)


def coef_kernel(taps_ref, skip_ref, taps_out, skip_out, turned):
    depth = skip_out.shape[0]
    me = lax.axis_index("seq")
    per = LANE // depth
    cols = pl.ds(pl.multiple_of(me // per * LANE, LANE), LANE)
    k, v = taps_ref[1, :, cols], taps_ref[2, :, cols]

    def pairs(w, order):
        return [w[i : i + 1] for i in order for _ in range(2)]

    rows = pairs(k, (0, 1)) + pairs(v, (0, 1)) + pairs(k, (1, 2)) + pairs(v, (1, 2))
    zeros = jnp.zeros((LANE - len(rows), LANE), jnp.float32)
    mine = pl.ds(pl.multiple_of(me % per * depth, depth), depth)
    turned[...] = jnp.concatenate(rows + [zeros], 0).T
    taps_out[...] = turned[mine, :]
    turned[...] = jnp.broadcast_to(skip_ref[:, cols], (LANE, LANE)).T
    skip_out[...] = turned[mine, :]


def coefficients(taps, skip, depth):
    shape = jax.ShapeDtypeStruct((depth, LANE), jnp.float32)
    return pl.pallas_call(
        coef_kernel,
        out_shape=(shape, shape),
        scratch_shapes=[pltpu.VMEM((LANE, LANE), jnp.float32)],
        compiler_params=params(4),
    )(taps, skip[None, :])


def put_turned(out_ref, j, block):
    depth = out_ref.shape[2]
    per = LANE // depth
    for g in range(block.shape[1] // LANE):
        turned = block[:, g * LANE : (g + 1) * LANE].T
        out_ref[g * per : (g + 1) * per, j] = turned.reshape(per, depth, LANE).astype(out_ref.dtype)


def pack_kernel(*refs):
    ins, outs = refs[:Z_SIZE], refs[Z_SIZE:]
    for d, out_ref in enumerate(outs):
        for kz, in_ref in enumerate(ins):
            out_ref[kz] = in_ref[d // 2, d % 2]


def pack(parts):
    shape = jax.ShapeDtypeStruct((Z_SIZE, *parts[0].shape[2:]), parts[0].dtype)
    return pl.pallas_call(
        pack_kernel,
        out_shape=(shape,) * (X_SIZE * 2),
        cost_estimate=cost(20),
        compiler_params=params(6),
    )(*parts)


def shift(block, dz, dx, dc):
    route = []
    for z in range(Z_SIZE):
        for x in range(X_SIZE):
            for c in range(2):
                to = ((z + dz) % Z_SIZE * X_SIZE + (x + dx) % X_SIZE) * 2 + (c + dc) % 2
                route.append(((z * X_SIZE + x) * 2 + c, to))
    return lax.ppermute(block, "seq", route)


def spread(parts):
    parts = [parts[0]] + [shift(parts[k], k, 0, 0) for k in range(1, Z_SIZE)]
    parts = pack(parts)
    return [parts[0]] + [shift(parts[d], 0, d // 2, d % 2) for d in range(1, X_SIZE * 2)]


def extend(ext_ref, x_ref, edge):
    rows = x_ref.shape[0]
    ext_ref[0:8, :] = edge
    ext_ref[8 : 8 + rows, :] = x_ref[...].astype(jnp.float32)


def taps_of(ext_ref, taps, start, size):
    return (
        taps[0:1, :] * ext_ref[start + 8 : start + 8 + size, :]
        + taps[1:2, :] * ext_ref[start + 7 : start + 7 + size, :]
        + taps[2:3, :] * ext_ref[start + 6 : start + 6 + size, :]
    )


def product_kernel(k_ref, v_ref, f_ref, taps_ref, out_ref, k_ext, v_ext, out_buf, sem):
    slabs = k_ref.shape[0] // LANE
    copies = []

    def put(j, block):
        put_turned(out_buf, j, block)
        copies.append(send(out_buf.at[:, j], out_ref.at[:, j], sem.at[j]))

    for j in range(AHEAD, slabs):
        put(slabs + j - AHEAD, f_ref[j * LANE : (j + 1) * LANE, :].astype(jnp.float32))
    zero = jnp.zeros((8, k_ref.shape[1]), jnp.float32)
    k_ext[0:8, :] = zero
    v_ext[0:8, :] = zero
    for j in range(slabs):
        rows, ext = slice(j * LANE, (j + 1) * LANE), slice(8 + j * LANE, 8 + (j + 1) * LANE)
        k_ext[ext, :] = k_ref[rows, :].astype(jnp.float32)
        v_ext[ext, :] = v_ref[rows, :].astype(jnp.float32)
        kf = taps_of(k_ext, taps_ref[1], j * LANE, LANE)
        vf = taps_of(v_ext, taps_ref[2], j * LANE, LANE)
        put(j, kf * vf)
    wait_all(copies)


def product(k, v, f, taps, groups):
    rows, width = k.shape
    ext = pltpu.VMEM((rows + 8, width), jnp.float32)
    slabs = rows // LANE * 2 - AHEAD
    shape = jax.ShapeDtypeStruct((groups, slabs, width // groups, LANE), k.dtype)
    return pl.pallas_call(
        product_kernel,
        in_specs=[VMEM] * 4,
        out_specs=HBM,
        out_shape=shape,
        scratch_shapes=[ext, ext, pltpu.VMEM(shape.shape, shape.dtype), pltpu.SemaphoreType.DMA((slabs,))],
        cost_estimate=cost(20),
        compiler_params=params(12),
    )(k, v, f, taps)


def gate_kernel(q_ref, edge_ref, taps_ref, out_ref, q_ext):
    extend(q_ext, q_ref, edge_ref[EDGE - 8 :, :].astype(jnp.float32))
    for j in range(out_ref.shape[0] // LANE):
        qf = taps_of(q_ext, taps_ref[0], j * LANE, LANE)
        out_ref[j * LANE : (j + 1) * LANE, :] = qf.astype(out_ref.dtype)


def gate(q, edge, taps):
    rows, width = q.shape
    return pl.pallas_call(
        gate_kernel,
        out_shape=jax.ShapeDtypeStruct(q.shape, q.dtype),
        scratch_shapes=[pltpu.VMEM((rows + 8, width), jnp.float32)],
        compiler_params=params(8),
    )(q, edge, taps)


def mix(table, data):
    return jnp.dot(table, data, preferred_element_type=jnp.float32)


def mend(u_wide, edges, taps):
    depth = taps.shape[0]
    rows = edges.shape[0] - depth
    lane = lax.broadcasted_iota(jnp.int32, (rows, LANE), 1)
    sources = rows // depth
    weights = jnp.broadcast_to(taps[...][None], (sources, depth, LANE)).reshape(rows, LANE)
    terms = jnp.where(lane < 8, edges[depth:, :], edges[:rows, :]) * weights

    def after(x, steps):
        return pltpu.roll(x, LANE - steps, 1)

    terms = terms + after(terms, 2)
    terms = terms + after(terms, 8)
    fixed = (terms * after(terms, 4)).astype(jnp.bfloat16).astype(jnp.float32)
    size = u_wide.shape[0] // sources
    for i in range(sources):
        part, at = slice(i * depth, (i + 1) * depth), slice(i * size, i * size + depth)
        u_wide[at, :] = jnp.where(lane[part] < 2, fixed[part], u_wide[at, :])


def conv_kernel(u_ref, q_ref, taps_ref, skip_ref, t1, t2, t2_inv, t1_inv, tw_c, tw_s, *rest):
    f_refs, (y_ref, q_edge, u_wide, f_wide, y_wide, edges, y_buf, q_sem, y_sem) = rest[:-9], rest[-9:]
    q_copy = send(q_ref.at[pl.ds(q_ref.shape[0] - EDGE, EDGE), :], q_edge, q_sem)
    depth = skip_ref.shape[0]
    edges[:depth, :] = jnp.zeros((depth, LANE), jnp.float32)
    z, x, c = place()
    sources = u_ref.shape[0]
    size = u_wide.shape[0] // sources
    ahead = AHEAD * depth
    for i in range(sources):
        both = u_ref[i].astype(jnp.float32).reshape(-1, LANE)
        u_wide[i * size : (i + 1) * size, :] = both[:size]
        f_wide[i * size + ahead : (i + 1) * size, :] = both[size:]
    for d, f_ref in enumerate(f_refs):
        for kz in range(Z_SIZE):
            src = ((z - kz + Z_SIZE) % Z_SIZE * X_SIZE + (x - d // 2 + X_SIZE) % X_SIZE) * 2 + (c + d) % 2
            row = pl.multiple_of(src * size, size)
            f_wide[pl.ds(row, ahead), :] = f_ref[kz, :AHEAD].reshape(ahead, LANE).astype(jnp.float32)
            row = pl.multiple_of((src + 1) * depth, depth)
            edges[pl.ds(row, depth), :] = f_ref[kz, AHEAD].astype(jnp.float32)
    mend(u_wide, edges, taps_ref)
    low = jnp.bfloat16

    def part(x, i):
        return x[:, i * LANE : (i + 1) * LANE]

    for start in range(0, depth, GROUP):
        chans = range(start, start + GROUP)
        rows = [pl.ds(c, LANE, stride=depth) for c in chans]
        data = [u_wide[r, :].astype(low) for r in rows] + [f_wide[r, :].astype(low) for r in rows]
        first = mix(t1[...], jnp.concatenate(data, 1))
        turned = []
        for i in range(2 * GROUP):
            re, im = part(first[:LANE], i), part(first[LANE:], i)
            c, s = tw_c[...], tw_s[...]
            turned.append(jnp.concatenate([re * c - im * s, re * s + im * c], 1).astype(low))
        spec = mix(jnp.concatenate(turned, 0), t2[...])
        prod = []
        for i in range(GROUP):
            a = spec[i * LANE : (i + 1) * LANE]
            b = spec[(GROUP + i) * LANE : (GROUP + i + 1) * LANE]
            ar, ai, br, bi = a[:, :LANE], a[:, LANE:], b[:, :LANE], b[:, LANE:]
            prod.append(jnp.concatenate([ar * br - ai * bi, ar * bi + ai * br], 1).astype(low))
        back = mix(jnp.concatenate(prod, 0), t2_inv[...])
        cols = []
        for i in range(GROUP):
            v = back[i * LANE : (i + 1) * LANE]
            re, im = v[:, :LANE], v[:, LANE:]
            c, s = tw_c[...], tw_s[...]
            cols.append(jnp.concatenate([re * c + im * s, im * c - re * s], 0).astype(low))
        conv = mix(t1_inv[...], jnp.concatenate(cols, 1))
        for i, r in enumerate(rows):
            y_wide[r, :] = part(conv, i)
    copies = []
    parts = y_sem.shape[0]
    rows = y_ref.shape[0] // parts
    shape = (rows // depth, depth, LANE)
    for i in range(parts):
        at = slice(i * rows, (i + 1) * rows)
        y = y_wide[at, :].reshape(shape) + skip_ref[...][None] * u_wide[at, :].reshape(shape)
        y_buf[at, :] = y.reshape(rows, LANE).astype(y_buf.dtype)
        copies.append(send(y_buf.at[at, :], y_ref.at[at, :], y_sem.at[i]))
    wait_all(copies + [q_copy])


def long_conv(u, f, q, taps, skip):
    sources, slabs, depth, _ = u.shape
    slabs = (slabs + AHEAD) // 2
    flat = (sources * slabs * depth, LANE)
    wide = pltpu.VMEM(flat, jnp.float32)
    edges = pltpu.VMEM(((sources + 1) * depth, LANE), jnp.float32)
    operands = (u, q, taps, skip, *tables(), *f)
    y, q_edge = pl.pallas_call(
        conv_kernel,
        in_specs=[HBM if x is q else VMEM for x in operands],
        out_specs=(HBM, VMEM),
        out_shape=(jax.ShapeDtypeStruct(flat, u.dtype), jax.ShapeDtypeStruct((EDGE, q.shape[1]), q.dtype)),
        scratch_shapes=[wide] * 3
        + [edges, pltpu.VMEM(flat, u.dtype), pltpu.SemaphoreType.DMA, pltpu.SemaphoreType.DMA((4,))],
        compiler_params=params(40),
    )(*operands)
    return y.reshape(sources, slabs, depth, LANE), q_edge


def join_kernel(y_ref, qf_ref, stream_ref, gain_ref, out_ref, sum_ref, sq_ref, out_buf, sem):
    groups, slabs, depth, _ = y_ref.shape
    per = LANE // depth
    sq_ref[...] = jnp.zeros_like(sq_ref)
    copies = []
    for j in range(slabs):
        rows = slice(j * LANE, (j + 1) * LANE)
        squares = jnp.zeros((LANE, LANE), jnp.float32)
        for g in range(groups // per):
            cols = slice(g * LANE, (g + 1) * LANE)
            y = y_ref[g * per : (g + 1) * per, j].reshape(LANE, LANE).astype(jnp.float32).T
            gated = (qf_ref[rows, cols].astype(jnp.float32) * y).astype(jnp.bfloat16)
            summed = stream_ref[rows, cols].astype(jnp.float32) + gated.astype(jnp.float32)
            out_buf[rows, cols] = summed.astype(out_buf.dtype)
            sum_ref[rows, cols] = summed * gain_ref[:, cols]
            squares = squares + summed * summed
        copies.append(send(out_buf.at[rows, :], out_ref.at[rows, :], sem.at[j]))
        total = jnp.sum(squares.T, axis=0, keepdims=True)
        for d in range(sq_ref.shape[0]):
            sq_ref[d, j : j + 1, :] = total
    wait_all(copies)


def join(y, qf, stream, gain, fan):
    rows, _ = stream.shape
    return pl.pallas_call(
        join_kernel,
        in_specs=[VMEM] * 4,
        out_specs=(HBM, VMEM, VMEM),
        out_shape=(
            jax.ShapeDtypeStruct(stream.shape, stream.dtype),
            jax.ShapeDtypeStruct(stream.shape, jnp.float32),
            jax.ShapeDtypeStruct((fan, 8, LANE), jnp.float32),
        ),
        scratch_shapes=[
            pltpu.VMEM(stream.shape, stream.dtype),
            pltpu.SemaphoreType.DMA((rows // LANE,)),
        ],
        compiler_params=params(12),
    )(y, qf, stream, gain[None, :])


def norm_kernel(channels, sum_ref, sq_ref, out_ref, out_buf, sem):
    squares = jnp.sum(sq_ref[...], axis=0)
    scale = 1.0 / jnp.sqrt(squares / channels + 1e-05)
    copies = []
    for j in range(out_ref.shape[0] // LANE):
        rows = slice(j * LANE, (j + 1) * LANE)
        column = jnp.broadcast_to(scale[j : j + 1, :], (LANE, LANE)).T
        for g in range(out_ref.shape[1] // LANE):
            cols = slice(g * LANE, (g + 1) * LANE)
            out_buf[rows, cols] = (sum_ref[rows, cols] * column).astype(out_buf.dtype)
        copies.append(send(out_buf.at[rows, :], out_ref.at[rows, :], sem.at[j]))
    wait_all(copies)


def norm(summed, squares):
    channels = summed.shape[1] * squares.shape[0]

    def kernel(*refs):
        norm_kernel(channels, *refs)

    return pl.pallas_call(
        kernel,
        in_specs=[VMEM] * 2,
        out_specs=HBM,
        out_shape=jax.ShapeDtypeStruct(summed.shape, jnp.bfloat16),
        scratch_shapes=[
            pltpu.VMEM(summed.shape, jnp.bfloat16),
            pltpu.SemaphoreType.DMA((summed.shape[0] // LANE,)),
        ],
        compiler_params=params(8),
    )(summed, squares)


def exchange(x, axis):
    return lax.all_to_all(x, axis, split_axis=0, concat_axis=0, tiled=True)


def shards(queries, keys, values, filters, short_weights, skip_gain, stream, norm_gain):
    groups = lax.axis_size("seq")
    fan = lax.axis_size("ch")
    rows, width = queries.shape
    slab = width // groups
    parts = lead(keys, values, filters, groups)
    u_all = exchange(product(keys, values, filters, short_weights, groups), "seq")
    f_all = spread(parts)
    taps, skip = coefficients(short_weights, skip_gain, slab)
    y, q_edge = long_conv(u_all, f_all, queries, taps, skip)
    y_home = exchange(y, "seq")
    q_edge = lax.ppermute(q_edge, "seq", [(i, i + 1) for i in range(groups - 1)])
    qf = gate(queries, q_edge, short_weights)
    stream_out, summed, squares = join(y_home, qf, stream, norm_gain, fan)
    normed = norm(summed, exchange(squares, "ch"))
    return (stream_out, normed)


def solution(mesh):
    wide = P("seq", "ch")
    in_specs = (wide, wide, wide, wide, P(None, None, "ch"), P("ch"), wide, P("ch"))
    return jax.shard_map(shards, mesh=mesh, in_specs=in_specs, out_specs=(wide, wide), check_vma=False)
```

time: 84.9 us -> 82.5 us (0.972)
  blocking collectives: 16.3 us -> 18.3 us
  local copies, waits for them, and re-layouts: 1.69 us -> 0.08 us
  starting transfers between devices: 32.2 us -> 30.6 us
  waiting for transfers between devices: 22.6 us -> 21.1 us
    all_to_all x2, waiting for transfers between devices: 16.9 us -> 14.3 us  [exchange(): return lax.all_to_all(x, axis, split_axis=0, concat_axis=0, tiled=True)]
    all_to_all x2, starting transfers between devices: 13.3 us -> 11 us  [exchange(): return lax.all_to_all(x, axis, split_axis=0, concat_axis=0, tiled=True)]
    all_to_all x1, blocking collectives: 16.3 us -> 18.3 us  [exchange(): return lax.all_to_all(x, axis, split_axis=0, concat_axis=0, tiled=True)]
    ppermute x10, starting transfers between devices: 14.3 us -> 16 us  [shift(): return lax.ppermute(block, 'seq', route)]
    ppermute x1, starting transfers between devices: 4.64 us -> 3.67 us  [shards(): lax.ppermute(q_edge, 'seq', [(i, i + 1) for i in range(groups - 1)])]
  transfers between devices with their start and end apart: 13 -> 13, of which waited for: 6 -> 8; matrix products, arithmetic and copies ran while one was open for 1% -> 0% of each run, Pallas kernels for 3% -> 3%
where the time goes in v3:
time: 82.5 us; the launch traced here: 82.1 us
  starting transfers between devices  30.6 us (37%)
  waiting for transfers between devices  21.1 us (26%)
  blocking collectives  18.3 us (22%)
  Pallas kernels  11 us (13%)
  between operations  1.03 us (1%)
    all_to_all x1, blocking collectives, exchange(): return lax.all_to_all(x, axis, split_axis=0, concat_axis=0, tiled=True)  18.3 us
    ppermute x10, starting transfers between devices, shift(): return lax.ppermute(block, 'seq', route)  16 us
    all_to_all x2, waiting for transfers between devices, exchange(): return lax.all_to_all(x, axis, split_axis=0, concat_axis=0, tiled=True)  14.3 us
    all_to_all x2, starting transfers between devices, exchange(): return lax.all_to_all(x, axis, split_axis=0, concat_axis=0, tiled=True)  11 us
    ppermute x10, waiting for transfers between devices, shift(): return lax.ppermute(block, 'seq', route)  6.02 us
    pallas_call x1, Pallas kernels, long_conv(): pl.pallas_call(conv_kernel, in_specs=[HBM if x is q else VMEM for x in op...  4 us
    ppermute x1, starting transfers between devices, shards(): lax.ppermute(q_edge, 'seq', [(i, i + 1) for i in range(groups - 1)])  3.67 us
    pallas_call x1, Pallas kernels, lead(): pl.pallas_call(lead_kernel, in_specs=[HBM] * 3, out_specs=(HBM,) * Z_SIZE...  2.37 us
  transfers between devices with their start and end apart: 13, of which 8 were waited for; matrix products, arithmetic and copies ran while one was open for 0% of the time, Pallas kernels for 3%

profile of v3, /device:TPU:1, one launch (start us, length us, event | category | flops | bytes accessed | tf_op | source)
XLA Modules:
  0.0 82.1 jit_solution(15348495406937876792)
XLA Ops:
  0.6 0.0 copy-start.13
  0.6 0.0 copy-start.12
  0.7 0.0 copy-start.11
  0.7 0.0 copy-start.4
  0.7 2.4 %shard_map.151 = (bf16[4,2,4,16,128]{4,3,2,1,0:T(8,128)(2,1)}, bf16[4,2,4,16,128]{4,3,2,1,0:T(8,128)(2,1)}, bf16[4,2,4,16,128]{4,3,2,1,0:T(8,128)(2,1)}, bf16[4,2,4,16,128]{4,3,2,1,0:T(8,128)(2,1)}) custom-call(bf16[512,512]{1,0:T(8,128)(2,1)} %k_ref.3, bf16[512,512]{1,0:T(8,128)(2,1)} %v_ref.3, bf16[512,512]{1,0:T(8,128)(2,1)} %f_ref.3), custom_call_target="tpu_custom_call" | custom-call | flops 10000000000 | tf_op jit(solution)/shard_map/pallas_call | solution.py:112
  3.1 2.5 %collective-permute-start = (bf16[4,2,4,16,128]{4,3,2,1,0:T(8,128)(2,1)}, bf16[4,2,4,16,128]{4,3,2,1,0:T(8,128)(2,1)S(1)}, u32[]{:S(2)}, u32[]{:S(2)}) collective-permute-start(bf16[4,2,4,16,128]{4,3,2,1,0:T(8,128)(2,1)} %get-tuple-element.24), channel_id=1, source_target_pairs={{0,64},{8,72},{16,80},{24,88},{32,96},{40,104},{48,112},{56,120},{... | collective-permute-start | bytes 393224 | tf_op jit(solution)/shard_map/ppermute | solution.py:191
  5.6 3.0 %collective-permute-start.1 = (bf16[4,2,4,16,128]{4,3,2,1,0:T(8,128)(2,1)}, bf16[4,2,4,16,128]{4,3,2,1,0:T(8,128)(2,1)S(1)}, u32[]{:S(2)}, u32[]{:S(2)}) collective-permute-start(bf16[4,2,4,16,128]{4,3,2,1,0:T(8,128)(2,1)} %get-tuple-element.25), channel_id=1, source_target_pairs={{0,128},{8,136},{16,144},{24,152},{32,160},{40,168},{48,176},{56,1... | collective-permute-start | bytes 393224 | tf_op jit(solution)/shard_map/ppermute | solution.py:191
  8.6 0.7 collective-permute-start.2
  9.3 0.0 copy-done.13
  9.3 0.0 copy-done.12
  9.3 1.7 %shard_map.149 = bf16[32,5,16,128]{3,2,1,0:T(8,128)(2,1)} custom-call(bf16[512,512]{1,0:T(8,128)(2,1)S(1)} %copy-done.11, bf16[512,512]{1,0:T(8,128)(2,1)S(1)} %copy-done.12, bf16[512,512]{1,0:T(8,128)(2,1)S(1)} %copy-done.13, f32[3,3,512]{2,1,0:T(4,128)S(1)} %copy-done.4), custom_call_target="tpu_custom_call" | custom-call | flops 20000000000 | tf_op jit(solution)/shard_map/pallas_call | solution.py:242
  11.1 0.0 copy-start.14
  11.1 6.6 %all-to-all-start = ((bf16[32,5,16,128]{3,2,1,0:T(8,128)(2,1)}), bf16[32,5,16,128]{3,2,1,0:T(8,128)(2,1)S(1)}, u32[]{:S(2)}, u32[]{:S(2)}) async-start(bf16[32,5,16,128]{3,2,1,0:T(8,128)(2,1)} %shard_map.149), calls=%async_computation | async-start | bytes 1310720 | tf_op jit(solution)/shard_map/all_to_all | solution.py:454
  17.7 0.0 collective-permute-done.refs_1_
  17.7 0.5 collective-permute-done.1.refs_2_
  18.1 0.0 collective-permute-done.2.refs_3_
  18.1 0.0 copy-start.2
  18.2 0.0 copy-start.3
  18.2 0.0 copy-start.5
  18.2 0.0 copy-start.6
  18.2 0.0 copy-start.7
  18.2 0.0 copy-start.8
  18.3 0.8 collective-permute-start.3
  19.0 1.1 %collective-permute-start.4 = (bf16[4,4,16,128]{3,2,1,0:T(8,128)(2,1)S(1)}, bf16[4,4,16,128]{3,2,1,0:T(8,128)(2,1)S(1)}, u32[]{:S(2)}, u32[]{:S(2)}) collective-permute-start(bf16[4,4,16,128]{3,2,1,0:T(8,128)(2,1)S(1)} %get-tuple-element.29), channel_id=1, source_target_pairs={{0,16},{8,24},{16,32},{24,40},{32,48},{40,56},{48,0},{56,8},{64,80... | collective-permute-start | bytes 196616 | tf_op jit(solution)/shard_map/ppermute | solution.py:191
  20.1 1.5 %collective-permute-start.5 = (bf16[4,4,16,128]{3,2,1,0:T(8,128)(2,1)S(1)}, bf16[4,4,16,128]{3,2,1,0:T(8,128)(2,1)S(1)}, u32[]{:S(2)}, u32[]{:S(2)}) collective-permute-start(bf16[4,4,16,128]{3,2,1,0:T(8,128)(2,1)S(1)} %get-tuple-element.30), channel_id=1, source_target_pairs={{0,24},{8,16},{16,40},{24,32},{32,56},{40,48},{48,8},{56,0},{64,88... | collective-permute-start | bytes 196616 | tf_op jit(solution)/shard_map/ppermute | solution.py:191
  21.6 1.6 %collective-permute-start.6 = (bf16[4,4,16,128]{3,2,1,0:T(8,128)(2,1)S(1)}, bf16[4,4,16,128]{3,2,1,0:T(8,128)(2,1)S(1)}, u32[]{:S(2)}, u32[]{:S(2)}) collective-permute-start(bf16[4,4,16,128]{3,2,1,0:T(8,128)(2,1)S(1)} %get-tuple-element.31), channel_id=1, source_target_pairs={{0,32},{8,40},{16,48},{24,56},{32,0},{40,8},{48,16},{56,24},{64,96... | collective-permute-start | bytes 196616 | tf_op jit(solution)/shard_map/ppermute | solution.py:191
  23.1 1.7 %collective-permute-start.7 = (bf16[4,4,16,128]{3,2,1,0:T(8,128)(2,1)S(1)}, bf16[4,4,16,128]{3,2,1,0:T(8,128)(2,1)S(1)}, u32[]{:S(2)}, u32[]{:S(2)}) collective-permute-start(bf16[4,4,16,128]{3,2,1,0:T(8,128)(2,1)S(1)} %get-tuple-element.32), channel_id=1, source_target_pairs={{0,40},{8,32},{16,56},{24,48},{32,8},{40,0},{48,24},{56,16},{64,10... | collective-permute-start | bytes 196616 | tf_op jit(solution)/shard_map/ppermute | solution.py:191
  24.9 0.0 collective-permute-done.3.rest_1_
  24.9 1.5 %collective-permute-start.8 = (bf16[4,4,16,128]{3,2,1,0:T(8,128)(2,1)S(1)}, bf16[4,4,16,128]{3,2,1,0:T(8,128)(2,1)S(1)}, u32[]{:S(2)}, u32[]{:S(2)}) collective-permute-start(bf16[4,4,16,128]{3,2,1,0:T(8,128)(2,1)S(1)} %get-tuple-element.33), channel_id=1, source_target_pairs={{0,48},{8,56},{16,0},{24,8},{32,16},{40,24},{48,32},{56,40},{64,11... | collective-permute-start | bytes 196616 | tf_op jit(solution)/shard_map/ppermute | solution.py:191
  26.4 0.3 collective-permute-done.4.rest_2_
  26.7 1.6 %collective-permute-start.9 = (bf16[4,4,16,128]{3,2,1,0:T(8,128)(2,1)S(1)}, bf16[4,4,16,128]{3,2,1,0:T(8,128)(2,1)S(1)}, u32[]{:S(2)}, u32[]{:S(2)}) collective-permute-start(bf16[4,4,16,128]{3,2,1,0:T(8,128)(2,1)S(1)} %get-tuple-element.34), channel_id=1, source_target_pairs={{0,56},{8,48},{16,8},{24,0},{32,24},{40,16},{48,40},{56,32},{64,12... | collective-permute-start | bytes 196616 | tf_op jit(solution)/shard_map/ppermute | solution.py:191
  28.3 0.1 shard_map.150
  28.4 0.9 %collective-permute-done.5.rest_3_ = bf16[4,4,16,128]{3,2,1,0:T(8,128)(2,1)S(1)} collective-permute-done((bf16[4,4,16,128]{3,2,1,0:T(8,128)(2,1)S(1)}, bf16[4,4,16,128]{3,2,1,0:T(8,128)(2,1)S(1)}, u32[]{:S(2)}, u32[]{:S(2)}) %collective-permute-start.5) | collective-permute-done | bytes 65568 | tf_op jit(solution)/shard_map/ppermute | solution.py:191
  29.3 2.3 %collective-permute-done.6.rest_4_ = bf16[4,4,16,128]{3,2,1,0:T(8,128)(2,1)S(1)} collective-permute-done((bf16[4,4,16,128]{3,2,1,0:T(8,128)(2,1)S(1)}, bf16[4,4,16,128]{3,2,1,0:T(8,128)(2,1)S(1)}, u32[]{:S(2)}, u32[]{:S(2)}) %collective-permute-start.6) | collective-permute-done | bytes 65568 | tf_op jit(solution)/shard_map/ppermute | solution.py:191
  31.6 2.1 %collective-permute-done.7.rest_5_ = bf16[4,4,16,128]{3,2,1,0:T(8,128)(2,1)S(1)} collective-permute-done((bf16[4,4,16,128]{3,2,1,0:T(8,128)(2,1)S(1)}, bf16[4,4,16,128]{3,2,1,0:T(8,128)(2,1)S(1)}, u32[]{:S(2)}, u32[]{:S(2)}) %collective-permute-start.7) | collective-permute-done | bytes 65568 | tf_op jit(solution)/shard_map/ppermute | solution.py:191
  33.6 0.0 collective-permute-done.8.rest_6_
  33.7 0.0 collective-permute-done.9.rest_7_
  33.7 2.9 %all-to-all-done.u_ref = bf16[32,5,16,128]{3,2,1,0:T(8,128)(2,1)S(1)} async-done(((bf16[32,5,16,128]{3,2,1,0:T(8,128)(2,1)}), bf16[32,5,16,128]{3,2,1,0:T(8,128)(2,1)S(1)}, u32[]{:S(2)}, u32[]{:S(2)}) %all-to-all-start) | async-done | bytes 655392 | tf_op jit(solution)/shard_map/all_to_all | solution.py:454
  36.7 4.0 %shard_map.153 = (bf16[2048,128]{1,0:T(8,128)(2,1)}, bf16[16,512]{1,0:T(8,128)(2,1)S(1)}) custom-call(bf16[32,5,16,128]{3,2,1,0:T(8,128)(2,1)S(1)} %all-to-all-done.u_ref, bf16[512,512]{1,0:T(8,128)(2,1)S(1)} %copy-done, f32[16,128]{1,0:T(8,128)S(1)} %get-tuple-element.21.taps_ref, f32[16,128]{1,0:T(8,128)S(1)} %get-tuple-element.22.skip_ref, ...), custom_call_target="tpu_custom_call" | custom-call | tf_op jit(solution)/shard_map/pallas_call | solution.py:366
  40.7 4.4 %all-to-all-start.1 = ((bf16[32,4,16,128]{3,2,1,0:T(8,128)(2,1)}), bf16[32,4,16,128]{3,2,1,0:T(8,128)(2,1)S(1)}, u32[]{:S(2)}, u32[]{:S(2)}) async-start(bf16[32,4,16,128]{3,2,1,0:T(8,128)(2,1)} %bitcast.1), calls=%async_computation.1 | async-start | bytes 1048576 | tf_op jit(solution)/shard_map/all_to_all | solution.py:454
  45.1 0.0 copy-start.1
  45.1 3.7 %collective-permute-start.10 = (bf16[16,512]{1,0:T(8,128)(2,1)S(1)}, bf16[16,512]{1,0:T(8,128)(2,1)S(1)}, u32[]{:S(2)}, u32[]{:S(2)}) collective-permute-start(bf16[16,512]{1,0:T(8,128)(2,1)S(1)} %get-tuple-element.36), channel_id=1, source_target_pairs={{0,8},{8,16},{16,24},{24,32},{32,40},{40,48},{48,56},{56,64},{64,7... | collective-permute-start | bytes 49160 | tf_op jit(solution)/shard_map/ppermute | solution.py:468
  48.8 0.8 %collective-permute-done.10.edge_ref = bf16[16,512]{1,0:T(8,128)(2,1)S(1)} collective-permute-done((bf16[16,512]{1,0:T(8,128)(2,1)S(1)}, bf16[16,512]{1,0:T(8,128)(2,1)S(1)}, u32[]{:S(2)}, u32[]{:S(2)}) %collective-permute-start.10) | collective-permute-done | bytes 16416 | tf_op jit(solution)/shard_map/ppermute | solution.py:468
  49.6 0.5 shard_map.154.qf_ref
  50.2 11.3 %all-to-all-done.1.y_ref = bf16[32,4,16,128]{3,2,1,0:T(8,128)(2,1)S(1)} async-done(((bf16[32,4,16,128]{3,2,1,0:T(8,128)(2,1)}), bf16[32,4,16,128]{3,2,1,0:T(8,128)(2,1)S(1)}, u32[]{:S(2)}, u32[]{:S(2)}) %all-to-all-start.1) | async-done | bytes 524320 | tf_op jit(solution)/shard_map/all_to_all | solution.py:454
  61.5 1.3 %shard_map.155 = (bf16[512,512]{1,0:T(8,128)(2,1)}, f32[512,512]{1,0:T(8,128)S(1)}, f32[8,8,128]{2,1,0:T(8,128)S(1)}) custom-call(bf16[32,4,16,128]{3,2,1,0:T(8,128)(2,1)S(1)} %all-to-all-done.1.y_ref, bf16[512,512]{1,0:T(8,128)(2,1)S(1)} %shard_map.154.qf_ref, bf16[512,512]{1,0:T(8,128)(2,1)S(1)} %copy-done.1, f32[1,512]{1,0:T(1,128)S(1)} %bitcast.3), custom_call_target="tpu_custom_call" | custom-call | tf_op jit(solution)/shard_map/pallas_call | solution.py:403
  62.8 18.3 %all_to_all.15.refs_1_ = f32[8,8,128]{2,1,0:T(8,128)S(1)} all-to-all(f32[8,8,128]{2,1,0:T(8,128)S(1)} %get-tuple-element.39), channel_id=1, replica_groups=mesh['seq'=32,'ch'=8] {'ch'}, dimensions={0} | all-to-all | bytes 65536 | tf_op jit(solution)/shard_map/all_to_all | solution.py:454
  81.0 0.9 %shard_map.156 = bf16[512,512]{1,0:T(8,128)(2,1)} custom-call(f32[512,512]{1,0:T(8,128)S(1)} %get-tuple-element.38.refs_0_, f32[8,8,128]{2,1,0:T(8,128)S(1)} %all_to_all.15.refs_1_), custom_call_target="tpu_custom_call" | custom-call | tf_op jit(solution)/shard_map/pallas_call | solution.py:440
  (17 shorter events, 0.1 us)
Async XLA Ops:
  0.6 8.7 %copy-start.13 = (bf16[512,512]{1,0:T(8,128)(2,1)S(1)}, bf16[512,512]{1,0:T(8,128)(2,1)}, u32[]{:S(2)}) copy-start(bf16[512,512]{1,0:T(8,128)(2,1)} %f_ref.3) | copy-start | bytes 1572868
  0.6 8.7 %copy-start.12 = (bf16[512,512]{1,0:T(8,128)(2,1)S(1)}, bf16[512,512]{1,0:T(8,128)(2,1)}, u32[]{:S(2)}) copy-start(bf16[512,512]{1,0:T(8,128)(2,1)} %v_ref.3) | copy-start | bytes 1572868
  0.7 8.7 %copy-start.11 = (bf16[512,512]{1,0:T(8,128)(2,1)S(1)}, bf16[512,512]{1,0:T(8,128)(2,1)}, u32[]{:S(2)}) copy-start(bf16[512,512]{1,0:T(8,128)(2,1)} %k_ref.3) | copy-start | bytes 1572868
  0.7 8.7 %copy-start.4 = (f32[3,3,512]{2,1,0:T(4,128)S(1)}, f32[3,3,512]{2,1,0:T(4,128)}, u32[]{:S(2)}) copy-start(f32[3,3,512]{2,1,0:T(4,128)} %taps_ref.5) | copy-start | bytes 55300
  3.1 14.6 %collective-permute-start = (bf16[4,2,4,16,128]{4,3,2,1,0:T(8,128)(2,1)}, bf16[4,2,4,16,128]{4,3,2,1,0:T(8,128)(2,1)S(1)}, u32[]{:S(2)}, u32[]{:S(2)}) collective-permute-start(bf16[4,2,4,16,128]{4,3,2,1,0:T(8,128)(2,1)} %get-tuple-element.24), channel_id=1, source_target_pairs={{0,64},{8,72},{16,80},{24,88},{32,96},{40,104},{48,112},{56,120},{... | collective-permute-start | bytes 393224 | tf_op jit(solution)/shard_map/ppermute | solution.py:191
  5.6 12.5 %collective-permute-start.1 = (bf16[4,2,4,16,128]{4,3,2,1,0:T(8,128)(2,1)}, bf16[4,2,4,16,128]{4,3,2,1,0:T(8,128)(2,1)S(1)}, u32[]{:S(2)}, u32[]{:S(2)}) collective-permute-start(bf16[4,2,4,16,128]{4,3,2,1,0:T(8,128)(2,1)} %get-tuple-element.25), channel_id=1, source_target_pairs={{0,128},{8,136},{16,144},{24,152},{32,160},{40,168},{48,176},{56,1... | collective-permute-start | bytes 393224 | tf_op jit(solution)/shard_map/ppermute | solution.py:191
  8.6 9.5 %collective-permute-start.2 = (bf16[4,2,4,16,128]{4,3,2,1,0:T(8,128)(2,1)}, bf16[4,2,4,16,128]{4,3,2,1,0:T(8,128)(2,1)S(1)}, u32[]{:S(2)}, u32[]{:S(2)}) collective-permute-start(bf16[4,2,4,16,128]{4,3,2,1,0:T(8,128)(2,1)} %get-tuple-element.26), channel_id=1, source_target_pairs={{0,192},{8,200},{16,208},{24,216},{32,224},{40,232},{48,240},{56,2... | collective-permute-start | bytes 393224 | tf_op jit(solution)/shard_map/ppermute | solution.py:191
  11.1 7.1 %copy-start.14 = (bf16[4,2,4,16,128]{4,3,2,1,0:T(8,128)(2,1)S(1)}, bf16[4,2,4,16,128]{4,3,2,1,0:T(8,128)(2,1)}, u32[]{:S(2)}) copy-start(bf16[4,2,4,16,128]{4,3,2,1,0:T(8,128)(2,1)} %get-tuple-element.23.refs_0_) | copy-start | bytes 393220
  11.1 25.5 %all-to-all-start = ((bf16[32,5,16,128]{3,2,1,0:T(8,128)(2,1)}), bf16[32,5,16,128]{3,2,1,0:T(8,128)(2,1)S(1)}, u32[]{:S(2)}, u32[]{:S(2)}) async-start(bf16[32,5,16,128]{3,2,1,0:T(8,128)(2,1)} %shard_map.149), calls=%async_computation | async-start | bytes 1310720 | tf_op jit(solution)/shard_map/all_to_all | solution.py:454
  18.1 18.5 %copy-start = (bf16[512,512]{1,0:T(8,128)(2,1)S(1)}, bf16[512,512]{1,0:T(8,128)(2,1)}, u32[]{:S(2)}) copy-start(bf16[512,512]{1,0:T(8,128)(2,1)} %q_ref.3) | copy-start | bytes 1572868
  18.1 18.5 %copy-start.2 = (bf16[256,256]{1,0:T(8,128)(2,1)S(1)}, bf16[256,256]{1,0:T(8,128)(2,1)}, u32[]{:S(2)}) copy-start(bf16[256,256]{1,0:T(8,128)(2,1)} %constant.14.clone.t2_inv) | copy-start | bytes 393220
  18.2 18.5 %copy-start.3 = (bf16[256,256]{1,0:T(8,128)(2,1)S(1)}, bf16[256,256]{1,0:T(8,128)(2,1)}, u32[]{:S(2)}) copy-start(bf16[256,256]{1,0:T(8,128)(2,1)} %constant.13.clone.t2) | copy-start | bytes 393220
  18.2 18.4 %copy-start.5 = (f32[128,128]{1,0:T(8,128)S(1)}, f32[128,128]{1,0:T(8,128)}, u32[]{:S(2)}) copy-start(f32[128,128]{1,0:T(8,128)} %constant.17.clone.tw_s) | copy-start | bytes 196612
  18.2 18.4 %copy-start.6 = (f32[128,128]{1,0:T(8,128)S(1)}, f32[128,128]{1,0:T(8,128)}, u32[]{:S(2)}) copy-start(f32[128,128]{1,0:T(8,128)} %constant.16.clone.tw_c) | copy-start | bytes 196612
  18.2 18.4 %copy-start.7 = (bf16[128,256]{1,0:T(8,128)(2,1)S(1)}, bf16[128,256]{1,0:T(8,128)(2,1)}, u32[]{:S(2)}) copy-start(bf16[128,256]{1,0:T(8,128)(2,1)} %constant.15.clone.t1_inv) | copy-start | bytes 196612
  18.2 18.4 %copy-start.8 = (bf16[256,128]{1,0:T(8,128)(2,1)S(1)}, bf16[256,128]{1,0:T(8,128)(2,1)}, u32[]{:S(2)}) copy-start(bf16[256,128]{1,0:T(8,128)(2,1)} %constant.12.clone.t1) | copy-start | bytes 196612
  18.3 6.6 %collective-permute-start.3 = (bf16[4,4,16,128]{3,2,1,0:T(8,128)(2,1)S(1)}, bf16[4,4,16,128]{3,2,1,0:T(8,128)(2,1)S(1)}, u32[]{:S(2)}, u32[]{:S(2)}) collective-permute-start(bf16[4,4,16,128]{3,2,1,0:T(8,128)(2,1)S(1)} %get-tuple-element.28), channel_id=1, source_target_pairs={{0,8},{8,0},{16,24},{24,16},{32,40},{40,32},{48,56},{56,48},{64,72... | collective-permute-start | bytes 196616 | tf_op jit(solution)/shard_map/ppermute | solution.py:191
  19.0 7.6 %collective-permute-start.4 = (bf16[4,4,16,128]{3,2,1,0:T(8,128)(2,1)S(1)}, bf16[4,4,16,128]{3,2,1,0:T(8,128)(2,1)S(1)}, u32[]{:S(2)}, u32[]{:S(2)}) collective-permute-start(bf16[4,4,16,128]{3,2,1,0:T(8,128)(2,1)S(1)} %get-tuple-element.29), channel_id=1, source_target_pairs={{0,16},{8,24},{16,32},{24,40},{32,48},{40,56},{48,0},{56,8},{64,80... | collective-permute-start | bytes 196616 | tf_op jit(solution)/shard_map/ppermute | solution.py:191
  20.1 9.2 %collective-permute-start.5 = (bf16[4,4,16,128]{3,2,1,0:T(8,128)(2,1)S(1)}, bf16[4,4,16,128]{3,2,1,0:T(8,128)(2,1)S(1)}, u32[]{:S(2)}, u32[]{:S(2)}) collective-permute-start(bf16[4,4,16,128]{3,2,1,0:T(8,128)(2,1)S(1)} %get-tuple-element.30), channel_id=1, source_target_pairs={{0,24},{8,16},{16,40},{24,32},{32,56},{40,48},{48,8},{56,0},{64,88... | collective-permute-start | bytes 196616 | tf_op jit(solution)/shard_map/ppermute | solution.py:191
  21.6 10.0 %collective-permute-start.6 = (bf16[4,4,16,128]{3,2,1,0:T(8,128)(2,1)S(1)}, bf16[4,4,16,128]{3,2,1,0:T(8,128)(2,1)S(1)}, u32[]{:S(2)}, u32[]{:S(2)}) collective-permute-start(bf16[4,4,16,128]{3,2,1,0:T(8,128)(2,1)S(1)} %get-tuple-element.31), channel_id=1, source_target_pairs={{0,32},{8,40},{16,48},{24,56},{32,0},{40,8},{48,16},{56,24},{64,96... | collective-permute-start | bytes 196616 | tf_op jit(solution)/shard_map/ppermute | solution.py:191
  23.1 10.5 %collective-permute-start.7 = (bf16[4,4,16,128]{3,2,1,0:T(8,128)(2,1)S(1)}, bf16[4,4,16,128]{3,2,1,0:T(8,128)(2,1)S(1)}, u32[]{:S(2)}, u32[]{:S(2)}) collective-permute-start(bf16[4,4,16,128]{3,2,1,0:T(8,128)(2,1)S(1)} %get-tuple-element.32), channel_id=1, source_target_pairs={{0,40},{8,32},{16,56},{24,48},{32,8},{40,0},{48,24},{56,16},{64,10... | collective-permute-start | bytes 196616 | tf_op jit(solution)/shard_map/ppermute | solution.py:191
  24.9 3.4 %copy-start.10 = (f32[512]{0:T(512)S(1)}, f32[512]{0:T(512)}, u32[]{:S(2)}) copy-start(f32[512]{0:T(512)} %param.19) | copy-start | bytes 6148
  24.9 8.8 %collective-permute-start.8 = (bf16[4,4,16,128]{3,2,1,0:T(8,128)(2,1)S(1)}, bf16[4,4,16,128]{3,2,1,0:T(8,128)(2,1)S(1)}, u32[]{:S(2)}, u32[]{:S(2)}) collective-permute-start(bf16[4,4,16,128]{3,2,1,0:T(8,128)(2,1)S(1)} %get-tuple-element.33), channel_id=1, source_target_pairs={{0,48},{8,56},{16,0},{24,8},{32,16},{40,24},{48,32},{56,40},{64,11... | collective-permute-start | bytes 196616 | tf_op jit(solution)/shard_map/ppermute | solution.py:191
  26.7 7.0 %collective-permute-start.9 = (bf16[4,4,16,128]{3,2,1,0:T(8,128)(2,1)S(1)}, bf16[4,4,16,128]{3,2,1,0:T(8,128)(2,1)S(1)}, u32[]{:S(2)}, u32[]{:S(2)}) collective-permute-start(bf16[4,4,16,128]{3,2,1,0:T(8,128)(2,1)S(1)} %get-tuple-element.34), channel_id=1, source_target_pairs={{0,56},{8,48},{16,8},{24,0},{32,24},{40,16},{48,40},{56,32},{64,12... | collective-permute-start | bytes 196616 | tf_op jit(solution)/shard_map/ppermute | solution.py:191
  40.7 20.8 %all-to-all-start.1 = ((bf16[32,4,16,128]{3,2,1,0:T(8,128)(2,1)}), bf16[32,4,16,128]{3,2,1,0:T(8,128)(2,1)S(1)}, u32[]{:S(2)}, u32[]{:S(2)}) async-start(bf16[32,4,16,128]{3,2,1,0:T(8,128)(2,1)} %bitcast.1), calls=%async_computation.1 | async-start | bytes 1048576 | tf_op jit(solution)/shard_map/all_to_all | solution.py:454
  45.1 16.4 %copy-start.1 = (bf16[512,512]{1,0:T(8,128)(2,1)S(1)}, bf16[512,512]{1,0:T(8,128)(2,1)}, u32[]{:S(2)}) copy-start(bf16[512,512]{1,0:T(8,128)(2,1)} %stream_ref.1) | copy-start | bytes 1572868
  45.1 4.5 %collective-permute-start.10 = (bf16[16,512]{1,0:T(8,128)(2,1)S(1)}, bf16[16,512]{1,0:T(8,128)(2,1)S(1)}, u32[]{:S(2)}, u32[]{:S(2)}) collective-permute-start(bf16[16,512]{1,0:T(8,128)(2,1)S(1)} %get-tuple-element.36), channel_id=1, source_target_pairs={{0,8},{8,16},{16,24},{24,32},{32,40},{40,48},{48,56},{56,64},{64,7... | collective-permute-start | bytes 49160 | tf_op jit(solution)/shard_map/ppermute | solution.py:468
  49.6 11.9 %copy-start.9 = (f32[512]{0:T(512)S(1)}, f32[512]{0:T(512)}, u32[]{:S(2)}) copy-start(f32[512]{0:T(512)} %param.21) | copy-start | bytes 6148

commit v4 on v3

--- a/solution.py
+++ b/solution.py
@@ -11,7 +11,8 @@
 GROUP = 8
 Z_SIZE = 4
 X_SIZE = 4
-AHEAD = 3
+AHEAD = 4
+Y_SIZE = 4
 MIB = 1024 * 1024
 
 
@@ -68,59 +69,48 @@
 def lead_kernel(k_ref, v_ref, f_ref, *rest):
     outs, (f_buf, e_buf, out_buf, f_sem, e_sem, out_sem) = rest[:Z_SIZE], rest[Z_SIZE:]
     rows = f_ref.shape[0]
-    slabs = outs[0].shape[2] - 1
     head, tail = pl.ds(0, EDGE), pl.ds(rows - EDGE, EDGE)
-    pieces = [pl.ds(j * LANE, LANE) for j in range(slabs)]
+    pieces = [pl.ds(j * LANE, LANE) for j in range(AHEAD)]
     f_copies = [send(f_ref.at[p, :], f_buf.at[p, :], f_sem.at[j]) for j, p in enumerate(pieces)]
     sources = [k_ref.at[head, :], k_ref.at[tail, :], v_ref.at[head, :], v_ref.at[tail, :]]
     e_copies = [send(x, e_buf.at[i], e_sem.at[i]) for i, x in enumerate(sources)]
     z, x, c = place()
-    depth = outs[0].shape[3]
-    out_copies = []
-
-    def put(j, block_of):
-        for kz in range(Z_SIZE):
-            g = (z + kz) % Z_SIZE
-            block = block_of(pl.ds(pl.multiple_of(g * LANE, LANE), LANE))
-            turned = block.T.astype(out_buf.dtype)
-            for d in range(X_SIZE * 2):
-                tile = turned[d * depth : (d + 1) * depth]
-                out_buf[kz, (d // 2 - x + X_SIZE) % X_SIZE, (d % 2 - c + 2) % 2, j] = tile
-        for kz, out_ref in enumerate(outs):
-            out_copies.append(send(out_buf.at[kz, :, :, j], out_ref.at[:, :, j], out_sem.at[kz, j]))
-
+    depth = out_buf.shape[2]
+    cols = [pl.ds(pl.multiple_of((z + kz) % Z_SIZE * LANE, LANE), LANE) for kz in range(Z_SIZE)]
     for j, p in enumerate(pieces):
         f_copies[j].wait()
-        put(j, lambda cols, p=p: f_buf[p, cols].astype(jnp.float32))
+        for kz in range(Z_SIZE):
+            turned = f_buf[p, cols[kz]].astype(jnp.float32).T.astype(out_buf.dtype)
+            for d in range(X_SIZE * 2):
+                to = (d // 2 - x + X_SIZE) % X_SIZE * 2 + (d % 2 - c + 2) % 2
+                out_buf[kz, to * AHEAD + j] = turned[d * depth : (d + 1) * depth]
     wait_all(e_copies)
-
-    def edge_block(cols):
-        k0, k1, v0, v1 = [e_buf[i, :, cols].astype(jnp.float32) for i in range(len(sources))]
+    copies = []
+    for kz, out_ref in enumerate(outs):
+        k0, k1, v0, v1 = [e_buf[i, :, cols[kz]].astype(jnp.float32) for i in range(len(sources))]
         own_k, next_k = edge_rows(k0, k1)
         own_v, next_v = edge_rows(v0, v1)
-        listed = own_k + own_v + next_k + next_v
-        return jnp.concatenate(listed + [jnp.zeros((LANE - len(listed), LANE), jnp.float32)], 0)
-
-    put(slabs, edge_block)
-    wait_all(out_copies)
+        edge = jnp.concatenate(own_k + own_v + next_k + next_v, 0)
+        out_buf[kz, X_SIZE * 2 * AHEAD] = edge.astype(out_buf.dtype)
+        copies.append(send(out_buf.at[kz], out_ref, out_sem.at[kz]))
+    wait_all(copies)
 
 
 def lead(k, v, f, groups):
     rows, width = f.shape
-    slabs = AHEAD
-    shape = jax.ShapeDtypeStruct((X_SIZE, 2, slabs + 1, width // groups, LANE), f.dtype)
+    shape = jax.ShapeDtypeStruct((X_SIZE * 2 * AHEAD + 1, width // groups, LANE), f.dtype)
     return pl.pallas_call(
         lead_kernel,
         in_specs=[HBM] * 3,
         out_specs=(HBM,) * Z_SIZE,
         out_shape=(shape,) * Z_SIZE,
         scratch_shapes=[
-            pltpu.VMEM((slabs * LANE, width), f.dtype),
+            pltpu.VMEM((AHEAD * LANE, width), f.dtype),
             pltpu.VMEM((4, EDGE, width), f.dtype),
             pltpu.VMEM((Z_SIZE, *shape.shape), f.dtype),
-            pltpu.SemaphoreType.DMA((slabs,)),
+            pltpu.SemaphoreType.DMA((AHEAD,)),
             pltpu.SemaphoreType.DMA((4,)),
-            pltpu.SemaphoreType.DMA((Z_SIZE, slabs + 1)),
+            pltpu.SemaphoreType.DMA((Z_SIZE,)),
         ],
         cost_estimate=cost(10),
         compiler_params=params(60),
@@ -165,17 +155,26 @@
 
 
 def pack_kernel(*refs):
-    ins, outs = refs[:Z_SIZE], refs[Z_SIZE:]
+    ins, outs, turned = refs[:Z_SIZE], refs[Z_SIZE:-1], refs[-1]
+    last = ins[0].shape[0] - 1
+    depth = ins[0].shape[1]
+    edges = [in_ref[last].astype(jnp.float32) for in_ref in ins]
+    zeros = jnp.zeros((LANE - Z_SIZE * depth, LANE), jnp.float32)
+    turned[...] = jnp.concatenate(edges + [zeros], 0).T
+    _, x, c = place()
     for d, out_ref in enumerate(outs):
         for kz, in_ref in enumerate(ins):
-            out_ref[kz] = in_ref[d // 2, d % 2]
+            out_ref[kz * AHEAD : (kz + 1) * AHEAD] = in_ref[d * AHEAD : (d + 1) * AHEAD]
+        at = ((x + d // 2) % X_SIZE * 2 + (c + d) % 2) * depth
+        out_ref[Z_SIZE * AHEAD] = turned[pl.ds(pl.multiple_of(at, depth), depth), :].astype(out_ref.dtype)
 
 
 def pack(parts):
-    shape = jax.ShapeDtypeStruct((Z_SIZE, *parts[0].shape[2:]), parts[0].dtype)
+    shape = jax.ShapeDtypeStruct((Z_SIZE * AHEAD + 1, *parts[0].shape[1:]), parts[0].dtype)
     return pl.pallas_call(
         pack_kernel,
         out_shape=(shape,) * (X_SIZE * 2),
+        scratch_shapes=[pltpu.VMEM((LANE, LANE), jnp.float32)],
         cost_estimate=cost(20),
         compiler_params=params(6),
     )(*parts)
@@ -303,35 +302,41 @@
     for i in range(sources):
         both = u_ref[i].astype(jnp.float32).reshape(-1, LANE)
         u_wide[i * size : (i + 1) * size, :] = both[:size]
-        f_wide[i * size + ahead : (i + 1) * size, :] = both[size:]
+        if ahead < size:
+            f_wide[i * size + ahead : (i + 1) * size, :] = both[size:]
     for d, f_ref in enumerate(f_refs):
+        edge = f_ref[Z_SIZE * AHEAD].astype(jnp.float32)
         for kz in range(Z_SIZE):
             src = ((z - kz + Z_SIZE) % Z_SIZE * X_SIZE + (x - d // 2 + X_SIZE) % X_SIZE) * 2 + (c + d) % 2
             row = pl.multiple_of(src * size, size)
-            f_wide[pl.ds(row, ahead), :] = f_ref[kz, :AHEAD].reshape(ahead, LANE).astype(jnp.float32)
+            tiles = f_ref[kz * AHEAD : (kz + 1) * AHEAD].reshape(ahead, LANE)
+            f_wide[pl.ds(row, ahead), :] = tiles.astype(jnp.float32)
             row = pl.multiple_of((src + 1) * depth, depth)
-            edges[pl.ds(row, depth), :] = f_ref[kz, AHEAD].astype(jnp.float32)
-    mend(u_wide, edges, taps_ref)
+            edges[pl.ds(row, depth), :] = pltpu.roll(edge, LANE - kz * depth, 1) if kz else edge
     low = jnp.bfloat16
 
     def part(x, i):
         return x[:, i * LANE : (i + 1) * LANE]
 
-    for start in range(0, depth, GROUP):
-        chans = range(start, start + GROUP)
-        rows = [pl.ds(c, LANE, stride=depth) for c in chans]
-        data = [u_wide[r, :].astype(low) for r in rows] + [f_wide[r, :].astype(low) for r in rows]
+    def spectra(wide, rows):
+        data = [wide[r, :].astype(low) for r in rows]
         first = mix(t1[...], jnp.concatenate(data, 1))
         turned = []
-        for i in range(2 * GROUP):
+        for i in range(len(rows)):
             re, im = part(first[:LANE], i), part(first[LANE:], i)
             c, s = tw_c[...], tw_s[...]
             turned.append(jnp.concatenate([re * c - im * s, re * s + im * c], 1).astype(low))
-        spec = mix(jnp.concatenate(turned, 0), t2[...])
+        return mix(jnp.concatenate(turned, 0), t2[...])
+
+    for start in range(0, depth, GROUP):
+        rows = [pl.ds(ch, LANE, stride=depth) for ch in range(start, start + GROUP)]
+        f_spec = spectra(f_wide, rows)
+        if start == 0:
+            mend(u_wide, edges, taps_ref)
+        u_spec = spectra(u_wide, rows)
         prod = []
         for i in range(GROUP):
-            a = spec[i * LANE : (i + 1) * LANE]
-            b = spec[(GROUP + i) * LANE : (GROUP + i + 1) * LANE]
+            a, b = u_spec[i * LANE : (i + 1) * LANE], f_spec[i * LANE : (i + 1) * LANE]
             ar, ai, br, bi = a[:, :LANE], a[:, LANE:], b[:, :LANE], b[:, LANE:]
             prod.append(jnp.concatenate([ar * br - ai * bi, ar * bi + ai * br], 1).astype(low))
         back = mix(jnp.concatenate(prod, 0), t2_inv[...])
@@ -375,11 +380,10 @@
     return y.reshape(sources, slabs, depth, LANE), q_edge
 
 
-def join_kernel(y_ref, qf_ref, stream_ref, gain_ref, out_ref, sum_ref, sq_ref, out_buf, sem):
+def join_kernel(y_ref, qf_ref, stream_ref, gain_ref, out_ref, sum_ref, sq_ref):
     groups, slabs, depth, _ = y_ref.shape
     per = LANE // depth
     sq_ref[...] = jnp.zeros_like(sq_ref)
-    copies = []
     for j in range(slabs):
         rows = slice(j * LANE, (j + 1) * LANE)
         squares = jnp.zeros((LANE, LANE), jnp.float32)
@@ -388,39 +392,31 @@
             y = y_ref[g * per : (g + 1) * per, j].reshape(LANE, LANE).astype(jnp.float32).T
             gated = (qf_ref[rows, cols].astype(jnp.float32) * y).astype(jnp.bfloat16)
             summed = stream_ref[rows, cols].astype(jnp.float32) + gated.astype(jnp.float32)
-            out_buf[rows, cols] = summed.astype(out_buf.dtype)
+            out_ref[rows, cols] = summed.astype(out_ref.dtype)
             sum_ref[rows, cols] = summed * gain_ref[:, cols]
             squares = squares + summed * summed
-        copies.append(send(out_buf.at[rows, :], out_ref.at[rows, :], sem.at[j]))
         total = jnp.sum(squares.T, axis=0, keepdims=True)
-        for d in range(sq_ref.shape[0]):
-            sq_ref[d, j : j + 1, :] = total
-    wait_all(copies)
-
-
-def join(y, qf, stream, gain, fan):
-    rows, _ = stream.shape
+        sq_ref[j : j + 1, :] = total
+
+
+def join(y, qf, stream, gain):
     return pl.pallas_call(
         join_kernel,
         in_specs=[VMEM] * 4,
-        out_specs=(HBM, VMEM, VMEM),
         out_shape=(
             jax.ShapeDtypeStruct(stream.shape, stream.dtype),
             jax.ShapeDtypeStruct(stream.shape, jnp.float32),
-            jax.ShapeDtypeStruct((fan, 8, LANE), jnp.float32),
+            jax.ShapeDtypeStruct((8, LANE), jnp.float32),
         ),
-        scratch_shapes=[
-            pltpu.VMEM(stream.shape, stream.dtype),
-            pltpu.SemaphoreType.DMA((rows // LANE,)),
-        ],
         compiler_params=params(12),
     )(y, qf, stream, gain[None, :])
 
 
-def norm_kernel(channels, sum_ref, sq_ref, out_ref, out_buf, sem):
-    squares = jnp.sum(sq_ref[...], axis=0)
+def norm_kernel(channels, low_ref, sum_ref, *rest):
+    sq_refs, (low_out, out_ref, out_buf, low_sem, sem) = rest[:-5], rest[-5:]
+    copies = [send(low_ref, low_out, low_sem)]
+    squares = sum(ref[...] for ref in sq_refs)
     scale = 1.0 / jnp.sqrt(squares / channels + 1e-05)
-    copies = []
     for j in range(out_ref.shape[0] // LANE):
         rows = slice(j * LANE, (j + 1) * LANE)
         column = jnp.broadcast_to(scale[j : j + 1, :], (LANE, LANE)).T
@@ -431,27 +427,32 @@
     wait_all(copies)
 
 
-def norm(summed, squares):
-    channels = summed.shape[1] * squares.shape[0]
+def norm(low, summed, squares, channels):
 
     def kernel(*refs):
         norm_kernel(channels, *refs)
 
     return pl.pallas_call(
         kernel,
-        in_specs=[VMEM] * 2,
-        out_specs=HBM,
-        out_shape=jax.ShapeDtypeStruct(summed.shape, jnp.bfloat16),
+        in_specs=[VMEM] * (2 + len(squares)),
+        out_specs=(HBM,) * 2,
+        out_shape=(jax.ShapeDtypeStruct(summed.shape, low.dtype),) * 2,
         scratch_shapes=[
-            pltpu.VMEM(summed.shape, jnp.bfloat16),
+            pltpu.VMEM(summed.shape, low.dtype),
+            pltpu.SemaphoreType.DMA,
             pltpu.SemaphoreType.DMA((summed.shape[0] // LANE,)),
         ],
         compiler_params=params(8),
-    )(summed, squares)
+    )(low, summed, *squares)
 
 
 def exchange(x, axis):
     return lax.all_to_all(x, axis, split_axis=0, concat_axis=0, tiled=True)
+
+
+def across(block, fan, dz, dy):
+    route = [(i, (i + dz) % fan // Y_SIZE * Y_SIZE + (i + dy) % Y_SIZE) for i in range(fan)]
+    return lax.ppermute(block, "ch", route)
 
 
 def shards(queries, keys, values, filters, short_weights, skip_gain, stream, norm_gain):
@@ -467,9 +468,10 @@
     y_home = exchange(y, "seq")
     q_edge = lax.ppermute(q_edge, "seq", [(i, i + 1) for i in range(groups - 1)])
     qf = gate(queries, q_edge, short_weights)
-    stream_out, summed, squares = join(y_home, qf, stream, norm_gain, fan)
-    normed = norm(summed, exchange(squares, "ch"))
-    return (stream_out, normed)
+    low, summed, squares = join(y_home, qf, stream, norm_gain)
+    squares = squares + across(squares, fan, Y_SIZE, 0)
+    squares = [squares] + [across(squares, fan, 0, k) for k in range(1, Y_SIZE)]
+    return norm(low, summed, squares, width * fan)
 
 
 def solution(mesh):

time: 82.5 us -> 76.9 us (0.932)
  blocking collectives: 18.3 us -> 0 us
  starting transfers between devices: 30.6 us -> 41.8 us
  waiting for transfers between devices: 21.1 us -> 22.8 us
    all_to_all x1 -> x0, blocking collectives: 18.3 us -> none  [exchange(): return lax.all_to_all(x, axis, split_axis=0, concat_axis=0, tiled=True)]
    ppermute x0 -> x4, starting transfers between devices: none -> 9.05 us  [across(): return lax.ppermute(block, 'ch', route)]
    ppermute x0 -> x4, waiting for transfers between devices: none -> 4.16 us  [across(): return lax.ppermute(block, 'ch', route)]
    all_to_all x2, starting transfers between devices: 11 us -> 13.2 us  [exchange(): return lax.all_to_all(x, axis, split_axis=0, concat_axis=0, tiled=True)]
    all_to_all x2, waiting for transfers between devices: 14.3 us -> 12.2 us  [exchange(): return lax.all_to_all(x, axis, split_axis=0, concat_axis=0, tiled=True)]
  transfers between devices with their start and end apart: 13 -> 17, of which waited for: 8 -> 10; matrix products, arithmetic and copies ran while one was open for 0% -> 0% of each run, Pallas kernels for 3% -> 3%
where the time goes in v4:
time: 76.9 us; the launch traced here: 75.9 us
  starting transfers between devices  41.8 us (54%)
  waiting for transfers between devices  22.8 us (30%)
  Pallas kernels  10.2 us (13%)
  between operations  1.02 us (1%)
    ppermute x10, starting transfers between devices, shift(): return lax.ppermute(block, 'seq', route)  15.9 us
    all_to_all x2, starting transfers between devices, exchange(): return lax.all_to_all(x, axis, split_axis=0, concat_axis=0, tiled=True)  13.2 us
    all_to_all x2, waiting for transfers between devices, exchange(): return lax.all_to_all(x, axis, split_axis=0, concat_axis=0, tiled=True)  12.2 us
    ppermute x4, starting transfers between devices, across(): return lax.ppermute(block, 'ch', route)  9.05 us
    ppermute x10, waiting for transfers between devices, shift(): return lax.ppermute(block, 'seq', route)  5.6 us
    ppermute x4, waiting for transfers between devices, across(): return lax.ppermute(block, 'ch', route)  4.16 us
    pallas_call x1, Pallas kernels, long_conv(): pl.pallas_call(conv_kernel, in_specs=[HBM if x is q else VMEM for x in op...  3.73 us
    ppermute x1, starting transfers between devices, shards(): lax.ppermute(q_edge, 'seq', [(i, i + 1) for i in range(groups - 1)])  3.67 us
  transfers between devices with their start and end apart: 17, of which 10 were waited for; matrix products, arithmetic and copies ran while one was open for 0% of the time, Pallas kernels for 3%

profile of v4, /device:TPU:1, one launch (start us, length us, event | category | flops | bytes accessed | tf_op | source)
XLA Modules:
  0.0 75.9 jit_solution(8385448932473123779)
XLA Ops:
  0.7 2.4 %shard_map.151 = (bf16[33,16,128]{2,1,0:T(8,128)(2,1)}, bf16[33,16,128]{2,1,0:T(8,128)(2,1)}, bf16[33,16,128]{2,1,0:T(8,128)(2,1)}, bf16[33,16,128]{2,1,0:T(8,128)(2,1)}) custom-call(bf16[512,512]{1,0:T(8,128)(2,1)} %k_ref.3, bf16[512,512]{1,0:T(8,128)(2,1)} %v_ref.3, bf16[512,512]{1,0:T(8,128)(2,1)} %f_ref.3), custom_call_target="tpu_custom_call" | custom-call | flops 10000000000 | tf_op jit(solution)/shard_map/pallas_call | solution.py:102
  3.1 2.5 %collective-permute-start = (bf16[33,16,128]{2,1,0:T(8,128)(2,1)}, bf16[33,16,128]{2,1,0:T(8,128)(2,1)S(1)}, u32[]{:S(2)}, u32[]{:S(2)}) collective-permute-start(bf16[33,16,128]{2,1,0:T(8,128)(2,1)} %get-tuple-element.24), channel_id=1, source_target_pairs={{0,64},{8,72},{16,80},{24,88},{32,96},{40,104},{48,112},{56,120},{... | collective-permute-start | bytes 405512 | tf_op jit(solution)/shard_map/ppermute | solution.py:190
  5.6 3.0 %collective-permute-start.1 = (bf16[33,16,128]{2,1,0:T(8,128)(2,1)}, bf16[33,16,128]{2,1,0:T(8,128)(2,1)S(1)}, u32[]{:S(2)}, u32[]{:S(2)}) collective-permute-start(bf16[33,16,128]{2,1,0:T(8,128)(2,1)} %get-tuple-element.25), channel_id=1, source_target_pairs={{0,128},{8,136},{16,144},{24,152},{32,160},{40,168},{48,176},{56,1... | collective-permute-start | bytes 405512 | tf_op jit(solution)/shard_map/ppermute | solution.py:190
  8.6 0.7 collective-permute-start.2
  9.4 1.7 %shard_map.149 = bf16[32,4,16,128]{3,2,1,0:T(8,128)(2,1)} custom-call(bf16[512,512]{1,0:T(8,128)(2,1)S(1)} %copy-done.11, bf16[512,512]{1,0:T(8,128)(2,1)S(1)} %copy-done.12, bf16[512,512]{1,0:T(8,128)(2,1)S(1)} %copy-done.13, f32[3,3,512]{2,1,0:T(4,128)S(1)} %copy-done.4), custom_call_target="tpu_custom_call" | custom-call | flops 20000000000 | tf_op jit(solution)/shard_map/pallas_call | solution.py:241
  11.0 0.0 copy-start.14
  11.0 6.6 %all-to-all-start = ((bf16[32,4,16,128]{3,2,1,0:T(8,128)(2,1)}), bf16[32,4,16,128]{3,2,1,0:T(8,128)(2,1)S(1)}, u32[]{:S(2)}, u32[]{:S(2)}) async-start(bf16[32,4,16,128]{3,2,1,0:T(8,128)(2,1)} %shard_map.149), calls=%async_computation | async-start | bytes 1048576 | tf_op jit(solution)/shard_map/all_to_all | solution.py:450
  17.6 0.0 collective-permute-done.refs_1_
  17.6 0.8 collective-permute-done.1.refs_2_
  18.4 0.0 collective-permute-done.2.refs_3_
  18.4 0.0 copy-start.2
  18.4 0.0 copy-start.3
  18.4 0.0 copy-start.5
  18.4 0.0 copy-start.6
  18.4 0.0 copy-start.7
  18.5 0.0 copy-start.8
  18.5 0.1 shard_map.152
  18.6 0.8 collective-permute-start.3
  19.3 1.1 %collective-permute-start.4 = (bf16[17,16,128]{2,1,0:T(8,128)(2,1)S(1)}, bf16[17,16,128]{2,1,0:T(8,128)(2,1)S(1)}, u32[]{:S(2)}, u32[]{:S(2)}) collective-permute-start(bf16[17,16,128]{2,1,0:T(8,128)(2,1)S(1)} %get-tuple-element.29), channel_id=1, source_target_pairs={{0,16},{8,24},{16,32},{24,40},{32,48},{40,56},{48,0},{56,8},{64,80... | collective-permute-start | bytes 208904 | tf_op jit(solution)/shard_map/ppermute | solution.py:190
  20.5 1.5 %collective-permute-start.5 = (bf16[17,16,128]{2,1,0:T(8,128)(2,1)S(1)}, bf16[17,16,128]{2,1,0:T(8,128)(2,1)S(1)}, u32[]{:S(2)}, u32[]{:S(2)}) collective-permute-start(bf16[17,16,128]{2,1,0:T(8,128)(2,1)S(1)} %get-tuple-element.30), channel_id=1, source_target_pairs={{0,24},{8,16},{16,40},{24,32},{32,56},{40,48},{48,8},{56,0},{64,88... | collective-permute-start | bytes 208904 | tf_op jit(solution)/shard_map/ppermute | solution.py:190
  21.9 1.5 %collective-permute-start.6 = (bf16[17,16,128]{2,1,0:T(8,128)(2,1)S(1)}, bf16[17,16,128]{2,1,0:T(8,128)(2,1)S(1)}, u32[]{:S(2)}, u32[]{:S(2)}) collective-permute-start(bf16[17,16,128]{2,1,0:T(8,128)(2,1)S(1)} %get-tuple-element.31), channel_id=1, source_target_pairs={{0,32},{8,40},{16,48},{24,56},{32,0},{40,8},{48,16},{56,24},{64,96... | collective-permute-start | bytes 208904 | tf_op jit(solution)/shard_map/ppermute | solution.py:190
  23.5 1.8 %collective-permute-start.7 = (bf16[17,16,128]{2,1,0:T(8,128)(2,1)S(1)}, bf16[17,16,128]{2,1,0:T(8,128)(2,1)S(1)}, u32[]{:S(2)}, u32[]{:S(2)}) collective-permute-start(bf16[17,16,128]{2,1,0:T(8,128)(2,1)S(1)} %get-tuple-element.32), channel_id=1, source_target_pairs={{0,40},{8,32},{16,56},{24,48},{32,8},{40,0},{48,24},{56,16},{64,10... | collective-permute-start | bytes 208904 | tf_op jit(solution)/shard_map/ppermute | solution.py:190
  25.2 0.0 collective-permute-done.3.rest_1_
  25.2 1.5 %collective-permute-start.8 = (bf16[17,16,128]{2,1,0:T(8,128)(2,1)S(1)}, bf16[17,16,128]{2,1,0:T(8,128)(2,1)S(1)}, u32[]{:S(2)}, u32[]{:S(2)}) collective-permute-start(bf16[17,16,128]{2,1,0:T(8,128)(2,1)S(1)} %get-tuple-element.33), channel_id=1, source_target_pairs={{0,48},{8,56},{16,0},{24,8},{32,16},{40,24},{48,32},{56,40},{64,11... | collective-permute-start | bytes 208904 | tf_op jit(solution)/shard_map/ppermute | solution.py:190
  26.7 0.0 collective-permute-done.4.rest_2_
  26.7 1.6 %collective-permute-start.9 = (bf16[17,16,128]{2,1,0:T(8,128)(2,1)S(1)}, bf16[17,16,128]{2,1,0:T(8,128)(2,1)S(1)}, u32[]{:S(2)}, u32[]{:S(2)}) collective-permute-start(bf16[17,16,128]{2,1,0:T(8,128)(2,1)S(1)} %get-tuple-element.34), channel_id=1, source_target_pairs={{0,56},{8,48},{16,8},{24,0},{32,24},{40,16},{48,40},{56,32},{64,12... | collective-permute-start | bytes 208904 | tf_op jit(solution)/shard_map/ppermute | solution.py:190
  28.3 0.1 shard_map.150
  28.4 0.6 collective-permute-done.5.rest_3_
  29.0 1.5 %collective-permute-done.6.rest_4_ = bf16[17,16,128]{2,1,0:T(8,128)(2,1)S(1)} collective-permute-done((bf16[17,16,128]{2,1,0:T(8,128)(2,1)S(1)}, bf16[17,16,128]{2,1,0:T(8,128)(2,1)S(1)}, u32[]{:S(2)}, u32[]{:S(2)}) %collective-permute-start.6) | collective-permute-done | bytes 69664 | tf_op jit(solution)/shard_map/ppermute | solution.py:190
  30.5 2.7 %collective-permute-done.7.rest_5_ = bf16[17,16,128]{2,1,0:T(8,128)(2,1)S(1)} collective-permute-done((bf16[17,16,128]{2,1,0:T(8,128)(2,1)S(1)}, bf16[17,16,128]{2,1,0:T(8,128)(2,1)S(1)}, u32[]{:S(2)}, u32[]{:S(2)}) %collective-permute-start.7) | collective-permute-done | bytes 69664 | tf_op jit(solution)/shard_map/ppermute | solution.py:190
  33.2 0.0 collective-permute-done.9.rest_7_
  33.2 0.9 %all-to-all-done.u_ref = bf16[32,4,16,128]{3,2,1,0:T(8,128)(2,1)S(1)} async-done(((bf16[32,4,16,128]{3,2,1,0:T(8,128)(2,1)}), bf16[32,4,16,128]{3,2,1,0:T(8,128)(2,1)S(1)}, u32[]{:S(2)}, u32[]{:S(2)}) %all-to-all-start) | async-done | bytes 524320 | tf_op jit(solution)/shard_map/all_to_all | solution.py:450
  34.2 3.7 %shard_map.153 = (bf16[2048,128]{1,0:T(8,128)(2,1)}, bf16[16,512]{1,0:T(8,128)(2,1)S(1)}) custom-call(bf16[32,4,16,128]{3,2,1,0:T(8,128)(2,1)S(1)} %all-to-all-done.u_ref, bf16[512,512]{1,0:T(8,128)(2,1)S(1)} %copy-done, f32[16,128]{1,0:T(8,128)S(1)} %get-tuple-element.21.taps_ref, f32[16,128]{1,0:T(8,128)S(1)} %get-tuple-element.22.skip_ref, ...), custom_call_target="tpu_custom_call" | custom-call | tf_op jit(solution)/shard_map/pallas_call | solution.py:371
  37.9 6.6 %all-to-all-start.1 = ((bf16[32,4,16,128]{3,2,1,0:T(8,128)(2,1)}), bf16[32,4,16,128]{3,2,1,0:T(8,128)(2,1)S(1)}, u32[]{:S(2)}, u32[]{:S(2)}) async-start(bf16[32,4,16,128]{3,2,1,0:T(8,128)(2,1)} %bitcast.1), calls=%async_computation.1 | async-start | bytes 1048576 | tf_op jit(solution)/shard_map/all_to_all | solution.py:450
  44.5 0.0 copy-start.1
  44.5 3.7 %collective-permute-start.10 = (bf16[16,512]{1,0:T(8,128)(2,1)S(1)}, bf16[16,512]{1,0:T(8,128)(2,1)S(1)}, u32[]{:S(2)}, u32[]{:S(2)}) collective-permute-start(bf16[16,512]{1,0:T(8,128)(2,1)S(1)} %get-tuple-element.36), channel_id=1, source_target_pairs={{0,8},{8,16},{16,24},{24,32},{32,40},{40,48},{48,56},{56,64},{64,7... | collective-permute-start | bytes 49160 | tf_op jit(solution)/shard_map/ppermute | solution.py:469
  48.2 0.8 %collective-permute-done.10.edge_ref = bf16[16,512]{1,0:T(8,128)(2,1)S(1)} collective-permute-done((bf16[16,512]{1,0:T(8,128)(2,1)S(1)}, bf16[16,512]{1,0:T(8,128)(2,1)S(1)}, u32[]{:S(2)}, u32[]{:S(2)}) %collective-permute-start.10) | collective-permute-done | bytes 16416 | tf_op jit(solution)/shard_map/ppermute | solution.py:469
  49.1 0.5 shard_map.154.qf_ref
  49.6 11.3 %all-to-all-done.1.y_ref = bf16[32,4,16,128]{3,2,1,0:T(8,128)(2,1)S(1)} async-done(((bf16[32,4,16,128]{3,2,1,0:T(8,128)(2,1)}), bf16[32,4,16,128]{3,2,1,0:T(8,128)(2,1)S(1)}, u32[]{:S(2)}, u32[]{:S(2)}) %all-to-all-start.1) | async-done | bytes 524320 | tf_op jit(solution)/shard_map/all_to_all | solution.py:450
  60.9 0.6 shard_map.155
  61.6 5.3 %collective-permute-start.11 = (f32[8,128]{1,0:T(8,128)S(1)}, f32[8,128]{1,0:T(8,128)S(1)}, u32[]{:S(2)}, u32[]{:S(2)}) collective-permute-start(f32[8,128]{1,0:T(8,128)S(1)} %get-tuple-element.39), channel_id=1, source_target_pairs={{0,4},{1,5},{2,6},{3,7},{4,0},{5,1},{6,2},{7,3},{8,12},{9,13},{10,... | collective-permute-start | bytes 12296 | tf_op jit(solution)/shard_map/ppermute | solution.py:455
  66.9 1.2 %collective-permute-done.11 = f32[8,128]{1,0:T(8,128)S(1)} collective-permute-done((f32[8,128]{1,0:T(8,128)S(1)}, f32[8,128]{1,0:T(8,128)S(1)}, u32[]{:S(2)}, u32[]{:S(2)}) %collective-permute-start.11) | collective-permute-done | bytes 4128 | tf_op jit(solution)/shard_map/ppermute | solution.py:455
  68.0 2.7 %collective-permute-start.14 = (f32[8,128]{1,0:T(8,128)S(1)}, f32[8,128]{1,0:T(8,128)S(1)}, u32[]{:S(2)}, u32[]{:S(2)}) collective-permute-start(f32[8,128]{1,0:T(8,128)S(1)} %add.3.refs_2_), channel_id=1, source_target_pairs={{0,3},{1,0},{2,1},{3,2},{4,7},{5,4},{6,5},{7,6},{8,11},{9,8},{10,9... | collective-permute-start | bytes 12296 | tf_op jit(solution)/shard_map/ppermute | solution.py:455
  70.8 0.4 collective-permute-start.13
  71.1 0.7 collective-permute-start.12
  71.8 2.9 %collective-permute-done.13.refs_4_ = f32[8,128]{1,0:T(8,128)S(1)} collective-permute-done((f32[8,128]{1,0:T(8,128)S(1)}, f32[8,128]{1,0:T(8,128)S(1)}, u32[]{:S(2)}, u32[]{:S(2)}) %collective-permute-start.13) | collective-permute-done | bytes 4128 | tf_op jit(solution)/shard_map/ppermute | solution.py:455
  74.7 0.1 collective-permute-done.12.refs_3_
  74.8 1.0 %shard_map.156 = (bf16[512,512]{1,0:T(8,128)(2,1)}, bf16[512,512]{1,0:T(8,128)(2,1)}) custom-call(bf16[512,512]{1,0:T(8,128)(2,1)S(1)} %get-tuple-element.37.refs_0_, f32[512,512]{1,0:T(8,128)S(1)} %get-tuple-element.38.refs_1_, f32[8,128]{1,0:T(8,128)S(1)} %add.3.refs_2_, f32[8,128]{1,0:T(8,128)S(1)} %collective-permute-done.12.refs_3_, ...), custom_call_target="tpu_custom_call" | custom-call | tf_op jit(solution)/shard_map/pallas_call | solution.py:435
  (25 shorter events, 0.1 us)
Async XLA Ops:
  0.6 8.7 %copy-start.13 = (bf16[512,512]{1,0:T(8,128)(2,1)S(1)}, bf16[512,512]{1,0:T(8,128)(2,1)}, u32[]{:S(2)}) copy-start(bf16[512,512]{1,0:T(8,128)(2,1)} %f_ref.3) | copy-start | bytes 1572868
  0.6 8.7 %copy-start.12 = (bf16[512,512]{1,0:T(8,128)(2,1)S(1)}, bf16[512,512]{1,0:T(8,128)(2,1)}, u32[]{:S(2)}) copy-start(bf16[512,512]{1,0:T(8,128)(2,1)} %v_ref.3) | copy-start | bytes 1572868
  0.7 8.7 %copy-start.11 = (bf16[512,512]{1,0:T(8,128)(2,1)S(1)}, bf16[512,512]{1,0:T(8,128)(2,1)}, u32[]{:S(2)}) copy-start(bf16[512,512]{1,0:T(8,128)(2,1)} %k_ref.3) | copy-start | bytes 1572868
  0.7 8.7 %copy-start.4 = (f32[3,3,512]{2,1,0:T(4,128)S(1)}, f32[3,3,512]{2,1,0:T(4,128)}, u32[]{:S(2)}) copy-start(f32[3,3,512]{2,1,0:T(4,128)} %taps_ref.5) | copy-start | bytes 55300
  3.1 14.5 %collective-permute-start = (bf16[33,16,128]{2,1,0:T(8,128)(2,1)}, bf16[33,16,128]{2,1,0:T(8,128)(2,1)S(1)}, u32[]{:S(2)}, u32[]{:S(2)}) collective-permute-start(bf16[33,16,128]{2,1,0:T(8,128)(2,1)} %get-tuple-element.24), channel_id=1, source_target_pairs={{0,64},{8,72},{16,80},{24,88},{32,96},{40,104},{48,112},{56,120},{... | collective-permute-start | bytes 405512 | tf_op jit(solution)/shard_map/ppermute | solution.py:190
  5.6 12.8 %collective-permute-start.1 = (bf16[33,16,128]{2,1,0:T(8,128)(2,1)}, bf16[33,16,128]{2,1,0:T(8,128)(2,1)S(1)}, u32[]{:S(2)}, u32[]{:S(2)}) collective-permute-start(bf16[33,16,128]{2,1,0:T(8,128)(2,1)} %get-tuple-element.25), channel_id=1, source_target_pairs={{0,128},{8,136},{16,144},{24,152},{32,160},{40,168},{48,176},{56,1... | collective-permute-start | bytes 405512 | tf_op jit(solution)/shard_map/ppermute | solution.py:190
  8.6 9.8 %collective-permute-start.2 = (bf16[33,16,128]{2,1,0:T(8,128)(2,1)}, bf16[33,16,128]{2,1,0:T(8,128)(2,1)S(1)}, u32[]{:S(2)}, u32[]{:S(2)}) collective-permute-start(bf16[33,16,128]{2,1,0:T(8,128)(2,1)} %get-tuple-element.26), channel_id=1, source_target_pairs={{0,192},{8,200},{16,208},{24,216},{32,224},{40,232},{48,240},{56,2... | collective-permute-start | bytes 405512 | tf_op jit(solution)/shard_map/ppermute | solution.py:190
  11.0 7.4 %copy-start.14 = (bf16[33,16,128]{2,1,0:T(8,128)(2,1)S(1)}, bf16[33,16,128]{2,1,0:T(8,128)(2,1)}, u32[]{:S(2)}) copy-start(bf16[33,16,128]{2,1,0:T(8,128)(2,1)} %get-tuple-element.23.refs_0_) | copy-start | bytes 405508
  11.0 23.1 %all-to-all-start = ((bf16[32,4,16,128]{3,2,1,0:T(8,128)(2,1)}), bf16[32,4,16,128]{3,2,1,0:T(8,128)(2,1)S(1)}, u32[]{:S(2)}, u32[]{:S(2)}) async-start(bf16[32,4,16,128]{3,2,1,0:T(8,128)(2,1)} %shard_map.149), calls=%async_computation | async-start | bytes 1048576 | tf_op jit(solution)/shard_map/all_to_all | solution.py:450
  18.4 15.8 %copy-start = (bf16[512,512]{1,0:T(8,128)(2,1)S(1)}, bf16[512,512]{1,0:T(8,128)(2,1)}, u32[]{:S(2)}) copy-start(bf16[512,512]{1,0:T(8,128)(2,1)} %q_ref.3) | copy-start | bytes 1572868
  18.4 15.8 %copy-start.2 = (bf16[256,256]{1,0:T(8,128)(2,1)S(1)}, bf16[256,256]{1,0:T(8,128)(2,1)}, u32[]{:S(2)}) copy-start(bf16[256,256]{1,0:T(8,128)(2,1)} %constant.14.clone.t2_inv) | copy-start | bytes 393220
  18.4 15.7 %copy-start.3 = (bf16[256,256]{1,0:T(8,128)(2,1)S(1)}, bf16[256,256]{1,0:T(8,128)(2,1)}, u32[]{:S(2)}) copy-start(bf16[256,256]{1,0:T(8,128)(2,1)} %constant.13.clone.t2) | copy-start | bytes 393220
  18.4 15.7 %copy-start.5 = (f32[128,128]{1,0:T(8,128)S(1)}, f32[128,128]{1,0:T(8,128)}, u32[]{:S(2)}) copy-start(f32[128,128]{1,0:T(8,128)} %constant.17.clone.tw_s) | copy-start | bytes 196612
  18.4 15.7 %copy-start.6 = (f32[128,128]{1,0:T(8,128)S(1)}, f32[128,128]{1,0:T(8,128)}, u32[]{:S(2)}) copy-start(f32[128,128]{1,0:T(8,128)} %constant.16.clone.tw_c) | copy-start | bytes 196612
  18.4 15.7 %copy-start.7 = (bf16[128,256]{1,0:T(8,128)(2,1)S(1)}, bf16[128,256]{1,0:T(8,128)(2,1)}, u32[]{:S(2)}) copy-start(bf16[128,256]{1,0:T(8,128)(2,1)} %constant.15.clone.t1_inv) | copy-start | bytes 196612
  18.5 15.7 %copy-start.8 = (bf16[256,128]{1,0:T(8,128)(2,1)S(1)}, bf16[256,128]{1,0:T(8,128)(2,1)}, u32[]{:S(2)}) copy-start(bf16[256,128]{1,0:T(8,128)(2,1)} %constant.12.clone.t1) | copy-start | bytes 196612
  18.6 6.7 %collective-permute-start.3 = (bf16[17,16,128]{2,1,0:T(8,128)(2,1)S(1)}, bf16[17,16,128]{2,1,0:T(8,128)(2,1)S(1)}, u32[]{:S(2)}, u32[]{:S(2)}) collective-permute-start(bf16[17,16,128]{2,1,0:T(8,128)(2,1)S(1)} %get-tuple-element.28), channel_id=1, source_target_pairs={{0,8},{8,0},{16,24},{24,16},{32,40},{40,32},{48,56},{56,48},{64,72... | collective-permute-start | bytes 208904 | tf_op jit(solution)/shard_map/ppermute | solution.py:190
  19.3 7.4 %collective-permute-start.4 = (bf16[17,16,128]{2,1,0:T(8,128)(2,1)S(1)}, bf16[17,16,128]{2,1,0:T(8,128)(2,1)S(1)}, u32[]{:S(2)}, u32[]{:S(2)}) collective-permute-start(bf16[17,16,128]{2,1,0:T(8,128)(2,1)S(1)} %get-tuple-element.29), channel_id=1, source_target_pairs={{0,16},{8,24},{16,32},{24,40},{32,48},{40,56},{48,0},{56,8},{64,80... | collective-permute-start | bytes 208904 | tf_op jit(solution)/shard_map/ppermute | solution.py:190
  20.5 8.6 %collective-permute-start.5 = (bf16[17,16,128]{2,1,0:T(8,128)(2,1)S(1)}, bf16[17,16,128]{2,1,0:T(8,128)(2,1)S(1)}, u32[]{:S(2)}, u32[]{:S(2)}) collective-permute-start(bf16[17,16,128]{2,1,0:T(8,128)(2,1)S(1)} %get-tuple-element.30), channel_id=1, source_target_pairs={{0,24},{8,16},{16,40},{24,32},{32,56},{40,48},{48,8},{56,0},{64,88... | collective-permute-start | bytes 208904 | tf_op jit(solution)/shard_map/ppermute | solution.py:190
  21.9 8.6 %collective-permute-start.6 = (bf16[17,16,128]{2,1,0:T(8,128)(2,1)S(1)}, bf16[17,16,128]{2,1,0:T(8,128)(2,1)S(1)}, u32[]{:S(2)}, u32[]{:S(2)}) collective-permute-start(bf16[17,16,128]{2,1,0:T(8,128)(2,1)S(1)} %get-tuple-element.31), channel_id=1, source_target_pairs={{0,32},{8,40},{16,48},{24,56},{32,0},{40,8},{48,16},{56,24},{64,96... | collective-permute-start | bytes 208904 | tf_op jit(solution)/shard_map/ppermute | solution.py:190
  23.5 9.8 %collective-permute-start.7 = (bf16[17,16,128]{2,1,0:T(8,128)(2,1)S(1)}, bf16[17,16,128]{2,1,0:T(8,128)(2,1)S(1)}, u32[]{:S(2)}, u32[]{:S(2)}) collective-permute-start(bf16[17,16,128]{2,1,0:T(8,128)(2,1)S(1)} %get-tuple-element.32), channel_id=1, source_target_pairs={{0,40},{8,32},{16,56},{24,48},{32,8},{40,0},{48,24},{56,16},{64,10... | collective-permute-start | bytes 208904 | tf_op jit(solution)/shard_map/ppermute | solution.py:190
  25.2 3.0 %copy-start.10 = (f32[512]{0:T(512)S(1)}, f32[512]{0:T(512)}, u32[]{:S(2)}) copy-start(f32[512]{0:T(512)} %param.19) | copy-start | bytes 6148
  25.2 8.0 %collective-permute-start.8 = (bf16[17,16,128]{2,1,0:T(8,128)(2,1)S(1)}, bf16[17,16,128]{2,1,0:T(8,128)(2,1)S(1)}, u32[]{:S(2)}, u32[]{:S(2)}) collective-permute-start(bf16[17,16,128]{2,1,0:T(8,128)(2,1)S(1)} %get-tuple-element.33), channel_id=1, source_target_pairs={{0,48},{8,56},{16,0},{24,8},{32,16},{40,24},{48,32},{56,40},{64,11... | collective-permute-start | bytes 208904 | tf_op jit(solution)/shard_map/ppermute | solution.py:190
  26.7 6.5 %collective-permute-start.9 = (bf16[17,16,128]{2,1,0:T(8,128)(2,1)S(1)}, bf16[17,16,128]{2,1,0:T(8,128)(2,1)S(1)}, u32[]{:S(2)}, u32[]{:S(2)}) collective-permute-start(bf16[17,16,128]{2,1,0:T(8,128)(2,1)S(1)} %get-tuple-element.34), channel_id=1, source_target_pairs={{0,56},{8,48},{16,8},{24,0},{32,24},{40,16},{48,40},{56,32},{64,12... | collective-permute-start | bytes 208904 | tf_op jit(solution)/shard_map/ppermute | solution.py:190
  37.9 23.0 %all-to-all-start.1 = ((bf16[32,4,16,128]{3,2,1,0:T(8,128)(2,1)}), bf16[32,4,16,128]{3,2,1,0:T(8,128)(2,1)S(1)}, u32[]{:S(2)}, u32[]{:S(2)}) async-start(bf16[32,4,16,128]{3,2,1,0:T(8,128)(2,1)} %bitcast.1), calls=%async_computation.1 | async-start | bytes 1048576 | tf_op jit(solution)/shard_map/all_to_all | solution.py:450
  44.5 16.4 %copy-start.1 = (bf16[512,512]{1,0:T(8,128)(2,1)S(1)}, bf16[512,512]{1,0:T(8,128)(2,1)}, u32[]{:S(2)}) copy-start(bf16[512,512]{1,0:T(8,128)(2,1)} %stream_ref.1) | copy-start | bytes 1572868
  44.5 4.5 %collective-permute-start.10 = (bf16[16,512]{1,0:T(8,128)(2,1)S(1)}, bf16[16,512]{1,0:T(8,128)(2,1)S(1)}, u32[]{:S(2)}, u32[]{:S(2)}) collective-permute-start(bf16[16,512]{1,0:T(8,128)(2,1)S(1)} %get-tuple-element.36), channel_id=1, source_target_pairs={{0,8},{8,16},{16,24},{24,32},{32,40},{40,48},{48,56},{56,64},{64,7... | collective-permute-start | bytes 49160 | tf_op jit(solution)/shard_map/ppermute | solution.py:469
  49.1 11.9 %copy-start.9 = (f32[512]{0:T(512)S(1)}, f32[512]{0:T(512)}, u32[]{:S(2)}) copy-start(f32[512]{0:T(512)} %param.21) | copy-start | bytes 6148
  61.6 6.5 %collective-permute-start.11 = (f32[8,128]{1,0:T(8,128)S(1)}, f32[8,128]{1,0:T(8,128)S(1)}, u32[]{:S(2)}, u32[]{:S(2)}) collective-permute-start(f32[8,128]{1,0:T(8,128)S(1)} %get-tuple-element.39), channel_id=1, source_target_pairs={{0,4},{1,5},{2,6},{3,7},{4,0},{5,1},{6,2},{7,3},{8,12},{9,13},{10,... | collective-permute-start | bytes 12296 | tf_op jit(solution)/shard_map/ppermute | solution.py:455
  68.0 3.8 %collective-permute-start.14 = (f32[8,128]{1,0:T(8,128)S(1)}, f32[8,128]{1,0:T(8,128)S(1)}, u32[]{:S(2)}, u32[]{:S(2)}) collective-permute-start(f32[8,128]{1,0:T(8,128)S(1)} %add.3.refs_2_), channel_id=1, source_target_pairs={{0,3},{1,0},{2,1},{3,2},{4,7},{5,4},{6,5},{7,6},{8,11},{9,8},{10,9... | collective-permute-start | bytes 12296 | tf_op jit(solution)/shard_map/ppermute | solution.py:455
  70.8 4.0 %collective-permute-start.13 = (f32[8,128]{1,0:T(8,128)S(1)}, f32[8,128]{1,0:T(8,128)S(1)}, u32[]{:S(2)}, u32[]{:S(2)}) collective-permute-start(f32[8,128]{1,0:T(8,128)S(1)} %add.3.refs_2_), channel_id=1, source_target_pairs={{0,2},{1,3},{2,0},{3,1},{4,6},{5,7},{6,4},{7,5},{8,10},{9,11},{10,... | collective-permute-start | bytes 12296 | tf_op jit(solution)/shard_map/ppermute | solution.py:455
  71.1 3.7 %collective-permute-start.12 = (f32[8,128]{1,0:T(8,128)S(1)}, f32[8,128]{1,0:T(8,128)S(1)}, u32[]{:S(2)}, u32[]{:S(2)}) collective-permute-start(f32[8,128]{1,0:T(8,128)S(1)} %add.3.refs_2_), channel_id=1, source_target_pairs={{0,1},{1,2},{2,3},{3,0},{4,5},{5,6},{6,7},{7,4},{8,9},{9,10},{10,1... | collective-permute-start | bytes 12296 | tf_op jit(solution)/shard_map/ppermute | solution.py:455

commit v5 on v4

--- a/solution.py
+++ b/solution.py
@@ -66,55 +66,59 @@
     return own, passed
 
 
-def lead_kernel(k_ref, v_ref, f_ref, *rest):
-    outs, (f_buf, e_buf, out_buf, f_sem, e_sem, out_sem) = rest[:Z_SIZE], rest[Z_SIZE:]
+def lead_kernel(q_ref, k_ref, v_ref, f_ref, *rest):
+    outs, (f_buf, e_buf, f_sem, e_sem) = rest[:Z_SIZE], rest[Z_SIZE:]
     rows = f_ref.shape[0]
     head, tail = pl.ds(0, EDGE), pl.ds(rows - EDGE, EDGE)
     pieces = [pl.ds(j * LANE, LANE) for j in range(AHEAD)]
     f_copies = [send(f_ref.at[p, :], f_buf.at[p, :], f_sem.at[j]) for j, p in enumerate(pieces)]
     sources = [k_ref.at[head, :], k_ref.at[tail, :], v_ref.at[head, :], v_ref.at[tail, :]]
-    e_copies = [send(x, e_buf.at[i], e_sem.at[i]) for i, x in enumerate(sources)]
+    e_copies = [send(x, e_buf.at[i], e_sem.at[i]) for i, x in enumerate(sources + [q_ref.at[tail, :]])]
     z, x, c = place()
-    depth = out_buf.shape[2]
+    depth = outs[0].shape[1]
     cols = [pl.ds(pl.multiple_of((z + kz) % Z_SIZE * LANE, LANE), LANE) for kz in range(Z_SIZE)]
     for j, p in enumerate(pieces):
         f_copies[j].wait()
-        for kz in range(Z_SIZE):
-            turned = f_buf[p, cols[kz]].astype(jnp.float32).T.astype(out_buf.dtype)
+        for kz, out_ref in enumerate(outs):
+            turned = f_buf[p, cols[kz]].astype(jnp.float32).T.astype(out_ref.dtype)
             for d in range(X_SIZE * 2):
                 to = (d // 2 - x + X_SIZE) % X_SIZE * 2 + (d % 2 - c + 2) % 2
-                out_buf[kz, to * AHEAD + j] = turned[d * depth : (d + 1) * depth]
+                out_ref[to * AHEAD + j] = turned[d * depth : (d + 1) * depth]
     wait_all(e_copies)
-    copies = []
+    edge_at = X_SIZE * 2 * AHEAD
+    q_rows = e_buf[len(sources)].astype(jnp.float32)
+    parts = [slice(g * LANE, (g + 1) * LANE) for g in range(q_rows.shape[1] // LANE)]
+    q_list = [q_rows[r : r + 1, p] for r in (EDGE - 2, EDGE - 1) for p in parts]
+    q_tile = jnp.concatenate(q_list + [jnp.zeros((EDGE - len(q_list), LANE), jnp.float32)], 0)
     for kz, out_ref in enumerate(outs):
         k0, k1, v0, v1 = [e_buf[i, :, cols[kz]].astype(jnp.float32) for i in range(len(sources))]
         own_k, next_k = edge_rows(k0, k1)
         own_v, next_v = edge_rows(v0, v1)
         edge = jnp.concatenate(own_k + own_v + next_k + next_v, 0)
-        out_buf[kz, X_SIZE * 2 * AHEAD] = edge.astype(out_buf.dtype)
-        copies.append(send(out_buf.at[kz], out_ref, out_sem.at[kz]))
-    wait_all(copies)
-
-
-def lead(k, v, f, groups):
+        out_ref[edge_at] = edge.astype(out_ref.dtype)
+        if kz < 2:
+            out_ref[edge_at + 1] = q_tile.astype(out_ref.dtype)
+
+
+def lead(q, k, v, f, groups):
     rows, width = f.shape
-    shape = jax.ShapeDtypeStruct((X_SIZE * 2 * AHEAD + 1, width // groups, LANE), f.dtype)
+    tile = (width // groups, LANE)
+    edge_at = X_SIZE * 2 * AHEAD
     return pl.pallas_call(
         lead_kernel,
-        in_specs=[HBM] * 3,
-        out_specs=(HBM,) * Z_SIZE,
-        out_shape=(shape,) * Z_SIZE,
+        in_specs=[HBM] * 4,
+        out_shape=tuple(
+            pltpu.VMEM((edge_at + (2 if kz < 2 else 1), *tile), f.dtype) for kz in range(Z_SIZE)
+        ),
         scratch_shapes=[
             pltpu.VMEM((AHEAD * LANE, width), f.dtype),
-            pltpu.VMEM((4, EDGE, width), f.dtype),
-            pltpu.VMEM((Z_SIZE, *shape.shape), f.dtype),
+            pltpu.VMEM((5, EDGE, width), f.dtype),
             pltpu.SemaphoreType.DMA((AHEAD,)),
-            pltpu.SemaphoreType.DMA((4,)),
-            pltpu.SemaphoreType.DMA((Z_SIZE,)),
+            pltpu.SemaphoreType.DMA((5,)),
         ],
         cost_estimate=cost(10),
         compiler_params=params(60),
-    )(k, v, f)
+    )(q, k, v, f)
 
 
 def coef_kernel(taps_ref, skip_ref, taps_out, skip_out, turned):
@@ -154,9 +158,13 @@
         out_ref[g * per : (g + 1) * per, j] = turned.reshape(per, depth, LANE).astype(out_ref.dtype)
 
 
+def query_tiles(d):
+    return {1: 1, 3: 2}.get(d, 0)
+
+
 def pack_kernel(*refs):
     ins, outs, turned = refs[:Z_SIZE], refs[Z_SIZE:-1], refs[-1]
-    last = ins[0].shape[0] - 1
+    last = X_SIZE * 2 * AHEAD
     depth = ins[0].shape[1]
     edges = [in_ref[last].astype(jnp.float32) for in_ref in ins]
     zeros = jnp.zeros((LANE - Z_SIZE * depth, LANE), jnp.float32)
@@ -167,13 +175,17 @@
             out_ref[kz * AHEAD : (kz + 1) * AHEAD] = in_ref[d * AHEAD : (d + 1) * AHEAD]
         at = ((x + d // 2) % X_SIZE * 2 + (c + d) % 2) * depth
         out_ref[Z_SIZE * AHEAD] = turned[pl.ds(pl.multiple_of(at, depth), depth), :].astype(out_ref.dtype)
+        for i in range(query_tiles(d)):
+            out_ref[Z_SIZE * AHEAD + 1 + i] = ins[i][last + 1]
 
 
 def pack(parts):
-    shape = jax.ShapeDtypeStruct((Z_SIZE * AHEAD + 1, *parts[0].shape[1:]), parts[0].dtype)
+    tile, dtype = parts[0].shape[1:], parts[0].dtype
     return pl.pallas_call(
         pack_kernel,
-        out_shape=(shape,) * (X_SIZE * 2),
+        out_shape=tuple(
+            jax.ShapeDtypeStruct((Z_SIZE * AHEAD + 1 + query_tiles(d), *tile), dtype) for d in range(X_SIZE * 2)
+        ),
         scratch_shapes=[pltpu.VMEM((LANE, LANE), jnp.float32)],
         cost_estimate=cost(20),
         compiler_params=params(6),
@@ -194,12 +206,6 @@
     parts = [parts[0]] + [shift(parts[k], k, 0, 0) for k in range(1, Z_SIZE)]
     parts = pack(parts)
     return [parts[0]] + [shift(parts[d], 0, d // 2, d % 2) for d in range(1, X_SIZE * 2)]
-
-
-def extend(ext_ref, x_ref, edge):
-    rows = x_ref.shape[0]
-    ext_ref[0:8, :] = edge
-    ext_ref[8 : 8 + rows, :] = x_ref[...].astype(jnp.float32)
 
 
 def taps_of(ext_ref, taps, start, size):
@@ -249,21 +255,32 @@
     )(k, v, f, taps)
 
 
-def gate_kernel(q_ref, edge_ref, taps_ref, out_ref, q_ext):
-    extend(q_ext, q_ref, edge_ref[EDGE - 8 :, :].astype(jnp.float32))
-    for j in range(out_ref.shape[0] // LANE):
+def gate_kernel(q_ref, core_ref, step_ref, taps_ref, out_ref, q_ext):
+    rows, width = q_ref.shape
+    z, x, c = place()
+    at = Z_SIZE * AHEAD + 1
+    tiles = [core_ref[at], step_ref[at], step_ref[at + 1]]
+    core, step, round_z = [t.astype(jnp.float32) for t in tiles]
+    halo = jnp.where(c == 1, core, jnp.where(x > 0, step, jnp.where(z > 0, round_z, 0.0)))
+    parts = width // LANE
+    for r in range(2):
+        for g in range(parts):
+            i = r * parts + g
+            q_ext[6 + r : 7 + r, g * LANE : (g + 1) * LANE] = halo[i : i + 1]
+    q_ext[8 : 8 + rows, :] = q_ref[...].astype(jnp.float32)
+    for j in range(rows // LANE):
         qf = taps_of(q_ext, taps_ref[0], j * LANE, LANE)
         out_ref[j * LANE : (j + 1) * LANE, :] = qf.astype(out_ref.dtype)
 
 
-def gate(q, edge, taps):
+def gate(q, core, step, taps):
     rows, width = q.shape
     return pl.pallas_call(
         gate_kernel,
         out_shape=jax.ShapeDtypeStruct(q.shape, q.dtype),
         scratch_shapes=[pltpu.VMEM((rows + 8, width), jnp.float32)],
         compiler_params=params(8),
-    )(q, edge, taps)
+    )(q, core, step, taps)
 
 
 def mix(table, data):
@@ -290,9 +307,8 @@
         u_wide[at, :] = jnp.where(lane[part] < 2, fixed[part], u_wide[at, :])
 
 
-def conv_kernel(u_ref, q_ref, taps_ref, skip_ref, t1, t2, t2_inv, t1_inv, tw_c, tw_s, *rest):
-    f_refs, (y_ref, q_edge, u_wide, f_wide, y_wide, edges, y_buf, q_sem, y_sem) = rest[:-9], rest[-9:]
-    q_copy = send(q_ref.at[pl.ds(q_ref.shape[0] - EDGE, EDGE), :], q_edge, q_sem)
+def conv_kernel(u_ref, after_ref, taps_ref, skip_ref, t1, t2, t2_inv, t1_inv, tw_c, tw_s, *rest):
+    f_refs, (y_ref, u_wide, f_wide, y_wide, edges) = rest[:-5], rest[-5:]
     depth = skip_ref.shape[0]
     edges[:depth, :] = jnp.zeros((depth, LANE), jnp.float32)
     z, x, c = place()
@@ -349,35 +365,26 @@
         conv = mix(t1_inv[...], jnp.concatenate(cols, 1))
         for i, r in enumerate(rows):
             y_wide[r, :] = part(conv, i)
-    copies = []
-    parts = y_sem.shape[0]
-    rows = y_ref.shape[0] // parts
-    shape = (rows // depth, depth, LANE)
-    for i in range(parts):
-        at = slice(i * rows, (i + 1) * rows)
-        y = y_wide[at, :].reshape(shape) + skip_ref[...][None] * u_wide[at, :].reshape(shape)
-        y_buf[at, :] = y.reshape(rows, LANE).astype(y_buf.dtype)
-        copies.append(send(y_buf.at[at, :], y_ref.at[at, :], y_sem.at[i]))
-    wait_all(copies + [q_copy])
-
-
-def long_conv(u, f, q, taps, skip):
+    shape = (LANE, depth, LANE)
+    y = y_wide[...].reshape(shape) + skip_ref[...][None] * u_wide[...].reshape(shape)
+    y_ref[...] = y.reshape(y_ref.shape).astype(y_ref.dtype)
+
+
+def long_conv(u, f, after, taps, skip):
     sources, slabs, depth, _ = u.shape
     slabs = (slabs + AHEAD) // 2
     flat = (sources * slabs * depth, LANE)
     wide = pltpu.VMEM(flat, jnp.float32)
     edges = pltpu.VMEM(((sources + 1) * depth, LANE), jnp.float32)
-    operands = (u, q, taps, skip, *tables(), *f)
-    y, q_edge = pl.pallas_call(
+    operands = (u, after, taps, skip, *tables(), *f)
+    y = pl.pallas_call(
         conv_kernel,
-        in_specs=[HBM if x is q else VMEM for x in operands],
-        out_specs=(HBM, VMEM),
-        out_shape=(jax.ShapeDtypeStruct(flat, u.dtype), jax.ShapeDtypeStruct((EDGE, q.shape[1]), q.dtype)),
-        scratch_shapes=[wide] * 3
-        + [edges, pltpu.VMEM(flat, u.dtype), pltpu.SemaphoreType.DMA, pltpu.SemaphoreType.DMA((4,))],
+        in_specs=[HBM if x is after else VMEM for x in operands],
+        out_shape=jax.ShapeDtypeStruct(flat, u.dtype),
+        scratch_shapes=[wide] * 3 + [edges],
         compiler_params=params(40),
     )(*operands)
-    return y.reshape(sources, slabs, depth, LANE), q_edge
+    return y.reshape(sources, slabs, depth, LANE)
 
 
 def join_kernel(y_ref, qf_ref, stream_ref, gain_ref, out_ref, sum_ref, sq_ref):
@@ -460,14 +467,12 @@
     fan = lax.axis_size("ch")
     rows, width = queries.shape
     slab = width // groups
-    parts = lead(keys, values, filters, groups)
+    parts = lead(queries, keys, values, filters, groups)
     u_all = exchange(product(keys, values, filters, short_weights, groups), "seq")
     f_all = spread(parts)
     taps, skip = coefficients(short_weights, skip_gain, slab)
-    y, q_edge = long_conv(u_all, f_all, queries, taps, skip)
-    y_home = exchange(y, "seq")
-    q_edge = lax.ppermute(q_edge, "seq", [(i, i + 1) for i in range(groups - 1)])
-    qf = gate(queries, q_edge, short_weights)
+    qf = gate(queries, f_all[1], f_all[3], short_weights)
+    y_home = exchange(long_conv(u_all, f_all, qf, taps, skip), "seq")
     low, summed, squares = join(y_home, qf, stream, norm_gain)
     squares = squares + across(squares, fan, Y_SIZE, 0)
     squares = [squares] + [across(squares, fan, 0, k) for k in range(1, Y_SIZE)]

time: 76.9 us -> 75.1 us (0.977)
  blocking collectives: 0 us -> 22 us
  waiting for transfers between devices: 22.8 us -> 11.3 us
  starting transfers between devices: 41.8 us -> 31.4 us
  Pallas kernels: 10.2 us -> 8.62 us
    all_to_all x0 -> x1, blocking collectives: none -> 22 us  [exchange(): return lax.all_to_all(x, axis, split_axis=0, concat_axis=0, tiled=True)]
    all_to_all x2 -> x1, waiting for transfers between devices: 12.2 us -> 0.75 us  [exchange(): return lax.all_to_all(x, axis, split_axis=0, concat_axis=0, tiled=True)]
    all_to_all x2 -> x1, starting transfers between devices: 13.2 us -> 8.48 us  [exchange(): return lax.all_to_all(x, axis, split_axis=0, concat_axis=0, tiled=True)]
    ppermute x1 -> x0, starting transfers between devices: 3.67 us -> none  [shards(): lax.ppermute(q_edge, 'seq', [(i, i + 1) for i in range(groups - 1)])]
    ppermute x10, starting transfers between devices: 15.9 us -> 13.9 us  [shift(): return lax.ppermute(block, 'seq', route)]
    pallas_call x3, Pallas kernels: 6.25 us -> 4.64 us  [the longest x1 2.95 us: long_conv(): pl.pallas_call(conv_kernel, in_specs=[HBM if x is after else VMEM for x i...]
    ppermute x1 -> x0, waiting for transfers between devices: 0.85 us -> none  [shards(): lax.ppermute(q_edge, 'seq', [(i, i + 1) for i in range(groups - 1)])]
    ppermute x10, waiting for transfers between devices: 5.6 us -> 6.4 us  [shift(): return lax.ppermute(block, 'seq', route)]
  transfers between devices with their start and end apart: 17 -> 15, of which waited for: 10 -> 8; matrix products, arithmetic and copies ran while one was open for 0% -> 0% of each run, Pallas kernels for 3% -> 3%
where the time goes in v5:
time: 75.1 us; the launch traced here: 74.4 us
  starting transfers between devices  31.4 us (42%)
  blocking collectives  22 us (29%)
  waiting for transfers between devices  11.3 us (15%)
  Pallas kernels  8.62 us (11%)
  between operations  1.02 us (1%)
    all_to_all x1, blocking collectives, exchange(): return lax.all_to_all(x, axis, split_axis=0, concat_axis=0, tiled=True)  22 us
    ppermute x10, starting transfers between devices, shift(): return lax.ppermute(block, 'seq', route)  13.9 us
    ppermute x4, starting transfers between devices, across(): return lax.ppermute(block, 'ch', route)  9.1 us
    all_to_all x1, starting transfers between devices, exchange(): return lax.all_to_all(x, axis, split_axis=0, concat_axis=0, tiled=True)  8.48 us
    ppermute x10, waiting for transfers between devices, shift(): return lax.ppermute(block, 'seq', route)  6.4 us
    ppermute x4, waiting for transfers between devices, across(): return lax.ppermute(block, 'ch', route)  4.1 us
    pallas_call x1, Pallas kernels, long_conv(): pl.pallas_call(conv_kernel, in_specs=[HBM if x is after else VMEM for x i...  2.95 us
    pallas_call x1, Pallas kernels, product(): pl.pallas_call(product_kernel, in_specs=[VMEM] * 4, out_specs=HBM, out_sh...  1.67 us
  transfers between devices with their start and end apart: 15, of which 8 were waited for; matrix products, arithmetic and copies ran while one was open for 0% of the time, Pallas kernels for 3%

profile of v5, /device:TPU:1, one launch (start us, length us, event | category | flops | bytes accessed | tf_op | source)
XLA Modules:
  0.0 74.4 jit_solution(8873273623586664645)
XLA Ops:
  0.7 1.6 %shard_map.150 = (bf16[34,16,128]{2,1,0:T(8,128)(2,1)S(1)}, bf16[34,16,128]{2,1,0:T(8,128)(2,1)S(1)}, bf16[33,16,128]{2,1,0:T(8,128)(2,1)S(1)}, bf16[33,16,128]{2,1,0:T(8,128)(2,1)S(1)}) custom-call(bf16[512,512]{1,0:T(8,128)(2,1)} %q_ref.3, bf16[512,512]{1,0:T(8,128)(2,1)} %k_ref.3, bf16[512,512]{1,0:T(8,128)(2,1)} %v_ref.3, bf16[512,512]{1,0:T(8,128)(2,1)} %f_ref.3), custom_call_target="tpu_custom_call" | custom-call | flops 10000000000 | tf_op jit(solution)/shard_map/pallas_call | solution.py:107
  2.2 3.9 %collective-permute-start.1 = (bf16[33,16,128]{2,1,0:T(8,128)(2,1)S(1)}, bf16[33,16,128]{2,1,0:T(8,128)(2,1)S(1)}, u32[]{:S(2)}, u32[]{:S(2)}) collective-permute-start(bf16[33,16,128]{2,1,0:T(8,128)(2,1)S(1)} %get-tuple-element.21), channel_id=1, source_target_pairs={{0,128},{8,136},{16,144},{24,152},{32,160},{40,168},{48,176},{56,1... | collective-permute-start | bytes 405512 | tf_op jit(solution)/shard_map/ppermute | solution.py:202
  6.2 1.4 %collective-permute-start.2 = (bf16[33,16,128]{2,1,0:T(8,128)(2,1)S(1)}, bf16[33,16,128]{2,1,0:T(8,128)(2,1)S(1)}, u32[]{:S(2)}, u32[]{:S(2)}) collective-permute-start(bf16[33,16,128]{2,1,0:T(8,128)(2,1)S(1)} %get-tuple-element.22), channel_id=1, source_target_pairs={{0,192},{8,200},{16,208},{24,216},{32,224},{40,232},{48,240},{56,2... | collective-permute-start | bytes 405512 | tf_op jit(solution)/shard_map/ppermute | solution.py:202
  7.6 0.2 collective-permute-start
  7.8 1.7 %shard_map.149 = bf16[32,4,16,128]{3,2,1,0:T(8,128)(2,1)} custom-call(bf16[512,512]{1,0:T(8,128)(2,1)S(1)} %copy-done.11, bf16[512,512]{1,0:T(8,128)(2,1)S(1)} %copy-done.12, bf16[512,512]{1,0:T(8,128)(2,1)S(1)} %copy-done.13, f32[3,3,512]{2,1,0:T(4,128)S(1)} %copy-done.4), custom_call_target="tpu_custom_call" | custom-call | flops 20000000000 | tf_op jit(solution)/shard_map/pallas_call | solution.py:247
  9.5 8.5 %all-to-all-start = ((bf16[32,4,16,128]{3,2,1,0:T(8,128)(2,1)}), bf16[32,4,16,128]{3,2,1,0:T(8,128)(2,1)S(1)}, u32[]{:S(2)}, u32[]{:S(2)}) async-start(bf16[32,4,16,128]{3,2,1,0:T(8,128)(2,1)} %shard_map.149), calls=%async_computation | async-start | bytes 1048576 | tf_op jit(solution)/shard_map/all_to_all | solution.py:457
  18.0 0.0 collective-permute-done.1.refs_2_
  18.0 0.0 collective-permute-done.2.refs_3_
  18.0 0.0 collective-permute-done.refs_1_
  18.0 0.0 copy-start
  18.0 0.1 shard_map.151
  18.1 1.7 %collective-permute-start.4 = (bf16[19,16,128]{2,1,0:T(8,128)(2,1)S(1)}, bf16[19,16,128]{2,1,0:T(8,128)(2,1)S(1)}, u32[]{:S(2)}, u32[]{:S(2)}) collective-permute-start(bf16[19,16,128]{2,1,0:T(8,128)(2,1)S(1)} %get-tuple-element.24), channel_id=1, source_target_pairs={{0,24},{8,16},{16,40},{24,32},{32,56},{40,48},{48,8},{56,0},{64,88... | collective-permute-start | bytes 233480 | tf_op jit(solution)/shard_map/ppermute | solution.py:202
  19.8 0.1 collective-permute-start.3
  20.0 1.2 %collective-permute-start.5 = (bf16[17,16,128]{2,1,0:T(8,128)(2,1)S(1)}, bf16[17,16,128]{2,1,0:T(8,128)(2,1)S(1)}, u32[]{:S(2)}, u32[]{:S(2)}) collective-permute-start(bf16[17,16,128]{2,1,0:T(8,128)(2,1)S(1)} %get-tuple-element.28), channel_id=1, source_target_pairs={{0,16},{8,24},{16,32},{24,40},{32,48},{40,56},{48,0},{56,8},{64,80... | collective-permute-start | bytes 208904 | tf_op jit(solution)/shard_map/ppermute | solution.py:202
  21.2 1.3 %collective-permute-start.6 = (bf16[17,16,128]{2,1,0:T(8,128)(2,1)S(1)}, bf16[17,16,128]{2,1,0:T(8,128)(2,1)S(1)}, u32[]{:S(2)}, u32[]{:S(2)}) collective-permute-start(bf16[17,16,128]{2,1,0:T(8,128)(2,1)S(1)} %get-tuple-element.29), channel_id=1, source_target_pairs={{0,32},{8,40},{16,48},{24,56},{32,0},{40,8},{48,16},{56,24},{64,96... | collective-permute-start | bytes 208904 | tf_op jit(solution)/shard_map/ppermute | solution.py:202
  22.5 2.5 %collective-permute-start.7 = (bf16[17,16,128]{2,1,0:T(8,128)(2,1)S(1)}, bf16[17,16,128]{2,1,0:T(8,128)(2,1)S(1)}, u32[]{:S(2)}, u32[]{:S(2)}) collective-permute-start(bf16[17,16,128]{2,1,0:T(8,128)(2,1)S(1)} %get-tuple-element.30), channel_id=1, source_target_pairs={{0,40},{8,32},{16,56},{24,48},{32,8},{40,0},{48,24},{56,16},{64,10... | collective-permute-start | bytes 208904 | tf_op jit(solution)/shard_map/ppermute | solution.py:202
  25.0 0.0 collective-permute-done.3.core_ref.rest_1_
  25.0 1.5 %collective-permute-start.8 = (bf16[17,16,128]{2,1,0:T(8,128)(2,1)S(1)}, bf16[17,16,128]{2,1,0:T(8,128)(2,1)S(1)}, u32[]{:S(2)}, u32[]{:S(2)}) collective-permute-start(bf16[17,16,128]{2,1,0:T(8,128)(2,1)S(1)} %get-tuple-element.31), channel_id=1, source_target_pairs={{0,48},{8,56},{16,0},{24,8},{32,16},{40,24},{48,32},{56,40},{64,11... | collective-permute-start | bytes 208904 | tf_op jit(solution)/shard_map/ppermute | solution.py:202
  26.5 1.2 %collective-permute-done.4.step_ref.rest_3_ = bf16[19,16,128]{2,1,0:T(8,128)(2,1)S(1)} collective-permute-done((bf16[19,16,128]{2,1,0:T(8,128)(2,1)S(1)}, bf16[19,16,128]{2,1,0:T(8,128)(2,1)S(1)}, u32[]{:S(2)}, u32[]{:S(2)}) %collective-permute-start.4) | collective-permute-done | bytes 77856 | tf_op jit(solution)/shard_map/ppermute | solution.py:202
  27.7 0.0 collective-permute-start.9
  27.7 0.1 shard_map.153
  27.8 0.0 copy-start.2
  27.8 0.0 copy-start.3
  27.8 0.0 copy-start.5
  27.8 0.0 copy-start.6
  27.9 0.0 copy-start.7
  27.9 0.0 copy-start.8
  27.9 0.6 shard_map.152.after_ref.qf_ref
  28.4 0.2 collective-permute-done.5.rest_2_
  28.7 2.7 %collective-permute-done.6.rest_4_ = bf16[17,16,128]{2,1,0:T(8,128)(2,1)S(1)} collective-permute-done((bf16[17,16,128]{2,1,0:T(8,128)(2,1)S(1)}, bf16[17,16,128]{2,1,0:T(8,128)(2,1)S(1)}, u32[]{:S(2)}, u32[]{:S(2)}) %collective-permute-start.6) | collective-permute-done | bytes 69664 | tf_op jit(solution)/shard_map/ppermute | solution.py:202
  31.3 2.3 %collective-permute-done.7.rest_5_ = bf16[17,16,128]{2,1,0:T(8,128)(2,1)S(1)} collective-permute-done((bf16[17,16,128]{2,1,0:T(8,128)(2,1)S(1)}, bf16[17,16,128]{2,1,0:T(8,128)(2,1)S(1)}, u32[]{:S(2)}, u32[]{:S(2)}) %collective-permute-start.7) | collective-permute-done | bytes 69664 | tf_op jit(solution)/shard_map/ppermute | solution.py:202
  33.6 0.0 collective-permute-done.8.rest_6_
  33.6 0.0 collective-permute-done.9.rest_7_
  33.6 0.8 %all-to-all-done.u_ref = bf16[32,4,16,128]{3,2,1,0:T(8,128)(2,1)S(1)} async-done(((bf16[32,4,16,128]{3,2,1,0:T(8,128)(2,1)}), bf16[32,4,16,128]{3,2,1,0:T(8,128)(2,1)S(1)}, u32[]{:S(2)}, u32[]{:S(2)}) %all-to-all-start) | async-done | bytes 524320 | tf_op jit(solution)/shard_map/all_to_all | solution.py:457
  34.4 0.0 copy-start.9
  34.4 3.0 %shard_map.154 = bf16[2048,128]{1,0:T(8,128)(2,1)S(1)} custom-call(bf16[32,4,16,128]{3,2,1,0:T(8,128)(2,1)S(1)} %all-to-all-done.u_ref, bf16[512,512]{1,0:T(8,128)(2,1)S(1)} %shard_map.152.after_ref.qf_ref, f32[16,128]{1,0:T(8,128)S(1)} %get-tuple-element.25.taps_ref, f32[16,128]{1,0:T(8,128)S(1)} %get-tuple-element.26.skip_ref, ...), custom_call_target="tpu_custom_call" | custom-call | tf_op jit(solution)/shard_map/pallas_call | solution.py:380
  37.4 0.0 copy-start.1
  37.4 22.0 %all_to_all.10.y_ref = bf16[32,4,16,128]{3,2,1,0:T(8,128)(2,1)S(1)} all-to-all(bf16[32,4,16,128]{3,2,1,0:T(8,128)(2,1)S(1)} %bitcast.3), channel_id=1, replica_groups=mesh['seq'=32,'ch'=8] {'seq'}, dimensions={0} | all-to-all | bytes 1048576 | tf_op jit(solution)/shard_map/all_to_all | solution.py:457
  59.4 0.6 shard_map.155
  60.0 5.3 %collective-permute-start.10 = (f32[8,128]{1,0:T(8,128)S(1)}, f32[8,128]{1,0:T(8,128)S(1)}, u32[]{:S(2)}, u32[]{:S(2)}) collective-permute-start(f32[8,128]{1,0:T(8,128)S(1)} %get-tuple-element.35), channel_id=1, source_target_pairs={{0,4},{1,5},{2,6},{3,7},{4,0},{5,1},{6,2},{7,3},{8,12},{9,13},{10,... | collective-permute-start | bytes 12296 | tf_op jit(solution)/shard_map/ppermute | solution.py:462
  65.4 1.1 %collective-permute-done.10 = f32[8,128]{1,0:T(8,128)S(1)} collective-permute-done((f32[8,128]{1,0:T(8,128)S(1)}, f32[8,128]{1,0:T(8,128)S(1)}, u32[]{:S(2)}, u32[]{:S(2)}) %collective-permute-start.10) | collective-permute-done | bytes 4128 | tf_op jit(solution)/shard_map/ppermute | solution.py:462
  66.5 2.7 %collective-permute-start.13 = (f32[8,128]{1,0:T(8,128)S(1)}, f32[8,128]{1,0:T(8,128)S(1)}, u32[]{:S(2)}, u32[]{:S(2)}) collective-permute-start(f32[8,128]{1,0:T(8,128)S(1)} %add.3.refs_2_), channel_id=1, source_target_pairs={{0,3},{1,0},{2,1},{3,2},{4,7},{5,4},{6,5},{7,6},{8,11},{9,8},{10,9... | collective-permute-start | bytes 12296 | tf_op jit(solution)/shard_map/ppermute | solution.py:462
  69.2 0.3 collective-permute-start.12
  69.6 0.7 collective-permute-start.11
  70.3 0.0 collective-permute-done.13.refs_5_
  70.3 2.9 %collective-permute-done.12.refs_4_ = f32[8,128]{1,0:T(8,128)S(1)} collective-permute-done((f32[8,128]{1,0:T(8,128)S(1)}, f32[8,128]{1,0:T(8,128)S(1)}, u32[]{:S(2)}, u32[]{:S(2)}) %collective-permute-start.12) | collective-permute-done | bytes 4128 | tf_op jit(solution)/shard_map/ppermute | solution.py:462
  73.2 0.1 collective-permute-done.11.refs_3_
  73.3 1.0 %shard_map.156 = (bf16[512,512]{1,0:T(8,128)(2,1)}, bf16[512,512]{1,0:T(8,128)(2,1)}) custom-call(bf16[512,512]{1,0:T(8,128)(2,1)S(1)} %get-tuple-element.33.refs_0_, f32[512,512]{1,0:T(8,128)S(1)} %get-tuple-element.34.refs_1_, f32[8,128]{1,0:T(8,128)S(1)} %add.3.refs_2_, f32[8,128]{1,0:T(8,128)S(1)} %collective-permute-done.11.refs_3_, ...), custom_call_target="tpu_custom_call" | custom-call | tf_op jit(solution)/shard_map/pallas_call | solution.py:442
  (20 shorter events, 0.0 us)
Async XLA Ops:
  0.6 7.2 %copy-start.13 = (bf16[512,512]{1,0:T(8,128)(2,1)S(1)}, bf16[512,512]{1,0:T(8,128)(2,1)}, u32[]{:S(2)}) copy-start(bf16[512,512]{1,0:T(8,128)(2,1)} %f_ref.3) | copy-start | bytes 1572868
  0.6 7.2 %copy-start.12 = (bf16[512,512]{1,0:T(8,128)(2,1)S(1)}, bf16[512,512]{1,0:T(8,128)(2,1)}, u32[]{:S(2)}) copy-start(bf16[512,512]{1,0:T(8,128)(2,1)} %v_ref.3) | copy-start | bytes 1572868
  0.7 7.2 %copy-start.11 = (bf16[512,512]{1,0:T(8,128)(2,1)S(1)}, bf16[512,512]{1,0:T(8,128)(2,1)}, u32[]{:S(2)}) copy-start(bf16[512,512]{1,0:T(8,128)(2,1)} %k_ref.3) | copy-start | bytes 1572868
  0.7 7.1 %copy-start.4 = (f32[3,3,512]{2,1,0:T(4,128)S(1)}, f32[3,3,512]{2,1,0:T(4,128)}, u32[]{:S(2)}) copy-start(f32[3,3,512]{2,1,0:T(4,128)} %taps_ref.5) | copy-start | bytes 55300
  2.2 15.7 %collective-permute-start.1 = (bf16[33,16,128]{2,1,0:T(8,128)(2,1)S(1)}, bf16[33,16,128]{2,1,0:T(8,128)(2,1)S(1)}, u32[]{:S(2)}, u32[]{:S(2)}) collective-permute-start(bf16[33,16,128]{2,1,0:T(8,128)(2,1)S(1)} %get-tuple-element.21), channel_id=1, source_target_pairs={{0,128},{8,136},{16,144},{24,152},{32,160},{40,168},{48,176},{56,1... | collective-permute-start | bytes 405512 | tf_op jit(solution)/shard_map/ppermute | solution.py:202
  6.2 11.8 %collective-permute-start.2 = (bf16[33,16,128]{2,1,0:T(8,128)(2,1)S(1)}, bf16[33,16,128]{2,1,0:T(8,128)(2,1)S(1)}, u32[]{:S(2)}, u32[]{:S(2)}) collective-permute-start(bf16[33,16,128]{2,1,0:T(8,128)(2,1)S(1)} %get-tuple-element.22), channel_id=1, source_target_pairs={{0,192},{8,200},{16,208},{24,216},{32,224},{40,232},{48,240},{56,2... | collective-permute-start | bytes 405512 | tf_op jit(solution)/shard_map/ppermute | solution.py:202
  7.6 10.4 %collective-permute-start = (bf16[34,16,128]{2,1,0:T(8,128)(2,1)S(1)}, bf16[34,16,128]{2,1,0:T(8,128)(2,1)S(1)}, u32[]{:S(2)}, u32[]{:S(2)}) collective-permute-start(bf16[34,16,128]{2,1,0:T(8,128)(2,1)S(1)} %get-tuple-element.20), channel_id=1, source_target_pairs={{0,64},{8,72},{16,80},{24,88},{32,96},{40,104},{48,112},{56,120},{... | collective-permute-start | bytes 417800 | tf_op jit(solution)/shard_map/ppermute | solution.py:202
  9.5 24.9 %all-to-all-start = ((bf16[32,4,16,128]{3,2,1,0:T(8,128)(2,1)}), bf16[32,4,16,128]{3,2,1,0:T(8,128)(2,1)S(1)}, u32[]{:S(2)}, u32[]{:S(2)}) async-start(bf16[32,4,16,128]{3,2,1,0:T(8,128)(2,1)} %shard_map.149), calls=%async_computation | async-start | bytes 1048576 | tf_op jit(solution)/shard_map/all_to_all | solution.py:457
  18.0 9.8 %copy-start = (bf16[512,512]{1,0:T(8,128)(2,1)S(1)}, bf16[512,512]{1,0:T(8,128)(2,1)}, u32[]{:S(2)}) copy-start(bf16[512,512]{1,0:T(8,128)(2,1)} %q_ref.3) | copy-start | bytes 1572868
  18.1 9.5 %collective-permute-start.4 = (bf16[19,16,128]{2,1,0:T(8,128)(2,1)S(1)}, bf16[19,16,128]{2,1,0:T(8,128)(2,1)S(1)}, u32[]{:S(2)}, u32[]{:S(2)}) collective-permute-start(bf16[19,16,128]{2,1,0:T(8,128)(2,1)S(1)} %get-tuple-element.24), channel_id=1, source_target_pairs={{0,24},{8,16},{16,40},{24,32},{32,56},{40,48},{48,8},{56,0},{64,88... | collective-permute-start | bytes 233480 | tf_op jit(solution)/shard_map/ppermute | solution.py:202
  19.8 5.1 %collective-permute-start.3 = (bf16[18,16,128]{2,1,0:T(8,128)(2,1)S(1)}, bf16[18,16,128]{2,1,0:T(8,128)(2,1)S(1)}, u32[]{:S(2)}, u32[]{:S(2)}) collective-permute-start(bf16[18,16,128]{2,1,0:T(8,128)(2,1)S(1)} %get-tuple-element.23), channel_id=1, source_target_pairs={{0,8},{8,0},{16,24},{24,16},{32,40},{40,32},{48,56},{56,48},{64,72... | collective-permute-start | bytes 221192 | tf_op jit(solution)/shard_map/ppermute | solution.py:202
  20.0 8.7 %collective-permute-start.5 = (bf16[17,16,128]{2,1,0:T(8,128)(2,1)S(1)}, bf16[17,16,128]{2,1,0:T(8,128)(2,1)S(1)}, u32[]{:S(2)}, u32[]{:S(2)}) collective-permute-start(bf16[17,16,128]{2,1,0:T(8,128)(2,1)S(1)} %get-tuple-element.28), channel_id=1, source_target_pairs={{0,16},{8,24},{16,32},{24,40},{32,48},{40,56},{48,0},{56,8},{64,80... | collective-permute-start | bytes 208904 | tf_op jit(solution)/shard_map/ppermute | solution.py:202
  21.2 10.2 %collective-permute-start.6 = (bf16[17,16,128]{2,1,0:T(8,128)(2,1)S(1)}, bf16[17,16,128]{2,1,0:T(8,128)(2,1)S(1)}, u32[]{:S(2)}, u32[]{:S(2)}) collective-permute-start(bf16[17,16,128]{2,1,0:T(8,128)(2,1)S(1)} %get-tuple-element.29), channel_id=1, source_target_pairs={{0,32},{8,40},{16,48},{24,56},{32,0},{40,8},{48,16},{56,24},{64,96... | collective-permute-start | bytes 208904 | tf_op jit(solution)/shard_map/ppermute | solution.py:202
  22.5 11.2 %collective-permute-start.7 = (bf16[17,16,128]{2,1,0:T(8,128)(2,1)S(1)}, bf16[17,16,128]{2,1,0:T(8,128)(2,1)S(1)}, u32[]{:S(2)}, u32[]{:S(2)}) collective-permute-start(bf16[17,16,128]{2,1,0:T(8,128)(2,1)S(1)} %get-tuple-element.30), channel_id=1, source_target_pairs={{0,40},{8,32},{16,56},{24,48},{32,8},{40,0},{48,24},{56,16},{64,10... | collective-permute-start | bytes 208904 | tf_op jit(solution)/shard_map/ppermute | solution.py:202
  25.0 2.7 %copy-start.10 = (f32[512]{0:T(512)S(1)}, f32[512]{0:T(512)}, u32[]{:S(2)}) copy-start(f32[512]{0:T(512)} %param.19) | copy-start | bytes 6148
  25.0 8.7 %collective-permute-start.8 = (bf16[17,16,128]{2,1,0:T(8,128)(2,1)S(1)}, bf16[17,16,128]{2,1,0:T(8,128)(2,1)S(1)}, u32[]{:S(2)}, u32[]{:S(2)}) collective-permute-start(bf16[17,16,128]{2,1,0:T(8,128)(2,1)S(1)} %get-tuple-element.31), channel_id=1, source_target_pairs={{0,48},{8,56},{16,0},{24,8},{32,16},{40,24},{48,32},{56,40},{64,11... | collective-permute-start | bytes 208904 | tf_op jit(solution)/shard_map/ppermute | solution.py:202
  27.7 6.0 %collective-permute-start.9 = (bf16[17,16,128]{2,1,0:T(8,128)(2,1)S(1)}, bf16[17,16,128]{2,1,0:T(8,128)(2,1)S(1)}, u32[]{:S(2)}, u32[]{:S(2)}) collective-permute-start(bf16[17,16,128]{2,1,0:T(8,128)(2,1)S(1)} %get-tuple-element.32), channel_id=1, source_target_pairs={{0,56},{8,48},{16,8},{24,0},{32,24},{40,16},{48,40},{56,32},{64,12... | collective-permute-start | bytes 208904 | tf_op jit(solution)/shard_map/ppermute | solution.py:202
  27.8 6.6 %copy-start.2 = (bf16[256,256]{1,0:T(8,128)(2,1)S(1)}, bf16[256,256]{1,0:T(8,128)(2,1)}, u32[]{:S(2)}) copy-start(bf16[256,256]{1,0:T(8,128)(2,1)} %constant.14.clone.t2_inv) | copy-start | bytes 393220
  27.8 6.6 %copy-start.3 = (bf16[256,256]{1,0:T(8,128)(2,1)S(1)}, bf16[256,256]{1,0:T(8,128)(2,1)}, u32[]{:S(2)}) copy-start(bf16[256,256]{1,0:T(8,128)(2,1)} %constant.13.clone.t2) | copy-start | bytes 393220
  27.8 6.6 %copy-start.5 = (f32[128,128]{1,0:T(8,128)S(1)}, f32[128,128]{1,0:T(8,128)}, u32[]{:S(2)}) copy-start(f32[128,128]{1,0:T(8,128)} %constant.17.clone.tw_s) | copy-start | bytes 196612
  27.8 6.6 %copy-start.6 = (f32[128,128]{1,0:T(8,128)S(1)}, f32[128,128]{1,0:T(8,128)}, u32[]{:S(2)}) copy-start(f32[128,128]{1,0:T(8,128)} %constant.16.clone.tw_c) | copy-start | bytes 196612
  27.9 6.6 %copy-start.7 = (bf16[128,256]{1,0:T(8,128)(2,1)S(1)}, bf16[128,256]{1,0:T(8,128)(2,1)}, u32[]{:S(2)}) copy-start(bf16[128,256]{1,0:T(8,128)(2,1)} %constant.15.clone.t1_inv) | copy-start | bytes 196612
  27.9 6.6 %copy-start.8 = (bf16[256,128]{1,0:T(8,128)(2,1)S(1)}, bf16[256,128]{1,0:T(8,128)(2,1)}, u32[]{:S(2)}) copy-start(bf16[256,128]{1,0:T(8,128)(2,1)} %constant.12.clone.t1) | copy-start | bytes 196612
  34.4 25.0 %copy-start.9 = (f32[512]{0:T(512)S(1)}, f32[512]{0:T(512)}, u32[]{:S(2)}) copy-start(f32[512]{0:T(512)} %param.21) | copy-start | bytes 6148
  37.4 22.0 %copy-start.1 = (bf16[512,512]{1,0:T(8,128)(2,1)S(1)}, bf16[512,512]{1,0:T(8,128)(2,1)}, u32[]{:S(2)}) copy-start(bf16[512,512]{1,0:T(8,128)(2,1)} %stream_ref.1) | copy-start | bytes 1572868
  60.0 6.5 %collective-permute-start.10 = (f32[8,128]{1,0:T(8,128)S(1)}, f32[8,128]{1,0:T(8,128)S(1)}, u32[]{:S(2)}, u32[]{:S(2)}) collective-permute-start(f32[8,128]{1,0:T(8,128)S(1)} %get-tuple-element.35), channel_id=1, source_target_pairs={{0,4},{1,5},{2,6},{3,7},{4,0},{5,1},{6,2},{7,3},{8,12},{9,13},{10,... | collective-permute-start | bytes 12296 | tf_op jit(solution)/shard_map/ppermute | solution.py:462
  66.5 3.8 %collective-permute-start.13 = (f32[8,128]{1,0:T(8,128)S(1)}, f32[8,128]{1,0:T(8,128)S(1)}, u32[]{:S(2)}, u32[]{:S(2)}) collective-permute-start(f32[8,128]{1,0:T(8,128)S(1)} %add.3.refs_2_), channel_id=1, source_target_pairs={{0,3},{1,0},{2,1},{3,2},{4,7},{5,4},{6,5},{7,6},{8,11},{9,8},{10,9... | collective-permute-start | bytes 12296 | tf_op jit(solution)/shard_map/ppermute | solution.py:462
  69.2 4.0 %collective-permute-start.12 = (f32[8,128]{1,0:T(8,128)S(1)}, f32[8,128]{1,0:T(8,128)S(1)}, u32[]{:S(2)}, u32[]{:S(2)}) collective-permute-start(f32[8,128]{1,0:T(8,128)S(1)} %add.3.refs_2_), channel_id=1, source_target_pairs={{0,2},{1,3},{2,0},{3,1},{4,6},{5,7},{6,4},{7,5},{8,10},{9,11},{10,... | collective-permute-start | bytes 12296 | tf_op jit(solution)/shard_map/ppermute | solution.py:462
  69.6 3.7 %collective-permute-start.11 = (f32[8,128]{1,0:T(8,128)S(1)}, f32[8,128]{1,0:T(8,128)S(1)}, u32[]{:S(2)}, u32[]{:S(2)}) collective-permute-start(f32[8,128]{1,0:T(8,128)S(1)} %add.3.refs_2_), channel_id=1, source_target_pairs={{0,1},{1,2},{2,3},{3,0},{4,5},{5,6},{6,7},{7,4},{8,9},{9,10},{10,1... | collective-permute-start | bytes 12296 | tf_op jit(solution)/shard_map/ppermute | solution.py:462

commit v6 on v5

--- a/solution.py
+++ b/solution.py
@@ -8,7 +8,7 @@
 
 LANE = 128
 EDGE = 16
-GROUP = 8
+GROUP = 16
 Z_SIZE = 4
 X_SIZE = 4
 AHEAD = 4
@@ -35,8 +35,7 @@
     t2 = np.block([[cos2, sin2], [-sin2, cos2]])
     t2_inv = np.block([[cos2, -sin2], [sin2, cos2]])
     t1_inv = np.concatenate([np.cos(first).T, np.sin(first).T], 1) / n
-    low = [jnp.asarray(t, jnp.bfloat16) for t in (t1, t2, t2_inv, t1_inv)]
-    return (*low, jnp.asarray(np.cos(twist), jnp.float32), jnp.asarray(np.sin(twist), jnp.float32))
+    return [jnp.asarray(t, jnp.bfloat16) for t in (t1, t2, t2_inv, t1_inv, np.cos(twist), np.sin(twist))]
 
 
 def place():
@@ -158,8 +157,12 @@
         out_ref[g * per : (g + 1) * per, j] = turned.reshape(per, depth, LANE).astype(out_ref.dtype)
 
 
+def step_x(step, core):
+    return jnp.where(core == 0, step, (X_SIZE - step) % X_SIZE)
+
+
 def query_tiles(d):
-    return {1: 1, 3: 2}.get(d, 0)
+    return {1: 1, 7: 2}.get(d, 0)
 
 
 def pack_kernel(*refs):
@@ -171,9 +174,10 @@
     turned[...] = jnp.concatenate(edges + [zeros], 0).T
     _, x, c = place()
     for d, out_ref in enumerate(outs):
+        kx = step_x(d // 2, c)
         for kz, in_ref in enumerate(ins):
-            out_ref[kz * AHEAD : (kz + 1) * AHEAD] = in_ref[d * AHEAD : (d + 1) * AHEAD]
-        at = ((x + d // 2) % X_SIZE * 2 + (c + d) % 2) * depth
+            out_ref[kz * AHEAD : (kz + 1) * AHEAD] = in_ref[pl.ds((kx * 2 + d % 2) * AHEAD, AHEAD)]
+        at = ((x + kx) % X_SIZE * 2 + (c + d) % 2) * depth
         out_ref[Z_SIZE * AHEAD] = turned[pl.ds(pl.multiple_of(at, depth), depth), :].astype(out_ref.dtype)
         for i in range(query_tiles(d)):
             out_ref[Z_SIZE * AHEAD + 1 + i] = ins[i][last + 1]
@@ -192,20 +196,27 @@
     )(*parts)
 
 
-def shift(block, dz, dx, dc):
-    route = []
-    for z in range(Z_SIZE):
-        for x in range(X_SIZE):
-            for c in range(2):
-                to = ((z + dz) % Z_SIZE * X_SIZE + (x + dx) % X_SIZE) * 2 + (c + dc) % 2
-                route.append(((z * X_SIZE + x) * 2 + c, to))
-    return lax.ppermute(block, "seq", route)
+def seq_index(z, x, c):
+    return (z % Z_SIZE * X_SIZE + x % X_SIZE) * 2 + c % 2
+
+
+def moved(block, target):
+    places = [(z, x, c) for z in range(Z_SIZE) for x in range(X_SIZE) for c in range(2)]
+    return lax.ppermute(block, "seq", [(seq_index(*p), seq_index(*target(*p))) for p in places])
+
+
+def along_z(block, dz):
+    return moved(block, lambda z, x, c: (z + dz, x, c))
+
+
+def cross(block, step, dc):
+    return moved(block, lambda z, x, c: (z, x + step * (1 - 2 * c), c + dc))
 
 
 def spread(parts):
-    parts = [parts[0]] + [shift(parts[k], k, 0, 0) for k in range(1, Z_SIZE)]
+    parts = [parts[0]] + [along_z(parts[k], k) for k in range(1, Z_SIZE)]
     parts = pack(parts)
-    return [parts[0]] + [shift(parts[d], 0, d // 2, d % 2) for d in range(1, X_SIZE * 2)]
+    return [parts[0]] + [cross(parts[d], d // 2, d % 2) for d in range(1, X_SIZE * 2)]
 
 
 def taps_of(ext_ref, taps, start, size):
@@ -321,9 +332,11 @@
         if ahead < size:
             f_wide[i * size + ahead : (i + 1) * size, :] = both[size:]
     for d, f_ref in enumerate(f_refs):
+        core = (c + d) % 2
+        kx = step_x(d // 2, core)
         edge = f_ref[Z_SIZE * AHEAD].astype(jnp.float32)
         for kz in range(Z_SIZE):
-            src = ((z - kz + Z_SIZE) % Z_SIZE * X_SIZE + (x - d // 2 + X_SIZE) % X_SIZE) * 2 + (c + d) % 2
+            src = ((z - kz + Z_SIZE) % Z_SIZE * X_SIZE + (x - kx + X_SIZE) % X_SIZE) * 2 + core
             row = pl.multiple_of(src * size, size)
             tiles = f_ref[kz * AHEAD : (kz + 1) * AHEAD].reshape(ahead, LANE)
             f_wide[pl.ds(row, ahead), :] = tiles.astype(jnp.float32)
@@ -339,9 +352,9 @@
         first = mix(t1[...], jnp.concatenate(data, 1))
         turned = []
         for i in range(len(rows)):
-            re, im = part(first[:LANE], i), part(first[LANE:], i)
+            re, im = part(first[:LANE], i).astype(low), part(first[LANE:], i).astype(low)
             c, s = tw_c[...], tw_s[...]
-            turned.append(jnp.concatenate([re * c - im * s, re * s + im * c], 1).astype(low))
+            turned.append(jnp.concatenate([re * c - im * s, re * s + im * c], 1))
         return mix(jnp.concatenate(turned, 0), t2[...])
 
     for start in range(0, depth, GROUP):
@@ -359,9 +372,9 @@
         cols = []
         for i in range(GROUP):
             v = back[i * LANE : (i + 1) * LANE]
-            re, im = v[:, :LANE], v[:, LANE:]
+            re, im = v[:, :LANE].astype(low), v[:, LANE:].astype(low)
             c, s = tw_c[...], tw_s[...]
-            cols.append(jnp.concatenate([re * c + im * s, im * c - re * s], 0).astype(low))
+            cols.append(jnp.concatenate([re * c + im * s, im * c - re * s], 0))
         conv = mix(t1_inv[...], jnp.concatenate(cols, 1))
         for i, r in enumerate(rows):
             y_wide[r, :] = part(conv, i)
@@ -471,7 +484,7 @@
     u_all = exchange(product(keys, values, filters, short_weights, groups), "seq")
     f_all = spread(parts)
     taps, skip = coefficients(short_weights, skip_gain, slab)
-    qf = gate(queries, f_all[1], f_all[3], short_weights)
+    qf = gate(queries, f_all[1], f_all[7], short_weights)
     y_home = exchange(long_conv(u_all, f_all, qf, taps, skip), "seq")
     low, summed, squares = join(y_home, qf, stream, norm_gain)
     squares = squares + across(squares, fan, Y_SIZE, 0)

time: 75.1 us -> 74.4 us (level)
  starting transfers between devices: 31.4 us -> 32.4 us
  transfers between devices with their start and end apart: 15 -> 15, of which waited for: 8 -> 7; matrix products, arithmetic and copies ran while one was open for 0% -> 0% of each run, Pallas kernels for 3% -> 3%
where the time goes in v6:
time: 74.4 us; the launch traced here: 74.2 us
  starting transfers between devices  32.4 us (44%)
  blocking collectives  21.6 us (29%)
  waiting for transfers between devices  10.7 us (14%)
  Pallas kernels  8.32 us (11%)
  between operations  1.03 us (1%)
    all_to_all x1, blocking collectives, exchange(): return lax.all_to_all(x, axis, split_axis=0, concat_axis=0, tiled=True)  21.6 us
    ppermute x10, starting transfers between devices, moved(): lax.ppermute(block, 'seq', [(seq_index(*p), seq_index(*target(*p))) for p...  14.5 us
    ppermute x4, starting transfers between devices, across(): return lax.ppermute(block, 'ch', route)  9.44 us
    all_to_all x1, starting transfers between devices, exchange(): return lax.all_to_all(x, axis, split_axis=0, concat_axis=0, tiled=True)  8.48 us
    ppermute x10, waiting for transfers between devices, moved(): lax.ppermute(block, 'seq', [(seq_index(*p), seq_index(*target(*p))) for p...  5.81 us
    ppermute x4, waiting for transfers between devices, across(): return lax.ppermute(block, 'ch', route)  4.22 us
    pallas_call x1, Pallas kernels, long_conv(): pl.pallas_call(conv_kernel, in_specs=[HBM if x is after else VMEM for x i...  2.66 us
    pallas_call x1, Pallas kernels, product(): pl.pallas_call(product_kernel, in_specs=[VMEM] * 4, out_specs=HBM, out_sh...  1.67 us
  transfers between devices with their start and end apart: 15, of which 7 were waited for; matrix products, arithmetic and copies ran while one was open for 0% of the time, Pallas kernels for 3%

profile of v6, /device:TPU:1, one launch (start us, length us, event | category | flops | bytes accessed | tf_op | source)
XLA Modules:
  0.0 74.2 jit_solution(9540330467884132023)
XLA Ops:
  0.7 1.6 %shard_map.150 = (bf16[34,16,128]{2,1,0:T(8,128)(2,1)S(1)}, bf16[34,16,128]{2,1,0:T(8,128)(2,1)S(1)}, bf16[33,16,128]{2,1,0:T(8,128)(2,1)S(1)}, bf16[33,16,128]{2,1,0:T(8,128)(2,1)S(1)}) custom-call(bf16[512,512]{1,0:T(8,128)(2,1)} %q_ref.3, bf16[512,512]{1,0:T(8,128)(2,1)} %k_ref.3, bf16[512,512]{1,0:T(8,128)(2,1)} %v_ref.3, bf16[512,512]{1,0:T(8,128)(2,1)} %f_ref.3), custom_call_target="tpu_custom_call" | custom-call | flops 10000000000 | tf_op jit(solution)/shard_map/pallas_call | solution.py:106
  2.2 3.9 %collective-permute-start.1 = (bf16[33,16,128]{2,1,0:T(8,128)(2,1)S(1)}, bf16[33,16,128]{2,1,0:T(8,128)(2,1)S(1)}, u32[]{:S(2)}, u32[]{:S(2)}) collective-permute-start(bf16[33,16,128]{2,1,0:T(8,128)(2,1)S(1)} %get-tuple-element.21), channel_id=1, source_target_pairs={{0,128},{8,136},{16,144},{24,152},{32,160},{40,168},{48,176},{56,1... | collective-permute-start | bytes 405512 | tf_op jit(solution)/shard_map/ppermute | solution.py:205
  6.2 1.4 %collective-permute-start.2 = (bf16[33,16,128]{2,1,0:T(8,128)(2,1)S(1)}, bf16[33,16,128]{2,1,0:T(8,128)(2,1)S(1)}, u32[]{:S(2)}, u32[]{:S(2)}) collective-permute-start(bf16[33,16,128]{2,1,0:T(8,128)(2,1)S(1)} %get-tuple-element.22), channel_id=1, source_target_pairs={{0,192},{8,200},{16,208},{24,216},{32,224},{40,232},{48,240},{56,2... | collective-permute-start | bytes 405512 | tf_op jit(solution)/shard_map/ppermute | solution.py:205
  7.6 0.2 collective-permute-start
  7.8 1.7 %shard_map.149 = bf16[32,4,16,128]{3,2,1,0:T(8,128)(2,1)} custom-call(bf16[512,512]{1,0:T(8,128)(2,1)S(1)} %copy-done.11, bf16[512,512]{1,0:T(8,128)(2,1)S(1)} %copy-done.12, bf16[512,512]{1,0:T(8,128)(2,1)S(1)} %copy-done.13, f32[3,3,512]{2,1,0:T(4,128)S(1)} %copy-done.4), custom_call_target="tpu_custom_call" | custom-call | flops 20000000000 | tf_op jit(solution)/shard_map/pallas_call | solution.py:258
  9.5 8.5 %all-to-all-start = ((bf16[32,4,16,128]{3,2,1,0:T(8,128)(2,1)}), bf16[32,4,16,128]{3,2,1,0:T(8,128)(2,1)S(1)}, u32[]{:S(2)}, u32[]{:S(2)}) async-start(bf16[32,4,16,128]{3,2,1,0:T(8,128)(2,1)} %shard_map.149), calls=%async_computation | async-start | bytes 1048576 | tf_op jit(solution)/shard_map/all_to_all | solution.py:470
  18.0 0.0 collective-permute-done.1.refs_2_
  18.0 0.0 collective-permute-done.2.refs_3_
  18.0 0.0 collective-permute-done.refs_1_
  18.0 0.0 copy-start
  18.0 0.1 shard_map.151
  18.1 1.7 %collective-permute-start.4 = (bf16[19,16,128]{2,1,0:T(8,128)(2,1)S(1)}, bf16[19,16,128]{2,1,0:T(8,128)(2,1)S(1)}, u32[]{:S(2)}, u32[]{:S(2)}) collective-permute-start(bf16[19,16,128]{2,1,0:T(8,128)(2,1)S(1)} %get-tuple-element.24), channel_id=1, source_target_pairs={{0,56},{8,16},{16,8},{24,32},{32,24},{40,48},{48,40},{56,0},{64,12... | collective-permute-start | bytes 233480 | tf_op jit(solution)/shard_map/ppermute | solution.py:205
  19.9 1.4 %collective-permute-start.3 = (bf16[18,16,128]{2,1,0:T(8,128)(2,1)S(1)}, bf16[18,16,128]{2,1,0:T(8,128)(2,1)S(1)}, u32[]{:S(2)}, u32[]{:S(2)}) collective-permute-start(bf16[18,16,128]{2,1,0:T(8,128)(2,1)S(1)} %get-tuple-element.23), channel_id=1, source_target_pairs={{0,8},{8,0},{16,24},{24,16},{32,40},{40,32},{48,56},{56,48},{64,72... | collective-permute-start | bytes 221192 | tf_op jit(solution)/shard_map/ppermute | solution.py:205
  21.2 0.6 collective-permute-start.5
  21.8 2.3 %collective-permute-start.6 = (bf16[17,16,128]{2,1,0:T(8,128)(2,1)S(1)}, bf16[17,16,128]{2,1,0:T(8,128)(2,1)S(1)}, u32[]{:S(2)}, u32[]{:S(2)}) collective-permute-start(bf16[17,16,128]{2,1,0:T(8,128)(2,1)S(1)} %get-tuple-element.29), channel_id=1, source_target_pairs={{0,24},{8,48},{16,40},{24,0},{32,56},{40,16},{48,8},{56,32},{64,88... | collective-permute-start | bytes 208904 | tf_op jit(solution)/shard_map/ppermute | solution.py:205
  24.1 0.3 collective-permute-start.7
  24.4 0.0 collective-permute-done.3.core_ref.rest_1_
  24.4 1.8 %collective-permute-start.8 = (bf16[17,16,128]{2,1,0:T(8,128)(2,1)S(1)}, bf16[17,16,128]{2,1,0:T(8,128)(2,1)S(1)}, u32[]{:S(2)}, u32[]{:S(2)}) collective-permute-start(bf16[17,16,128]{2,1,0:T(8,128)(2,1)S(1)} %get-tuple-element.31), channel_id=1, source_target_pairs={{0,40},{8,32},{16,56},{24,48},{32,8},{40,0},{48,24},{56,16},{64,10... | collective-permute-start | bytes 208904 | tf_op jit(solution)/shard_map/ppermute | solution.py:205
  26.2 0.0 collective-permute-done.4.step_ref.rest_7_
  26.2 0.9 %collective-permute-start.9 = (bf16[17,16,128]{2,1,0:T(8,128)(2,1)S(1)}, bf16[17,16,128]{2,1,0:T(8,128)(2,1)S(1)}, u32[]{:S(2)}, u32[]{:S(2)}) collective-permute-start(bf16[17,16,128]{2,1,0:T(8,128)(2,1)S(1)} %get-tuple-element.32), channel_id=1, source_target_pairs={{0,48},{8,24},{16,0},{24,40},{32,16},{40,56},{48,32},{56,8},{64,11... | collective-permute-start | bytes 208904 | tf_op jit(solution)/shard_map/ppermute | solution.py:205
  27.1 0.1 shard_map.153
  27.3 0.0 copy-start.2
  27.3 0.0 copy-start.3
  27.3 0.0 copy-start.5
  27.3 0.0 copy-start.6
  27.3 0.0 copy-start.7
  27.3 0.0 copy-start.8
  27.3 0.6 shard_map.152.after_ref.qf_ref
  27.9 0.0 collective-permute-done.5.rest_2_
  27.9 0.3 collective-permute-done.6.rest_3_
  28.2 2.1 %collective-permute-done.7.rest_4_ = bf16[17,16,128]{2,1,0:T(8,128)(2,1)S(1)} collective-permute-done((bf16[17,16,128]{2,1,0:T(8,128)(2,1)S(1)}, bf16[17,16,128]{2,1,0:T(8,128)(2,1)S(1)}, u32[]{:S(2)}, u32[]{:S(2)}) %collective-permute-start.7) | collective-permute-done | bytes 69664 | tf_op jit(solution)/shard_map/ppermute | solution.py:205
  30.3 2.4 %collective-permute-done.8.rest_5_ = bf16[17,16,128]{2,1,0:T(8,128)(2,1)S(1)} collective-permute-done((bf16[17,16,128]{2,1,0:T(8,128)(2,1)S(1)}, bf16[17,16,128]{2,1,0:T(8,128)(2,1)S(1)}, u32[]{:S(2)}, u32[]{:S(2)}) %collective-permute-start.8) | collective-permute-done | bytes 69664 | tf_op jit(solution)/shard_map/ppermute | solution.py:205
  32.8 0.9 %collective-permute-done.9.rest_6_ = bf16[17,16,128]{2,1,0:T(8,128)(2,1)S(1)} collective-permute-done((bf16[17,16,128]{2,1,0:T(8,128)(2,1)S(1)}, bf16[17,16,128]{2,1,0:T(8,128)(2,1)S(1)}, u32[]{:S(2)}, u32[]{:S(2)}) %collective-permute-start.9) | collective-permute-done | bytes 69664 | tf_op jit(solution)/shard_map/ppermute | solution.py:205
  33.7 0.7 all-to-all-done.u_ref
  34.4 0.0 copy-start.9
  34.4 2.7 %shard_map.154 = bf16[2048,128]{1,0:T(8,128)(2,1)S(1)} custom-call(bf16[32,4,16,128]{3,2,1,0:T(8,128)(2,1)S(1)} %all-to-all-done.u_ref, bf16[512,512]{1,0:T(8,128)(2,1)S(1)} %shard_map.152.after_ref.qf_ref, f32[16,128]{1,0:T(8,128)S(1)} %get-tuple-element.25.taps_ref, f32[16,128]{1,0:T(8,128)S(1)} %get-tuple-element.26.skip_ref, ...), custom_call_target="tpu_custom_call" | custom-call | tf_op jit(solution)/shard_map/pallas_call | solution.py:393
  37.1 0.0 copy-start.1
  37.1 21.6 %all_to_all.10.y_ref = bf16[32,4,16,128]{3,2,1,0:T(8,128)(2,1)S(1)} all-to-all(bf16[32,4,16,128]{3,2,1,0:T(8,128)(2,1)S(1)} %bitcast.3), channel_id=1, replica_groups=mesh['seq'=32,'ch'=8] {'seq'}, dimensions={0} | all-to-all | bytes 1048576 | tf_op jit(solution)/shard_map/all_to_all | solution.py:470
  58.7 0.6 shard_map.155
  59.3 5.7 %collective-permute-start.10 = (f32[8,128]{1,0:T(8,128)S(1)}, f32[8,128]{1,0:T(8,128)S(1)}, u32[]{:S(2)}, u32[]{:S(2)}) collective-permute-start(f32[8,128]{1,0:T(8,128)S(1)} %get-tuple-element.35), channel_id=1, source_target_pairs={{0,4},{1,5},{2,6},{3,7},{4,0},{5,1},{6,2},{7,3},{8,12},{9,13},{10,... | collective-permute-start | bytes 12296 | tf_op jit(solution)/shard_map/ppermute | solution.py:475
  65.0 1.3 %collective-permute-done.10 = f32[8,128]{1,0:T(8,128)S(1)} collective-permute-done((f32[8,128]{1,0:T(8,128)S(1)}, f32[8,128]{1,0:T(8,128)S(1)}, u32[]{:S(2)}, u32[]{:S(2)}) %collective-permute-start.10) | collective-permute-done | bytes 4128 | tf_op jit(solution)/shard_map/ppermute | solution.py:475
  66.2 2.7 %collective-permute-start.13 = (f32[8,128]{1,0:T(8,128)S(1)}, f32[8,128]{1,0:T(8,128)S(1)}, u32[]{:S(2)}, u32[]{:S(2)}) collective-permute-start(f32[8,128]{1,0:T(8,128)S(1)} %add.3.refs_2_), channel_id=1, source_target_pairs={{0,3},{1,0},{2,1},{3,2},{4,7},{5,4},{6,5},{7,6},{8,11},{9,8},{10,9... | collective-permute-start | bytes 12296 | tf_op jit(solution)/shard_map/ppermute | solution.py:475
  69.0 0.3 collective-permute-start.12
  69.3 0.7 collective-permute-start.11
  70.0 0.0 collective-permute-done.13.refs_5_
  70.0 2.9 %collective-permute-done.12.refs_4_ = f32[8,128]{1,0:T(8,128)S(1)} collective-permute-done((f32[8,128]{1,0:T(8,128)S(1)}, f32[8,128]{1,0:T(8,128)S(1)}, u32[]{:S(2)}, u32[]{:S(2)}) %collective-permute-start.12) | collective-permute-done | bytes 4128 | tf_op jit(solution)/shard_map/ppermute | solution.py:475
  73.0 0.1 collective-permute-done.11.refs_3_
  73.0 1.0 %shard_map.156 = (bf16[512,512]{1,0:T(8,128)(2,1)}, bf16[512,512]{1,0:T(8,128)(2,1)}) custom-call(bf16[512,512]{1,0:T(8,128)(2,1)S(1)} %get-tuple-element.33.refs_0_, f32[512,512]{1,0:T(8,128)S(1)} %get-tuple-element.34.refs_1_, f32[8,128]{1,0:T(8,128)S(1)} %add.3.refs_2_, f32[8,128]{1,0:T(8,128)S(1)} %collective-permute-done.11.refs_3_, ...), custom_call_target="tpu_custom_call" | custom-call | tf_op jit(solution)/shard_map/pallas_call | solution.py:455
  (20 shorter events, 0.0 us)
Async XLA Ops:
  0.6 7.2 %copy-start.13 = (bf16[512,512]{1,0:T(8,128)(2,1)S(1)}, bf16[512,512]{1,0:T(8,128)(2,1)}, u32[]{:S(2)}) copy-start(bf16[512,512]{1,0:T(8,128)(2,1)} %f_ref.3) | copy-start | bytes 1572868
  0.6 7.2 %copy-start.12 = (bf16[512,512]{1,0:T(8,128)(2,1)S(1)}, bf16[512,512]{1,0:T(8,128)(2,1)}, u32[]{:S(2)}) copy-start(bf16[512,512]{1,0:T(8,128)(2,1)} %v_ref.3) | copy-start | bytes 1572868
  0.7 7.2 %copy-start.11 = (bf16[512,512]{1,0:T(8,128)(2,1)S(1)}, bf16[512,512]{1,0:T(8,128)(2,1)}, u32[]{:S(2)}) copy-start(bf16[512,512]{1,0:T(8,128)(2,1)} %k_ref.3) | copy-start | bytes 1572868
  0.7 7.1 %copy-start.4 = (f32[3,3,512]{2,1,0:T(4,128)S(1)}, f32[3,3,512]{2,1,0:T(4,128)}, u32[]{:S(2)}) copy-start(f32[3,3,512]{2,1,0:T(4,128)} %taps_ref.5) | copy-start | bytes 55300
  2.2 15.7 %collective-permute-start.1 = (bf16[33,16,128]{2,1,0:T(8,128)(2,1)S(1)}, bf16[33,16,128]{2,1,0:T(8,128)(2,1)S(1)}, u32[]{:S(2)}, u32[]{:S(2)}) collective-permute-start(bf16[33,16,128]{2,1,0:T(8,128)(2,1)S(1)} %get-tuple-element.21), channel_id=1, source_target_pairs={{0,128},{8,136},{16,144},{24,152},{32,160},{40,168},{48,176},{56,1... | collective-permute-start | bytes 405512 | tf_op jit(solution)/shard_map/ppermute | solution.py:205
  6.2 11.8 %collective-permute-start.2 = (bf16[33,16,128]{2,1,0:T(8,128)(2,1)S(1)}, bf16[33,16,128]{2,1,0:T(8,128)(2,1)S(1)}, u32[]{:S(2)}, u32[]{:S(2)}) collective-permute-start(bf16[33,16,128]{2,1,0:T(8,128)(2,1)S(1)} %get-tuple-element.22), channel_id=1, source_target_pairs={{0,192},{8,200},{16,208},{24,216},{32,224},{40,232},{48,240},{56,2... | collective-permute-start | bytes 405512 | tf_op jit(solution)/shard_map/ppermute | solution.py:205
  7.6 10.4 %collective-permute-start = (bf16[34,16,128]{2,1,0:T(8,128)(2,1)S(1)}, bf16[34,16,128]{2,1,0:T(8,128)(2,1)S(1)}, u32[]{:S(2)}, u32[]{:S(2)}) collective-permute-start(bf16[34,16,128]{2,1,0:T(8,128)(2,1)S(1)} %get-tuple-element.20), channel_id=1, source_target_pairs={{0,64},{8,72},{16,80},{24,88},{32,96},{40,104},{48,112},{56,120},{... | collective-permute-start | bytes 417800 | tf_op jit(solution)/shard_map/ppermute | solution.py:205
  9.5 24.9 %all-to-all-start = ((bf16[32,4,16,128]{3,2,1,0:T(8,128)(2,1)}), bf16[32,4,16,128]{3,2,1,0:T(8,128)(2,1)S(1)}, u32[]{:S(2)}, u32[]{:S(2)}) async-start(bf16[32,4,16,128]{3,2,1,0:T(8,128)(2,1)} %shard_map.149), calls=%async_computation | async-start | bytes 1048576 | tf_op jit(solution)/shard_map/all_to_all | solution.py:470
  18.0 9.2 %copy-start = (bf16[512,512]{1,0:T(8,128)(2,1)S(1)}, bf16[512,512]{1,0:T(8,128)(2,1)}, u32[]{:S(2)}) copy-start(bf16[512,512]{1,0:T(8,128)(2,1)} %q_ref.3) | copy-start | bytes 1572868
  18.1 8.1 %collective-permute-start.4 = (bf16[19,16,128]{2,1,0:T(8,128)(2,1)S(1)}, bf16[19,16,128]{2,1,0:T(8,128)(2,1)S(1)}, u32[]{:S(2)}, u32[]{:S(2)}) collective-permute-start(bf16[19,16,128]{2,1,0:T(8,128)(2,1)S(1)} %get-tuple-element.24), channel_id=1, source_target_pairs={{0,56},{8,16},{16,8},{24,32},{32,24},{40,48},{48,40},{56,0},{64,12... | collective-permute-start | bytes 233480 | tf_op jit(solution)/shard_map/ppermute | solution.py:205
  19.9 4.5 %collective-permute-start.3 = (bf16[18,16,128]{2,1,0:T(8,128)(2,1)S(1)}, bf16[18,16,128]{2,1,0:T(8,128)(2,1)S(1)}, u32[]{:S(2)}, u32[]{:S(2)}) collective-permute-start(bf16[18,16,128]{2,1,0:T(8,128)(2,1)S(1)} %get-tuple-element.23), channel_id=1, source_target_pairs={{0,8},{8,0},{16,24},{24,16},{32,40},{40,32},{48,56},{56,48},{64,72... | collective-permute-start | bytes 221192 | tf_op jit(solution)/shard_map/ppermute | solution.py:205
  21.2 6.7 %collective-permute-start.5 = (bf16[17,16,128]{2,1,0:T(8,128)(2,1)S(1)}, bf16[17,16,128]{2,1,0:T(8,128)(2,1)S(1)}, u32[]{:S(2)}, u32[]{:S(2)}) collective-permute-start(bf16[17,16,128]{2,1,0:T(8,128)(2,1)S(1)} %get-tuple-element.28), channel_id=1, source_target_pairs={{0,16},{8,56},{16,32},{24,8},{32,48},{40,24},{48,0},{56,40},{64,80... | collective-permute-start | bytes 208904 | tf_op jit(solution)/shard_map/ppermute | solution.py:205
  21.8 6.4 %collective-permute-start.6 = (bf16[17,16,128]{2,1,0:T(8,128)(2,1)S(1)}, bf16[17,16,128]{2,1,0:T(8,128)(2,1)S(1)}, u32[]{:S(2)}, u32[]{:S(2)}) collective-permute-start(bf16[17,16,128]{2,1,0:T(8,128)(2,1)S(1)} %get-tuple-element.29), channel_id=1, source_target_pairs={{0,24},{8,48},{16,40},{24,0},{32,56},{40,16},{48,8},{56,32},{64,88... | collective-permute-start | bytes 208904 | tf_op jit(solution)/shard_map/ppermute | solution.py:205
  24.1 6.3 %collective-permute-start.7 = (bf16[17,16,128]{2,1,0:T(8,128)(2,1)S(1)}, bf16[17,16,128]{2,1,0:T(8,128)(2,1)S(1)}, u32[]{:S(2)}, u32[]{:S(2)}) collective-permute-start(bf16[17,16,128]{2,1,0:T(8,128)(2,1)S(1)} %get-tuple-element.30), channel_id=1, source_target_pairs={{0,32},{8,40},{16,48},{24,56},{32,0},{40,8},{48,16},{56,24},{64,96... | collective-permute-start | bytes 208904 | tf_op jit(solution)/shard_map/ppermute | solution.py:205
  24.4 2.7 %copy-start.10 = (f32[512]{0:T(512)S(1)}, f32[512]{0:T(512)}, u32[]{:S(2)}) copy-start(f32[512]{0:T(512)} %param.19) | copy-start | bytes 6148
  24.4 8.4 %collective-permute-start.8 = (bf16[17,16,128]{2,1,0:T(8,128)(2,1)S(1)}, bf16[17,16,128]{2,1,0:T(8,128)(2,1)S(1)}, u32[]{:S(2)}, u32[]{:S(2)}) collective-permute-start(bf16[17,16,128]{2,1,0:T(8,128)(2,1)S(1)} %get-tuple-element.31), channel_id=1, source_target_pairs={{0,40},{8,32},{16,56},{24,48},{32,8},{40,0},{48,24},{56,16},{64,10... | collective-permute-start | bytes 208904 | tf_op jit(solution)/shard_map/ppermute | solution.py:205
  26.2 7.5 %collective-permute-start.9 = (bf16[17,16,128]{2,1,0:T(8,128)(2,1)S(1)}, bf16[17,16,128]{2,1,0:T(8,128)(2,1)S(1)}, u32[]{:S(2)}, u32[]{:S(2)}) collective-permute-start(bf16[17,16,128]{2,1,0:T(8,128)(2,1)S(1)} %get-tuple-element.32), channel_id=1, source_target_pairs={{0,48},{8,24},{16,0},{24,40},{32,16},{40,56},{48,32},{56,8},{64,11... | collective-permute-start | bytes 208904 | tf_op jit(solution)/shard_map/ppermute | solution.py:205
  27.3 7.1 %copy-start.2 = (bf16[256,256]{1,0:T(8,128)(2,1)S(1)}, bf16[256,256]{1,0:T(8,128)(2,1)}, u32[]{:S(2)}) copy-start(bf16[256,256]{1,0:T(8,128)(2,1)} %constant.14.clone.t2_inv) | copy-start | bytes 393220
  27.3 7.1 %copy-start.3 = (bf16[256,256]{1,0:T(8,128)(2,1)S(1)}, bf16[256,256]{1,0:T(8,128)(2,1)}, u32[]{:S(2)}) copy-start(bf16[256,256]{1,0:T(8,128)(2,1)} %constant.13.clone.t2) | copy-start | bytes 393220
  27.3 7.1 %copy-start.5 = (bf16[128,256]{1,0:T(8,128)(2,1)S(1)}, bf16[128,256]{1,0:T(8,128)(2,1)}, u32[]{:S(2)}) copy-start(bf16[128,256]{1,0:T(8,128)(2,1)} %constant.15.clone.t1_inv) | copy-start | bytes 196612
  27.3 7.1 %copy-start.6 = (bf16[256,128]{1,0:T(8,128)(2,1)S(1)}, bf16[256,128]{1,0:T(8,128)(2,1)}, u32[]{:S(2)}) copy-start(bf16[256,128]{1,0:T(8,128)(2,1)} %constant.12.clone.t1) | copy-start | bytes 196612
  27.3 7.1 %copy-start.7 = (bf16[128,128]{1,0:T(8,128)(2,1)S(1)}, bf16[128,128]{1,0:T(8,128)(2,1)}, u32[]{:S(2)}) copy-start(bf16[128,128]{1,0:T(8,128)(2,1)} %constant.17.clone.tw_s) | copy-start | bytes 98308
  27.3 7.1 %copy-start.8 = (bf16[128,128]{1,0:T(8,128)(2,1)S(1)}, bf16[128,128]{1,0:T(8,128)(2,1)}, u32[]{:S(2)}) copy-start(bf16[128,128]{1,0:T(8,128)(2,1)} %constant.16.clone.tw_c) | copy-start | bytes 98308
  34.4 24.3 %copy-start.9 = (f32[512]{0:T(512)S(1)}, f32[512]{0:T(512)}, u32[]{:S(2)}) copy-start(f32[512]{0:T(512)} %param.21) | copy-start | bytes 6148
  37.1 21.6 %copy-start.1 = (bf16[512,512]{1,0:T(8,128)(2,1)S(1)}, bf16[512,512]{1,0:T(8,128)(2,1)}, u32[]{:S(2)}) copy-start(bf16[512,512]{1,0:T(8,128)(2,1)} %stream_ref.1) | copy-start | bytes 1572868
  59.3 6.9 %collective-permute-start.10 = (f32[8,128]{1,0:T(8,128)S(1)}, f32[8,128]{1,0:T(8,128)S(1)}, u32[]{:S(2)}, u32[]{:S(2)}) collective-permute-start(f32[8,128]{1,0:T(8,128)S(1)} %get-tuple-element.35), channel_id=1, source_target_pairs={{0,4},{1,5},{2,6},{3,7},{4,0},{5,1},{6,2},{7,3},{8,12},{9,13},{10,... | collective-permute-start | bytes 12296 | tf_op jit(solution)/shard_map/ppermute | solution.py:475
  66.2 3.8 %collective-permute-start.13 = (f32[8,128]{1,0:T(8,128)S(1)}, f32[8,128]{1,0:T(8,128)S(1)}, u32[]{:S(2)}, u32[]{:S(2)}) collective-permute-start(f32[8,128]{1,0:T(8,128)S(1)} %add.3.refs_2_), channel_id=1, source_target_pairs={{0,3},{1,0},{2,1},{3,2},{4,7},{5,4},{6,5},{7,6},{8,11},{9,8},{10,9... | collective-permute-start | bytes 12296 | tf_op jit(solution)/shard_map/ppermute | solution.py:475
  69.0 4.0 %collective-permute-start.12 = (f32[8,128]{1,0:T(8,128)S(1)}, f32[8,128]{1,0:T(8,128)S(1)}, u32[]{:S(2)}, u32[]{:S(2)}) collective-permute-start(f32[8,128]{1,0:T(8,128)S(1)} %add.3.refs_2_), channel_id=1, source_target_pairs={{0,2},{1,3},{2,0},{3,1},{4,6},{5,7},{6,4},{7,5},{8,10},{9,11},{10,... | collective-permute-start | bytes 12296 | tf_op jit(solution)/shard_map/ppermute | solution.py:475
  69.3 3.7 %collective-permute-start.11 = (f32[8,128]{1,0:T(8,128)S(1)}, f32[8,128]{1,0:T(8,128)S(1)}, u32[]{:S(2)}, u32[]{:S(2)}) collective-permute-start(f32[8,128]{1,0:T(8,128)S(1)} %add.3.refs_2_), channel_id=1, source_target_pairs={{0,1},{1,2},{2,3},{3,0},{4,5},{5,6},{6,7},{7,4},{8,9},{9,10},{10,1... | collective-permute-start | bytes 12296 | tf_op jit(solution)/shard_map/ppermute | solution.py:475

commit v7 on v6

--- a/solution.py
+++ b/solution.py
@@ -11,7 +11,7 @@
 GROUP = 16
 Z_SIZE = 4
 X_SIZE = 4
-AHEAD = 4
+SLABS = 4
 Y_SIZE = 4
 MIB = 1024 * 1024
 
@@ -35,7 +35,8 @@
     t2 = np.block([[cos2, sin2], [-sin2, cos2]])
     t2_inv = np.block([[cos2, -sin2], [sin2, cos2]])
     t1_inv = np.concatenate([np.cos(first).T, np.sin(first).T], 1) / n
-    return [jnp.asarray(t, jnp.bfloat16) for t in (t1, t2, t2_inv, t1_inv, np.cos(twist), np.sin(twist))]
+    low = [jnp.asarray(t, jnp.bfloat16) for t in (t1, t2, t2_inv, t1_inv)]
+    return (*low, jnp.asarray(np.cos(twist), jnp.float32), jnp.asarray(np.sin(twist), jnp.float32))
 
 
 def place():
@@ -69,7 +70,7 @@
     outs, (f_buf, e_buf, f_sem, e_sem) = rest[:Z_SIZE], rest[Z_SIZE:]
     rows = f_ref.shape[0]
     head, tail = pl.ds(0, EDGE), pl.ds(rows - EDGE, EDGE)
-    pieces = [pl.ds(j * LANE, LANE) for j in range(AHEAD)]
+    pieces = [pl.ds(j * LANE, LANE) for j in range(SLABS)]
     f_copies = [send(f_ref.at[p, :], f_buf.at[p, :], f_sem.at[j]) for j, p in enumerate(pieces)]
     sources = [k_ref.at[head, :], k_ref.at[tail, :], v_ref.at[head, :], v_ref.at[tail, :]]
     e_copies = [send(x, e_buf.at[i], e_sem.at[i]) for i, x in enumerate(sources + [q_ref.at[tail, :]])]
@@ -79,12 +80,12 @@
     for j, p in enumerate(pieces):
         f_copies[j].wait()
         for kz, out_ref in enumerate(outs):
-            turned = f_buf[p, cols[kz]].astype(jnp.float32).T.astype(out_ref.dtype)
+            turned = f_buf[p, cols[kz]].T
             for d in range(X_SIZE * 2):
                 to = (d // 2 - x + X_SIZE) % X_SIZE * 2 + (d % 2 - c + 2) % 2
-                out_ref[to * AHEAD + j] = turned[d * depth : (d + 1) * depth]
+                out_ref[to * SLABS + j] = turned[d * depth : (d + 1) * depth]
     wait_all(e_copies)
-    edge_at = X_SIZE * 2 * AHEAD
+    edge_at = X_SIZE * 2 * SLABS
     q_rows = e_buf[len(sources)].astype(jnp.float32)
     parts = [slice(g * LANE, (g + 1) * LANE) for g in range(q_rows.shape[1] // LANE)]
     q_list = [q_rows[r : r + 1, p] for r in (EDGE - 2, EDGE - 1) for p in parts]
@@ -102,7 +103,7 @@
 def lead(q, k, v, f, groups):
     rows, width = f.shape
     tile = (width // groups, LANE)
-    edge_at = X_SIZE * 2 * AHEAD
+    edge_at = X_SIZE * 2 * SLABS
     return pl.pallas_call(
         lead_kernel,
         in_specs=[HBM] * 4,
@@ -110,9 +111,9 @@
             pltpu.VMEM((edge_at + (2 if kz < 2 else 1), *tile), f.dtype) for kz in range(Z_SIZE)
         ),
         scratch_shapes=[
-            pltpu.VMEM((AHEAD * LANE, width), f.dtype),
+            pltpu.VMEM((SLABS * LANE, width), f.dtype),
             pltpu.VMEM((5, EDGE, width), f.dtype),
-            pltpu.SemaphoreType.DMA((AHEAD,)),
+            pltpu.SemaphoreType.DMA((SLABS,)),
             pltpu.SemaphoreType.DMA((5,)),
         ],
         cost_estimate=cost(10),
@@ -153,8 +154,8 @@
     depth = out_ref.shape[2]
     per = LANE // depth
     for g in range(block.shape[1] // LANE):
-        turned = block[:, g * LANE : (g + 1) * LANE].T
-        out_ref[g * per : (g + 1) * per, j] = turned.reshape(per, depth, LANE).astype(out_ref.dtype)
+        turned = block[:, g * LANE : (g + 1) * LANE].astype(out_ref.dtype).T
+        out_ref[g * per : (g + 1) * per, j] = turned.reshape(per, depth, LANE)
 
 
 def step_x(step, core):
@@ -167,7 +168,7 @@
 
 def pack_kernel(*refs):
     ins, outs, turned = refs[:Z_SIZE], refs[Z_SIZE:-1], refs[-1]
-    last = X_SIZE * 2 * AHEAD
+    last = X_SIZE * 2 * SLABS
     depth = ins[0].shape[1]
     edges = [in_ref[last].astype(jnp.float32) for in_ref in ins]
     zeros = jnp.zeros((LANE - Z_SIZE * depth, LANE), jnp.float32)
@@ -176,11 +177,11 @@
     for d, out_ref in enumerate(outs):
         kx = step_x(d // 2, c)
         for kz, in_ref in enumerate(ins):
-            out_ref[kz * AHEAD : (kz + 1) * AHEAD] = in_ref[pl.ds((kx * 2 + d % 2) * AHEAD, AHEAD)]
+            out_ref[kz * SLABS : (kz + 1) * SLABS] = in_ref[pl.ds((kx * 2 + d % 2) * SLABS, SLABS)]
         at = ((x + kx) % X_SIZE * 2 + (c + d) % 2) * depth
-        out_ref[Z_SIZE * AHEAD] = turned[pl.ds(pl.multiple_of(at, depth), depth), :].astype(out_ref.dtype)
+        out_ref[Z_SIZE * SLABS] = turned[pl.ds(pl.multiple_of(at, depth), depth), :].astype(out_ref.dtype)
         for i in range(query_tiles(d)):
-            out_ref[Z_SIZE * AHEAD + 1 + i] = ins[i][last + 1]
+            out_ref[Z_SIZE * SLABS + 1 + i] = ins[i][last + 1]
 
 
 def pack(parts):
@@ -188,7 +189,7 @@
     return pl.pallas_call(
         pack_kernel,
         out_shape=tuple(
-            jax.ShapeDtypeStruct((Z_SIZE * AHEAD + 1 + query_tiles(d), *tile), dtype) for d in range(X_SIZE * 2)
+            jax.ShapeDtypeStruct((Z_SIZE * SLABS + 1 + query_tiles(d), *tile), dtype) for d in range(X_SIZE * 2)
         ),
         scratch_shapes=[pltpu.VMEM((LANE, LANE), jnp.float32)],
         cost_estimate=cost(20),
@@ -227,7 +228,7 @@
     )
 
 
-def product_kernel(k_ref, v_ref, f_ref, taps_ref, out_ref, k_ext, v_ext, out_buf, sem):
+def product_kernel(k_ref, v_ref, taps_ref, out_ref, k_ext, v_ext, out_buf, sem):
     slabs = k_ref.shape[0] // LANE
     copies = []
 
@@ -235,8 +236,6 @@
         put_turned(out_buf, j, block)
         copies.append(send(out_buf.at[:, j], out_ref.at[:, j], sem.at[j]))
 
-    for j in range(AHEAD, slabs):
-        put(slabs + j - AHEAD, f_ref[j * LANE : (j + 1) * LANE, :].astype(jnp.float32))
     zero = jnp.zeros((8, k_ref.shape[1]), jnp.float32)
     k_ext[0:8, :] = zero
     v_ext[0:8, :] = zero
@@ -250,26 +249,26 @@
     wait_all(copies)
 
 
-def product(k, v, f, taps, groups):
+def product(k, v, taps, groups):
     rows, width = k.shape
     ext = pltpu.VMEM((rows + 8, width), jnp.float32)
-    slabs = rows // LANE * 2 - AHEAD
+    slabs = rows // LANE
     shape = jax.ShapeDtypeStruct((groups, slabs, width // groups, LANE), k.dtype)
     return pl.pallas_call(
         product_kernel,
-        in_specs=[VMEM] * 4,
+        in_specs=[VMEM] * 3,
         out_specs=HBM,
         out_shape=shape,
         scratch_shapes=[ext, ext, pltpu.VMEM(shape.shape, shape.dtype), pltpu.SemaphoreType.DMA((slabs,))],
         cost_estimate=cost(20),
         compiler_params=params(12),
-    )(k, v, f, taps)
+    )(k, v, taps)
 
 
 def gate_kernel(q_ref, core_ref, step_ref, taps_ref, out_ref, q_ext):
     rows, width = q_ref.shape
     z, x, c = place()
-    at = Z_SIZE * AHEAD + 1
+    at = Z_SIZE * SLABS + 1
     tiles = [core_ref[at], step_ref[at], step_ref[at + 1]]
     core, step, round_z = [t.astype(jnp.float32) for t in tiles]
     halo = jnp.where(c == 1, core, jnp.where(x > 0, step, jnp.where(z > 0, round_z, 0.0)))
@@ -325,21 +324,17 @@
     z, x, c = place()
     sources = u_ref.shape[0]
     size = u_wide.shape[0] // sources
-    ahead = AHEAD * depth
     for i in range(sources):
-        both = u_ref[i].astype(jnp.float32).reshape(-1, LANE)
-        u_wide[i * size : (i + 1) * size, :] = both[:size]
-        if ahead < size:
-            f_wide[i * size + ahead : (i + 1) * size, :] = both[size:]
+        u_wide[i * size : (i + 1) * size, :] = u_ref[i].astype(jnp.float32).reshape(size, LANE)
     for d, f_ref in enumerate(f_refs):
         core = (c + d) % 2
         kx = step_x(d // 2, core)
-        edge = f_ref[Z_SIZE * AHEAD].astype(jnp.float32)
+        edge = f_ref[Z_SIZE * SLABS].astype(jnp.float32)
         for kz in range(Z_SIZE):
             src = ((z - kz + Z_SIZE) % Z_SIZE * X_SIZE + (x - kx + X_SIZE) % X_SIZE) * 2 + core
             row = pl.multiple_of(src * size, size)
-            tiles = f_ref[kz * AHEAD : (kz + 1) * AHEAD].reshape(ahead, LANE)
-            f_wide[pl.ds(row, ahead), :] = tiles.astype(jnp.float32)
+            tiles = f_ref[kz * SLABS : (kz + 1) * SLABS].reshape(size, LANE)
+            f_wide[pl.ds(row, size), :] = tiles.astype(jnp.float32)
             row = pl.multiple_of((src + 1) * depth, depth)
             edges[pl.ds(row, depth), :] = pltpu.roll(edge, LANE - kz * depth, 1) if kz else edge
     low = jnp.bfloat16
@@ -352,9 +347,9 @@
         first = mix(t1[...], jnp.concatenate(data, 1))
         turned = []
         for i in range(len(rows)):
-            re, im = part(first[:LANE], i).astype(low), part(first[LANE:], i).astype(low)
+            re, im = part(first[:LANE], i), part(first[LANE:], i)
             c, s = tw_c[...], tw_s[...]
-            turned.append(jnp.concatenate([re * c - im * s, re * s + im * c], 1))
+            turned.append(jnp.concatenate([re * c - im * s, re * s + im * c], 1).astype(low))
         return mix(jnp.concatenate(turned, 0), t2[...])
 
     for start in range(0, depth, GROUP):
@@ -372,9 +367,9 @@
         cols = []
         for i in range(GROUP):
             v = back[i * LANE : (i + 1) * LANE]
-            re, im = v[:, :LANE].astype(low), v[:, LANE:].astype(low)
+            re, im = v[:, :LANE], v[:, LANE:]
             c, s = tw_c[...], tw_s[...]
-            cols.append(jnp.concatenate([re * c + im * s, im * c - re * s], 0))
+            cols.append(jnp.concatenate([re * c + im * s, im * c - re * s], 0).astype(low))
         conv = mix(t1_inv[...], jnp.concatenate(cols, 1))
         for i, r in enumerate(rows):
             y_wide[r, :] = part(conv, i)
@@ -385,7 +380,6 @@
 
 def long_conv(u, f, after, taps, skip):
     sources, slabs, depth, _ = u.shape
-    slabs = (slabs + AHEAD) // 2
     flat = (sources * slabs * depth, LANE)
     wide = pltpu.VMEM(flat, jnp.float32)
     edges = pltpu.VMEM(((sources + 1) * depth, LANE), jnp.float32)
@@ -409,7 +403,7 @@
         squares = jnp.zeros((LANE, LANE), jnp.float32)
         for g in range(groups // per):
             cols = slice(g * LANE, (g + 1) * LANE)
-            y = y_ref[g * per : (g + 1) * per, j].reshape(LANE, LANE).astype(jnp.float32).T
+            y = y_ref[g * per : (g + 1) * per, j].reshape(LANE, LANE).T.astype(jnp.float32)
             gated = (qf_ref[rows, cols].astype(jnp.float32) * y).astype(jnp.bfloat16)
             summed = stream_ref[rows, cols].astype(jnp.float32) + gated.astype(jnp.float32)
             out_ref[rows, cols] = summed.astype(out_ref.dtype)
@@ -481,7 +475,7 @@
     rows, width = queries.shape
     slab = width // groups
     parts = lead(queries, keys, values, filters, groups)
-    u_all = exchange(product(keys, values, filters, short_weights, groups), "seq")
+    u_all = exchange(product(keys, values, short_weights, groups), "seq")
     f_all = spread(parts)
     taps, skip = coefficients(short_weights, skip_gain, slab)
     qf = gate(queries, f_all[1], f_all[7], short_weights)

time: 74.4 us -> 74.3 us (level)
  transfers between devices with their start and end apart: 15 -> 15, of which waited for: 7 -> 8; matrix products, arithmetic and copies ran while one was open for 0% -> 0% of each run, Pallas kernels for 3% -> 3%
where the time goes in v7:
time: 74.3 us; the launch traced here: 74.1 us
  starting transfers between devices  32.4 us (44%)
  blocking collectives  21.6 us (29%)
  waiting for transfers between devices  10.7 us (14%)
  Pallas kernels  8.24 us (11%)
  between operations  1.02 us (1%)
    all_to_all x1, blocking collectives, exchange(): return lax.all_to_all(x, axis, split_axis=0, concat_axis=0, tiled=True)  21.6 us
    ppermute x10, starting transfers between devices, moved(): lax.ppermute(block, 'seq', [(seq_index(*p), seq_index(*target(*p))) for p...  14.5 us
    ppermute x4, starting transfers between devices, across(): return lax.ppermute(block, 'ch', route)  9.43 us
    all_to_all x1, starting transfers between devices, exchange(): return lax.all_to_all(x, axis, split_axis=0, concat_axis=0, tiled=True)  8.48 us
    ppermute x10, waiting for transfers between devices, moved(): lax.ppermute(block, 'seq', [(seq_index(*p), seq_index(*target(*p))) for p...  5.81 us
    ppermute x4, waiting for transfers between devices, across(): return lax.ppermute(block, 'ch', route)  4.23 us
    pallas_call x1, Pallas kernels, long_conv(): pl.pallas_call(conv_kernel, in_specs=[HBM if x is after else VMEM for x i...  2.93 us
    pallas_call x1, Pallas kernels, product(): pl.pallas_call(product_kernel, in_specs=[VMEM] * 3, out_specs=HBM, out_sh...  1.54 us
  transfers between devices with their start and end apart: 15, of which 8 were waited for; matrix products, arithmetic and copies ran while one was open for 0% of the time, Pallas kernels for 3%

profile of v7, /device:TPU:1, one launch (start us, length us, event | category | flops | bytes accessed | tf_op | source)
XLA Modules:
  0.0 74.1 jit_solution(14065508242113300862)
XLA Ops:
  0.7 1.5 %shard_map.150 = (bf16[34,16,128]{2,1,0:T(8,128)(2,1)S(1)}, bf16[34,16,128]{2,1,0:T(8,128)(2,1)S(1)}, bf16[33,16,128]{2,1,0:T(8,128)(2,1)S(1)}, bf16[33,16,128]{2,1,0:T(8,128)(2,1)S(1)}) custom-call(bf16[512,512]{1,0:T(8,128)(2,1)} %q_ref.3, bf16[512,512]{1,0:T(8,128)(2,1)} %k_ref.3, bf16[512,512]{1,0:T(8,128)(2,1)} %v_ref.3, bf16[512,512]{1,0:T(8,128)(2,1)} %f_ref.1), custom_call_target="tpu_custom_call" | custom-call | flops 10000000000 | tf_op jit(solution)/shard_map/pallas_call | solution.py:107
  2.1 3.9 %collective-permute-start.1 = (bf16[33,16,128]{2,1,0:T(8,128)(2,1)S(1)}, bf16[33,16,128]{2,1,0:T(8,128)(2,1)S(1)}, u32[]{:S(2)}, u32[]{:S(2)}) collective-permute-start(bf16[33,16,128]{2,1,0:T(8,128)(2,1)S(1)} %get-tuple-element.21), channel_id=1, source_target_pairs={{0,128},{8,136},{16,144},{24,152},{32,160},{40,168},{48,176},{56,1... | collective-permute-start | bytes 405512 | tf_op jit(solution)/shard_map/ppermute | solution.py:206
  6.0 1.4 %collective-permute-start.2 = (bf16[33,16,128]{2,1,0:T(8,128)(2,1)S(1)}, bf16[33,16,128]{2,1,0:T(8,128)(2,1)S(1)}, u32[]{:S(2)}, u32[]{:S(2)}) collective-permute-start(bf16[33,16,128]{2,1,0:T(8,128)(2,1)S(1)} %get-tuple-element.22), channel_id=1, source_target_pairs={{0,192},{8,200},{16,208},{24,216},{32,224},{40,232},{48,240},{56,2... | collective-permute-start | bytes 405512 | tf_op jit(solution)/shard_map/ppermute | solution.py:206
  7.5 0.2 collective-permute-start
  7.7 1.5 %shard_map.149 = bf16[32,4,16,128]{3,2,1,0:T(8,128)(2,1)} custom-call(bf16[512,512]{1,0:T(8,128)(2,1)S(1)} %copy-done.11, bf16[512,512]{1,0:T(8,128)(2,1)S(1)} %copy-done.12, f32[3,3,512]{2,1,0:T(4,128)S(1)} %copy-done.4), custom_call_target="tpu_custom_call" | custom-call | flops 20000000000 | tf_op jit(solution)/shard_map/pallas_call | solution.py:257
  9.2 8.5 %all-to-all-start = ((bf16[32,4,16,128]{3,2,1,0:T(8,128)(2,1)}), bf16[32,4,16,128]{3,2,1,0:T(8,128)(2,1)S(1)}, u32[]{:S(2)}, u32[]{:S(2)}) async-start(bf16[32,4,16,128]{3,2,1,0:T(8,128)(2,1)} %shard_map.149), calls=%async_computation | async-start | bytes 1048576 | tf_op jit(solution)/shard_map/all_to_all | solution.py:464
  17.7 0.0 collective-permute-done.1.refs_2_
  17.7 0.0 collective-permute-done.2.refs_3_
  17.8 0.0 collective-permute-done.refs_1_
  17.8 0.0 copy-start
  17.8 0.1 shard_map.151
  17.9 1.7 %collective-permute-start.4 = (bf16[19,16,128]{2,1,0:T(8,128)(2,1)S(1)}, bf16[19,16,128]{2,1,0:T(8,128)(2,1)S(1)}, u32[]{:S(2)}, u32[]{:S(2)}) collective-permute-start(bf16[19,16,128]{2,1,0:T(8,128)(2,1)S(1)} %get-tuple-element.24), channel_id=1, source_target_pairs={{0,56},{8,16},{16,8},{24,32},{32,24},{40,48},{48,40},{56,0},{64,12... | collective-permute-start | bytes 233480 | tf_op jit(solution)/shard_map/ppermute | solution.py:206
  19.6 1.4 %collective-permute-start.3 = (bf16[18,16,128]{2,1,0:T(8,128)(2,1)S(1)}, bf16[18,16,128]{2,1,0:T(8,128)(2,1)S(1)}, u32[]{:S(2)}, u32[]{:S(2)}) collective-permute-start(bf16[18,16,128]{2,1,0:T(8,128)(2,1)S(1)} %get-tuple-element.23), channel_id=1, source_target_pairs={{0,8},{8,0},{16,24},{24,16},{32,40},{40,32},{48,56},{56,48},{64,72... | collective-permute-start | bytes 221192 | tf_op jit(solution)/shard_map/ppermute | solution.py:206
  21.0 0.6 collective-permute-start.5
  21.6 2.3 %collective-permute-start.6 = (bf16[17,16,128]{2,1,0:T(8,128)(2,1)S(1)}, bf16[17,16,128]{2,1,0:T(8,128)(2,1)S(1)}, u32[]{:S(2)}, u32[]{:S(2)}) collective-permute-start(bf16[17,16,128]{2,1,0:T(8,128)(2,1)S(1)} %get-tuple-element.29), channel_id=1, source_target_pairs={{0,24},{8,48},{16,40},{24,0},{32,56},{40,16},{48,8},{56,32},{64,88... | collective-permute-start | bytes 208904 | tf_op jit(solution)/shard_map/ppermute | solution.py:206
  23.8 0.3 collective-permute-start.7
  24.2 0.0 collective-permute-done.3.core_ref.rest_1_
  24.2 1.8 %collective-permute-start.8 = (bf16[17,16,128]{2,1,0:T(8,128)(2,1)S(1)}, bf16[17,16,128]{2,1,0:T(8,128)(2,1)S(1)}, u32[]{:S(2)}, u32[]{:S(2)}) collective-permute-start(bf16[17,16,128]{2,1,0:T(8,128)(2,1)S(1)} %get-tuple-element.31), channel_id=1, source_target_pairs={{0,40},{8,32},{16,56},{24,48},{32,8},{40,0},{48,24},{56,16},{64,10... | collective-permute-start | bytes 208904 | tf_op jit(solution)/shard_map/ppermute | solution.py:206
  26.0 0.0 collective-permute-done.4.step_ref.rest_7_
  26.0 0.9 %collective-permute-start.9 = (bf16[17,16,128]{2,1,0:T(8,128)(2,1)S(1)}, bf16[17,16,128]{2,1,0:T(8,128)(2,1)S(1)}, u32[]{:S(2)}, u32[]{:S(2)}) collective-permute-start(bf16[17,16,128]{2,1,0:T(8,128)(2,1)S(1)} %get-tuple-element.32), channel_id=1, source_target_pairs={{0,48},{8,24},{16,0},{24,40},{32,16},{40,56},{48,32},{56,8},{64,11... | collective-permute-start | bytes 208904 | tf_op jit(solution)/shard_map/ppermute | solution.py:206
  26.9 0.1 shard_map.153
  27.0 0.0 copy-start.2
  27.0 0.0 copy-start.3
  27.0 0.0 copy-start.5
  27.0 0.0 copy-start.6
  27.1 0.0 copy-start.7
  27.1 0.0 copy-start.8
  27.1 0.6 shard_map.152.after_ref.qf_ref
  27.6 0.0 collective-permute-done.5.rest_2_
  27.7 0.3 collective-permute-done.6.rest_3_
  27.9 2.1 %collective-permute-done.7.rest_4_ = bf16[17,16,128]{2,1,0:T(8,128)(2,1)S(1)} collective-permute-done((bf16[17,16,128]{2,1,0:T(8,128)(2,1)S(1)}, bf16[17,16,128]{2,1,0:T(8,128)(2,1)S(1)}, u32[]{:S(2)}, u32[]{:S(2)}) %collective-permute-start.7) | collective-permute-done | bytes 69664 | tf_op jit(solution)/shard_map/ppermute | solution.py:206
  30.1 2.4 %collective-permute-done.8.rest_5_ = bf16[17,16,128]{2,1,0:T(8,128)(2,1)S(1)} collective-permute-done((bf16[17,16,128]{2,1,0:T(8,128)(2,1)S(1)}, bf16[17,16,128]{2,1,0:T(8,128)(2,1)S(1)}, u32[]{:S(2)}, u32[]{:S(2)}) %collective-permute-start.8) | collective-permute-done | bytes 69664 | tf_op jit(solution)/shard_map/ppermute | solution.py:206
  32.5 0.9 %collective-permute-done.9.rest_6_ = bf16[17,16,128]{2,1,0:T(8,128)(2,1)S(1)} collective-permute-done((bf16[17,16,128]{2,1,0:T(8,128)(2,1)S(1)}, bf16[17,16,128]{2,1,0:T(8,128)(2,1)S(1)}, u32[]{:S(2)}, u32[]{:S(2)}) %collective-permute-start.9) | collective-permute-done | bytes 69664 | tf_op jit(solution)/shard_map/ppermute | solution.py:206
  33.5 0.7 all-to-all-done.u_ref
  34.2 0.0 copy-start.9
  34.2 2.9 %shard_map.154 = bf16[2048,128]{1,0:T(8,128)(2,1)S(1)} custom-call(bf16[32,4,16,128]{3,2,1,0:T(8,128)(2,1)S(1)} %all-to-all-done.u_ref, bf16[512,512]{1,0:T(8,128)(2,1)S(1)} %shard_map.152.after_ref.qf_ref, f32[16,128]{1,0:T(8,128)S(1)} %get-tuple-element.25.taps_ref, f32[16,128]{1,0:T(8,128)S(1)} %get-tuple-element.26.skip_ref, ...), custom_call_target="tpu_custom_call" | custom-call | tf_op jit(solution)/shard_map/pallas_call | solution.py:387
  37.1 0.0 copy-start.1
  37.1 21.6 %all_to_all.10.y_ref = bf16[32,4,16,128]{3,2,1,0:T(8,128)(2,1)S(1)} all-to-all(bf16[32,4,16,128]{3,2,1,0:T(8,128)(2,1)S(1)} %bitcast.3), channel_id=1, replica_groups=mesh['seq'=32,'ch'=8] {'seq'}, dimensions={0} | all-to-all | bytes 1048576 | tf_op jit(solution)/shard_map/all_to_all | solution.py:464
  58.7 0.5 shard_map.155
  59.2 5.7 %collective-permute-start.10 = (f32[8,128]{1,0:T(8,128)S(1)}, f32[8,128]{1,0:T(8,128)S(1)}, u32[]{:S(2)}, u32[]{:S(2)}) collective-permute-start(f32[8,128]{1,0:T(8,128)S(1)} %get-tuple-element.35), channel_id=1, source_target_pairs={{0,4},{1,5},{2,6},{3,7},{4,0},{5,1},{6,2},{7,3},{8,12},{9,13},{10,... | collective-permute-start | bytes 12296 | tf_op jit(solution)/shard_map/ppermute | solution.py:469
  64.9 1.3 %collective-permute-done.10 = f32[8,128]{1,0:T(8,128)S(1)} collective-permute-done((f32[8,128]{1,0:T(8,128)S(1)}, f32[8,128]{1,0:T(8,128)S(1)}, u32[]{:S(2)}, u32[]{:S(2)}) %collective-permute-start.10) | collective-permute-done | bytes 4128 | tf_op jit(solution)/shard_map/ppermute | solution.py:469
  66.2 2.7 %collective-permute-start.13 = (f32[8,128]{1,0:T(8,128)S(1)}, f32[8,128]{1,0:T(8,128)S(1)}, u32[]{:S(2)}, u32[]{:S(2)}) collective-permute-start(f32[8,128]{1,0:T(8,128)S(1)} %add.3.refs_2_), channel_id=1, source_target_pairs={{0,3},{1,0},{2,1},{3,2},{4,7},{5,4},{6,5},{7,6},{8,11},{9,8},{10,9... | collective-permute-start | bytes 12296 | tf_op jit(solution)/shard_map/ppermute | solution.py:469
  68.9 0.4 collective-permute-start.12
  69.2 0.7 collective-permute-start.11
  69.9 0.0 collective-permute-done.13.refs_5_
  69.9 2.9 %collective-permute-done.12.refs_4_ = f32[8,128]{1,0:T(8,128)S(1)} collective-permute-done((f32[8,128]{1,0:T(8,128)S(1)}, f32[8,128]{1,0:T(8,128)S(1)}, u32[]{:S(2)}, u32[]{:S(2)}) %collective-permute-start.12) | collective-permute-done | bytes 4128 | tf_op jit(solution)/shard_map/ppermute | solution.py:469
  72.9 0.1 collective-permute-done.11.refs_3_
  72.9 1.0 %shard_map.156 = (bf16[512,512]{1,0:T(8,128)(2,1)}, bf16[512,512]{1,0:T(8,128)(2,1)}) custom-call(bf16[512,512]{1,0:T(8,128)(2,1)S(1)} %get-tuple-element.33.refs_0_, f32[512,512]{1,0:T(8,128)S(1)} %get-tuple-element.34.refs_1_, f32[8,128]{1,0:T(8,128)S(1)} %add.3.refs_2_, f32[8,128]{1,0:T(8,128)S(1)} %collective-permute-done.11.refs_3_, ...), custom_call_target="tpu_custom_call" | custom-call | tf_op jit(solution)/shard_map/pallas_call | solution.py:449
  (18 shorter events, 0.0 us)
Async XLA Ops:
  0.6 7.1 %copy-start.12 = (bf16[512,512]{1,0:T(8,128)(2,1)S(1)}, bf16[512,512]{1,0:T(8,128)(2,1)}, u32[]{:S(2)}) copy-start(bf16[512,512]{1,0:T(8,128)(2,1)} %v_ref.3) | copy-start | bytes 1572868
  0.6 7.1 %copy-start.11 = (bf16[512,512]{1,0:T(8,128)(2,1)S(1)}, bf16[512,512]{1,0:T(8,128)(2,1)}, u32[]{:S(2)}) copy-start(bf16[512,512]{1,0:T(8,128)(2,1)} %k_ref.3) | copy-start | bytes 1572868
  0.7 7.0 %copy-start.4 = (f32[3,3,512]{2,1,0:T(4,128)S(1)}, f32[3,3,512]{2,1,0:T(4,128)}, u32[]{:S(2)}) copy-start(f32[3,3,512]{2,1,0:T(4,128)} %taps_ref.5) | copy-start | bytes 55300
  2.1 15.6 %collective-permute-start.1 = (bf16[33,16,128]{2,1,0:T(8,128)(2,1)S(1)}, bf16[33,16,128]{2,1,0:T(8,128)(2,1)S(1)}, u32[]{:S(2)}, u32[]{:S(2)}) collective-permute-start(bf16[33,16,128]{2,1,0:T(8,128)(2,1)S(1)} %get-tuple-element.21), channel_id=1, source_target_pairs={{0,128},{8,136},{16,144},{24,152},{32,160},{40,168},{48,176},{56,1... | collective-permute-start | bytes 405512 | tf_op jit(solution)/shard_map/ppermute | solution.py:206
  6.0 11.7 %collective-permute-start.2 = (bf16[33,16,128]{2,1,0:T(8,128)(2,1)S(1)}, bf16[33,16,128]{2,1,0:T(8,128)(2,1)S(1)}, u32[]{:S(2)}, u32[]{:S(2)}) collective-permute-start(bf16[33,16,128]{2,1,0:T(8,128)(2,1)S(1)} %get-tuple-element.22), channel_id=1, source_target_pairs={{0,192},{8,200},{16,208},{24,216},{32,224},{40,232},{48,240},{56,2... | collective-permute-start | bytes 405512 | tf_op jit(solution)/shard_map/ppermute | solution.py:206
  7.5 10.3 %collective-permute-start = (bf16[34,16,128]{2,1,0:T(8,128)(2,1)S(1)}, bf16[34,16,128]{2,1,0:T(8,128)(2,1)S(1)}, u32[]{:S(2)}, u32[]{:S(2)}) collective-permute-start(bf16[34,16,128]{2,1,0:T(8,128)(2,1)S(1)} %get-tuple-element.20), channel_id=1, source_target_pairs={{0,64},{8,72},{16,80},{24,88},{32,96},{40,104},{48,112},{56,120},{... | collective-permute-start | bytes 417800 | tf_op jit(solution)/shard_map/ppermute | solution.py:206
  9.2 24.9 %all-to-all-start = ((bf16[32,4,16,128]{3,2,1,0:T(8,128)(2,1)}), bf16[32,4,16,128]{3,2,1,0:T(8,128)(2,1)S(1)}, u32[]{:S(2)}, u32[]{:S(2)}) async-start(bf16[32,4,16,128]{3,2,1,0:T(8,128)(2,1)} %shard_map.149), calls=%async_computation | async-start | bytes 1048576 | tf_op jit(solution)/shard_map/all_to_all | solution.py:464
  17.8 9.2 %copy-start = (bf16[512,512]{1,0:T(8,128)(2,1)S(1)}, bf16[512,512]{1,0:T(8,128)(2,1)}, u32[]{:S(2)}) copy-start(bf16[512,512]{1,0:T(8,128)(2,1)} %q_ref.3) | copy-start | bytes 1572868
  17.9 8.1 %collective-permute-start.4 = (bf16[19,16,128]{2,1,0:T(8,128)(2,1)S(1)}, bf16[19,16,128]{2,1,0:T(8,128)(2,1)S(1)}, u32[]{:S(2)}, u32[]{:S(2)}) collective-permute-start(bf16[19,16,128]{2,1,0:T(8,128)(2,1)S(1)} %get-tuple-element.24), channel_id=1, source_target_pairs={{0,56},{8,16},{16,8},{24,32},{32,24},{40,48},{48,40},{56,0},{64,12... | collective-permute-start | bytes 233480 | tf_op jit(solution)/shard_map/ppermute | solution.py:206
  19.6 4.5 %collective-permute-start.3 = (bf16[18,16,128]{2,1,0:T(8,128)(2,1)S(1)}, bf16[18,16,128]{2,1,0:T(8,128)(2,1)S(1)}, u32[]{:S(2)}, u32[]{:S(2)}) collective-permute-start(bf16[18,16,128]{2,1,0:T(8,128)(2,1)S(1)} %get-tuple-element.23), channel_id=1, source_target_pairs={{0,8},{8,0},{16,24},{24,16},{32,40},{40,32},{48,56},{56,48},{64,72... | collective-permute-start | bytes 221192 | tf_op jit(solution)/shard_map/ppermute | solution.py:206
  21.0 6.7 %collective-permute-start.5 = (bf16[17,16,128]{2,1,0:T(8,128)(2,1)S(1)}, bf16[17,16,128]{2,1,0:T(8,128)(2,1)S(1)}, u32[]{:S(2)}, u32[]{:S(2)}) collective-permute-start(bf16[17,16,128]{2,1,0:T(8,128)(2,1)S(1)} %get-tuple-element.28), channel_id=1, source_target_pairs={{0,16},{8,56},{16,32},{24,8},{32,48},{40,24},{48,0},{56,40},{64,80... | collective-permute-start | bytes 208904 | tf_op jit(solution)/shard_map/ppermute | solution.py:206
  21.6 6.4 %collective-permute-start.6 = (bf16[17,16,128]{2,1,0:T(8,128)(2,1)S(1)}, bf16[17,16,128]{2,1,0:T(8,128)(2,1)S(1)}, u32[]{:S(2)}, u32[]{:S(2)}) collective-permute-start(bf16[17,16,128]{2,1,0:T(8,128)(2,1)S(1)} %get-tuple-element.29), channel_id=1, source_target_pairs={{0,24},{8,48},{16,40},{24,0},{32,56},{40,16},{48,8},{56,32},{64,88... | collective-permute-start | bytes 208904 | tf_op jit(solution)/shard_map/ppermute | solution.py:206
  23.8 6.3 %collective-permute-start.7 = (bf16[17,16,128]{2,1,0:T(8,128)(2,1)S(1)}, bf16[17,16,128]{2,1,0:T(8,128)(2,1)S(1)}, u32[]{:S(2)}, u32[]{:S(2)}) collective-permute-start(bf16[17,16,128]{2,1,0:T(8,128)(2,1)S(1)} %get-tuple-element.30), channel_id=1, source_target_pairs={{0,32},{8,40},{16,48},{24,56},{32,0},{40,8},{48,16},{56,24},{64,96... | collective-permute-start | bytes 208904 | tf_op jit(solution)/shard_map/ppermute | solution.py:206
  24.2 2.7 %copy-start.10 = (f32[512]{0:T(512)S(1)}, f32[512]{0:T(512)}, u32[]{:S(2)}) copy-start(f32[512]{0:T(512)} %param.19) | copy-start | bytes 6148
  24.2 8.4 %collective-permute-start.8 = (bf16[17,16,128]{2,1,0:T(8,128)(2,1)S(1)}, bf16[17,16,128]{2,1,0:T(8,128)(2,1)S(1)}, u32[]{:S(2)}, u32[]{:S(2)}) collective-permute-start(bf16[17,16,128]{2,1,0:T(8,128)(2,1)S(1)} %get-tuple-element.31), channel_id=1, source_target_pairs={{0,40},{8,32},{16,56},{24,48},{32,8},{40,0},{48,24},{56,16},{64,10... | collective-permute-start | bytes 208904 | tf_op jit(solution)/shard_map/ppermute | solution.py:206
  26.0 7.5 %collective-permute-start.9 = (bf16[17,16,128]{2,1,0:T(8,128)(2,1)S(1)}, bf16[17,16,128]{2,1,0:T(8,128)(2,1)S(1)}, u32[]{:S(2)}, u32[]{:S(2)}) collective-permute-start(bf16[17,16,128]{2,1,0:T(8,128)(2,1)S(1)} %get-tuple-element.32), channel_id=1, source_target_pairs={{0,48},{8,24},{16,0},{24,40},{32,16},{40,56},{48,32},{56,8},{64,11... | collective-permute-start | bytes 208904 | tf_op jit(solution)/shard_map/ppermute | solution.py:206
  27.0 7.1 %copy-start.2 = (bf16[256,256]{1,0:T(8,128)(2,1)S(1)}, bf16[256,256]{1,0:T(8,128)(2,1)}, u32[]{:S(2)}) copy-start(bf16[256,256]{1,0:T(8,128)(2,1)} %constant.14.clone.t2_inv) | copy-start | bytes 393220
  27.0 7.1 %copy-start.3 = (bf16[256,256]{1,0:T(8,128)(2,1)S(1)}, bf16[256,256]{1,0:T(8,128)(2,1)}, u32[]{:S(2)}) copy-start(bf16[256,256]{1,0:T(8,128)(2,1)} %constant.13.clone.t2) | copy-start | bytes 393220
  27.0 7.1 %copy-start.5 = (f32[128,128]{1,0:T(8,128)S(1)}, f32[128,128]{1,0:T(8,128)}, u32[]{:S(2)}) copy-start(f32[128,128]{1,0:T(8,128)} %constant.17.clone.tw_s) | copy-start | bytes 196612
  27.0 7.1 %copy-start.6 = (f32[128,128]{1,0:T(8,128)S(1)}, f32[128,128]{1,0:T(8,128)}, u32[]{:S(2)}) copy-start(f32[128,128]{1,0:T(8,128)} %constant.16.clone.tw_c) | copy-start | bytes 196612
  27.1 7.1 %copy-start.7 = (bf16[128,256]{1,0:T(8,128)(2,1)S(1)}, bf16[128,256]{1,0:T(8,128)(2,1)}, u32[]{:S(2)}) copy-start(bf16[128,256]{1,0:T(8,128)(2,1)} %constant.15.clone.t1_inv) | copy-start | bytes 196612
  27.1 7.1 %copy-start.8 = (bf16[256,128]{1,0:T(8,128)(2,1)S(1)}, bf16[256,128]{1,0:T(8,128)(2,1)}, u32[]{:S(2)}) copy-start(bf16[256,128]{1,0:T(8,128)(2,1)} %constant.12.clone.t1) | copy-start | bytes 196612
  34.2 24.5 %copy-start.9 = (f32[512]{0:T(512)S(1)}, f32[512]{0:T(512)}, u32[]{:S(2)}) copy-start(f32[512]{0:T(512)} %param.21) | copy-start | bytes 6148
  37.1 21.6 %copy-start.1 = (bf16[512,512]{1,0:T(8,128)(2,1)S(1)}, bf16[512,512]{1,0:T(8,128)(2,1)}, u32[]{:S(2)}) copy-start(bf16[512,512]{1,0:T(8,128)(2,1)} %stream_ref.1) | copy-start | bytes 1572868
  59.2 6.9 %collective-permute-start.10 = (f32[8,128]{1,0:T(8,128)S(1)}, f32[8,128]{1,0:T(8,128)S(1)}, u32[]{:S(2)}, u32[]{:S(2)}) collective-permute-start(f32[8,128]{1,0:T(8,128)S(1)} %get-tuple-element.35), channel_id=1, source_target_pairs={{0,4},{1,5},{2,6},{3,7},{4,0},{5,1},{6,2},{7,3},{8,12},{9,13},{10,... | collective-permute-start | bytes 12296 | tf_op jit(solution)/shard_map/ppermute | solution.py:469
  66.2 3.8 %collective-permute-start.13 = (f32[8,128]{1,0:T(8,128)S(1)}, f32[8,128]{1,0:T(8,128)S(1)}, u32[]{:S(2)}, u32[]{:S(2)}) collective-permute-start(f32[8,128]{1,0:T(8,128)S(1)} %add.3.refs_2_), channel_id=1, source_target_pairs={{0,3},{1,0},{2,1},{3,2},{4,7},{5,4},{6,5},{7,6},{8,11},{9,8},{10,9... | collective-permute-start | bytes 12296 | tf_op jit(solution)/shard_map/ppermute | solution.py:469
  68.9 4.0 %collective-permute-start.12 = (f32[8,128]{1,0:T(8,128)S(1)}, f32[8,128]{1,0:T(8,128)S(1)}, u32[]{:S(2)}, u32[]{:S(2)}) collective-permute-start(f32[8,128]{1,0:T(8,128)S(1)} %add.3.refs_2_), channel_id=1, source_target_pairs={{0,2},{1,3},{2,0},{3,1},{4,6},{5,7},{6,4},{7,5},{8,10},{9,11},{10,... | collective-permute-start | bytes 12296 | tf_op jit(solution)/shard_map/ppermute | solution.py:469
  69.2 3.7 %collective-permute-start.11 = (f32[8,128]{1,0:T(8,128)S(1)}, f32[8,128]{1,0:T(8,128)S(1)}, u32[]{:S(2)}, u32[]{:S(2)}) collective-permute-start(f32[8,128]{1,0:T(8,128)S(1)} %add.3.refs_2_), channel_id=1, source_target_pairs={{0,1},{1,2},{2,3},{3,0},{4,5},{5,6},{6,7},{7,4},{8,9},{9,10},{10,1... | collective-permute-start | bytes 12296 | tf_op jit(solution)/shard_map/ppermute | solution.py:469

commit v8 on v7

--- a/solution.py
+++ b/solution.py
@@ -163,7 +163,7 @@
 
 
 def query_tiles(d):
-    return {1: 1, 7: 2}.get(d, 0)
+    return {1: 1, 7: 2, 4: 0, 5: 0}.get(d, 1)
 
 
 def pack_kernel(*refs):

time: 74.3 us -> 74 us (level)
  starting transfers between devices: 32.4 us -> 33.2 us
  waiting for transfers between devices: 10.7 us -> 9.93 us
    ppermute x10, waiting for transfers between devices: 5.81 us -> 5 us  [moved(): lax.ppermute(block, 'seq', [(seq_index(*p), seq_index(*target(*p))) for p...]
    ppermute x10, starting transfers between devices: 14.5 us -> 15.3 us  [moved(): lax.ppermute(block, 'seq', [(seq_index(*p), seq_index(*target(*p))) for p...]
  transfers between devices with their start and end apart: 15 -> 15, of which waited for: 8 -> 7; matrix products, arithmetic and copies ran while one was open for 0% -> 0% of each run, Pallas kernels for 3% -> 3%
where the time goes in v8:
time: 74 us; the launch traced here: 73.8 us
  starting transfers between devices  33.2 us (45%)
  blocking collectives  21.3 us (29%)
  waiting for transfers between devices  9.93 us (13%)
  Pallas kernels  8.24 us (11%)
  between operations  1.02 us (1%)
    all_to_all x1, blocking collectives, exchange(): return lax.all_to_all(x, axis, split_axis=0, concat_axis=0, tiled=True)  21.3 us
    ppermute x10, starting transfers between devices, moved(): lax.ppermute(block, 'seq', [(seq_index(*p), seq_index(*target(*p))) for p...  15.3 us
    ppermute x4, starting transfers between devices, across(): return lax.ppermute(block, 'ch', route)  9.44 us
    all_to_all x1, starting transfers between devices, exchange(): return lax.all_to_all(x, axis, split_axis=0, concat_axis=0, tiled=True)  8.48 us
    ppermute x10, waiting for transfers between devices, moved(): lax.ppermute(block, 'seq', [(seq_index(*p), seq_index(*target(*p))) for p...  5 us
    ppermute x4, waiting for transfers between devices, across(): return lax.ppermute(block, 'ch', route)  4.23 us
    pallas_call x1, Pallas kernels, long_conv(): pl.pallas_call(conv_kernel, in_specs=[HBM if x is after else VMEM for x i...  2.93 us
    pallas_call x1, Pallas kernels, product(): pl.pallas_call(product_kernel, in_specs=[VMEM] * 3, out_specs=HBM, out_sh...  1.54 us
  transfers between devices with their start and end apart: 15, of which 7 were waited for; matrix products, arithmetic and copies ran while one was open for 0% of the time, Pallas kernels for 3%

profile of v8, /device:TPU:1, one launch (start us, length us, event | category | flops | bytes accessed | tf_op | source)
XLA Modules:
  0.0 73.8 jit_solution(16842859611610750004)
XLA Ops:
  0.7 1.5 %shard_map.150 = (bf16[34,16,128]{2,1,0:T(8,128)(2,1)S(1)}, bf16[34,16,128]{2,1,0:T(8,128)(2,1)S(1)}, bf16[33,16,128]{2,1,0:T(8,128)(2,1)S(1)}, bf16[33,16,128]{2,1,0:T(8,128)(2,1)S(1)}) custom-call(bf16[512,512]{1,0:T(8,128)(2,1)} %q_ref.3, bf16[512,512]{1,0:T(8,128)(2,1)} %k_ref.3, bf16[512,512]{1,0:T(8,128)(2,1)} %v_ref.3, bf16[512,512]{1,0:T(8,128)(2,1)} %f_ref.1), custom_call_target="tpu_custom_call" | custom-call | flops 10000000000 | tf_op jit(solution)/shard_map/pallas_call | solution.py:107
  2.1 3.9 %collective-permute-start.1 = (bf16[33,16,128]{2,1,0:T(8,128)(2,1)S(1)}, bf16[33,16,128]{2,1,0:T(8,128)(2,1)S(1)}, u32[]{:S(2)}, u32[]{:S(2)}) collective-permute-start(bf16[33,16,128]{2,1,0:T(8,128)(2,1)S(1)} %get-tuple-element.21), channel_id=1, source_target_pairs={{0,128},{8,136},{16,144},{24,152},{32,160},{40,168},{48,176},{56,1... | collective-permute-start | bytes 405512 | tf_op jit(solution)/shard_map/ppermute | solution.py:206
  6.0 1.4 %collective-permute-start.2 = (bf16[33,16,128]{2,1,0:T(8,128)(2,1)S(1)}, bf16[33,16,128]{2,1,0:T(8,128)(2,1)S(1)}, u32[]{:S(2)}, u32[]{:S(2)}) collective-permute-start(bf16[33,16,128]{2,1,0:T(8,128)(2,1)S(1)} %get-tuple-element.22), channel_id=1, source_target_pairs={{0,192},{8,200},{16,208},{24,216},{32,224},{40,232},{48,240},{56,2... | collective-permute-start | bytes 405512 | tf_op jit(solution)/shard_map/ppermute | solution.py:206
  7.5 0.2 collective-permute-start
  7.7 1.5 %shard_map.149 = bf16[32,4,16,128]{3,2,1,0:T(8,128)(2,1)} custom-call(bf16[512,512]{1,0:T(8,128)(2,1)S(1)} %copy-done.11, bf16[512,512]{1,0:T(8,128)(2,1)S(1)} %copy-done.12, f32[3,3,512]{2,1,0:T(4,128)S(1)} %copy-done.4), custom_call_target="tpu_custom_call" | custom-call | flops 20000000000 | tf_op jit(solution)/shard_map/pallas_call | solution.py:257
  9.2 8.5 %all-to-all-start = ((bf16[32,4,16,128]{3,2,1,0:T(8,128)(2,1)}), bf16[32,4,16,128]{3,2,1,0:T(8,128)(2,1)S(1)}, u32[]{:S(2)}, u32[]{:S(2)}) async-start(bf16[32,4,16,128]{3,2,1,0:T(8,128)(2,1)} %shard_map.149), calls=%async_computation | async-start | bytes 1048576 | tf_op jit(solution)/shard_map/all_to_all | solution.py:464
  17.7 0.0 collective-permute-done.1.refs_2_
  17.7 0.0 collective-permute-done.2.refs_3_
  17.8 0.0 collective-permute-done.refs_1_
  17.8 0.0 copy-start
  17.8 0.1 shard_map.151
  17.9 1.7 %collective-permute-start.4 = (bf16[19,16,128]{2,1,0:T(8,128)(2,1)S(1)}, bf16[19,16,128]{2,1,0:T(8,128)(2,1)S(1)}, u32[]{:S(2)}, u32[]{:S(2)}) collective-permute-start(bf16[19,16,128]{2,1,0:T(8,128)(2,1)S(1)} %get-tuple-element.24), channel_id=1, source_target_pairs={{0,56},{8,16},{16,8},{24,32},{32,24},{40,48},{48,40},{56,0},{64,12... | collective-permute-start | bytes 233480 | tf_op jit(solution)/shard_map/ppermute | solution.py:206
  19.6 1.4 %collective-permute-start.3 = (bf16[18,16,128]{2,1,0:T(8,128)(2,1)S(1)}, bf16[18,16,128]{2,1,0:T(8,128)(2,1)S(1)}, u32[]{:S(2)}, u32[]{:S(2)}) collective-permute-start(bf16[18,16,128]{2,1,0:T(8,128)(2,1)S(1)} %get-tuple-element.23), channel_id=1, source_target_pairs={{0,8},{8,0},{16,24},{24,16},{32,40},{40,32},{48,56},{56,48},{64,72... | collective-permute-start | bytes 221192 | tf_op jit(solution)/shard_map/ppermute | solution.py:206
  21.0 0.6 collective-permute-start.5
  21.6 2.3 %collective-permute-start.6 = (bf16[18,16,128]{2,1,0:T(8,128)(2,1)S(1)}, bf16[18,16,128]{2,1,0:T(8,128)(2,1)S(1)}, u32[]{:S(2)}, u32[]{:S(2)}) collective-permute-start(bf16[18,16,128]{2,1,0:T(8,128)(2,1)S(1)} %get-tuple-element.29), channel_id=1, source_target_pairs={{0,24},{8,48},{16,40},{24,0},{32,56},{40,16},{48,8},{56,32},{64,88... | collective-permute-start | bytes 221192 | tf_op jit(solution)/shard_map/ppermute | solution.py:206
  23.8 0.0 collective-permute-start.9
  23.8 0.0 collective-permute-done.3.core_ref.rest_1_
  23.8 0.5 collective-permute-start.7
  24.4 0.4 collective-permute-done.4.step_ref.rest_7_
  24.7 3.3 %collective-permute-start.8 = (bf16[17,16,128]{2,1,0:T(8,128)(2,1)S(1)}, bf16[17,16,128]{2,1,0:T(8,128)(2,1)S(1)}, u32[]{:S(2)}, u32[]{:S(2)}) collective-permute-start(bf16[17,16,128]{2,1,0:T(8,128)(2,1)S(1)} %get-tuple-element.31), channel_id=1, source_target_pairs={{0,40},{8,32},{16,56},{24,48},{32,8},{40,0},{48,24},{56,16},{64,10... | collective-permute-start | bytes 208904 | tf_op jit(solution)/shard_map/ppermute | solution.py:206
  28.1 0.1 shard_map.153
  28.2 0.0 copy-start.2
  28.2 0.0 copy-start.3
  28.2 0.0 copy-start.5
  28.2 0.0 copy-start.6
  28.2 0.0 copy-start.7
  28.2 0.0 copy-start.8
  28.3 0.6 shard_map.152.after_ref.qf_ref
  28.8 2.4 %collective-permute-done.7.rest_4_ = bf16[17,16,128]{2,1,0:T(8,128)(2,1)S(1)} collective-permute-done((bf16[17,16,128]{2,1,0:T(8,128)(2,1)S(1)}, bf16[17,16,128]{2,1,0:T(8,128)(2,1)S(1)}, u32[]{:S(2)}, u32[]{:S(2)}) %collective-permute-start.7) | collective-permute-done | bytes 69664 | tf_op jit(solution)/shard_map/ppermute | solution.py:206
  31.2 2.2 %collective-permute-done.8.rest_5_ = bf16[17,16,128]{2,1,0:T(8,128)(2,1)S(1)} collective-permute-done((bf16[17,16,128]{2,1,0:T(8,128)(2,1)S(1)}, bf16[17,16,128]{2,1,0:T(8,128)(2,1)S(1)}, u32[]{:S(2)}, u32[]{:S(2)}) %collective-permute-start.8) | collective-permute-done | bytes 69664 | tf_op jit(solution)/shard_map/ppermute | solution.py:206
  33.4 0.0 collective-permute-done.5.rest_2_
  33.4 0.0 collective-permute-done.6.rest_3_
  33.4 0.0 collective-permute-done.9.rest_6_
  33.4 0.7 all-to-all-done.u_ref
  34.2 0.0 copy-start.9
  34.2 2.9 %shard_map.154 = bf16[2048,128]{1,0:T(8,128)(2,1)S(1)} custom-call(bf16[32,4,16,128]{3,2,1,0:T(8,128)(2,1)S(1)} %all-to-all-done.u_ref, bf16[512,512]{1,0:T(8,128)(2,1)S(1)} %shard_map.152.after_ref.qf_ref, f32[16,128]{1,0:T(8,128)S(1)} %get-tuple-element.25.taps_ref, f32[16,128]{1,0:T(8,128)S(1)} %get-tuple-element.26.skip_ref, ...), custom_call_target="tpu_custom_call" | custom-call | tf_op jit(solution)/shard_map/pallas_call | solution.py:387
  37.1 0.0 copy-start.1
  37.1 21.3 %all_to_all.10.y_ref = bf16[32,4,16,128]{3,2,1,0:T(8,128)(2,1)S(1)} all-to-all(bf16[32,4,16,128]{3,2,1,0:T(8,128)(2,1)S(1)} %bitcast.3), channel_id=1, replica_groups=mesh['seq'=32,'ch'=8] {'seq'}, dimensions={0} | all-to-all | bytes 1048576 | tf_op jit(solution)/shard_map/all_to_all | solution.py:464
  58.4 0.5 shard_map.155
  58.9 5.7 %collective-permute-start.10 = (f32[8,128]{1,0:T(8,128)S(1)}, f32[8,128]{1,0:T(8,128)S(1)}, u32[]{:S(2)}, u32[]{:S(2)}) collective-permute-start(f32[8,128]{1,0:T(8,128)S(1)} %get-tuple-element.35), channel_id=1, source_target_pairs={{0,4},{1,5},{2,6},{3,7},{4,0},{5,1},{6,2},{7,3},{8,12},{9,13},{10,... | collective-permute-start | bytes 12296 | tf_op jit(solution)/shard_map/ppermute | solution.py:469
  64.6 1.3 %collective-permute-done.10 = f32[8,128]{1,0:T(8,128)S(1)} collective-permute-done((f32[8,128]{1,0:T(8,128)S(1)}, f32[8,128]{1,0:T(8,128)S(1)}, u32[]{:S(2)}, u32[]{:S(2)}) %collective-permute-start.10) | collective-permute-done | bytes 4128 | tf_op jit(solution)/shard_map/ppermute | solution.py:469
  65.9 2.7 %collective-permute-start.13 = (f32[8,128]{1,0:T(8,128)S(1)}, f32[8,128]{1,0:T(8,128)S(1)}, u32[]{:S(2)}, u32[]{:S(2)}) collective-permute-start(f32[8,128]{1,0:T(8,128)S(1)} %add.3.refs_2_), channel_id=1, source_target_pairs={{0,3},{1,0},{2,1},{3,2},{4,7},{5,4},{6,5},{7,6},{8,11},{9,8},{10,9... | collective-permute-start | bytes 12296 | tf_op jit(solution)/shard_map/ppermute | solution.py:469
  68.6 0.3 collective-permute-start.12
  68.9 0.7 collective-permute-start.11
  69.6 0.0 collective-permute-done.13.refs_5_
  69.6 2.9 %collective-permute-done.12.refs_4_ = f32[8,128]{1,0:T(8,128)S(1)} collective-permute-done((f32[8,128]{1,0:T(8,128)S(1)}, f32[8,128]{1,0:T(8,128)S(1)}, u32[]{:S(2)}, u32[]{:S(2)}) %collective-permute-start.12) | collective-permute-done | bytes 4128 | tf_op jit(solution)/shard_map/ppermute | solution.py:469
  72.6 0.1 collective-permute-done.11.refs_3_
  72.6 1.0 %shard_map.156 = (bf16[512,512]{1,0:T(8,128)(2,1)}, bf16[512,512]{1,0:T(8,128)(2,1)}) custom-call(bf16[512,512]{1,0:T(8,128)(2,1)S(1)} %get-tuple-element.33.refs_0_, f32[512,512]{1,0:T(8,128)S(1)} %get-tuple-element.34.refs_1_, f32[8,128]{1,0:T(8,128)S(1)} %add.3.refs_2_, f32[8,128]{1,0:T(8,128)S(1)} %collective-permute-done.11.refs_3_, ...), custom_call_target="tpu_custom_call" | custom-call | tf_op jit(solution)/shard_map/pallas_call | solution.py:449
  (18 shorter events, 0.0 us)
Async XLA Ops:
  0.6 7.1 %copy-start.12 = (bf16[512,512]{1,0:T(8,128)(2,1)S(1)}, bf16[512,512]{1,0:T(8,128)(2,1)}, u32[]{:S(2)}) copy-start(bf16[512,512]{1,0:T(8,128)(2,1)} %v_ref.3) | copy-start | bytes 1572868
  0.6 7.1 %copy-start.11 = (bf16[512,512]{1,0:T(8,128)(2,1)S(1)}, bf16[512,512]{1,0:T(8,128)(2,1)}, u32[]{:S(2)}) copy-start(bf16[512,512]{1,0:T(8,128)(2,1)} %k_ref.3) | copy-start | bytes 1572868
  0.7 7.0 %copy-start.4 = (f32[3,3,512]{2,1,0:T(4,128)S(1)}, f32[3,3,512]{2,1,0:T(4,128)}, u32[]{:S(2)}) copy-start(f32[3,3,512]{2,1,0:T(4,128)} %taps_ref.5) | copy-start | bytes 55300
  2.1 15.6 %collective-permute-start.1 = (bf16[33,16,128]{2,1,0:T(8,128)(2,1)S(1)}, bf16[33,16,128]{2,1,0:T(8,128)(2,1)S(1)}, u32[]{:S(2)}, u32[]{:S(2)}) collective-permute-start(bf16[33,16,128]{2,1,0:T(8,128)(2,1)S(1)} %get-tuple-element.21), channel_id=1, source_target_pairs={{0,128},{8,136},{16,144},{24,152},{32,160},{40,168},{48,176},{56,1... | collective-permute-start | bytes 405512 | tf_op jit(solution)/shard_map/ppermute | solution.py:206
  6.0 11.7 %collective-permute-start.2 = (bf16[33,16,128]{2,1,0:T(8,128)(2,1)S(1)}, bf16[33,16,128]{2,1,0:T(8,128)(2,1)S(1)}, u32[]{:S(2)}, u32[]{:S(2)}) collective-permute-start(bf16[33,16,128]{2,1,0:T(8,128)(2,1)S(1)} %get-tuple-element.22), channel_id=1, source_target_pairs={{0,192},{8,200},{16,208},{24,216},{32,224},{40,232},{48,240},{56,2... | collective-permute-start | bytes 405512 | tf_op jit(solution)/shard_map/ppermute | solution.py:206
  7.5 10.3 %collective-permute-start = (bf16[34,16,128]{2,1,0:T(8,128)(2,1)S(1)}, bf16[34,16,128]{2,1,0:T(8,128)(2,1)S(1)}, u32[]{:S(2)}, u32[]{:S(2)}) collective-permute-start(bf16[34,16,128]{2,1,0:T(8,128)(2,1)S(1)} %get-tuple-element.20), channel_id=1, source_target_pairs={{0,64},{8,72},{16,80},{24,88},{32,96},{40,104},{48,112},{56,120},{... | collective-permute-start | bytes 417800 | tf_op jit(solution)/shard_map/ppermute | solution.py:206
  9.2 24.9 %all-to-all-start = ((bf16[32,4,16,128]{3,2,1,0:T(8,128)(2,1)}), bf16[32,4,16,128]{3,2,1,0:T(8,128)(2,1)S(1)}, u32[]{:S(2)}, u32[]{:S(2)}) async-start(bf16[32,4,16,128]{3,2,1,0:T(8,128)(2,1)} %shard_map.149), calls=%async_computation | async-start | bytes 1048576 | tf_op jit(solution)/shard_map/all_to_all | solution.py:464
  17.8 10.4 %copy-start = (bf16[512,512]{1,0:T(8,128)(2,1)S(1)}, bf16[512,512]{1,0:T(8,128)(2,1)}, u32[]{:S(2)}) copy-start(bf16[512,512]{1,0:T(8,128)(2,1)} %q_ref.3) | copy-start | bytes 1572868
  17.9 6.8 %collective-permute-start.4 = (bf16[19,16,128]{2,1,0:T(8,128)(2,1)S(1)}, bf16[19,16,128]{2,1,0:T(8,128)(2,1)S(1)}, u32[]{:S(2)}, u32[]{:S(2)}) collective-permute-start(bf16[19,16,128]{2,1,0:T(8,128)(2,1)S(1)} %get-tuple-element.24), channel_id=1, source_target_pairs={{0,56},{8,16},{16,8},{24,32},{32,24},{40,48},{48,40},{56,0},{64,12... | collective-permute-start | bytes 233480 | tf_op jit(solution)/shard_map/ppermute | solution.py:206
  19.6 4.2 %collective-permute-start.3 = (bf16[18,16,128]{2,1,0:T(8,128)(2,1)S(1)}, bf16[18,16,128]{2,1,0:T(8,128)(2,1)S(1)}, u32[]{:S(2)}, u32[]{:S(2)}) collective-permute-start(bf16[18,16,128]{2,1,0:T(8,128)(2,1)S(1)} %get-tuple-element.23), channel_id=1, source_target_pairs={{0,8},{8,0},{16,24},{24,16},{32,40},{40,32},{48,56},{56,48},{64,72... | collective-permute-start | bytes 221192 | tf_op jit(solution)/shard_map/ppermute | solution.py:206
  21.0 12.5 %collective-permute-start.5 = (bf16[18,16,128]{2,1,0:T(8,128)(2,1)S(1)}, bf16[18,16,128]{2,1,0:T(8,128)(2,1)S(1)}, u32[]{:S(2)}, u32[]{:S(2)}) collective-permute-start(bf16[18,16,128]{2,1,0:T(8,128)(2,1)S(1)} %get-tuple-element.28), channel_id=1, source_target_pairs={{0,16},{8,56},{16,32},{24,8},{32,48},{40,24},{48,0},{56,40},{64,80... | collective-permute-start | bytes 221192 | tf_op jit(solution)/shard_map/ppermute | solution.py:206
  21.6 11.9 %collective-permute-start.6 = (bf16[18,16,128]{2,1,0:T(8,128)(2,1)S(1)}, bf16[18,16,128]{2,1,0:T(8,128)(2,1)S(1)}, u32[]{:S(2)}, u32[]{:S(2)}) collective-permute-start(bf16[18,16,128]{2,1,0:T(8,128)(2,1)S(1)} %get-tuple-element.29), channel_id=1, source_target_pairs={{0,24},{8,48},{16,40},{24,0},{32,56},{40,16},{48,8},{56,32},{64,88... | collective-permute-start | bytes 221192 | tf_op jit(solution)/shard_map/ppermute | solution.py:206
  23.8 9.6 %collective-permute-start.9 = (bf16[18,16,128]{2,1,0:T(8,128)(2,1)S(1)}, bf16[18,16,128]{2,1,0:T(8,128)(2,1)S(1)}, u32[]{:S(2)}, u32[]{:S(2)}) collective-permute-start(bf16[18,16,128]{2,1,0:T(8,128)(2,1)S(1)} %get-tuple-element.32), channel_id=1, source_target_pairs={{0,48},{8,24},{16,0},{24,40},{32,16},{40,56},{48,32},{56,8},{64,11... | collective-permute-start | bytes 221192 | tf_op jit(solution)/shard_map/ppermute | solution.py:206
  23.8 4.2 %copy-start.10 = (f32[512]{0:T(512)S(1)}, f32[512]{0:T(512)}, u32[]{:S(2)}) copy-start(f32[512]{0:T(512)} %param.19) | copy-start | bytes 6148
  23.8 7.3 %collective-permute-start.7 = (bf16[17,16,128]{2,1,0:T(8,128)(2,1)S(1)}, bf16[17,16,128]{2,1,0:T(8,128)(2,1)S(1)}, u32[]{:S(2)}, u32[]{:S(2)}) collective-permute-start(bf16[17,16,128]{2,1,0:T(8,128)(2,1)S(1)} %get-tuple-element.30), channel_id=1, source_target_pairs={{0,32},{8,40},{16,48},{24,56},{32,0},{40,8},{48,16},{56,24},{64,96... | collective-permute-start | bytes 208904 | tf_op jit(solution)/shard_map/ppermute | solution.py:206
  24.7 8.7 %collective-permute-start.8 = (bf16[17,16,128]{2,1,0:T(8,128)(2,1)S(1)}, bf16[17,16,128]{2,1,0:T(8,128)(2,1)S(1)}, u32[]{:S(2)}, u32[]{:S(2)}) collective-permute-start(bf16[17,16,128]{2,1,0:T(8,128)(2,1)S(1)} %get-tuple-element.31), channel_id=1, source_target_pairs={{0,40},{8,32},{16,56},{24,48},{32,8},{40,0},{48,24},{56,16},{64,10... | collective-permute-start | bytes 208904 | tf_op jit(solution)/shard_map/ppermute | solution.py:206
  28.2 6.0 %copy-start.2 = (bf16[256,256]{1,0:T(8,128)(2,1)S(1)}, bf16[256,256]{1,0:T(8,128)(2,1)}, u32[]{:S(2)}) copy-start(bf16[256,256]{1,0:T(8,128)(2,1)} %constant.14.clone.t2_inv) | copy-start | bytes 393220
  28.2 6.0 %copy-start.3 = (bf16[256,256]{1,0:T(8,128)(2,1)S(1)}, bf16[256,256]{1,0:T(8,128)(2,1)}, u32[]{:S(2)}) copy-start(bf16[256,256]{1,0:T(8,128)(2,1)} %constant.13.clone.t2) | copy-start | bytes 393220
  28.2 5.9 %copy-start.5 = (f32[128,128]{1,0:T(8,128)S(1)}, f32[128,128]{1,0:T(8,128)}, u32[]{:S(2)}) copy-start(f32[128,128]{1,0:T(8,128)} %constant.17.clone.tw_s) | copy-start | bytes 196612
  28.2 5.9 %copy-start.6 = (f32[128,128]{1,0:T(8,128)S(1)}, f32[128,128]{1,0:T(8,128)}, u32[]{:S(2)}) copy-start(f32[128,128]{1,0:T(8,128)} %constant.16.clone.tw_c) | copy-start | bytes 196612
  28.2 5.9 %copy-start.7 = (bf16[128,256]{1,0:T(8,128)(2,1)S(1)}, bf16[128,256]{1,0:T(8,128)(2,1)}, u32[]{:S(2)}) copy-start(bf16[128,256]{1,0:T(8,128)(2,1)} %constant.15.clone.t1_inv) | copy-start | bytes 196612
  28.2 5.9 %copy-start.8 = (bf16[256,128]{1,0:T(8,128)(2,1)S(1)}, bf16[256,128]{1,0:T(8,128)(2,1)}, u32[]{:S(2)}) copy-start(bf16[256,128]{1,0:T(8,128)(2,1)} %constant.12.clone.t1) | copy-start | bytes 196612
  34.2 24.2 %copy-start.9 = (f32[512]{0:T(512)S(1)}, f32[512]{0:T(512)}, u32[]{:S(2)}) copy-start(f32[512]{0:T(512)} %param.21) | copy-start | bytes 6148
  37.1 21.3 %copy-start.1 = (bf16[512,512]{1,0:T(8,128)(2,1)S(1)}, bf16[512,512]{1,0:T(8,128)(2,1)}, u32[]{:S(2)}) copy-start(bf16[512,512]{1,0:T(8,128)(2,1)} %stream_ref.1) | copy-start | bytes 1572868
  58.9 6.9 %collective-permute-start.10 = (f32[8,128]{1,0:T(8,128)S(1)}, f32[8,128]{1,0:T(8,128)S(1)}, u32[]{:S(2)}, u32[]{:S(2)}) collective-permute-start(f32[8,128]{1,0:T(8,128)S(1)} %get-tuple-element.35), channel_id=1, source_target_pairs={{0,4},{1,5},{2,6},{3,7},{4,0},{5,1},{6,2},{7,3},{8,12},{9,13},{10,... | collective-permute-start | bytes 12296 | tf_op jit(solution)/shard_map/ppermute | solution.py:469
  65.9 3.8 %collective-permute-start.13 = (f32[8,128]{1,0:T(8,128)S(1)}, f32[8,128]{1,0:T(8,128)S(1)}, u32[]{:S(2)}, u32[]{:S(2)}) collective-permute-start(f32[8,128]{1,0:T(8,128)S(1)} %add.3.refs_2_), channel_id=1, source_target_pairs={{0,3},{1,0},{2,1},{3,2},{4,7},{5,4},{6,5},{7,6},{8,11},{9,8},{10,9... | collective-permute-start | bytes 12296 | tf_op jit(solution)/shard_map/ppermute | solution.py:469
  68.6 4.0 %collective-permute-start.12 = (f32[8,128]{1,0:T(8,128)S(1)}, f32[8,128]{1,0:T(8,128)S(1)}, u32[]{:S(2)}, u32[]{:S(2)}) collective-permute-start(f32[8,128]{1,0:T(8,128)S(1)} %add.3.refs_2_), channel_id=1, source_target_pairs={{0,2},{1,3},{2,0},{3,1},{4,6},{5,7},{6,4},{7,5},{8,10},{9,11},{10,... | collective-permute-start | bytes 12296 | tf_op jit(solution)/shard_map/ppermute | solution.py:469
  68.9 3.7 %collective-permute-start.11 = (f32[8,128]{1,0:T(8,128)S(1)}, f32[8,128]{1,0:T(8,128)S(1)}, u32[]{:S(2)}, u32[]{:S(2)}) collective-permute-start(f32[8,128]{1,0:T(8,128)S(1)} %add.3.refs_2_), channel_id=1, source_target_pairs={{0,1},{1,2},{2,3},{3,0},{4,5},{5,6},{6,7},{7,4},{8,9},{9,10},{10,1... | collective-permute-start | bytes 12296 | tf_op jit(solution)/shard_map/ppermute | solution.py:469

commit v9 on v8

--- a/solution.py
+++ b/solution.py
@@ -35,8 +35,7 @@
     t2 = np.block([[cos2, sin2], [-sin2, cos2]])
     t2_inv = np.block([[cos2, -sin2], [sin2, cos2]])
     t1_inv = np.concatenate([np.cos(first).T, np.sin(first).T], 1) / n
-    low = [jnp.asarray(t, jnp.bfloat16) for t in (t1, t2, t2_inv, t1_inv)]
-    return (*low, jnp.asarray(np.cos(twist), jnp.float32), jnp.asarray(np.sin(twist), jnp.float32))
+    return [jnp.asarray(t, jnp.bfloat16) for t in (t1, t2, t2_inv, t1_inv, np.cos(twist), np.sin(twist))]
 
 
 def place():
@@ -347,9 +346,9 @@
         first = mix(t1[...], jnp.concatenate(data, 1))
         turned = []
         for i in range(len(rows)):
-            re, im = part(first[:LANE], i), part(first[LANE:], i)
+            re, im = part(first[:LANE], i).astype(low), part(first[LANE:], i).astype(low)
             c, s = tw_c[...], tw_s[...]
-            turned.append(jnp.concatenate([re * c - im * s, re * s + im * c], 1).astype(low))
+            turned.append(jnp.concatenate([re * c - im * s, re * s + im * c], 1))
         return mix(jnp.concatenate(turned, 0), t2[...])
 
     for start in range(0, depth, GROUP):
@@ -367,9 +366,9 @@
         cols = []
         for i in range(GROUP):
             v = back[i * LANE : (i + 1) * LANE]
-            re, im = v[:, :LANE], v[:, LANE:]
+            re, im = v[:, :LANE].astype(low), v[:, LANE:].astype(low)
             c, s = tw_c[...], tw_s[...]
-            cols.append(jnp.concatenate([re * c + im * s, im * c - re * s], 0).astype(low))
+            cols.append(jnp.concatenate([re * c + im * s, im * c - re * s], 0))
         conv = mix(t1_inv[...], jnp.concatenate(cols, 1))
         for i, r in enumerate(rows):
             y_wide[r, :] = part(conv, i)

time: 74 us -> 73.8 us (level)
  no operation moved by 1% of the time
where the time goes in v9:
time: 73.8 us; the launch traced here: 73.5 us
  starting transfers between devices  33.2 us (45%)
  blocking collectives  21.3 us (29%)
  waiting for transfers between devices  9.93 us (13%)
  Pallas kernels  7.98 us (11%)
  between operations  1.02 us (1%)
    all_to_all x1, blocking collectives, exchange(): return lax.all_to_all(x, axis, split_axis=0, concat_axis=0, tiled=True)  21.3 us
    ppermute x10, starting transfers between devices, moved(): lax.ppermute(block, 'seq', [(seq_index(*p), seq_index(*target(*p))) for p...  15.3 us
    ppermute x4, starting transfers between devices, across(): return lax.ppermute(block, 'ch', route)  9.44 us
    all_to_all x1, starting transfers between devices, exchange(): return lax.all_to_all(x, axis, split_axis=0, concat_axis=0, tiled=True)  8.48 us
    ppermute x10, waiting for transfers between devices, moved(): lax.ppermute(block, 'seq', [(seq_index(*p), seq_index(*target(*p))) for p...  5 us
    ppermute x4, waiting for transfers between devices, across(): return lax.ppermute(block, 'ch', route)  4.23 us
    pallas_call x1, Pallas kernels, long_conv(): pl.pallas_call(conv_kernel, in_specs=[HBM if x is after else VMEM for x i...  2.67 us
    pallas_call x1, Pallas kernels, product(): pl.pallas_call(product_kernel, in_specs=[VMEM] * 3, out_specs=HBM, out_sh...  1.54 us
  transfers between devices with their start and end apart: 15, of which 7 were waited for; matrix products, arithmetic and copies ran while one was open for 0% of the time, Pallas kernels for 3%

profile of v9, /device:TPU:1, one launch (start us, length us, event | category | flops | bytes accessed | tf_op | source)
XLA Modules:
  0.0 73.5 jit_solution(17854561463681921221)
XLA Ops:
  0.7 1.5 %shard_map.150 = (bf16[34,16,128]{2,1,0:T(8,128)(2,1)S(1)}, bf16[34,16,128]{2,1,0:T(8,128)(2,1)S(1)}, bf16[33,16,128]{2,1,0:T(8,128)(2,1)S(1)}, bf16[33,16,128]{2,1,0:T(8,128)(2,1)S(1)}) custom-call(bf16[512,512]{1,0:T(8,128)(2,1)} %q_ref.3, bf16[512,512]{1,0:T(8,128)(2,1)} %k_ref.3, bf16[512,512]{1,0:T(8,128)(2,1)} %v_ref.3, bf16[512,512]{1,0:T(8,128)(2,1)} %f_ref.1), custom_call_target="tpu_custom_call" | custom-call | flops 10000000000 | tf_op jit(solution)/shard_map/pallas_call | solution.py:106
  2.1 3.9 %collective-permute-start.1 = (bf16[33,16,128]{2,1,0:T(8,128)(2,1)S(1)}, bf16[33,16,128]{2,1,0:T(8,128)(2,1)S(1)}, u32[]{:S(2)}, u32[]{:S(2)}) collective-permute-start(bf16[33,16,128]{2,1,0:T(8,128)(2,1)S(1)} %get-tuple-element.21), channel_id=1, source_target_pairs={{0,128},{8,136},{16,144},{24,152},{32,160},{40,168},{48,176},{56,1... | collective-permute-start | bytes 405512 | tf_op jit(solution)/shard_map/ppermute | solution.py:205
  6.0 1.4 %collective-permute-start.2 = (bf16[33,16,128]{2,1,0:T(8,128)(2,1)S(1)}, bf16[33,16,128]{2,1,0:T(8,128)(2,1)S(1)}, u32[]{:S(2)}, u32[]{:S(2)}) collective-permute-start(bf16[33,16,128]{2,1,0:T(8,128)(2,1)S(1)} %get-tuple-element.22), channel_id=1, source_target_pairs={{0,192},{8,200},{16,208},{24,216},{32,224},{40,232},{48,240},{56,2... | collective-permute-start | bytes 405512 | tf_op jit(solution)/shard_map/ppermute | solution.py:205
  7.5 0.2 collective-permute-start
  7.7 1.5 %shard_map.149 = bf16[32,4,16,128]{3,2,1,0:T(8,128)(2,1)} custom-call(bf16[512,512]{1,0:T(8,128)(2,1)S(1)} %copy-done.11, bf16[512,512]{1,0:T(8,128)(2,1)S(1)} %copy-done.12, f32[3,3,512]{2,1,0:T(4,128)S(1)} %copy-done.4), custom_call_target="tpu_custom_call" | custom-call | flops 20000000000 | tf_op jit(solution)/shard_map/pallas_call | solution.py:256
  9.2 8.5 %all-to-all-start = ((bf16[32,4,16,128]{3,2,1,0:T(8,128)(2,1)}), bf16[32,4,16,128]{3,2,1,0:T(8,128)(2,1)S(1)}, u32[]{:S(2)}, u32[]{:S(2)}) async-start(bf16[32,4,16,128]{3,2,1,0:T(8,128)(2,1)} %shard_map.149), calls=%async_computation | async-start | bytes 1048576 | tf_op jit(solution)/shard_map/all_to_all | solution.py:463
  17.7 0.0 collective-permute-done.1.refs_2_
  17.7 0.0 collective-permute-done.2.refs_3_
  17.8 0.0 collective-permute-done.refs_1_
  17.8 0.0 copy-start
  17.8 0.1 shard_map.151
  17.9 1.7 %collective-permute-start.4 = (bf16[19,16,128]{2,1,0:T(8,128)(2,1)S(1)}, bf16[19,16,128]{2,1,0:T(8,128)(2,1)S(1)}, u32[]{:S(2)}, u32[]{:S(2)}) collective-permute-start(bf16[19,16,128]{2,1,0:T(8,128)(2,1)S(1)} %get-tuple-element.24), channel_id=1, source_target_pairs={{0,56},{8,16},{16,8},{24,32},{32,24},{40,48},{48,40},{56,0},{64,12... | collective-permute-start | bytes 233480 | tf_op jit(solution)/shard_map/ppermute | solution.py:205
  19.6 1.4 %collective-permute-start.3 = (bf16[18,16,128]{2,1,0:T(8,128)(2,1)S(1)}, bf16[18,16,128]{2,1,0:T(8,128)(2,1)S(1)}, u32[]{:S(2)}, u32[]{:S(2)}) collective-permute-start(bf16[18,16,128]{2,1,0:T(8,128)(2,1)S(1)} %get-tuple-element.23), channel_id=1, source_target_pairs={{0,8},{8,0},{16,24},{24,16},{32,40},{40,32},{48,56},{56,48},{64,72... | collective-permute-start | bytes 221192 | tf_op jit(solution)/shard_map/ppermute | solution.py:205
  21.0 0.6 collective-permute-start.5
  21.6 2.3 %collective-permute-start.6 = (bf16[18,16,128]{2,1,0:T(8,128)(2,1)S(1)}, bf16[18,16,128]{2,1,0:T(8,128)(2,1)S(1)}, u32[]{:S(2)}, u32[]{:S(2)}) collective-permute-start(bf16[18,16,128]{2,1,0:T(8,128)(2,1)S(1)} %get-tuple-element.29), channel_id=1, source_target_pairs={{0,24},{8,48},{16,40},{24,0},{32,56},{40,16},{48,8},{56,32},{64,88... | collective-permute-start | bytes 221192 | tf_op jit(solution)/shard_map/ppermute | solution.py:205
  23.8 0.0 collective-permute-start.9
  23.8 0.0 collective-permute-done.3.core_ref.rest_1_
  23.8 0.5 collective-permute-start.7
  24.4 0.4 collective-permute-done.4.step_ref.rest_7_
  24.7 3.3 %collective-permute-start.8 = (bf16[17,16,128]{2,1,0:T(8,128)(2,1)S(1)}, bf16[17,16,128]{2,1,0:T(8,128)(2,1)S(1)}, u32[]{:S(2)}, u32[]{:S(2)}) collective-permute-start(bf16[17,16,128]{2,1,0:T(8,128)(2,1)S(1)} %get-tuple-element.31), channel_id=1, source_target_pairs={{0,40},{8,32},{16,56},{24,48},{32,8},{40,0},{48,24},{56,16},{64,10... | collective-permute-start | bytes 208904 | tf_op jit(solution)/shard_map/ppermute | solution.py:205
  28.1 0.1 shard_map.153
  28.2 0.0 copy-start.2
  28.2 0.0 copy-start.3
  28.2 0.0 copy-start.5
  28.2 0.0 copy-start.6
  28.2 0.0 copy-start.7
  28.2 0.0 copy-start.8
  28.3 0.6 shard_map.152.after_ref.qf_ref
  28.8 2.4 %collective-permute-done.7.rest_4_ = bf16[17,16,128]{2,1,0:T(8,128)(2,1)S(1)} collective-permute-done((bf16[17,16,128]{2,1,0:T(8,128)(2,1)S(1)}, bf16[17,16,128]{2,1,0:T(8,128)(2,1)S(1)}, u32[]{:S(2)}, u32[]{:S(2)}) %collective-permute-start.7) | collective-permute-done | bytes 69664 | tf_op jit(solution)/shard_map/ppermute | solution.py:205
  31.2 2.2 %collective-permute-done.8.rest_5_ = bf16[17,16,128]{2,1,0:T(8,128)(2,1)S(1)} collective-permute-done((bf16[17,16,128]{2,1,0:T(8,128)(2,1)S(1)}, bf16[17,16,128]{2,1,0:T(8,128)(2,1)S(1)}, u32[]{:S(2)}, u32[]{:S(2)}) %collective-permute-start.8) | collective-permute-done | bytes 69664 | tf_op jit(solution)/shard_map/ppermute | solution.py:205
  33.4 0.0 collective-permute-done.5.rest_2_
  33.4 0.0 collective-permute-done.6.rest_3_
  33.4 0.0 collective-permute-done.9.rest_6_
  33.4 0.7 all-to-all-done.u_ref
  34.2 0.0 copy-start.9
  34.2 2.7 %shard_map.154 = bf16[2048,128]{1,0:T(8,128)(2,1)S(1)} custom-call(bf16[32,4,16,128]{3,2,1,0:T(8,128)(2,1)S(1)} %all-to-all-done.u_ref, bf16[512,512]{1,0:T(8,128)(2,1)S(1)} %shard_map.152.after_ref.qf_ref, f32[16,128]{1,0:T(8,128)S(1)} %get-tuple-element.25.taps_ref, f32[16,128]{1,0:T(8,128)S(1)} %get-tuple-element.26.skip_ref, ...), custom_call_target="tpu_custom_call" | custom-call | tf_op jit(solution)/shard_map/pallas_call | solution.py:386
  36.9 0.0 copy-start.1
  36.9 21.3 %all_to_all.10.y_ref = bf16[32,4,16,128]{3,2,1,0:T(8,128)(2,1)S(1)} all-to-all(bf16[32,4,16,128]{3,2,1,0:T(8,128)(2,1)S(1)} %bitcast.3), channel_id=1, replica_groups=mesh['seq'=32,'ch'=8] {'seq'}, dimensions={0} | all-to-all | bytes 1048576 | tf_op jit(solution)/shard_map/all_to_all | solution.py:463
  58.1 0.5 shard_map.155
  58.7 5.7 %collective-permute-start.10 = (f32[8,128]{1,0:T(8,128)S(1)}, f32[8,128]{1,0:T(8,128)S(1)}, u32[]{:S(2)}, u32[]{:S(2)}) collective-permute-start(f32[8,128]{1,0:T(8,128)S(1)} %get-tuple-element.35), channel_id=1, source_target_pairs={{0,4},{1,5},{2,6},{3,7},{4,0},{5,1},{6,2},{7,3},{8,12},{9,13},{10,... | collective-permute-start | bytes 12296 | tf_op jit(solution)/shard_map/ppermute | solution.py:468
  64.3 1.3 %collective-permute-done.10 = f32[8,128]{1,0:T(8,128)S(1)} collective-permute-done((f32[8,128]{1,0:T(8,128)S(1)}, f32[8,128]{1,0:T(8,128)S(1)}, u32[]{:S(2)}, u32[]{:S(2)}) %collective-permute-start.10) | collective-permute-done | bytes 4128 | tf_op jit(solution)/shard_map/ppermute | solution.py:468
  65.6 2.7 %collective-permute-start.13 = (f32[8,128]{1,0:T(8,128)S(1)}, f32[8,128]{1,0:T(8,128)S(1)}, u32[]{:S(2)}, u32[]{:S(2)}) collective-permute-start(f32[8,128]{1,0:T(8,128)S(1)} %add.3.refs_2_), channel_id=1, source_target_pairs={{0,3},{1,0},{2,1},{3,2},{4,7},{5,4},{6,5},{7,6},{8,11},{9,8},{10,9... | collective-permute-start | bytes 12296 | tf_op jit(solution)/shard_map/ppermute | solution.py:468
  68.3 0.4 collective-permute-start.12
  68.7 0.7 collective-permute-start.11
  69.4 0.0 collective-permute-done.13.refs_5_
  69.4 2.9 %collective-permute-done.12.refs_4_ = f32[8,128]{1,0:T(8,128)S(1)} collective-permute-done((f32[8,128]{1,0:T(8,128)S(1)}, f32[8,128]{1,0:T(8,128)S(1)}, u32[]{:S(2)}, u32[]{:S(2)}) %collective-permute-start.12) | collective-permute-done | bytes 4128 | tf_op jit(solution)/shard_map/ppermute | solution.py:468
  72.3 0.1 collective-permute-done.11.refs_3_
  72.3 1.0 %shard_map.156 = (bf16[512,512]{1,0:T(8,128)(2,1)}, bf16[512,512]{1,0:T(8,128)(2,1)}) custom-call(bf16[512,512]{1,0:T(8,128)(2,1)S(1)} %get-tuple-element.33.refs_0_, f32[512,512]{1,0:T(8,128)S(1)} %get-tuple-element.34.refs_1_, f32[8,128]{1,0:T(8,128)S(1)} %add.3.refs_2_, f32[8,128]{1,0:T(8,128)S(1)} %collective-permute-done.11.refs_3_, ...), custom_call_target="tpu_custom_call" | custom-call | tf_op jit(solution)/shard_map/pallas_call | solution.py:448
  (18 shorter events, 0.0 us)
Async XLA Ops:
  0.6 7.1 %copy-start.12 = (bf16[512,512]{1,0:T(8,128)(2,1)S(1)}, bf16[512,512]{1,0:T(8,128)(2,1)}, u32[]{:S(2)}) copy-start(bf16[512,512]{1,0:T(8,128)(2,1)} %v_ref.3) | copy-start | bytes 1572868
  0.6 7.1 %copy-start.11 = (bf16[512,512]{1,0:T(8,128)(2,1)S(1)}, bf16[512,512]{1,0:T(8,128)(2,1)}, u32[]{:S(2)}) copy-start(bf16[512,512]{1,0:T(8,128)(2,1)} %k_ref.3) | copy-start | bytes 1572868
  0.7 7.0 %copy-start.4 = (f32[3,3,512]{2,1,0:T(4,128)S(1)}, f32[3,3,512]{2,1,0:T(4,128)}, u32[]{:S(2)}) copy-start(f32[3,3,512]{2,1,0:T(4,128)} %taps_ref.5) | copy-start | bytes 55300
  2.1 15.6 %collective-permute-start.1 = (bf16[33,16,128]{2,1,0:T(8,128)(2,1)S(1)}, bf16[33,16,128]{2,1,0:T(8,128)(2,1)S(1)}, u32[]{:S(2)}, u32[]{:S(2)}) collective-permute-start(bf16[33,16,128]{2,1,0:T(8,128)(2,1)S(1)} %get-tuple-element.21), channel_id=1, source_target_pairs={{0,128},{8,136},{16,144},{24,152},{32,160},{40,168},{48,176},{56,1... | collective-permute-start | bytes 405512 | tf_op jit(solution)/shard_map/ppermute | solution.py:205
  6.0 11.7 %collective-permute-start.2 = (bf16[33,16,128]{2,1,0:T(8,128)(2,1)S(1)}, bf16[33,16,128]{2,1,0:T(8,128)(2,1)S(1)}, u32[]{:S(2)}, u32[]{:S(2)}) collective-permute-start(bf16[33,16,128]{2,1,0:T(8,128)(2,1)S(1)} %get-tuple-element.22), channel_id=1, source_target_pairs={{0,192},{8,200},{16,208},{24,216},{32,224},{40,232},{48,240},{56,2... | collective-permute-start | bytes 405512 | tf_op jit(solution)/shard_map/ppermute | solution.py:205
  7.5 10.3 %collective-permute-start = (bf16[34,16,128]{2,1,0:T(8,128)(2,1)S(1)}, bf16[34,16,128]{2,1,0:T(8,128)(2,1)S(1)}, u32[]{:S(2)}, u32[]{:S(2)}) collective-permute-start(bf16[34,16,128]{2,1,0:T(8,128)(2,1)S(1)} %get-tuple-element.20), channel_id=1, source_target_pairs={{0,64},{8,72},{16,80},{24,88},{32,96},{40,104},{48,112},{56,120},{... | collective-permute-start | bytes 417800 | tf_op jit(solution)/shard_map/ppermute | solution.py:205
  9.2 24.9 %all-to-all-start = ((bf16[32,4,16,128]{3,2,1,0:T(8,128)(2,1)}), bf16[32,4,16,128]{3,2,1,0:T(8,128)(2,1)S(1)}, u32[]{:S(2)}, u32[]{:S(2)}) async-start(bf16[32,4,16,128]{3,2,1,0:T(8,128)(2,1)} %shard_map.149), calls=%async_computation | async-start | bytes 1048576 | tf_op jit(solution)/shard_map/all_to_all | solution.py:463
  17.8 10.4 %copy-start = (bf16[512,512]{1,0:T(8,128)(2,1)S(1)}, bf16[512,512]{1,0:T(8,128)(2,1)}, u32[]{:S(2)}) copy-start(bf16[512,512]{1,0:T(8,128)(2,1)} %q_ref.3) | copy-start | bytes 1572868
  17.9 6.8 %collective-permute-start.4 = (bf16[19,16,128]{2,1,0:T(8,128)(2,1)S(1)}, bf16[19,16,128]{2,1,0:T(8,128)(2,1)S(1)}, u32[]{:S(2)}, u32[]{:S(2)}) collective-permute-start(bf16[19,16,128]{2,1,0:T(8,128)(2,1)S(1)} %get-tuple-element.24), channel_id=1, source_target_pairs={{0,56},{8,16},{16,8},{24,32},{32,24},{40,48},{48,40},{56,0},{64,12... | collective-permute-start | bytes 233480 | tf_op jit(solution)/shard_map/ppermute | solution.py:205
  19.6 4.2 %collective-permute-start.3 = (bf16[18,16,128]{2,1,0:T(8,128)(2,1)S(1)}, bf16[18,16,128]{2,1,0:T(8,128)(2,1)S(1)}, u32[]{:S(2)}, u32[]{:S(2)}) collective-permute-start(bf16[18,16,128]{2,1,0:T(8,128)(2,1)S(1)} %get-tuple-element.23), channel_id=1, source_target_pairs={{0,8},{8,0},{16,24},{24,16},{32,40},{40,32},{48,56},{56,48},{64,72... | collective-permute-start | bytes 221192 | tf_op jit(solution)/shard_map/ppermute | solution.py:205
  21.0 12.5 %collective-permute-start.5 = (bf16[18,16,128]{2,1,0:T(8,128)(2,1)S(1)}, bf16[18,16,128]{2,1,0:T(8,128)(2,1)S(1)}, u32[]{:S(2)}, u32[]{:S(2)}) collective-permute-start(bf16[18,16,128]{2,1,0:T(8,128)(2,1)S(1)} %get-tuple-element.28), channel_id=1, source_target_pairs={{0,16},{8,56},{16,32},{24,8},{32,48},{40,24},{48,0},{56,40},{64,80... | collective-permute-start | bytes 221192 | tf_op jit(solution)/shard_map/ppermute | solution.py:205
  21.6 11.9 %collective-permute-start.6 = (bf16[18,16,128]{2,1,0:T(8,128)(2,1)S(1)}, bf16[18,16,128]{2,1,0:T(8,128)(2,1)S(1)}, u32[]{:S(2)}, u32[]{:S(2)}) collective-permute-start(bf16[18,16,128]{2,1,0:T(8,128)(2,1)S(1)} %get-tuple-element.29), channel_id=1, source_target_pairs={{0,24},{8,48},{16,40},{24,0},{32,56},{40,16},{48,8},{56,32},{64,88... | collective-permute-start | bytes 221192 | tf_op jit(solution)/shard_map/ppermute | solution.py:205
  23.8 9.6 %collective-permute-start.9 = (bf16[18,16,128]{2,1,0:T(8,128)(2,1)S(1)}, bf16[18,16,128]{2,1,0:T(8,128)(2,1)S(1)}, u32[]{:S(2)}, u32[]{:S(2)}) collective-permute-start(bf16[18,16,128]{2,1,0:T(8,128)(2,1)S(1)} %get-tuple-element.32), channel_id=1, source_target_pairs={{0,48},{8,24},{16,0},{24,40},{32,16},{40,56},{48,32},{56,8},{64,11... | collective-permute-start | bytes 221192 | tf_op jit(solution)/shard_map/ppermute | solution.py:205
  23.8 4.2 %copy-start.10 = (f32[512]{0:T(512)S(1)}, f32[512]{0:T(512)}, u32[]{:S(2)}) copy-start(f32[512]{0:T(512)} %param.19) | copy-start | bytes 6148
  23.8 7.3 %collective-permute-start.7 = (bf16[17,16,128]{2,1,0:T(8,128)(2,1)S(1)}, bf16[17,16,128]{2,1,0:T(8,128)(2,1)S(1)}, u32[]{:S(2)}, u32[]{:S(2)}) collective-permute-start(bf16[17,16,128]{2,1,0:T(8,128)(2,1)S(1)} %get-tuple-element.30), channel_id=1, source_target_pairs={{0,32},{8,40},{16,48},{24,56},{32,0},{40,8},{48,16},{56,24},{64,96... | collective-permute-start | bytes 208904 | tf_op jit(solution)/shard_map/ppermute | solution.py:205
  24.7 8.7 %collective-permute-start.8 = (bf16[17,16,128]{2,1,0:T(8,128)(2,1)S(1)}, bf16[17,16,128]{2,1,0:T(8,128)(2,1)S(1)}, u32[]{:S(2)}, u32[]{:S(2)}) collective-permute-start(bf16[17,16,128]{2,1,0:T(8,128)(2,1)S(1)} %get-tuple-element.31), channel_id=1, source_target_pairs={{0,40},{8,32},{16,56},{24,48},{32,8},{40,0},{48,24},{56,16},{64,10... | collective-permute-start | bytes 208904 | tf_op jit(solution)/shard_map/ppermute | solution.py:205
  28.2 6.0 %copy-start.2 = (bf16[256,256]{1,0:T(8,128)(2,1)S(1)}, bf16[256,256]{1,0:T(8,128)(2,1)}, u32[]{:S(2)}) copy-start(bf16[256,256]{1,0:T(8,128)(2,1)} %constant.14.clone.t2_inv) | copy-start | bytes 393220
  28.2 6.0 %copy-start.3 = (bf16[256,256]{1,0:T(8,128)(2,1)S(1)}, bf16[256,256]{1,0:T(8,128)(2,1)}, u32[]{:S(2)}) copy-start(bf16[256,256]{1,0:T(8,128)(2,1)} %constant.13.clone.t2) | copy-start | bytes 393220
  28.2 5.9 %copy-start.5 = (bf16[128,256]{1,0:T(8,128)(2,1)S(1)}, bf16[128,256]{1,0:T(8,128)(2,1)}, u32[]{:S(2)}) copy-start(bf16[128,256]{1,0:T(8,128)(2,1)} %constant.15.clone.t1_inv) | copy-start | bytes 196612
  28.2 5.9 %copy-start.6 = (bf16[256,128]{1,0:T(8,128)(2,1)S(1)}, bf16[256,128]{1,0:T(8,128)(2,1)}, u32[]{:S(2)}) copy-start(bf16[256,128]{1,0:T(8,128)(2,1)} %constant.12.clone.t1) | copy-start | bytes 196612
  28.2 5.9 %copy-start.7 = (bf16[128,128]{1,0:T(8,128)(2,1)S(1)}, bf16[128,128]{1,0:T(8,128)(2,1)}, u32[]{:S(2)}) copy-start(bf16[128,128]{1,0:T(8,128)(2,1)} %constant.17.clone.tw_s) | copy-start | bytes 98308
  28.2 5.9 %copy-start.8 = (bf16[128,128]{1,0:T(8,128)(2,1)S(1)}, bf16[128,128]{1,0:T(8,128)(2,1)}, u32[]{:S(2)}) copy-start(bf16[128,128]{1,0:T(8,128)(2,1)} %constant.16.clone.tw_c) | copy-start | bytes 98308
  34.2 24.0 %copy-start.9 = (f32[512]{0:T(512)S(1)}, f32[512]{0:T(512)}, u32[]{:S(2)}) copy-start(f32[512]{0:T(512)} %param.21) | copy-start | bytes 6148
  36.9 21.3 %copy-start.1 = (bf16[512,512]{1,0:T(8,128)(2,1)S(1)}, bf16[512,512]{1,0:T(8,128)(2,1)}, u32[]{:S(2)}) copy-start(bf16[512,512]{1,0:T(8,128)(2,1)} %stream_ref.1) | copy-start | bytes 1572868
  58.7 6.9 %collective-permute-start.10 = (f32[8,128]{1,0:T(8,128)S(1)}, f32[8,128]{1,0:T(8,128)S(1)}, u32[]{:S(2)}, u32[]{:S(2)}) collective-permute-start(f32[8,128]{1,0:T(8,128)S(1)} %get-tuple-element.35), channel_id=1, source_target_pairs={{0,4},{1,5},{2,6},{3,7},{4,0},{5,1},{6,2},{7,3},{8,12},{9,13},{10,... | collective-permute-start | bytes 12296 | tf_op jit(solution)/shard_map/ppermute | solution.py:468
  65.6 3.8 %collective-permute-start.13 = (f32[8,128]{1,0:T(8,128)S(1)}, f32[8,128]{1,0:T(8,128)S(1)}, u32[]{:S(2)}, u32[]{:S(2)}) collective-permute-start(f32[8,128]{1,0:T(8,128)S(1)} %add.3.refs_2_), channel_id=1, source_target_pairs={{0,3},{1,0},{2,1},{3,2},{4,7},{5,4},{6,5},{7,6},{8,11},{9,8},{10,9... | collective-permute-start | bytes 12296 | tf_op jit(solution)/shard_map/ppermute | solution.py:468
  68.3 4.0 %collective-permute-start.12 = (f32[8,128]{1,0:T(8,128)S(1)}, f32[8,128]{1,0:T(8,128)S(1)}, u32[]{:S(2)}, u32[]{:S(2)}) collective-permute-start(f32[8,128]{1,0:T(8,128)S(1)} %add.3.refs_2_), channel_id=1, source_target_pairs={{0,2},{1,3},{2,0},{3,1},{4,6},{5,7},{6,4},{7,5},{8,10},{9,11},{10,... | collective-permute-start | bytes 12296 | tf_op jit(solution)/shard_map/ppermute | solution.py:468
  68.7 3.7 %collective-permute-start.11 = (f32[8,128]{1,0:T(8,128)S(1)}, f32[8,128]{1,0:T(8,128)S(1)}, u32[]{:S(2)}, u32[]{:S(2)}) collective-permute-start(f32[8,128]{1,0:T(8,128)S(1)} %add.3.refs_2_), channel_id=1, source_target_pairs={{0,1},{1,2},{2,3},{3,0},{4,5},{5,6},{6,7},{7,4},{8,9},{9,10},{10,1... | collective-permute-start | bytes 12296 | tf_op jit(solution)/shard_map/ppermute | solution.py:468

commit v10 on v9

--- a/solution.py
+++ b/solution.py
@@ -396,7 +396,6 @@
 def join_kernel(y_ref, qf_ref, stream_ref, gain_ref, out_ref, sum_ref, sq_ref):
     groups, slabs, depth, _ = y_ref.shape
     per = LANE // depth
-    sq_ref[...] = jnp.zeros_like(sq_ref)
     for j in range(slabs):
         rows = slice(j * LANE, (j + 1) * LANE)
         squares = jnp.zeros((LANE, LANE), jnp.float32)
@@ -419,7 +418,7 @@
         out_shape=(
             jax.ShapeDtypeStruct(stream.shape, stream.dtype),
             jax.ShapeDtypeStruct(stream.shape, jnp.float32),
-            jax.ShapeDtypeStruct((8, LANE), jnp.float32),
+            jax.ShapeDtypeStruct((stream.shape[0] // LANE, LANE), jnp.float32),
         ),
         compiler_params=params(12),
     )(y, qf, stream, gain[None, :])

time: 73.8 us -> 73.7 us (level)
  no operation moved by 1% of the time
where the time goes in v10:
time: 73.7 us; the launch traced here: 73.5 us
  starting transfers between devices  33.2 us (45%)
  blocking collectives  21.3 us (29%)
  waiting for transfers between devices  9.89 us (13%)
  Pallas kernels  7.98 us (11%)
  between operations  1.02 us (1%)
    all_to_all x1, blocking collectives, exchange(): return lax.all_to_all(x, axis, split_axis=0, concat_axis=0, tiled=True)  21.3 us
    ppermute x10, starting transfers between devices, moved(): lax.ppermute(block, 'seq', [(seq_index(*p), seq_index(*target(*p))) for p...  15.3 us
    ppermute x4, starting transfers between devices, across(): return lax.ppermute(block, 'ch', route)  9.44 us
    all_to_all x1, starting transfers between devices, exchange(): return lax.all_to_all(x, axis, split_axis=0, concat_axis=0, tiled=True)  8.48 us
    ppermute x10, waiting for transfers between devices, moved(): lax.ppermute(block, 'seq', [(seq_index(*p), seq_index(*target(*p))) for p...  5 us
    ppermute x4, waiting for transfers between devices, across(): return lax.ppermute(block, 'ch', route)  4.18 us
    pallas_call x1, Pallas kernels, long_conv(): pl.pallas_call(conv_kernel, in_specs=[HBM if x is after else VMEM for x i...  2.67 us
    pallas_call x1, Pallas kernels, product(): pl.pallas_call(product_kernel, in_specs=[VMEM] * 3, out_specs=HBM, out_sh...  1.54 us
  transfers between devices with their start and end apart: 15, of which 7 were waited for; matrix products, arithmetic and copies ran while one was open for 0% of the time, Pallas kernels for 3%

profile of v10, /device:TPU:1, one launch (start us, length us, event | category | flops | bytes accessed | tf_op | source)
XLA Modules:
  0.0 73.5 jit_solution(3333750826391456999)
XLA Ops:
  0.7 1.5 %shard_map.150 = (bf16[34,16,128]{2,1,0:T(8,128)(2,1)S(1)}, bf16[34,16,128]{2,1,0:T(8,128)(2,1)S(1)}, bf16[33,16,128]{2,1,0:T(8,128)(2,1)S(1)}, bf16[33,16,128]{2,1,0:T(8,128)(2,1)S(1)}) custom-call(bf16[512,512]{1,0:T(8,128)(2,1)} %q_ref.3, bf16[512,512]{1,0:T(8,128)(2,1)} %k_ref.3, bf16[512,512]{1,0:T(8,128)(2,1)} %v_ref.3, bf16[512,512]{1,0:T(8,128)(2,1)} %f_ref.1), custom_call_target="tpu_custom_call" | custom-call | flops 10000000000 | tf_op jit(solution)/shard_map/pallas_call | solution.py:106
  2.1 3.9 %collective-permute-start.1 = (bf16[33,16,128]{2,1,0:T(8,128)(2,1)S(1)}, bf16[33,16,128]{2,1,0:T(8,128)(2,1)S(1)}, u32[]{:S(2)}, u32[]{:S(2)}) collective-permute-start(bf16[33,16,128]{2,1,0:T(8,128)(2,1)S(1)} %get-tuple-element.21), channel_id=1, source_target_pairs={{0,128},{8,136},{16,144},{24,152},{32,160},{40,168},{48,176},{56,1... | collective-permute-start | bytes 405512 | tf_op jit(solution)/shard_map/ppermute | solution.py:205
  6.0 1.4 %collective-permute-start.2 = (bf16[33,16,128]{2,1,0:T(8,128)(2,1)S(1)}, bf16[33,16,128]{2,1,0:T(8,128)(2,1)S(1)}, u32[]{:S(2)}, u32[]{:S(2)}) collective-permute-start(bf16[33,16,128]{2,1,0:T(8,128)(2,1)S(1)} %get-tuple-element.22), channel_id=1, source_target_pairs={{0,192},{8,200},{16,208},{24,216},{32,224},{40,232},{48,240},{56,2... | collective-permute-start | bytes 405512 | tf_op jit(solution)/shard_map/ppermute | solution.py:205
  7.5 0.2 collective-permute-start
  7.7 1.5 %shard_map.149 = bf16[32,4,16,128]{3,2,1,0:T(8,128)(2,1)} custom-call(bf16[512,512]{1,0:T(8,128)(2,1)S(1)} %copy-done.11, bf16[512,512]{1,0:T(8,128)(2,1)S(1)} %copy-done.12, f32[3,3,512]{2,1,0:T(4,128)S(1)} %copy-done.4), custom_call_target="tpu_custom_call" | custom-call | flops 20000000000 | tf_op jit(solution)/shard_map/pallas_call | solution.py:256
  9.2 8.5 %all-to-all-start = ((bf16[32,4,16,128]{3,2,1,0:T(8,128)(2,1)}), bf16[32,4,16,128]{3,2,1,0:T(8,128)(2,1)S(1)}, u32[]{:S(2)}, u32[]{:S(2)}) async-start(bf16[32,4,16,128]{3,2,1,0:T(8,128)(2,1)} %shard_map.149), calls=%async_computation | async-start | bytes 1048576 | tf_op jit(solution)/shard_map/all_to_all | solution.py:462
  17.7 0.0 collective-permute-done.1.refs_2_
  17.7 0.0 collective-permute-done.2.refs_3_
  17.8 0.0 collective-permute-done.refs_1_
  17.8 0.0 copy-start
  17.8 0.1 shard_map.151
  17.9 1.7 %collective-permute-start.4 = (bf16[19,16,128]{2,1,0:T(8,128)(2,1)S(1)}, bf16[19,16,128]{2,1,0:T(8,128)(2,1)S(1)}, u32[]{:S(2)}, u32[]{:S(2)}) collective-permute-start(bf16[19,16,128]{2,1,0:T(8,128)(2,1)S(1)} %get-tuple-element.24), channel_id=1, source_target_pairs={{0,56},{8,16},{16,8},{24,32},{32,24},{40,48},{48,40},{56,0},{64,12... | collective-permute-start | bytes 233480 | tf_op jit(solution)/shard_map/ppermute | solution.py:205
  19.6 1.4 %collective-permute-start.3 = (bf16[18,16,128]{2,1,0:T(8,128)(2,1)S(1)}, bf16[18,16,128]{2,1,0:T(8,128)(2,1)S(1)}, u32[]{:S(2)}, u32[]{:S(2)}) collective-permute-start(bf16[18,16,128]{2,1,0:T(8,128)(2,1)S(1)} %get-tuple-element.23), channel_id=1, source_target_pairs={{0,8},{8,0},{16,24},{24,16},{32,40},{40,32},{48,56},{56,48},{64,72... | collective-permute-start | bytes 221192 | tf_op jit(solution)/shard_map/ppermute | solution.py:205
  21.0 0.6 collective-permute-start.5
  21.6 2.3 %collective-permute-start.6 = (bf16[18,16,128]{2,1,0:T(8,128)(2,1)S(1)}, bf16[18,16,128]{2,1,0:T(8,128)(2,1)S(1)}, u32[]{:S(2)}, u32[]{:S(2)}) collective-permute-start(bf16[18,16,128]{2,1,0:T(8,128)(2,1)S(1)} %get-tuple-element.29), channel_id=1, source_target_pairs={{0,24},{8,48},{16,40},{24,0},{32,56},{40,16},{48,8},{56,32},{64,88... | collective-permute-start | bytes 221192 | tf_op jit(solution)/shard_map/ppermute | solution.py:205
  23.8 0.0 collective-permute-start.9
  23.8 0.0 collective-permute-done.3.core_ref.rest_1_
  23.8 0.5 collective-permute-start.7
  24.4 0.4 collective-permute-done.4.step_ref.rest_7_
  24.7 3.3 %collective-permute-start.8 = (bf16[17,16,128]{2,1,0:T(8,128)(2,1)S(1)}, bf16[17,16,128]{2,1,0:T(8,128)(2,1)S(1)}, u32[]{:S(2)}, u32[]{:S(2)}) collective-permute-start(bf16[17,16,128]{2,1,0:T(8,128)(2,1)S(1)} %get-tuple-element.31), channel_id=1, source_target_pairs={{0,40},{8,32},{16,56},{24,48},{32,8},{40,0},{48,24},{56,16},{64,10... | collective-permute-start | bytes 208904 | tf_op jit(solution)/shard_map/ppermute | solution.py:205
  28.1 0.1 shard_map.153
  28.2 0.0 copy-start.2
  28.2 0.0 copy-start.3
  28.2 0.0 copy-start.5
  28.2 0.0 copy-start.6
  28.2 0.0 copy-start.7
  28.2 0.0 copy-start.8
  28.3 0.6 shard_map.152.after_ref.qf_ref
  28.8 2.4 %collective-permute-done.7.rest_4_ = bf16[17,16,128]{2,1,0:T(8,128)(2,1)S(1)} collective-permute-done((bf16[17,16,128]{2,1,0:T(8,128)(2,1)S(1)}, bf16[17,16,128]{2,1,0:T(8,128)(2,1)S(1)}, u32[]{:S(2)}, u32[]{:S(2)}) %collective-permute-start.7) | collective-permute-done | bytes 69664 | tf_op jit(solution)/shard_map/ppermute | solution.py:205
  31.2 2.2 %collective-permute-done.8.rest_5_ = bf16[17,16,128]{2,1,0:T(8,128)(2,1)S(1)} collective-permute-done((bf16[17,16,128]{2,1,0:T(8,128)(2,1)S(1)}, bf16[17,16,128]{2,1,0:T(8,128)(2,1)S(1)}, u32[]{:S(2)}, u32[]{:S(2)}) %collective-permute-start.8) | collective-permute-done | bytes 69664 | tf_op jit(solution)/shard_map/ppermute | solution.py:205
  33.4 0.0 collective-permute-done.5.rest_2_
  33.4 0.0 collective-permute-done.6.rest_3_
  33.4 0.0 collective-permute-done.9.rest_6_
  33.4 0.7 all-to-all-done.u_ref
  34.2 0.0 copy-start.9
  34.2 2.7 %shard_map.154 = bf16[2048,128]{1,0:T(8,128)(2,1)S(1)} custom-call(bf16[32,4,16,128]{3,2,1,0:T(8,128)(2,1)S(1)} %all-to-all-done.u_ref, bf16[512,512]{1,0:T(8,128)(2,1)S(1)} %shard_map.152.after_ref.qf_ref, f32[16,128]{1,0:T(8,128)S(1)} %get-tuple-element.25.taps_ref, f32[16,128]{1,0:T(8,128)S(1)} %get-tuple-element.26.skip_ref, ...), custom_call_target="tpu_custom_call" | custom-call | tf_op jit(solution)/shard_map/pallas_call | solution.py:386
  36.9 0.0 copy-start.1
  36.9 21.3 %all_to_all.10.y_ref = bf16[32,4,16,128]{3,2,1,0:T(8,128)(2,1)S(1)} all-to-all(bf16[32,4,16,128]{3,2,1,0:T(8,128)(2,1)S(1)} %bitcast.3), channel_id=1, replica_groups=mesh['seq'=32,'ch'=8] {'seq'}, dimensions={0} | all-to-all | bytes 1048576 | tf_op jit(solution)/shard_map/all_to_all | solution.py:462
  58.1 0.5 shard_map.155
  58.7 5.7 %collective-permute-start.10 = (f32[4,128]{1,0:T(4,128)S(1)}, f32[4,128]{1,0:T(4,128)S(1)}, u32[]{:S(2)}, u32[]{:S(2)}) collective-permute-start(f32[4,128]{1,0:T(4,128)S(1)} %get-tuple-element.35), channel_id=1, source_target_pairs={{0,4},{1,5},{2,6},{3,7},{4,0},{5,1},{6,2},{7,3},{8,12},{9,13},{10,... | collective-permute-start | bytes 6152 | tf_op jit(solution)/shard_map/ppermute | solution.py:467
  64.3 1.2 %collective-permute-done.10 = f32[4,128]{1,0:T(4,128)S(1)} collective-permute-done((f32[4,128]{1,0:T(4,128)S(1)}, f32[4,128]{1,0:T(4,128)S(1)}, u32[]{:S(2)}, u32[]{:S(2)}) %collective-permute-start.10) | collective-permute-done | bytes 2080 | tf_op jit(solution)/shard_map/ppermute | solution.py:467
  65.6 2.7 %collective-permute-start.13 = (f32[4,128]{1,0:T(4,128)S(1)}, f32[4,128]{1,0:T(4,128)S(1)}, u32[]{:S(2)}, u32[]{:S(2)}) collective-permute-start(f32[4,128]{1,0:T(4,128)S(1)} %add.3.refs_2_), channel_id=1, source_target_pairs={{0,3},{1,0},{2,1},{3,2},{4,7},{5,4},{6,5},{7,6},{8,11},{9,8},{10,9... | collective-permute-start | bytes 6152 | tf_op jit(solution)/shard_map/ppermute | solution.py:467
  68.3 0.4 collective-permute-start.12
  68.7 0.7 collective-permute-start.11
  69.3 0.0 collective-permute-done.13.refs_5_
  69.3 2.9 %collective-permute-done.12.refs_4_ = f32[4,128]{1,0:T(4,128)S(1)} collective-permute-done((f32[4,128]{1,0:T(4,128)S(1)}, f32[4,128]{1,0:T(4,128)S(1)}, u32[]{:S(2)}, u32[]{:S(2)}) %collective-permute-start.12) | collective-permute-done | bytes 2080 | tf_op jit(solution)/shard_map/ppermute | solution.py:467
  72.2 0.1 collective-permute-done.11.refs_3_
  72.3 1.0 %shard_map.156 = (bf16[512,512]{1,0:T(8,128)(2,1)}, bf16[512,512]{1,0:T(8,128)(2,1)}) custom-call(bf16[512,512]{1,0:T(8,128)(2,1)S(1)} %get-tuple-element.33.refs_0_, f32[512,512]{1,0:T(8,128)S(1)} %get-tuple-element.34.refs_1_, f32[4,128]{1,0:T(4,128)S(1)} %add.3.refs_2_, f32[4,128]{1,0:T(4,128)S(1)} %collective-permute-done.11.refs_3_, ...), custom_call_target="tpu_custom_call" | custom-call | tf_op jit(solution)/shard_map/pallas_call | solution.py:447
  (18 shorter events, 0.0 us)
Async XLA Ops:
  0.6 7.1 %copy-start.12 = (bf16[512,512]{1,0:T(8,128)(2,1)S(1)}, bf16[512,512]{1,0:T(8,128)(2,1)}, u32[]{:S(2)}) copy-start(bf16[512,512]{1,0:T(8,128)(2,1)} %v_ref.3) | copy-start | bytes 1572868
  0.6 7.1 %copy-start.11 = (bf16[512,512]{1,0:T(8,128)(2,1)S(1)}, bf16[512,512]{1,0:T(8,128)(2,1)}, u32[]{:S(2)}) copy-start(bf16[512,512]{1,0:T(8,128)(2,1)} %k_ref.3) | copy-start | bytes 1572868
  0.7 7.0 %copy-start.4 = (f32[3,3,512]{2,1,0:T(4,128)S(1)}, f32[3,3,512]{2,1,0:T(4,128)}, u32[]{:S(2)}) copy-start(f32[3,3,512]{2,1,0:T(4,128)} %taps_ref.5) | copy-start | bytes 55300
  2.1 15.6 %collective-permute-start.1 = (bf16[33,16,128]{2,1,0:T(8,128)(2,1)S(1)}, bf16[33,16,128]{2,1,0:T(8,128)(2,1)S(1)}, u32[]{:S(2)}, u32[]{:S(2)}) collective-permute-start(bf16[33,16,128]{2,1,0:T(8,128)(2,1)S(1)} %get-tuple-element.21), channel_id=1, source_target_pairs={{0,128},{8,136},{16,144},{24,152},{32,160},{40,168},{48,176},{56,1... | collective-permute-start | bytes 405512 | tf_op jit(solution)/shard_map/ppermute | solution.py:205
  6.0 11.7 %collective-permute-start.2 = (bf16[33,16,128]{2,1,0:T(8,128)(2,1)S(1)}, bf16[33,16,128]{2,1,0:T(8,128)(2,1)S(1)}, u32[]{:S(2)}, u32[]{:S(2)}) collective-permute-start(bf16[33,16,128]{2,1,0:T(8,128)(2,1)S(1)} %get-tuple-element.22), channel_id=1, source_target_pairs={{0,192},{8,200},{16,208},{24,216},{32,224},{40,232},{48,240},{56,2... | collective-permute-start | bytes 405512 | tf_op jit(solution)/shard_map/ppermute | solution.py:205
  7.5 10.3 %collective-permute-start = (bf16[34,16,128]{2,1,0:T(8,128)(2,1)S(1)}, bf16[34,16,128]{2,1,0:T(8,128)(2,1)S(1)}, u32[]{:S(2)}, u32[]{:S(2)}) collective-permute-start(bf16[34,16,128]{2,1,0:T(8,128)(2,1)S(1)} %get-tuple-element.20), channel_id=1, source_target_pairs={{0,64},{8,72},{16,80},{24,88},{32,96},{40,104},{48,112},{56,120},{... | collective-permute-start | bytes 417800 | tf_op jit(solution)/shard_map/ppermute | solution.py:205
  9.2 24.9 %all-to-all-start = ((bf16[32,4,16,128]{3,2,1,0:T(8,128)(2,1)}), bf16[32,4,16,128]{3,2,1,0:T(8,128)(2,1)S(1)}, u32[]{:S(2)}, u32[]{:S(2)}) async-start(bf16[32,4,16,128]{3,2,1,0:T(8,128)(2,1)} %shard_map.149), calls=%async_computation | async-start | bytes 1048576 | tf_op jit(solution)/shard_map/all_to_all | solution.py:462
  17.8 10.4 %copy-start = (bf16[512,512]{1,0:T(8,128)(2,1)S(1)}, bf16[512,512]{1,0:T(8,128)(2,1)}, u32[]{:S(2)}) copy-start(bf16[512,512]{1,0:T(8,128)(2,1)} %q_ref.3) | copy-start | bytes 1572868
  17.9 6.8 %collective-permute-start.4 = (bf16[19,16,128]{2,1,0:T(8,128)(2,1)S(1)}, bf16[19,16,128]{2,1,0:T(8,128)(2,1)S(1)}, u32[]{:S(2)}, u32[]{:S(2)}) collective-permute-start(bf16[19,16,128]{2,1,0:T(8,128)(2,1)S(1)} %get-tuple-element.24), channel_id=1, source_target_pairs={{0,56},{8,16},{16,8},{24,32},{32,24},{40,48},{48,40},{56,0},{64,12... | collective-permute-start | bytes 233480 | tf_op jit(solution)/shard_map/ppermute | solution.py:205
  19.6 4.2 %collective-permute-start.3 = (bf16[18,16,128]{2,1,0:T(8,128)(2,1)S(1)}, bf16[18,16,128]{2,1,0:T(8,128)(2,1)S(1)}, u32[]{:S(2)}, u32[]{:S(2)}) collective-permute-start(bf16[18,16,128]{2,1,0:T(8,128)(2,1)S(1)} %get-tuple-element.23), channel_id=1, source_target_pairs={{0,8},{8,0},{16,24},{24,16},{32,40},{40,32},{48,56},{56,48},{64,72... | collective-permute-start | bytes 221192 | tf_op jit(solution)/shard_map/ppermute | solution.py:205
  21.0 12.5 %collective-permute-start.5 = (bf16[18,16,128]{2,1,0:T(8,128)(2,1)S(1)}, bf16[18,16,128]{2,1,0:T(8,128)(2,1)S(1)}, u32[]{:S(2)}, u32[]{:S(2)}) collective-permute-start(bf16[18,16,128]{2,1,0:T(8,128)(2,1)S(1)} %get-tuple-element.28), channel_id=1, source_target_pairs={{0,16},{8,56},{16,32},{24,8},{32,48},{40,24},{48,0},{56,40},{64,80... | collective-permute-start | bytes 221192 | tf_op jit(solution)/shard_map/ppermute | solution.py:205
  21.6 11.9 %collective-permute-start.6 = (bf16[18,16,128]{2,1,0:T(8,128)(2,1)S(1)}, bf16[18,16,128]{2,1,0:T(8,128)(2,1)S(1)}, u32[]{:S(2)}, u32[]{:S(2)}) collective-permute-start(bf16[18,16,128]{2,1,0:T(8,128)(2,1)S(1)} %get-tuple-element.29), channel_id=1, source_target_pairs={{0,24},{8,48},{16,40},{24,0},{32,56},{40,16},{48,8},{56,32},{64,88... | collective-permute-start | bytes 221192 | tf_op jit(solution)/shard_map/ppermute | solution.py:205
  23.8 9.6 %collective-permute-start.9 = (bf16[18,16,128]{2,1,0:T(8,128)(2,1)S(1)}, bf16[18,16,128]{2,1,0:T(8,128)(2,1)S(1)}, u32[]{:S(2)}, u32[]{:S(2)}) collective-permute-start(bf16[18,16,128]{2,1,0:T(8,128)(2,1)S(1)} %get-tuple-element.32), channel_id=1, source_target_pairs={{0,48},{8,24},{16,0},{24,40},{32,16},{40,56},{48,32},{56,8},{64,11... | collective-permute-start | bytes 221192 | tf_op jit(solution)/shard_map/ppermute | solution.py:205
  23.8 4.2 %copy-start.10 = (f32[512]{0:T(512)S(1)}, f32[512]{0:T(512)}, u32[]{:S(2)}) copy-start(f32[512]{0:T(512)} %param.19) | copy-start | bytes 6148
  23.8 7.3 %collective-permute-start.7 = (bf16[17,16,128]{2,1,0:T(8,128)(2,1)S(1)}, bf16[17,16,128]{2,1,0:T(8,128)(2,1)S(1)}, u32[]{:S(2)}, u32[]{:S(2)}) collective-permute-start(bf16[17,16,128]{2,1,0:T(8,128)(2,1)S(1)} %get-tuple-element.30), channel_id=1, source_target_pairs={{0,32},{8,40},{16,48},{24,56},{32,0},{40,8},{48,16},{56,24},{64,96... | collective-permute-start | bytes 208904 | tf_op jit(solution)/shard_map/ppermute | solution.py:205
  24.7 8.7 %collective-permute-start.8 = (bf16[17,16,128]{2,1,0:T(8,128)(2,1)S(1)}, bf16[17,16,128]{2,1,0:T(8,128)(2,1)S(1)}, u32[]{:S(2)}, u32[]{:S(2)}) collective-permute-start(bf16[17,16,128]{2,1,0:T(8,128)(2,1)S(1)} %get-tuple-element.31), channel_id=1, source_target_pairs={{0,40},{8,32},{16,56},{24,48},{32,8},{40,0},{48,24},{56,16},{64,10... | collective-permute-start | bytes 208904 | tf_op jit(solution)/shard_map/ppermute | solution.py:205
  28.2 6.0 %copy-start.2 = (bf16[256,256]{1,0:T(8,128)(2,1)S(1)}, bf16[256,256]{1,0:T(8,128)(2,1)}, u32[]{:S(2)}) copy-start(bf16[256,256]{1,0:T(8,128)(2,1)} %constant.14.clone.t2_inv) | copy-start | bytes 393220
  28.2 6.0 %copy-start.3 = (bf16[256,256]{1,0:T(8,128)(2,1)S(1)}, bf16[256,256]{1,0:T(8,128)(2,1)}, u32[]{:S(2)}) copy-start(bf16[256,256]{1,0:T(8,128)(2,1)} %constant.13.clone.t2) | copy-start | bytes 393220
  28.2 5.9 %copy-start.5 = (bf16[128,256]{1,0:T(8,128)(2,1)S(1)}, bf16[128,256]{1,0:T(8,128)(2,1)}, u32[]{:S(2)}) copy-start(bf16[128,256]{1,0:T(8,128)(2,1)} %constant.15.clone.t1_inv) | copy-start | bytes 196612
  28.2 5.9 %copy-start.6 = (bf16[256,128]{1,0:T(8,128)(2,1)S(1)}, bf16[256,128]{1,0:T(8,128)(2,1)}, u32[]{:S(2)}) copy-start(bf16[256,128]{1,0:T(8,128)(2,1)} %constant.12.clone.t1) | copy-start | bytes 196612
  28.2 5.9 %copy-start.7 = (bf16[128,128]{1,0:T(8,128)(2,1)S(1)}, bf16[128,128]{1,0:T(8,128)(2,1)}, u32[]{:S(2)}) copy-start(bf16[128,128]{1,0:T(8,128)(2,1)} %constant.17.clone.tw_s) | copy-start | bytes 98308
  28.2 5.9 %copy-start.8 = (bf16[128,128]{1,0:T(8,128)(2,1)S(1)}, bf16[128,128]{1,0:T(8,128)(2,1)}, u32[]{:S(2)}) copy-start(bf16[128,128]{1,0:T(8,128)(2,1)} %constant.16.clone.tw_c) | copy-start | bytes 98308
  34.2 24.0 %copy-start.9 = (f32[512]{0:T(512)S(1)}, f32[512]{0:T(512)}, u32[]{:S(2)}) copy-start(f32[512]{0:T(512)} %param.21) | copy-start | bytes 6148
  36.9 21.3 %copy-start.1 = (bf16[512,512]{1,0:T(8,128)(2,1)S(1)}, bf16[512,512]{1,0:T(8,128)(2,1)}, u32[]{:S(2)}) copy-start(bf16[512,512]{1,0:T(8,128)(2,1)} %stream_ref.1) | copy-start | bytes 1572868
  58.7 6.9 %collective-permute-start.10 = (f32[4,128]{1,0:T(4,128)S(1)}, f32[4,128]{1,0:T(4,128)S(1)}, u32[]{:S(2)}, u32[]{:S(2)}) collective-permute-start(f32[4,128]{1,0:T(4,128)S(1)} %get-tuple-element.35), channel_id=1, source_target_pairs={{0,4},{1,5},{2,6},{3,7},{4,0},{5,1},{6,2},{7,3},{8,12},{9,13},{10,... | collective-permute-start | bytes 6152 | tf_op jit(solution)/shard_map/ppermute | solution.py:467
  65.6 3.8 %collective-permute-start.13 = (f32[4,128]{1,0:T(4,128)S(1)}, f32[4,128]{1,0:T(4,128)S(1)}, u32[]{:S(2)}, u32[]{:S(2)}) collective-permute-start(f32[4,128]{1,0:T(4,128)S(1)} %add.3.refs_2_), channel_id=1, source_target_pairs={{0,3},{1,0},{2,1},{3,2},{4,7},{5,4},{6,5},{7,6},{8,11},{9,8},{10,9... | collective-permute-start | bytes 6152 | tf_op jit(solution)/shard_map/ppermute | solution.py:467
  68.3 3.9 %collective-permute-start.12 = (f32[4,128]{1,0:T(4,128)S(1)}, f32[4,128]{1,0:T(4,128)S(1)}, u32[]{:S(2)}, u32[]{:S(2)}) collective-permute-start(f32[4,128]{1,0:T(4,128)S(1)} %add.3.refs_2_), channel_id=1, source_target_pairs={{0,2},{1,3},{2,0},{3,1},{4,6},{5,7},{6,4},{7,5},{8,10},{9,11},{10,... | collective-permute-start | bytes 6152 | tf_op jit(solution)/shard_map/ppermute | solution.py:467
  68.7 3.6 %collective-permute-start.11 = (f32[4,128]{1,0:T(4,128)S(1)}, f32[4,128]{1,0:T(4,128)S(1)}, u32[]{:S(2)}, u32[]{:S(2)}) collective-permute-start(f32[4,128]{1,0:T(4,128)S(1)} %add.3.refs_2_), channel_id=1, source_target_pairs={{0,1},{1,2},{2,3},{3,0},{4,5},{5,6},{6,7},{7,4},{8,9},{9,10},{10,1... | collective-permute-start | bytes 6152 | tf_op jit(solution)/shard_map/ppermute | solution.py:467
